TPU v7x, 32 devices: a whole 2x2x4 slice. The times are simulated.
32 devices in a mesh: groups: 2 (over y), rep: 4 (over x, core), tp: 4 (over z).
Axes of the slice: x: 2, y: 2, z: 4, core: 2. Of those that a mesh axis runs over, the one named last changes fastest.
Arguments:
- tokens: bfloat16 [3072, 8192], P(('groups', 'rep', 'tp')), parts along dimension 0, may hold values from -6 to 6
- base_weight: bfloat16 [8192, 2048], P(None, 'tp'), may hold values from -0.0625 to 0.0625
- delta_codes: bfloat16 [32768, 2048], P(('groups', 'rep'), 'tp'), parts along dimension 0, may hold values from -4 to 4
- delta_scales: bfloat16 [256, 16], P(('groups', 'rep'), 'tp'), parts along dimension 0, may hold values from 0.0019989014 to 0.011962891
- replica_variant: int32 [8], P('groups'), parts along dimension 0, may hold values from 0 to 1
- block_home: int32 [4, 64], P('groups'), parts along dimension 0, may hold values from 0 to 127, as said below
Outputs:
- key_value: bfloat16 [3072, 2048], P(('groups', 'rep'), 'tp'), parts along dimension 0
There are 2 independent parts, one for each index of `groups`. A program takes and returns all parts, laid end to end along the dimension named above; an argument that names none is the same for every part. Nothing has to cross between parts.
Inputs may be any that keep to these rules, and one draw needn't show every extreme that they name: `block_home`: the entries are a permutation of 0 to 127; entry e stands for slot e % 32 of holder e // 32, that is rows e * 128 to (e + 1) * 128 - 1 of delta_codes. At most 24 blocks of one variant lie with one holder, and in every draw some holders hold exactly 24 blocks of a variant.
All inputs are finite; a program needn't handle non-finite values.
Results may differ from a plain program's by a relative error of at most 0.0049.
Values may be sent and summed in bfloat16 or wider, within the bound.
No kernel may reach another device: no remote copies, remote signals or barrier semaphores. Data moves between devices by JAX's collectives and lax.ppermute only.
A program may use at most 128 MiB of HBM per device.

v0:
```python
import jax
import jax.numpy as jnp
from jax import lax
from jax.sharding import PartitionSpec as P


def local(tokens, base_weight, delta_codes, delta_scales, replica_variant, block_home):
    holders = lax.axis_size("rep")
    holder_self = lax.axis_index("rep")
    variants = block_home.shape[0]
    blocks = block_home.shape[1]
    slots = blocks // 2
    capacity = 3 * blocks // (2 * holders)
    width = base_weight.shape[1]
    col_blocks = delta_scales.shape[1]
    block_size = width // col_blocks
    variant_hot = (
        replica_variant[:, None] == jnp.arange(variants, dtype=jnp.int32)[None, :]
    ).astype(jnp.int32)
    homes_each = jnp.sum(variant_hot[:, :, None] * block_home[None, :, :], axis=1)
    holder_each = homes_each // slots
    slot_each = homes_each % slots
    block_index = jnp.arange(blocks, dtype=jnp.int32)
    before = block_index[None, :] < block_index[:, None]
    same_holder = holder_each[:, :, None] == holder_each[:, None, :]
    rank_each = jnp.sum((same_holder & before[None, :, :]).astype(jnp.int32), axis=2)
    mine = holder_each == holder_self
    slot_index = jnp.arange(capacity, dtype=jnp.int32)
    picked = mine[:, None, :] & (rank_each[:, None, :] == slot_index[None, :, None])
    slot_send = jnp.sum(picked.astype(jnp.int32) * slot_each[:, None, :], axis=2)
    valid = jnp.any(picked, axis=2)
    code_store = delta_codes.reshape(slots, block_size, width)
    flat_slots = slot_send.reshape(-1)
    send_codes = code_store[flat_slots].reshape(holders, capacity, block_size, width)
    send_codes = jnp.where(valid[:, :, None, None], send_codes, jnp.zeros_like(send_codes))
    send_scales = delta_scales[flat_slots].reshape(holders, capacity, col_blocks)
    send_scales = jnp.where(valid[:, :, None], send_scales, jnp.zeros_like(send_scales))
    got_codes, got_scales = (
        lax.all_to_all(send_codes, "rep", split_axis=0, concat_axis=0, tiled=True),
        lax.all_to_all(send_scales, "rep", split_axis=0, concat_axis=0, tiled=True),
    )
    self_hot = (jnp.arange(holders, dtype=jnp.int32) == holder_self).astype(jnp.int32)
    source = jnp.sum(self_hot[:, None] * (holder_each * capacity + rank_each), axis=0)
    code_vals = got_codes.reshape(holders * capacity, block_size, width)[source].astype(jnp.float32)
    scale_vals = got_scales.reshape(holders * capacity, col_blocks)[source].astype(jnp.float32)
    scale_full = jnp.broadcast_to(
        scale_vals[:, None, :, None], (blocks, block_size, col_blocks, block_size)
    ).reshape(blocks, block_size, width)
    delta_full = (code_vals * scale_full).reshape(blocks * block_size, width)
    merged = (base_weight.astype(jnp.float32) + delta_full).astype(jnp.bfloat16)
    result = jnp.dot(
        lax.all_gather(tokens, "tp", axis=0, tiled=True), merged, preferred_element_type=jnp.float32
    )
    return result.astype(jnp.bfloat16)


def solution(mesh):
    in_specs = (
        P(("groups", "rep", "tp"), None),
        P(None, "tp"),
        P(("groups", "rep"), "tp"),
        P(("groups", "rep"), "tp"),
        P("groups"),
        P("groups", None),
    )
    out_specs = P(("groups", "rep"), "tp")
    return jax.shard_map(local, mesh=mesh, in_specs=in_specs, out_specs=out_specs, check_vma=False)
```

profile of v0, /device:TPU:0, one launch (start us, length us, event | category | flops | bytes accessed | tf_op | source)
XLA Modules:
  0.0 220.3 jit_solution(15624572698284385272)
XLA Ops:
  6.6 0.7 compare_convert_fusion.1
  7.2 0.8 multiply_reduce_fusion
  8.0 0.8 copy.13
  8.8 0.2 convert_reduce_fusion
  9.0 0.2 fusion.11
  9.2 0.2 select_reduce_fusion
  9.3 0.1 reshape.164
  9.4 0.7 gather_fusion.2
  10.1 0.1 copy.14
  10.2 0.6 broadcast_select_fusion.1
  10.8 4.2 %all-to-all-start.1 = ((bf16[4,24,4]{1,2,0:T(4,128)(2,1)}), bf16[4,24,4]{1,2,0:T(4,128)(2,1)S(1)}, u32[]{:S(2)}, u32[]{:S(2)}) async-start(bf16[4,24,4]{1,2,0:T(4,128)(2,1)} %broadcast_select_fusion.1), calls=%async_computation.1 | async-start | bytes 8192 | tf_op jit(solution)/shard_map/all_to_all | solution.py:40
  15.0 9.1 %gather_fusion = bf16[96,128,512]{2,1,0:T(8,128)(2,1)} fusion(bf16[32,128,512]{2,1,0:T(8,128)(2,1)} %bitcast.31, s32[1024]{0:T(1024)S(1)} %pad_clamp_fusion.1), kind=kCustom, calls=%fused_computation | custom fusion | bytes 25166208 | tf_op jit(solution)/shard_map/gather | solution.py:34
  24.1 10.7 %broadcast_select_fusion = bf16[4,24,128,512]{3,2,1,0:T(8,128)(2,1)} fusion(bf16[4,24,128,512]{3,2,1,0:T(8,128)(2,1)} %bitcast.30, pred[4,24]{1,0:T(4,128)(4,1)S(1)} %fusion.11), kind=kLoop, calls=%fused_computation.7 | loop fusion | flops 6291456 | bytes 25165920 | tf_op jit(solution)/shard_map/jit(_where)/select_n | solution.py:35
  34.8 0.0 all-to-all-done.1
  34.8 6.3 %all-to-all-start = ((bf16[4,24,128,512]{3,2,1,0:T(8,128)(2,1)}), bf16[4,24,128,512]{3,2,1,0:T(8,128)(2,1)}, u32[]{:S(2)}, u32[]{:S(2)}) async-start(bf16[4,24,128,512]{3,2,1,0:T(8,128)(2,1)} %broadcast_select_fusion), calls=%async_computation | async-start | bytes 25165824 | tf_op jit(solution)/shard_map/all_to_all | solution.py:39
  41.2 0.0 all-gather.2.cloned.1.call-start
  41.2 0.7 all-gather.2.cloned.1.call-update
  41.9 0.1 multiply_reduce_fusion.1
  42.0 0.1 copy.15
  42.1 0.6 gather_fusion.3
  42.8 136.5 %all-to-all-done = bf16[4,24,128,512]{3,2,1,0:T(8,128)(2,1)} async-done(((bf16[4,24,128,512]{3,2,1,0:T(8,128)(2,1)}), bf16[4,24,128,512]{3,2,1,0:T(8,128)(2,1)}, u32[]{:S(2)}, u32[]{:S(2)}) %all-to-all-start) | async-done | bytes 12582944 | tf_op jit(solution)/shard_map/all_to_all | solution.py:39
  179.3 10.1 %gather_fusion.1 = bf16[64,128,512]{2,1,0:T(8,128)(2,1)} fusion(bf16[96,128,512]{2,1,0:T(8,128)(2,1)} %bitcast.3, s32[1024]{0:T(1024)S(1)} %pad_clamp_fusion), kind=kCustom, calls=%fused_computation.1 | custom fusion | bytes 16777472 | tf_op jit(solution)/shard_map/gather | solution.py:44
  189.4 0.0 all-gather.2.cloned.1.call-done
  189.4 6.1 %broadcast_in_dim.23 = f32[64,128,4,128]{3,2,1,0:T(4,128)} broadcast(bf16[64,4]{1,0:T(8,128)(2,1)S(1)} %gather_fusion.3), dimensions={0,2} | broadcast | bytes 16777728 | tf_op jit(solution)/shard_map/broadcast_in_dim | solution.py:46
  195.4 17.1 %fusion.7 = bf16[384,512]{0,1:T(8,128)(2,1)S(1)} fusion(bf16[384,8192]{1,0:T(8,128)(2,1)} %all-gather.2.cloned.1.call-done, f32[1024,8,4,128]{3,2,1,0:T(4,128)} %bitcast.29, bf16[8192,512]{1,0:T(8,128)(2,1)} %bitcast.32, bf16[8192,512]{1,0:T(8,128)(2,1)} %param.7), kind=kOutput, calls=%fused_computation.10 | convolution fusion | flops 3242393600 | bytes 40239104 | tf_op jit(solution)/shard_map/dot_general | solution.py:51
  212.6 0.9 copy.16
  (8 shorter events, 0.1 us)
Async XLA Ops:
  10.8 24.0 %all-to-all-start.1 = ((bf16[4,24,4]{1,2,0:T(4,128)(2,1)}), bf16[4,24,4]{1,2,0:T(4,128)(2,1)S(1)}, u32[]{:S(2)}, u32[]{:S(2)}) async-start(bf16[4,24,4]{1,2,0:T(4,128)(2,1)} %broadcast_select_fusion.1), calls=%async_computation.1 | async-start | bytes 8192 | tf_op jit(solution)/shard_map/all_to_all | solution.py:40
  34.8 144.5 %all-to-all-start = ((bf16[4,24,128,512]{3,2,1,0:T(8,128)(2,1)}), bf16[4,24,128,512]{3,2,1,0:T(8,128)(2,1)}, u32[]{:S(2)}, u32[]{:S(2)}) async-start(bf16[4,24,128,512]{3,2,1,0:T(8,128)(2,1)} %broadcast_select_fusion), calls=%async_computation | async-start | bytes 25165824 | tf_op jit(solution)/shard_map/all_to_all | solution.py:39
  41.2 148.2 %all-gather.2.cloned.1.call-start = ((), (), s32[]{:S(2)}) async-start(), calls=%async_computation.2 | async-start | bytes 7864320 | tf_op jit(solution)/shard_map/all_gather | solution.py:52
Sparse Core Ops, SparseCore 0:
  43.6 117.6 all-gather.1
where the time goes:
time: 221 us; the launch traced here: 220 us
  waiting for transfers between devices  137 us (62%)
  local copies, waits for them, and re-layouts  28.6 us (13%)
  matrix products  17.1 us (8%)
  other arithmetic  13.4 us (6%)
  between operations  13.4 us (6%)
  starting transfers between devices  10.6 us (5%)
    all_to_all x1, waiting for transfers between devices, local(): lax.all_to_all(send_codes, 'rep', split_axis=0, concat_axis=0, tiled=True)  137 us
    dot_general x1, matrix products, local(): jnp.dot(lax.all_gather(tokens, 'tp', axis=0, tiled=True), merged, preferr...  17.1 us
    select_n x1, other arithmetic, local(): jnp.where(valid[:, :, None, None], send_codes, jnp.zeros_like(send_codes))  10.7 us
    gather x1, local copies, waits for them, and re-layouts, local(): got_codes.reshape(holders * capacity, block_size, width)[source]  10.1 us
    gather x1, local copies, waits for them, and re-layouts, local(): code_store[flat_slots].reshape(holders, capacity, block_size, width)  9.07 us
    all_to_all x1, starting transfers between devices, local(): lax.all_to_all(send_codes, 'rep', split_axis=0, concat_axis=0, tiled=True)  6.33 us
    broadcast_in_dim x1, local copies, waits for them, and re-layouts, local(): jnp.broadcast_to(scale_vals[:, None, :, None], (blocks, block_size, col_b...  6.05 us
  transfers between devices with their start and end apart: 3, of which 1 were waited for; matrix products, arithmetic and copies ran while one was open for 14% of the time, Pallas kernels for 0%

commit v1 on v0

v1 whole, which is shorter than its diff:
```python
import functools
import jax
import jax.numpy as jnp
from jax import lax
from jax.experimental import pallas as pl
from jax.experimental.pallas import tpu as pltpu
from jax.sharding import PartitionSpec as P

CORES = 2
CHUNK_BLOCKS = 8


def kernel(dims, me_ref, variant_ref, home_ref, scale_ref, base_ref, *refs):
    ranks, reps, block, slots, variants = dims
    token_refs = refs[: 2 * ranks - 1]
    own, rights, lefts = token_refs[0], token_refs[1:ranks], token_refs[ranks:]
    stores = refs[2 * ranks - 1 : 2 * ranks - 1 + reps]
    out_ref, token_buf, base_buf, code_buf, total, sems, code_sems = refs[2 * ranks - 1 + reps :]
    rows = own.shape[0]
    depth = own.shape[1]
    span = CHUNK_BLOCKS * block
    chunks = depth // span
    rank, rep = me_ref[0], me_ref[1]
    variant = variant_ref[rep]

    def base_copy(chunk):
        at = pl.ds(pl.multiple_of(chunk * span, span), span)
        return pltpu.make_async_copy(base_ref.at[at, :], base_buf.at[at, :], sems.at[chunk, ranks])

    def token_copy(chunk, hop, source):
        at = pl.ds(pl.multiple_of(chunk * span, span), span)
        row = pl.multiple_of(lax.rem(rank - hop + ranks, ranks) * rows, rows)
        return pltpu.make_async_copy(
            source.at[:, at], token_buf.at[pl.ds(row, rows), at], sems.at[chunk, hop]
        )

    def code_copy(chunk, index, source, slot):
        return pltpu.make_async_copy(
            source.at[pl.ds(pl.multiple_of(slot * block, block), block), :],
            code_buf.at[pl.ds(pl.multiple_of((chunk * CHUNK_BLOCKS + index) * block, block), block), :],
            code_sems.at[chunk, index],
        )

    @pl.loop(0, chunks)
    def _(chunk):
        base_copy(chunk).start()
        token_copy(chunk, 0, own).start()
        for hop in range(1, ranks):
            from_left = rank >= hop

            @pl.when(from_left)
            def _():
                token_copy(chunk, hop, rights[hop - 1]).start()

            @pl.when(jnp.logical_not(from_left))
            def _():
                token_copy(chunk, hop, lefts[ranks - hop - 1]).start()

        @pl.loop(0, CHUNK_BLOCKS)
        def _(index):
            home = home_ref[variant, chunk * CHUNK_BLOCKS + index]
            holder, slot = home // slots, home % slots
            place = (rep // CORES - holder // CORES + reps // CORES) % (reps // CORES)
            place = place * CORES + (rep % CORES + holder % CORES) % CORES
            for at in range(reps):

                @pl.when(place == at)
                def _():
                    code_copy(chunk, index, stores[at], slot).start()

    total[...] = jnp.zeros_like(total)

    @pl.loop(0, chunks)
    def _(chunk):
        base_copy(chunk).wait()
        for hop in range(ranks):
            token_copy(chunk, hop, own).wait()
        for index in range(CHUNK_BLOCKS):
            code_copy(chunk, index, stores[0], 0).wait()
        merged = []
        for index in range(CHUNK_BLOCKS):
            at = pl.ds(pl.multiple_of(chunk * span + index * block, block), block)
            home = home_ref[variant, chunk * CHUNK_BLOCKS + index]
            delta = code_buf[at, :].astype(jnp.float32) * scale_ref[pl.ds(home, 1), :]
            merged.append((base_buf[at, :].astype(jnp.float32) + delta).astype(jnp.bfloat16))
        at = pl.ds(pl.multiple_of(chunk * span, span), span)
        total[...] += jnp.dot(
            token_buf[:, at], jnp.concatenate(merged, axis=0), preferred_element_type=jnp.float32
        )

    out_ref[...] = total[...].astype(out_ref.dtype)


def local(tokens, base_weight, delta_codes, delta_scales, replica_variant, block_home):
    ranks, reps = lax.axis_size("tp"), lax.axis_size("rep")
    rank, rep = lax.axis_index("tp"), lax.axis_index("rep")
    variants, blocks = block_home.shape
    depth, width = base_weight.shape
    rows = tokens.shape[0]
    block = depth // blocks
    slots = delta_scales.shape[0]
    chips = reps // CORES

    rights, lefts = [tokens], [tokens]
    stores = [delta_codes]
    ring = [(i, (i + CORES) % reps) for i in range(reps)]
    swap = [(i, i // CORES * CORES + (i + 1) % CORES) for i in range(reps)]
    for hop in range(1, ranks):
        rights.append(lax.ppermute(rights[-1], "tp", [(i, i + 1) for i in range(hop - 1, ranks - 1)]))
        lefts.append(lax.ppermute(lefts[-1], "tp", [(i, i - 1) for i in range(1, ranks - hop + 1)]))
    for _ in range(1, chips):
        stores.append(lax.ppermute(stores[-1], "rep", ring))
    placed = []
    for store in stores:
        placed += [store, lax.ppermute(store, "rep", swap)]
    scales = lax.all_gather(delta_scales, "rep", axis=0, tiled=True).astype(jnp.float32)
    scales = jnp.repeat(scales, width // delta_scales.shape[1], axis=1)
    me = jnp.stack([rank, rep]).astype(jnp.int32)

    chunks = blocks // CHUNK_BLOCKS
    smem = pl.BlockSpec(memory_space=pltpu.SMEM)
    whole = pl.BlockSpec(memory_space=pltpu.VMEM)
    hbm = pl.BlockSpec(memory_space=pl.ANY)
    arrays = rights + lefts[1:] + placed
    return pl.pallas_call(
        functools.partial(kernel, (ranks, reps, block, slots, variants)),
        out_shape=jax.ShapeDtypeStruct((ranks * rows, width), jnp.bfloat16),
        in_specs=[smem, smem, smem, whole, hbm] + [hbm] * len(arrays),
        out_specs=whole,
        scratch_shapes=[
            pltpu.VMEM((ranks * rows, depth), jnp.bfloat16),
            pltpu.VMEM((depth, width), jnp.bfloat16),
            pltpu.VMEM((depth, width), jnp.bfloat16),
            pltpu.VMEM((ranks * rows, width), jnp.float32),
            pltpu.SemaphoreType.DMA((chunks, ranks + 1)),
            pltpu.SemaphoreType.DMA((chunks, CHUNK_BLOCKS)),
        ],
        compiler_params=pltpu.CompilerParams(vmem_limit_bytes=56 * 1024 * 1024),
        cost_estimate=pl.CostEstimate(
            flops=2 * ranks * rows * depth * width,
            bytes_accessed=2 * (2 * depth * width + ranks * rows * depth),
            transcendentals=0,
        ),
    )(me, replica_variant, block_home, scales, base_weight, *arrays)


def solution(mesh):
    in_specs = (
        P(("groups", "rep", "tp"), None),
        P(None, "tp"),
        P(("groups", "rep"), "tp"),
        P(("groups", "rep"), "tp"),
        P("groups"),
        P("groups", None),
    )
    out_specs = P(("groups", "rep"), "tp")
    return jax.shard_map(local, mesh=mesh, in_specs=in_specs, out_specs=out_specs, check_vma=False)
```

time: 221 us -> 187 us (0.85)
  local copies, waits for them, and re-layouts: 28.6 us -> 1.06 us
  matrix products: 17.1 us -> 0 us
  waiting for transfers between devices: 137 us -> 154 us
  between operations: 13.4 us -> 0.07 us
  other arithmetic: 13.4 us -> 0.66 us
  Pallas kernels: 0 us -> 11 us
  blocking collectives: 0 us -> 5.28 us
  starting transfers between devices: 10.6 us -> 14.1 us
    ppermute x0 -> x9, waiting for transfers between devices: none -> 154 us  [the longest x1 85.9 us: local(): stores.append(lax.ppermute(stores[-1], 'rep', ring))]
    all_to_all x2 -> x0, waiting for transfers between devices: 137 us -> none  [the longest x1 137 us: local(): lax.all_to_all(send_codes, 'rep', split_axis=0, concat_axis=0, tiled=True)]
    gather x4 -> x0, local copies, waits for them, and re-layouts: 20.5 us -> none  [the longest x1 10.1 us: local(): got_codes.reshape(holders * capacity, block_size, width)[source]]
    dot_general x1 -> x0, matrix products: 17.1 us -> none  [local(): jnp.dot(lax.all_gather(tokens, 'tp', axis=0, tiled=True), merged, preferr...]
    ppermute x0 -> x9, starting transfers between devices: none -> 14.1 us  [the longest x3 7.19 us: local(): lax.ppermute(rights[-1], 'tp', [(i, i + 1) for i in range(hop - 1, ranks...]
    select_n x5 -> x0, other arithmetic: 11.3 us -> none  [the longest x1 10.7 us: local(): jnp.where(valid[:, :, None, None], send_codes, jnp.zeros_like(send_codes))]
    pallas_call x0 -> x1, Pallas kernels: none -> 11 us  [local(): pl.pallas_call(functools.partial(kernel, (ranks, reps, block, slots, vari...]
    all_to_all x2 -> x0, starting transfers between devices: 10.5 us -> none  [the longest x1 6.33 us: local(): lax.all_to_all(send_codes, 'rep', split_axis=0, concat_axis=0, tiled=True)]
  transfers between devices with their start and end apart: 3 -> 9, of which waited for: 1 -> 3; matrix products, arithmetic and copies ran while one was open for 14% -> 1% of each run, Pallas kernels for 0% -> 0%
where the time goes in v1:
time: 187 us; the launch traced here: 186 us
  waiting for transfers between devices  154 us (82%)
  starting transfers between devices  14.1 us (8%)
  Pallas kernels  11 us (6%)
  blocking collectives  5.28 us (3%)
    ppermute x1, waiting for transfers between devices, local(): stores.append(lax.ppermute(stores[-1], 'rep', ring))  85.9 us
    ppermute x3, waiting for transfers between devices, local(): lax.ppermute(lefts[-1], 'tp', [(i, i - 1) for i in range(1, ranks - hop +...  68.2 us
    pallas_call x1, Pallas kernels, local(): pl.pallas_call(functools.partial(kernel, (ranks, reps, block, slots, vari...  11 us
    ppermute x3, starting transfers between devices, local(): lax.ppermute(rights[-1], 'tp', [(i, i + 1) for i in range(hop - 1, ranks...  7.19 us
    all_gather x1, blocking collectives, local(): lax.all_gather(delta_scales, 'rep', axis=0, tiled=True).astype(jnp.float32)  5.28 us
    ppermute x3, starting transfers between devices, local(): lax.ppermute(lefts[-1], 'tp', [(i, i - 1) for i in range(1, ranks - hop +...  3.85 us
  transfers between devices with their start and end apart: 9, of which 3 were waited for; matrix products, arithmetic and copies ran while one was open for 1% of the time, Pallas kernels for 0%

profile of v1, /device:TPU:0, one launch (start us, length us, event | category | flops | bytes accessed | tf_op | source)
XLA Modules:
  0.0 186.3 jit_solution(6011283413073369682)
XLA Ops:
  0.0 2.9 %collective-permute-start.7 = (bf16[4096,512]{1,0:T(8,128)(2,1)}, bf16[4096,512]{1,0:T(8,128)(2,1)}, u32[]{:S(2)}, u32[]{:S(2)}) collective-permute-start(bf16[4096,512]{1,0:T(8,128)(2,1)} %refs_7_.1), channel_id=1, source_target_pairs={{0,8},{4,12},{8,0},{12,4},{1,9},{5,13},{9,1},{13,5},{2,10},{6,14},... | collective-permute-start | bytes 12582920 | tf_op jit(solution)/shard_map/ppermute | solution.py:112
  2.9 3.6 %collective-permute-start = (bf16[96,8192]{1,0:T(8,128)(2,1)}, bf16[96,8192]{1,0:T(8,128)(2,1)S(1)}, u32[]{:S(2)}, u32[]{:S(2)}) collective-permute-start(bf16[96,8192]{1,0:T(8,128)(2,1)} %refs_0_.1), channel_id=1, source_target_pairs={{0,1},{1,2},{2,3},{4,5},{5,6},{6,7},{8,9},{9,10},{10,11},{12,13},{... | collective-permute-start | bytes 4718600 | tf_op jit(solution)/shard_map/ppermute | solution.py:109
  6.5 1.3 collective-permute-start.3
  7.8 0.1 collective-permute-start.6
  7.9 85.9 %collective-permute-done.7.refs_9_ = bf16[4096,512]{1,0:T(8,128)(2,1)} collective-permute-done((bf16[4096,512]{1,0:T(8,128)(2,1)}, bf16[4096,512]{1,0:T(8,128)(2,1)}, u32[]{:S(2)}, u32[]{:S(2)}) %collective-permute-start.7) | collective-permute-done | bytes 4194336 | tf_op jit(solution)/shard_map/ppermute | solution.py:112
  93.8 0.0 collective-permute-start.8
  93.8 0.0 collective-permute-done.refs_1_
  93.8 0.0 copy-start
  93.8 1.8 collective-permute-start.1
  95.6 0.0 collective-permute-done.3.refs_4_
  95.6 0.0 copy-start.1
  95.6 1.3 collective-permute-start.4
  96.9 0.0 collective-permute-done.1.refs_2_
  96.9 1.8 collective-permute-start.2
  98.8 38.3 %collective-permute-done.4.refs_5_ = bf16[96,8192]{1,0:T(8,128)(2,1)} collective-permute-done((bf16[96,8192]{1,0:T(8,128)(2,1)S(1)}, bf16[96,8192]{1,0:T(8,128)(2,1)}, u32[]{:S(2)}, u32[]{:S(2)}) %collective-permute-start.4) | collective-permute-done | bytes 1572896 | tf_op jit(solution)/shard_map/ppermute | solution.py:110
  137.1 1.3 collective-permute-start.5
  138.4 5.3 %all-gather = bf16[4,32,4]{1,2,0:T(4,128)(2,1)S(1)} all-gather(bf16[1,32,4]{1,2,0:T(4,128)(2,1)} %bitcast.11), channel_id=1, replica_groups=mesh['groups'=2,'rep'=4,'tp'=4] {'rep'}, dimensions={0}, use_global_device_ids=true | all-gather | bytes 1280 | tf_op jit(solution)/shard_map/all_gather | solution.py:116
  143.6 0.1 copy.11
  143.8 0.2 broadcast_in_dim.3
  143.9 0.7 copy.15
  144.7 0.7 pad_add_fusion.me_ref
  145.4 0.0 collective-permute-done.6.refs_8_
  145.4 0.0 collective-permute-done.2.refs_3_
  145.4 29.9 %collective-permute-done.5.refs_6_ = bf16[96,8192]{1,0:T(8,128)(2,1)} collective-permute-done((bf16[96,8192]{1,0:T(8,128)(2,1)}, bf16[96,8192]{1,0:T(8,128)(2,1)}, u32[]{:S(2)}, u32[]{:S(2)}) %collective-permute-start.5) | collective-permute-done | bytes 1572896 | tf_op jit(solution)/shard_map/ppermute | solution.py:110
  175.3 0.0 collective-permute-done.8.refs_10_
  175.3 0.0 copy-done
  175.3 0.0 copy-done.1
  175.3 11.0 %shard_map.64 = bf16[384,512]{1,0:T(8,128)(2,1)} custom-call(s32[2]{0:T(128)} %pad_add_fusion.me_ref, s32[4]{0:T(128)} %variant_ref.1, s32[2,64]{1,0:T(2,128)} %home_ref.1, f32[128,512]{1,0:T(8,128)} %bitcast.8, bf16[8192,512]{1,0:T(8,128)(2,1)} %base_ref.1, bf16[96,8192]{1,0:T(8,128)(2,1)} %refs_0_.1, bf16[96,8192]{1,0:T(8,128)(2,1)} %copy-done, ...), custom_call_target="tpu_custom_call" | custom-call | flops 3221225472 | bytes 23068672 | tf_op jit(solution)/shard_map/pallas_call | solution.py:125
Async XLA Ops:
  0.0 93.8 %collective-permute-start.7 = (bf16[4096,512]{1,0:T(8,128)(2,1)}, bf16[4096,512]{1,0:T(8,128)(2,1)}, u32[]{:S(2)}, u32[]{:S(2)}) collective-permute-start(bf16[4096,512]{1,0:T(8,128)(2,1)} %refs_7_.1), channel_id=1, source_target_pairs={{0,8},{4,12},{8,0},{12,4},{1,9},{5,13},{9,1},{13,5},{2,10},{6,14},... | collective-permute-start | bytes 12582920 | tf_op jit(solution)/shard_map/ppermute | solution.py:112
  2.9 90.9 %collective-permute-start = (bf16[96,8192]{1,0:T(8,128)(2,1)}, bf16[96,8192]{1,0:T(8,128)(2,1)S(1)}, u32[]{:S(2)}, u32[]{:S(2)}) collective-permute-start(bf16[96,8192]{1,0:T(8,128)(2,1)} %refs_0_.1), channel_id=1, source_target_pairs={{0,1},{1,2},{2,3},{4,5},{5,6},{6,7},{8,9},{9,10},{10,11},{12,13},{... | collective-permute-start | bytes 4718600 | tf_op jit(solution)/shard_map/ppermute | solution.py:109
  6.5 89.1 %collective-permute-start.3 = (bf16[96,8192]{1,0:T(8,128)(2,1)}, bf16[96,8192]{1,0:T(8,128)(2,1)S(1)}, u32[]{:S(2)}, u32[]{:S(2)}) collective-permute-start(bf16[96,8192]{1,0:T(8,128)(2,1)} %refs_0_.1), channel_id=1, source_target_pairs={{1,0},{2,1},{3,2},{5,4},{6,5},{7,6},{9,8},{10,9},{11,10},{13,12},{... | collective-permute-start | bytes 4718600 | tf_op jit(solution)/shard_map/ppermute | solution.py:110
  7.8 137.5 %collective-permute-start.6 = (bf16[4096,512]{1,0:T(8,128)(2,1)}, bf16[4096,512]{1,0:T(8,128)(2,1)}, u32[]{:S(2)}, u32[]{:S(2)}) collective-permute-start(bf16[4096,512]{1,0:T(8,128)(2,1)} %refs_7_.1), channel_id=1, source_target_pairs={{0,4},{4,0},{8,12},{12,8},{1,5},{5,1},{9,13},{13,9},{2,6},{6,2},{1... | collective-permute-start | bytes 12582920 | tf_op jit(solution)/shard_map/ppermute | solution.py:115
  93.8 81.5 %collective-permute-start.8 = (bf16[4096,512]{1,0:T(8,128)(2,1)}, bf16[4096,512]{1,0:T(8,128)(2,1)}, u32[]{:S(2)}, u32[]{:S(2)}) collective-permute-start(bf16[4096,512]{1,0:T(8,128)(2,1)} %collective-permute-done.7.refs_9_), channel_id=1, source_target_pairs={{0,4},{4,0},{8,12},{12,8},{1,5},{5,1},{9,13},{13,9},{2,6},{6,2},{1... | collective-permute-start | bytes 12582920 | tf_op jit(solution)/shard_map/ppermute | solution.py:115
  93.8 81.5 %copy-start = (bf16[96,8192]{1,0:T(8,128)(2,1)}, bf16[96,8192]{1,0:T(8,128)(2,1)S(1)}, u32[]{:S(2)}) copy-start(bf16[96,8192]{1,0:T(8,128)(2,1)S(1)} %collective-permute-done.refs_1_) | copy-start | bytes 4718596
  93.8 3.1 %collective-permute-start.1 = (bf16[96,8192]{1,0:T(8,128)(2,1)S(1)}, bf16[96,8192]{1,0:T(8,128)(2,1)}, u32[]{:S(2)}, u32[]{:S(2)}) collective-permute-start(bf16[96,8192]{1,0:T(8,128)(2,1)S(1)} %collective-permute-done.refs_1_), channel_id=1, source_target_pairs={{1,2},{2,3},{5,6},{6,7},{9,10},{10,11},{13,14},{14,15},{17,18},{18... | collective-permute-start | bytes 4718600 | tf_op jit(solution)/shard_map/ppermute | solution.py:109
  95.6 79.6 %copy-start.1 = (bf16[96,8192]{1,0:T(8,128)(2,1)}, bf16[96,8192]{1,0:T(8,128)(2,1)S(1)}, u32[]{:S(2)}) copy-start(bf16[96,8192]{1,0:T(8,128)(2,1)S(1)} %collective-permute-done.3.refs_4_) | copy-start | bytes 4718596
  95.6 41.4 %collective-permute-start.4 = (bf16[96,8192]{1,0:T(8,128)(2,1)S(1)}, bf16[96,8192]{1,0:T(8,128)(2,1)}, u32[]{:S(2)}, u32[]{:S(2)}) collective-permute-start(bf16[96,8192]{1,0:T(8,128)(2,1)S(1)} %collective-permute-done.3.refs_4_), channel_id=1, source_target_pairs={{1,0},{2,1},{5,4},{6,5},{9,8},{10,9},{13,12},{14,13},{17,16},{18,1... | collective-permute-start | bytes 4718600 | tf_op jit(solution)/shard_map/ppermute | solution.py:110
  96.9 48.4 %collective-permute-start.2 = (bf16[96,8192]{1,0:T(8,128)(2,1)}, bf16[96,8192]{1,0:T(8,128)(2,1)}, u32[]{:S(2)}, u32[]{:S(2)}) collective-permute-start(bf16[96,8192]{1,0:T(8,128)(2,1)} %collective-permute-done.1.refs_2_), channel_id=1, source_target_pairs={{2,3},{6,7},{10,11},{14,15},{18,19},{22,23},{26,27},{30,31}} | collective-permute-start | bytes 4718600 | tf_op jit(solution)/shard_map/ppermute | solution.py:109
  137.1 38.2 %collective-permute-start.5 = (bf16[96,8192]{1,0:T(8,128)(2,1)}, bf16[96,8192]{1,0:T(8,128)(2,1)}, u32[]{:S(2)}, u32[]{:S(2)}) collective-permute-start(bf16[96,8192]{1,0:T(8,128)(2,1)} %collective-permute-done.4.refs_5_), channel_id=1, source_target_pairs={{1,0},{5,4},{9,8},{13,12},{17,16},{21,20},{25,24},{29,28}} | collective-permute-start | bytes 4718600 | tf_op jit(solution)/shard_map/ppermute | solution.py:110

commit v2 on v1

--- a/solution.py
+++ b/solution.py
@@ -11,11 +11,12 @@
 
 
 def kernel(dims, me_ref, variant_ref, home_ref, scale_ref, base_ref, *refs):
-    ranks, reps, block, slots, variants = dims
+    ranks, reps, block, slots, cuts = dims
+    pieces = len(cuts) - 1
     token_refs = refs[: 2 * ranks - 1]
     own, rights, lefts = token_refs[0], token_refs[1:ranks], token_refs[ranks:]
-    stores = refs[2 * ranks - 1 : 2 * ranks - 1 + reps]
-    out_ref, token_buf, base_buf, code_buf, total, sems, code_sems = refs[2 * ranks - 1 + reps :]
+    stores = refs[2 * ranks - 1 : 2 * ranks - 1 + reps * pieces]
+    out_ref, token_buf, base_buf, code_buf, total, sems, code_sems = refs[2 * ranks - 1 + reps * pieces :]
     rows = own.shape[0]
     depth = own.shape[1]
     span = CHUNK_BLOCKS * block
@@ -63,10 +64,12 @@
             place = (rep // CORES - holder // CORES + reps // CORES) % (reps // CORES)
             place = place * CORES + (rep % CORES + holder % CORES) % CORES
             for at in range(reps):
+                for piece in range(pieces):
+                    low, high = cuts[piece] // block, cuts[piece + 1] // block
 
-                @pl.when(place == at)
-                def _():
-                    code_copy(chunk, index, stores[at], slot).start()
+                    @pl.when((place == at) & (slot >= low) & (slot < high))
+                    def _():
+                        code_copy(chunk, index, stores[at * pieces + piece], slot - low).start()
 
     total[...] = jnp.zeros_like(total)
 
@@ -101,18 +104,36 @@
     slots = delta_scales.shape[0]
     chips = reps // CORES
 
-    rights, lefts = [tokens], [tokens]
-    stores = [delta_codes]
     ring = [(i, (i + CORES) % reps) for i in range(reps)]
     swap = [(i, i // CORES * CORES + (i + 1) % CORES) for i in range(reps)]
-    for hop in range(1, ranks):
-        rights.append(lax.ppermute(rights[-1], "tp", [(i, i + 1) for i in range(hop - 1, ranks - 1)]))
-        lefts.append(lax.ppermute(lefts[-1], "tp", [(i, i - 1) for i in range(1, ranks - hop + 1)]))
-    for _ in range(1, chips):
-        stores.append(lax.ppermute(stores[-1], "rep", ring))
+    stages = ranks - 1
+    pieces = -(-stages // (chips - 1))
+    cuts = [slots * i // pieces * block for i in range(pieces + 1)]
+    held = [[delta_codes[cuts[i] : cuts[i + 1]] for i in range(pieces)]]
+    held += [[None] * pieces for _ in range(chips - 1)]
+    twin = [[None] * pieces for _ in range(chips)]
+    rights, lefts = [tokens], [tokens]
+    todo = [(hop, piece) for hop in range(1, chips) for piece in range(pieces)]
+    ready = [(0, piece) for piece in range(pieces)]
+    for stage in range(1, ranks):
+        due, todo = todo[: -(-len(todo) // (ranks - stage))], todo[-(-len(todo) // (ranks - stage)) :]
+        right = lax.ppermute(rights[-1], "tp", [(i, i + 1) for i in range(stage - 1, ranks - 1)])
+        left = lax.ppermute(lefts[-1], "tp", [(i, i - 1) for i in range(1, ranks - stage + 1)])
+        sent = [lax.ppermute(held[hop - 1][piece], "rep", ring) for hop, piece in due]
+        twins = [lax.ppermute(held[hop][piece], "rep", swap) for hop, piece in ready]
+        right, left, sent, twins = lax.optimization_barrier((right, left, sent, twins))
+        rights.append(right)
+        lefts.append(left)
+        for (hop, piece), value in zip(due, sent):
+            held[hop][piece] = value
+        for (hop, piece), value in zip(ready, twins):
+            twin[hop][piece] = value
+        ready = due
+    for hop, piece in ready:
+        twin[hop][piece] = lax.ppermute(held[hop][piece], "rep", swap)
     placed = []
-    for store in stores:
-        placed += [store, lax.ppermute(store, "rep", swap)]
+    for hop in range(chips):
+        placed += held[hop] + twin[hop]
     scales = lax.all_gather(delta_scales, "rep", axis=0, tiled=True).astype(jnp.float32)
     scales = jnp.repeat(scales, width // delta_scales.shape[1], axis=1)
     me = jnp.stack([rank, rep]).astype(jnp.int32)
@@ -123,7 +144,7 @@
     hbm = pl.BlockSpec(memory_space=pl.ANY)
     arrays = rights + lefts[1:] + placed
     return pl.pallas_call(
-        functools.partial(kernel, (ranks, reps, block, slots, variants)),
+        functools.partial(kernel, (ranks, reps, block, slots, tuple(cuts))),
         out_shape=jax.ShapeDtypeStruct((ranks * rows, width), jnp.bfloat16),
         in_specs=[smem, smem, smem, whole, hbm] + [hbm] * len(arrays),
         out_specs=whole,

time: 187 us -> 143 us (0.76)
  waiting for transfers between devices: 154 us -> 100 us
  local copies, waits for them, and re-layouts: 1.06 us -> 8.9 us
    ppermute x9 -> x15, waiting for transfers between devices: 154 us -> 100 us  [the longest x3 90.8 us: local(): lax.ppermute(held[hop - 1][piece], 'rep', ring)]
    unnamed x5 -> x37, local copies, waits for them, and re-layouts: 0.75 us -> 5.09 us
    slice x0 -> x2, local copies, waits for them, and re-layouts: none -> 3.51 us  [local(): held = [[delta_codes[cuts[i]:cuts[i + 1]] for i in range(pieces)]]]
    ppermute x9 -> x15, starting transfers between devices: 14.1 us -> 15.9 us  [the longest x3 6.25 us: local(): lax.ppermute(rights[-1], 'tp', [(i, i + 1) for i in range(stage - 1, rank...]
  transfers between devices with their start and end apart: 9 -> 15, of which waited for: 3 -> 6; matrix products, arithmetic and copies ran while one was open for 1% -> 3% of each run, Pallas kernels for 0% -> 0%
where the time goes in v2:
time: 143 us
  waiting for transfers between devices  100 us (70%)
  starting transfers between devices  15.9 us (11%)
  Pallas kernels  11.9 us (8%)
  local copies, waits for them, and re-layouts  8.9 us (6%)
  blocking collectives  5.06 us (4%)
    ppermute x3, waiting for transfers between devices, local(): lax.ppermute(held[hop - 1][piece], 'rep', ring)  90.8 us
    pallas_call x1, Pallas kernels, local(): pl.pallas_call(functools.partial(kernel, (ranks, reps, block, slots, tupl...  11.9 us
    ppermute x3, waiting for transfers between devices, local(): lax.ppermute(lefts[-1], 'tp', [(i, i - 1) for i in range(1, ranks - stage...  9.16 us
    ppermute x3, starting transfers between devices, local(): lax.ppermute(rights[-1], 'tp', [(i, i + 1) for i in range(stage - 1, rank...  6.25 us
    unnamed x37, local copies, waits for them, and re-layouts  5.09 us
    all_gather x1, blocking collectives, local(): lax.all_gather(delta_scales, 'rep', axis=0, tiled=True).astype(jnp.float32)  5.06 us
    ppermute x3, starting transfers between devices, local(): lax.ppermute(held[hop - 1][piece], 'rep', ring)  4.66 us
    ppermute x3, starting transfers between devices, local(): lax.ppermute(lefts[-1], 'tp', [(i, i - 1) for i in range(1, ranks - stage...  3.88 us
  transfers between devices with their start and end apart: 15, of which 6 were waited for; matrix products, arithmetic and copies ran while one was open for 3% of the time, Pallas kernels for 0%

profile of v2, /device:TPU:0, one launch (start us, length us, event | category | flops | bytes accessed | tf_op | source)
XLA Modules:
  0.0 142.6 jit_solution(16870225449387376352)
XLA Ops:
  0.0 1.5 %slice.9.refs_7_ = bf16[1280,512]{1,0:T(8,128)(2,1)S(1)} slice(bf16[4096,512]{1,0:T(8,128)(2,1)} %param.8), slice={[0:1280], [0:512]} | slice | bytes 2621440 | tf_op jit(solution)/shard_map/slice | solution.py:112
  1.5 0.0 copy-start.17
  1.5 0.5 collective-permute-start.3
  2.1 4.7 %collective-permute-start = (bf16[96,8192]{1,0:T(8,128)(2,1)S(1)}, bf16[96,8192]{1,0:T(8,128)(2,1)S(1)}, u32[]{:S(2)}, u32[]{:S(2)}) collective-permute-start(bf16[96,8192]{1,0:T(8,128)(2,1)S(1)} %copy-done.3), channel_id=1, source_target_pairs={{0,1},{1,2},{2,3},{4,5},{5,6},{6,7},{8,9},{9,10},{10,11},{12,13},{... | collective-permute-start | bytes 4718600 | tf_op jit(solution)/shard_map/ppermute | solution.py:120
  6.8 1.3 collective-permute-start.1
  8.1 2.0 %fusion = (bf16[1408,512]{1,0:T(8,128)(2,1)S(1)}, bf16[1408,512]{1,0:T(8,128)(2,1)S(1)}) fusion(bf16[4096,512]{1,0:T(8,128)(2,1)} %param.8), kind=kLoop, calls=%fused_computation.2 | loop fusion | bytes 5767168 | tf_op jit(solution)/shard_map/slice | solution.py:112
  10.1 0.1 collective-permute-start.5
  10.3 0.5 collective-permute-start.4
  10.7 1.6 %collective-permute-start.2 = (bf16[1280,512]{1,0:T(8,128)(2,1)S(1)}, bf16[1280,512]{1,0:T(8,128)(2,1)S(1)}, u32[]{:S(2)}, u32[]{:S(2)}) collective-permute-start(bf16[1280,512]{1,0:T(8,128)(2,1)S(1)} %slice.9.refs_7_), channel_id=1, source_target_pairs={{0,8},{4,12},{8,0},{12,4},{1,9},{5,13},{9,1},{13,5},{2,10},{6,14},... | collective-permute-start | bytes 3932168 | tf_op jit(solution)/shard_map/ppermute | solution.py:122
  12.3 29.3 %collective-permute-done.2.refs_13_ = bf16[1280,512]{1,0:T(8,128)(2,1)S(1)} collective-permute-done((bf16[1280,512]{1,0:T(8,128)(2,1)S(1)}, bf16[1280,512]{1,0:T(8,128)(2,1)S(1)}, u32[]{:S(2)}, u32[]{:S(2)}) %collective-permute-start.2) | collective-permute-done | bytes 1310752 | tf_op jit(solution)/shard_map/ppermute | solution.py:122
  41.6 0.0 collective-permute-done.4.refs_11_
  41.6 1.5 %copy-done.10 = bf16[1408,512]{1,0:T(8,128)(2,1)} copy-done((bf16[1408,512]{1,0:T(8,128)(2,1)}, bf16[1408,512]{1,0:T(8,128)(2,1)S(1)}, u32[]{:S(2)}) %copy-start.10) | copy-done | bytes 1441816
  43.1 0.4 copy-done.11
  43.5 1.5 %collective-permute-done.1.refs_4_ = bf16[96,8192]{1,0:T(8,128)(2,1)S(1)} collective-permute-done((bf16[96,8192]{1,0:T(8,128)(2,1)S(1)}, bf16[96,8192]{1,0:T(8,128)(2,1)S(1)}, u32[]{:S(2)}, u32[]{:S(2)}) %collective-permute-start.1) | collective-permute-done | bytes 1572896 | tf_op jit(solution)/shard_map/ppermute | solution.py:121
  45.1 0.8 collective-permute-start.6
  45.8 1.3 collective-permute-start.7
  47.1 1.6 %collective-permute-start.8 = (bf16[1408,512]{1,0:T(8,128)(2,1)S(1)}, bf16[1408,512]{1,0:T(8,128)(2,1)S(1)}, u32[]{:S(2)}, u32[]{:S(2)}) collective-permute-start(bf16[1408,512]{1,0:T(8,128)(2,1)S(1)} %get-tuple-element.34.refs_8_), channel_id=1, source_target_pairs={{0,8},{4,12},{8,0},{12,4},{1,9},{5,13},{9,1},{13,5},{2,10},{6,14},... | collective-permute-start | bytes 4325384 | tf_op jit(solution)/shard_map/ppermute | solution.py:122
  48.7 31.2 %collective-permute-done.8.refs_14_ = bf16[1408,512]{1,0:T(8,128)(2,1)S(1)} collective-permute-done((bf16[1408,512]{1,0:T(8,128)(2,1)S(1)}, bf16[1408,512]{1,0:T(8,128)(2,1)S(1)}, u32[]{:S(2)}, u32[]{:S(2)}) %collective-permute-start.8) | collective-permute-done | bytes 1441824 | tf_op jit(solution)/shard_map/ppermute | solution.py:122
  79.9 1.1 copy-done.16
  81.1 4.4 %collective-permute-done.7.refs_5_ = bf16[96,8192]{1,0:T(8,128)(2,1)S(1)} collective-permute-done((bf16[96,8192]{1,0:T(8,128)(2,1)S(1)}, bf16[96,8192]{1,0:T(8,128)(2,1)S(1)}, u32[]{:S(2)}, u32[]{:S(2)}) %collective-permute-start.7) | collective-permute-done | bytes 1572896 | tf_op jit(solution)/shard_map/ppermute | solution.py:121
  85.5 0.8 collective-permute-start.10
  86.3 1.3 collective-permute-start.11
  87.6 1.6 %collective-permute-start.12 = (bf16[1408,512]{1,0:T(8,128)(2,1)S(1)}, bf16[1408,512]{1,0:T(8,128)(2,1)}, u32[]{:S(2)}, u32[]{:S(2)}) collective-permute-start(bf16[1408,512]{1,0:T(8,128)(2,1)S(1)} %get-tuple-element.33.refs_9_), channel_id=1, source_target_pairs={{0,8},{4,12},{8,0},{12,4},{1,9},{5,13},{9,1},{13,5},{2,10},{6,14},... | collective-permute-start | bytes 4325384 | tf_op jit(solution)/shard_map/ppermute | solution.py:122
  89.1 30.4 %collective-permute-done.12.refs_15_ = bf16[1408,512]{1,0:T(8,128)(2,1)} collective-permute-done((bf16[1408,512]{1,0:T(8,128)(2,1)S(1)}, bf16[1408,512]{1,0:T(8,128)(2,1)}, u32[]{:S(2)}, u32[]{:S(2)}) %collective-permute-start.12) | collective-permute-done | bytes 1441824 | tf_op jit(solution)/shard_map/ppermute | solution.py:122
  119.6 3.2 %collective-permute-done.11.refs_6_ = bf16[96,8192]{1,0:T(8,128)(2,1)S(1)} collective-permute-done((bf16[96,8192]{1,0:T(8,128)(2,1)S(1)}, bf16[96,8192]{1,0:T(8,128)(2,1)S(1)}, u32[]{:S(2)}, u32[]{:S(2)}) %collective-permute-start.11) | collective-permute-done | bytes 1572896 | tf_op jit(solution)/shard_map/ppermute | solution.py:121
  122.8 1.2 copy-done.9
  124.0 5.1 %all-gather = bf16[4,32,4]{1,2,0:T(4,128)(2,1)S(1)} all-gather(bf16[1,32,4]{1,2,0:T(4,128)(2,1)S(1)} %bitcast.11), channel_id=1, replica_groups=mesh['groups'=2,'rep'=4,'tp'=4] {'rep'}, dimensions={0}, use_global_device_ids=true | all-gather | bytes 1280 | tf_op jit(solution)/shard_map/all_gather | solution.py:137
  129.0 0.1 copy.11
  129.1 0.2 broadcast_in_dim.3
  129.3 0.7 copy.15
  130.1 0.6 pad_add_fusion.me_ref
  130.7 11.9 %shard_map.64 = bf16[384,512]{1,0:T(8,128)(2,1)} custom-call(s32[2]{0:T(128)} %pad_add_fusion.me_ref, s32[4]{0:T(128)} %variant_ref.1, s32[2,64]{1,0:T(2,128)} %home_ref.1, f32[128,512]{1,0:T(8,128)} %bitcast.8, bf16[8192,512]{1,0:T(8,128)(2,1)} %base_ref.1, bf16[96,8192]{1,0:T(8,128)(2,1)} %refs_0_.1, bf16[96,8192]{1,0:T(8,128)(2,1)} %copy-done.4, ...), custom_call_target="tpu_custom_call" | custom-call | flops 3221225472 | bytes 23068672 | tf_op jit(solution)/shard_map/pallas_call | solution.py:146
  (42 shorter events, 0.1 us)
Async XLA Ops:
  0.0 2.1 %copy-start.3 = (bf16[96,8192]{1,0:T(8,128)(2,1)S(1)}, bf16[96,8192]{1,0:T(8,128)(2,1)}, u32[]{:S(2)}) copy-start(bf16[96,8192]{1,0:T(8,128)(2,1)} %refs_0_.1) | copy-start | bytes 4718596
  1.5 9.2 %copy-start.2 = (bf16[1280,512]{1,0:T(8,128)(2,1)}, bf16[1280,512]{1,0:T(8,128)(2,1)S(1)}, u32[]{:S(2)}) copy-start(bf16[1280,512]{1,0:T(8,128)(2,1)S(1)} %slice.9.refs_7_) | copy-start | bytes 3932164
  1.5 122.4 %copy-start.17 = (bf16[32,4]{0,1:T(4,128)(2,1)S(1)}, bf16[32,4]{0,1:T(4,128)(2,1)}, u32[]{:S(2)}) copy-start(bf16[32,4]{0,1:T(4,128)(2,1)} %param.9) | copy-start | bytes 772
  1.5 9.2 %collective-permute-start.3 = (bf16[1280,512]{1,0:T(8,128)(2,1)S(1)}, bf16[1280,512]{1,0:T(8,128)(2,1)S(1)}, u32[]{:S(2)}, u32[]{:S(2)}) collective-permute-start(bf16[1280,512]{1,0:T(8,128)(2,1)S(1)} %slice.9.refs_7_), channel_id=1, source_target_pairs={{0,4},{4,0},{8,12},{12,8},{1,5},{5,1},{9,13},{13,9},{2,6},{6,2},{1... | collective-permute-start | bytes 3932168 | tf_op jit(solution)/shard_map/ppermute | solution.py:123
  2.1 39.5 %collective-permute-start = (bf16[96,8192]{1,0:T(8,128)(2,1)S(1)}, bf16[96,8192]{1,0:T(8,128)(2,1)S(1)}, u32[]{:S(2)}, u32[]{:S(2)}) collective-permute-start(bf16[96,8192]{1,0:T(8,128)(2,1)S(1)} %copy-done.3), channel_id=1, source_target_pairs={{0,1},{1,2},{2,3},{4,5},{5,6},{6,7},{8,9},{9,10},{10,11},{12,13},{... | collective-permute-start | bytes 4718600 | tf_op jit(solution)/shard_map/ppermute | solution.py:120
  6.8 38.2 %collective-permute-start.1 = (bf16[96,8192]{1,0:T(8,128)(2,1)S(1)}, bf16[96,8192]{1,0:T(8,128)(2,1)S(1)}, u32[]{:S(2)}, u32[]{:S(2)}) collective-permute-start(bf16[96,8192]{1,0:T(8,128)(2,1)S(1)} %copy-done.3), channel_id=1, source_target_pairs={{1,0},{2,1},{3,2},{5,4},{6,5},{7,6},{9,8},{10,9},{11,10},{13,12},{... | collective-permute-start | bytes 4718600 | tf_op jit(solution)/shard_map/ppermute | solution.py:121
  10.1 120.5 %copy-start = (bf16[1408,512]{1,0:T(8,128)(2,1)}, bf16[1408,512]{1,0:T(8,128)(2,1)S(1)}, u32[]{:S(2)}) copy-start(bf16[1408,512]{1,0:T(8,128)(2,1)S(1)} %get-tuple-element.33.refs_9_) | copy-start | bytes 4325380
  10.1 120.5 %copy-start.1 = (bf16[1408,512]{1,0:T(8,128)(2,1)}, bf16[1408,512]{1,0:T(8,128)(2,1)S(1)}, u32[]{:S(2)}) copy-start(bf16[1408,512]{1,0:T(8,128)(2,1)S(1)} %get-tuple-element.34.refs_8_) | copy-start | bytes 4325380
  10.1 31.4 %collective-permute-start.5 = (bf16[1408,512]{1,0:T(8,128)(2,1)S(1)}, bf16[1408,512]{1,0:T(8,128)(2,1)S(1)}, u32[]{:S(2)}, u32[]{:S(2)}) collective-permute-start(bf16[1408,512]{1,0:T(8,128)(2,1)S(1)} %get-tuple-element.33.refs_9_), channel_id=1, source_target_pairs={{0,4},{4,0},{8,12},{12,8},{1,5},{5,1},{9,13},{13,9},{2,6},{6,2},{1... | collective-permute-start | bytes 4325384 | tf_op jit(solution)/shard_map/ppermute | solution.py:123
  10.3 31.3 %collective-permute-start.4 = (bf16[1408,512]{1,0:T(8,128)(2,1)S(1)}, bf16[1408,512]{1,0:T(8,128)(2,1)S(1)}, u32[]{:S(2)}, u32[]{:S(2)}) collective-permute-start(bf16[1408,512]{1,0:T(8,128)(2,1)S(1)} %get-tuple-element.34.refs_8_), channel_id=1, source_target_pairs={{0,4},{4,0},{8,12},{12,8},{1,5},{5,1},{9,13},{13,9},{2,6},{6,2},{1... | collective-permute-start | bytes 4325384 | tf_op jit(solution)/shard_map/ppermute | solution.py:123
  10.7 112.0 %copy-start.14 = (bf16[1280,512]{1,0:T(8,128)(2,1)}, bf16[1280,512]{1,0:T(8,128)(2,1)S(1)}, u32[]{:S(2)}) copy-start(bf16[1280,512]{1,0:T(8,128)(2,1)S(1)} %collective-permute-done.3.refs_10_) | copy-start | bytes 3932164
  10.7 30.8 %collective-permute-start.2 = (bf16[1280,512]{1,0:T(8,128)(2,1)S(1)}, bf16[1280,512]{1,0:T(8,128)(2,1)S(1)}, u32[]{:S(2)}, u32[]{:S(2)}) collective-permute-start(bf16[1280,512]{1,0:T(8,128)(2,1)S(1)} %slice.9.refs_7_), channel_id=1, source_target_pairs={{0,8},{4,12},{8,0},{12,4},{1,9},{5,13},{9,1},{13,5},{2,10},{6,14},... | collective-permute-start | bytes 3932168 | tf_op jit(solution)/shard_map/ppermute | solution.py:122
  41.5 38.3 %copy-start.15 = (bf16[1280,512]{1,0:T(8,128)(2,1)}, bf16[1280,512]{1,0:T(8,128)(2,1)S(1)}, u32[]{:S(2)}) copy-start(bf16[1280,512]{1,0:T(8,128)(2,1)S(1)} %collective-permute-done.2.refs_13_) | copy-start | bytes 3932164
  41.6 1.6 %copy-start.10 = (bf16[1408,512]{1,0:T(8,128)(2,1)}, bf16[1408,512]{1,0:T(8,128)(2,1)S(1)}, u32[]{:S(2)}) copy-start(bf16[1408,512]{1,0:T(8,128)(2,1)S(1)} %collective-permute-done.5.refs_12_) | copy-start | bytes 4325380
  41.6 2.0 %copy-start.11 = (bf16[1408,512]{1,0:T(8,128)(2,1)}, bf16[1408,512]{1,0:T(8,128)(2,1)S(1)}, u32[]{:S(2)}) copy-start(bf16[1408,512]{1,0:T(8,128)(2,1)S(1)} %collective-permute-done.4.refs_11_) | copy-start | bytes 4325380
  43.5 76.0 %copy-start.4 = (bf16[96,8192]{1,0:T(8,128)(2,1)}, bf16[96,8192]{1,0:T(8,128)(2,1)S(1)}, u32[]{:S(2)}) copy-start(bf16[96,8192]{1,0:T(8,128)(2,1)S(1)} %collective-permute-done.refs_1_) | copy-start | bytes 4718596
  45.1 74.4 %copy-start.5 = (bf16[96,8192]{1,0:T(8,128)(2,1)}, bf16[96,8192]{1,0:T(8,128)(2,1)S(1)}, u32[]{:S(2)}) copy-start(bf16[96,8192]{1,0:T(8,128)(2,1)S(1)} %collective-permute-done.1.refs_4_) | copy-start | bytes 4718596
  45.1 34.8 %collective-permute-start.6 = (bf16[96,8192]{1,0:T(8,128)(2,1)S(1)}, bf16[96,8192]{1,0:T(8,128)(2,1)S(1)}, u32[]{:S(2)}, u32[]{:S(2)}) collective-permute-start(bf16[96,8192]{1,0:T(8,128)(2,1)S(1)} %collective-permute-done.refs_1_), channel_id=1, source_target_pairs={{1,2},{2,3},{5,6},{6,7},{9,10},{10,11},{13,14},{14,15},{17,18},{18... | collective-permute-start | bytes 4718600 | tf_op jit(solution)/shard_map/ppermute | solution.py:120
  45.8 39.7 %collective-permute-start.7 = (bf16[96,8192]{1,0:T(8,128)(2,1)S(1)}, bf16[96,8192]{1,0:T(8,128)(2,1)S(1)}, u32[]{:S(2)}, u32[]{:S(2)}) collective-permute-start(bf16[96,8192]{1,0:T(8,128)(2,1)S(1)} %collective-permute-done.1.refs_4_), channel_id=1, source_target_pairs={{1,0},{2,1},{5,4},{6,5},{9,8},{10,9},{13,12},{14,13},{17,16},{18,1... | collective-permute-start | bytes 4718600 | tf_op jit(solution)/shard_map/ppermute | solution.py:121
  47.1 32.8 %collective-permute-start.8 = (bf16[1408,512]{1,0:T(8,128)(2,1)S(1)}, bf16[1408,512]{1,0:T(8,128)(2,1)S(1)}, u32[]{:S(2)}, u32[]{:S(2)}) collective-permute-start(bf16[1408,512]{1,0:T(8,128)(2,1)S(1)} %get-tuple-element.34.refs_8_), channel_id=1, source_target_pairs={{0,8},{4,12},{8,0},{12,4},{1,9},{5,13},{9,1},{13,5},{2,10},{6,14},... | collective-permute-start | bytes 4325384 | tf_op jit(solution)/shard_map/ppermute | solution.py:122
  48.7 31.2 %collective-permute-start.9 = (bf16[1280,512]{1,0:T(8,128)(2,1)S(1)}, bf16[1280,512]{1,0:T(8,128)(2,1)S(1)}, u32[]{:S(2)}, u32[]{:S(2)}) collective-permute-start(bf16[1280,512]{1,0:T(8,128)(2,1)S(1)} %collective-permute-done.2.refs_13_), channel_id=1, source_target_pairs={{0,4},{4,0},{8,12},{12,8},{1,5},{5,1},{9,13},{13,9},{2,6},{6,2},{1... | collective-permute-start | bytes 3932168 | tf_op jit(solution)/shard_map/ppermute | solution.py:123
  79.9 42.9 %copy-start.12 = (bf16[1408,512]{1,0:T(8,128)(2,1)}, bf16[1408,512]{1,0:T(8,128)(2,1)S(1)}, u32[]{:S(2)}) copy-start(bf16[1408,512]{1,0:T(8,128)(2,1)S(1)} %collective-permute-done.8.refs_14_) | copy-start | bytes 4325380
  81.1 38.5 %copy-start.6 = (bf16[96,8192]{1,0:T(8,128)(2,1)}, bf16[96,8192]{1,0:T(8,128)(2,1)S(1)}, u32[]{:S(2)}) copy-start(bf16[96,8192]{1,0:T(8,128)(2,1)S(1)} %collective-permute-done.6.refs_2_) | copy-start | bytes 4718596
  85.5 37.2 %copy-start.7 = (bf16[96,8192]{1,0:T(8,128)(2,1)}, bf16[96,8192]{1,0:T(8,128)(2,1)S(1)}, u32[]{:S(2)}) copy-start(bf16[96,8192]{1,0:T(8,128)(2,1)S(1)} %collective-permute-done.7.refs_5_) | copy-start | bytes 4718596
  85.5 34.0 %collective-permute-start.10 = (bf16[96,8192]{1,0:T(8,128)(2,1)S(1)}, bf16[96,8192]{1,0:T(8,128)(2,1)S(1)}, u32[]{:S(2)}, u32[]{:S(2)}) collective-permute-start(bf16[96,8192]{1,0:T(8,128)(2,1)S(1)} %collective-permute-done.6.refs_2_), channel_id=1, source_target_pairs={{2,3},{6,7},{10,11},{14,15},{18,19},{22,23},{26,27},{30,31}} | collective-permute-start | bytes 4718600 | tf_op jit(solution)/shard_map/ppermute | solution.py:120
  86.3 36.5 %collective-permute-start.11 = (bf16[96,8192]{1,0:T(8,128)(2,1)S(1)}, bf16[96,8192]{1,0:T(8,128)(2,1)S(1)}, u32[]{:S(2)}, u32[]{:S(2)}) collective-permute-start(bf16[96,8192]{1,0:T(8,128)(2,1)S(1)} %collective-permute-done.7.refs_5_), channel_id=1, source_target_pairs={{1,0},{5,4},{9,8},{13,12},{17,16},{21,20},{25,24},{29,28}} | collective-permute-start | bytes 4718600 | tf_op jit(solution)/shard_map/ppermute | solution.py:121
  87.6 31.9 %collective-permute-start.12 = (bf16[1408,512]{1,0:T(8,128)(2,1)S(1)}, bf16[1408,512]{1,0:T(8,128)(2,1)}, u32[]{:S(2)}, u32[]{:S(2)}) collective-permute-start(bf16[1408,512]{1,0:T(8,128)(2,1)S(1)} %get-tuple-element.33.refs_9_), channel_id=1, source_target_pairs={{0,8},{4,12},{8,0},{12,4},{1,9},{5,13},{9,1},{13,5},{2,10},{6,14},... | collective-permute-start | bytes 4325384 | tf_op jit(solution)/shard_map/ppermute | solution.py:122
  89.1 30.4 %collective-permute-start.13 = (bf16[1408,512]{1,0:T(8,128)(2,1)S(1)}, bf16[1408,512]{1,0:T(8,128)(2,1)S(1)}, u32[]{:S(2)}, u32[]{:S(2)}) collective-permute-start(bf16[1408,512]{1,0:T(8,128)(2,1)S(1)} %collective-permute-done.8.refs_14_), channel_id=1, source_target_pairs={{0,4},{4,0},{8,12},{12,8},{1,5},{5,1},{9,13},{13,9},{2,6},{6,2},{1... | collective-permute-start | bytes 4325384 | tf_op jit(solution)/shard_map/ppermute | solution.py:123
  119.5 3.3 %copy-start.13 = (bf16[1408,512]{1,0:T(8,128)(2,1)}, bf16[1408,512]{1,0:T(8,128)(2,1)S(1)}, u32[]{:S(2)}) copy-start(bf16[1408,512]{1,0:T(8,128)(2,1)S(1)} %collective-permute-done.13.refs_17_) | copy-start | bytes 4325380
  119.5 3.2 %copy-start.8 = (bf16[96,8192]{1,0:T(8,128)(2,1)}, bf16[96,8192]{1,0:T(8,128)(2,1)S(1)}, u32[]{:S(2)}) copy-start(bf16[96,8192]{1,0:T(8,128)(2,1)S(1)} %collective-permute-done.10.refs_3_) | copy-start | bytes 4718596
  122.7 1.2 copy-start.9
  122.7 7.9 %collective-permute-start.14 = (bf16[1408,512]{1,0:T(8,128)(2,1)}, bf16[1408,512]{1,0:T(8,128)(2,1)}, u32[]{:S(2)}, u32[]{:S(2)}) collective-permute-start(bf16[1408,512]{1,0:T(8,128)(2,1)} %collective-permute-done.12.refs_15_), channel_id=1, source_target_pairs={{0,4},{4,0},{8,12},{12,8},{1,5},{5,1},{9,13},{13,9},{2,6},{6,2},{1... | collective-permute-start | bytes 4325384 | tf_op jit(solution)/shard_map/ppermute | solution.py:133
  (1 other events, 1.2 us)

commit v3 on v2

--- a/solution.py
+++ b/solution.py
@@ -10,7 +10,7 @@
 CHUNK_BLOCKS = 8
 
 
-def kernel(dims, me_ref, variant_ref, home_ref, scale_ref, base_ref, *refs):
+def gather_kernel(dims, me_ref, variant_ref, home_ref, scale_ref, base_ref, *refs):
     ranks, reps, block, slots, cuts = dims
     pieces = len(cuts) - 1
     token_refs = refs[: 2 * ranks - 1]
@@ -94,7 +94,7 @@
     out_ref[...] = total[...].astype(out_ref.dtype)
 
 
-def local(tokens, base_weight, delta_codes, delta_scales, replica_variant, block_home):
+def gather_deltas(tokens, base_weight, delta_codes, delta_scales, replica_variant, block_home):
     ranks, reps = lax.axis_size("tp"), lax.axis_size("rep")
     rank, rep = lax.axis_index("tp"), lax.axis_index("rep")
     variants, blocks = block_home.shape
@@ -144,7 +144,7 @@
     hbm = pl.BlockSpec(memory_space=pl.ANY)
     arrays = rights + lefts[1:] + placed
     return pl.pallas_call(
-        functools.partial(kernel, (ranks, reps, block, slots, tuple(cuts))),
+        functools.partial(gather_kernel, (ranks, reps, block, slots, tuple(cuts))),
         out_shape=jax.ShapeDtypeStruct((ranks * rows, width), jnp.bfloat16),
         in_specs=[smem, smem, smem, whole, hbm] + [hbm] * len(arrays),
         out_specs=whole,
@@ -165,6 +165,346 @@
     )(me, replica_variant, block_home, scales, base_weight, *arrays)
 
 
+def survey(home_ref, slots, count_ref):
+    holders = count_ref.shape[0]
+    for holder in range(holders):
+        count_ref[holder] = 0
+
+    @pl.loop(0, home_ref.shape[1])
+    def _(index):
+        holder = lax.div(home_ref[0, index], slots)
+        count_ref[holder] = count_ref[holder] + 1
+
+
+def plan(variant, front, slots, share, count_ref, table_ref):
+    held = [
+        jnp.where(variant == 0, count_ref[holder], slots - count_ref[holder])
+        for holder in range(2 * CORES)
+    ]
+    for chip in range(2):
+        first, second = held[chip * CORES], held[chip * CORES + 1]
+        excess = jnp.maximum(first + second - share, 0)
+        move_first = jnp.minimum(jnp.maximum(first - share // CORES, 0), excess)
+        move_second = excess - move_first
+        keep_first, keep_second = first - move_first, second - move_second
+        table_ref[0, chip * CORES] = keep_first
+        table_ref[0, chip * CORES + 1] = keep_second
+        table_ref[1, chip * CORES] = front
+        table_ref[1, chip * CORES + 1] = keep_first
+        into = 1 - chip
+        kept_there = held[into * CORES] + held[into * CORES + 1]
+        table_ref[2, chip * CORES] = kept_there - keep_first
+        table_ref[2, chip * CORES + 1] = kept_there + move_first - keep_second
+
+
+def scan(home_ref, variant, front, slots, table_ref, rank_ref, visit):
+    for holder in range(2 * CORES):
+        rank_ref[holder] = 0
+
+    @pl.loop(0, home_ref.shape[1])
+    def _(index):
+        home = home_ref[variant, index]
+        holder = lax.div(home, slots)
+        slot = home - holder * slots
+        order = rank_ref[holder]
+        rank_ref[holder] = order + 1
+        core = lax.rem(holder, CORES)
+        here = lax.div(holder, CORES)
+        stays = order < table_ref[0, holder]
+        kept = jnp.where(order < front, core * front + order, table_ref[1, holder] + order)
+        place = jnp.where(stays, kept, table_ref[2, holder] + order)
+        chip = jnp.where(stays, here, 1 - here)
+        visit(index, home, holder, slot, order - table_ref[0, holder], chip, place)
+
+
+VMEM_LIMIT = 56 * 1024 * 1024
+SMEM = pl.BlockSpec(memory_space=pltpu.SMEM)
+VMEM = pl.BlockSpec(memory_space=pltpu.VMEM)
+HBM = pl.BlockSpec(memory_space=pl.ANY)
+
+
+def table_scratch():
+    return [
+        pltpu.SMEM((2 * CORES,), jnp.int32),
+        pltpu.SMEM((3, 2 * CORES), jnp.int32),
+        pltpu.SMEM((2 * CORES,), jnp.int32),
+    ]
+
+
+def split_kernel(dims, variant_ref, home_ref, tokens_ref, mine_ref, other_ref, count, table, rank, sems):
+    block, slots, share, front = dims
+    rep = lax.axis_index("rep")
+    chip = lax.div(rep, CORES)
+    variant = variant_ref[rep]
+    survey(home_ref, slots, count)
+    plan(variant, front, slots, share, count, table)
+
+    def visit(index, home, holder, slot, moved, place_chip, place):
+        source = tokens_ref.at[:, pl.ds(pl.multiple_of(index * block, block), block)]
+        at = pl.ds(pl.multiple_of(place * block, block), block)
+
+        @pl.when(place_chip == chip)
+        def _():
+            pltpu.make_async_copy(source, mine_ref.at[:, at], sems.at[0]).start()
+
+        @pl.when(place_chip != chip)
+        def _():
+            pltpu.make_async_copy(source, other_ref.at[:, at], sems.at[1]).start()
+
+    scan(home_ref, variant, front, slots, table, rank, visit)
+    half = tokens_ref.at[:, : share * block]
+    pltpu.make_async_copy(half, mine_ref, sems.at[0]).wait()
+    pltpu.make_async_copy(half, other_ref, sems.at[1]).wait()
+
+
+def moved_kernel(dims, home_ref, codes_ref, moved_ref, count, table, rank, sems):
+    block, slots, share, front = dims
+    rep = lax.axis_index("rep")
+    survey(home_ref, slots, count)
+    most = moved_ref.shape[0] // block
+
+    def copy(slot, moved):
+        return pltpu.make_async_copy(
+            codes_ref.at[pl.ds(pl.multiple_of(slot * block, block), block), :],
+            moved_ref.at[pl.ds(pl.multiple_of(moved * block, block), block), :],
+            sems.at[moved],
+        )
+
+    for variant in range(home_ref.shape[0]):
+        plan(variant, front, slots, share, count, table)
+
+        def visit(index, home, holder, slot, moved, place_chip, place):
+            @pl.when((holder == rep) & (moved >= 0) & (moved < most))
+            def _():
+                copy(slot, moved).start()
+
+        scan(home_ref, variant, front, slots, table, rank, visit)
+        leaving = rank[rep] - table[0, rep]
+
+        @pl.loop(0, jnp.minimum(leaving, most))
+        def _(moved):
+            copy(0, moved).wait()
+
+
+def merge_kernel(dims, variant_ref, home_ref, scale_ref, base_ref, own, twin, got, got_twin, out_ref, *scratch):
+    block, slots, share, front, chunk_blocks = dims
+    base_buf, code_buf, homes, count, table, rank, base_sems, code_sems = scratch
+    rep = lax.axis_index("rep")
+    chip, core = lax.div(rep, CORES), lax.rem(rep, CORES)
+    partner = (1 - chip) * CORES + core
+    survey(home_ref, slots, count)
+    chunks = 2 * share // chunk_blocks
+    span = chunk_blocks * block
+
+    for part, replica in enumerate((partner, rep)):
+        variant = variant_ref[replica]
+        plan(variant, front, slots, share, count, table)
+
+        def visit(index, home, holder, slot, moved, place_chip, place):
+            at = part * share + place
+            to = pl.ds(pl.multiple_of(at * block, block), block)
+
+            @pl.when(place_chip == chip)
+            def _():
+                homes[at] = home
+                pltpu.make_async_copy(
+                    base_ref.at[pl.ds(pl.multiple_of(index * block, block), block), :],
+                    base_buf.at[to, :],
+                    base_sems.at[at],
+                ).start()
+                near = lax.rem(holder, CORES) == core
+                local_chip = lax.div(holder, CORES) == chip
+                for store, row, chosen in (
+                    (own, slot, near & local_chip),
+                    (twin, slot, jnp.logical_not(near) & local_chip),
+                    (got, moved, near & jnp.logical_not(local_chip)),
+                    (got_twin, moved, jnp.logical_not(near | local_chip)),
+                ):
+
+                    @pl.when(chosen)
+                    def _():
+                        pltpu.make_async_copy(
+                            store.at[pl.ds(pl.multiple_of(row * block, block), block), :],
+                            code_buf.at[to, :],
+                            code_sems.at[at],
+                        ).start()
+
+        scan(home_ref, variant, front, slots, table, rank, visit)
+
+    @pl.loop(0, 2 * share)
+    def _(index):
+        at = pl.ds(pl.multiple_of(index * block, block), block)
+        pltpu.make_async_copy(base_ref.at[pl.ds(0, block), :], base_buf.at[at, :], base_sems.at[index]).wait()
+        pltpu.make_async_copy(own.at[pl.ds(0, block), :], code_buf.at[at, :], code_sems.at[index]).wait()
+        delta = code_buf[at, :].astype(jnp.float32) * scale_ref[pl.ds(homes[index], 1), :]
+        out_ref[at, :] = (base_buf[at, :].astype(jnp.float32) + delta).astype(jnp.bfloat16)
+
+
+def product_kernel(dims, weight_ref, *refs):
+    ranks, part, span = dims
+    token_refs = refs[: 2 * ranks - 1]
+    own, rights, lefts = token_refs[0], token_refs[1:ranks], token_refs[ranks:]
+    out_ref, token_buf, weight_buf, total, sems = refs[2 * ranks - 1 :]
+    rows, depth = own.shape
+    chunks = depth // span
+    rank = lax.axis_index("tp")
+
+    def weight_copy(chunk):
+        return pltpu.make_async_copy(
+            weight_ref.at[pl.ds(part * depth + chunk * span, span), :],
+            weight_buf.at[pl.ds(chunk * span, span), :],
+            sems.at[chunk, ranks],
+        )
+
+    def token_copy(chunk, hop, source):
+        at = pl.ds(chunk * span, span)
+        row = pl.multiple_of(lax.rem(rank - hop + ranks, ranks) * rows, rows)
+        return pltpu.make_async_copy(
+            source.at[:, at], token_buf.at[pl.ds(row, rows), at], sems.at[chunk, hop]
+        )
+
+    for chunk in range(chunks):
+        weight_copy(chunk).start()
+        token_copy(chunk, 0, own).start()
+        for hop in range(1, ranks):
+            from_left = rank >= hop
+
+            @pl.when(from_left)
+            def _():
+                token_copy(chunk, hop, rights[hop - 1]).start()
+
+            @pl.when(jnp.logical_not(from_left))
+            def _():
+                token_copy(chunk, hop, lefts[ranks - hop - 1]).start()
+
+    for chunk in range(chunks):
+        weight_copy(chunk).wait()
+        for hop in range(ranks):
+            token_copy(chunk, hop, own).wait()
+        at = pl.ds(chunk * span, span)
+        partial = jnp.dot(token_buf[:, at], weight_buf[at, :], preferred_element_type=jnp.float32)
+        if chunk == 0:
+            total[...] = partial
+        else:
+            total[...] += partial
+    out_ref[...] = total[...].astype(out_ref.dtype)
+
+
+def swap_tokens(tokens, base_weight, delta_codes, delta_scales, replica_variant, block_home):
+    ranks, reps = lax.axis_size("tp"), lax.axis_size("rep")
+    variants, blocks = block_home.shape
+    depth, width = base_weight.shape
+    rows = tokens.shape[0]
+    block = depth // blocks
+    slots = delta_scales.shape[0]
+    share = blocks // (reps // CORES)
+    most = blocks // (2 * reps)
+    front = 0
+    dims = (block, slots, share, front)
+    across = [(i, (i + CORES) % reps) for i in range(reps)]
+    swap = [(i, i // CORES * CORES + (i + 1) % CORES) for i in range(reps)]
+    params = pltpu.CompilerParams(vmem_limit_bytes=VMEM_LIMIT)
+
+    def tie(*values):
+        return lax.optimization_barrier(values)
+
+    def right(value, hop):
+        return lax.ppermute(value, "tp", [(i, i + 1) for i in range(hop - 1, ranks - 1)])
+
+    def left(value, hop):
+        return lax.ppermute(value, "tp", [(i, i - 1) for i in range(1, ranks - hop + 1)])
+
+    half = jax.ShapeDtypeStruct((rows, share * block), tokens.dtype)
+    mine, other = pl.pallas_call(
+        functools.partial(split_kernel, dims),
+        out_shape=[half, half],
+        in_specs=[SMEM, SMEM, HBM],
+        out_specs=[HBM, HBM],
+        scratch_shapes=table_scratch() + [pltpu.SemaphoreType.DMA((2,))],
+        compiler_params=params,
+    )(replica_variant, block_home, tokens)
+    other = lax.ppermute(other, "rep", across)
+    mine_right, mine_left = [mine, right(mine, 1)], [mine, left(mine, 1)]
+    twin = lax.ppermute(delta_codes, "rep", swap)
+    codes, _ = tie(delta_codes, mine)
+    moved = pl.pallas_call(
+        functools.partial(moved_kernel, dims),
+        out_shape=jax.ShapeDtypeStruct((most * block, width), codes.dtype),
+        in_specs=[SMEM, HBM],
+        out_specs=HBM,
+        scratch_shapes=table_scratch() + [pltpu.SemaphoreType.DMA((most,))],
+        compiler_params=params,
+    )(block_home, codes)
+    got = lax.ppermute(moved, "rep", across)
+    other_right, other_left = [other, right(other, 1)], [other, left(other, 1)]
+    scales, _ = tie(delta_scales, moved)
+    scales = lax.all_gather(scales, "rep", axis=0, tiled=True).astype(jnp.float32)
+    scales = jnp.repeat(scales, width // delta_scales.shape[1], axis=1)
+    for hop in range(2, ranks):
+        last = tie(mine_right[-1], mine_left[-1], other)
+        mine_right.append(right(last[0], hop))
+        mine_left.append(left(last[1], hop))
+        if hop == 2:
+            got, _ = tie(got, last[0])
+            got_twin = lax.ppermute(got, "rep", swap)
+        last = tie(other_right[-1], other_left[-1], last[0], got)
+        other_right.append(right(last[0], hop))
+        other_left.append(left(last[1], hop))
+        if hop == 2:
+            codes, twin, got, got_twin, _ = tie(codes, twin, got, got_twin, last[0])
+            weights = pl.pallas_call(
+                functools.partial(merge_kernel, dims + (CHUNK_BLOCKS,)),
+                out_shape=jax.ShapeDtypeStruct((2 * share * block, width), jnp.bfloat16),
+                in_specs=[SMEM, SMEM, VMEM] + [HBM] * 5,
+                out_specs=VMEM,
+                scratch_shapes=[
+                    pltpu.VMEM((2 * share * block, width), jnp.bfloat16),
+                    pltpu.VMEM((2 * share * block, width), jnp.bfloat16),
+                    pltpu.SMEM((2 * share,), jnp.int32),
+                ]
+                + table_scratch()
+                + [pltpu.SemaphoreType.DMA((2 * share,)), pltpu.SemaphoreType.DMA((2 * share,))],
+                compiler_params=params,
+                cost_estimate=pl.CostEstimate(
+                    flops=4 * share * block * width, bytes_accessed=12 * share * block * width, transcendentals=0
+                ),
+            )(replica_variant, block_home, scales, base_weight, codes, twin, got, got_twin)
+
+    def product(part, rights, lefts, kind):
+        span = CHUNK_BLOCKS * block
+        arrays = rights + lefts[1:]
+        return pl.pallas_call(
+            functools.partial(product_kernel, (ranks, part, span)),
+            out_shape=jax.ShapeDtypeStruct((ranks * rows, width), kind),
+            in_specs=[HBM] * (1 + len(arrays)),
+            out_specs=VMEM,
+            scratch_shapes=[
+                pltpu.VMEM((ranks * rows, share * block), jnp.bfloat16),
+                pltpu.VMEM((share * block, width), jnp.bfloat16),
+                pltpu.VMEM((ranks * rows, width), jnp.float32),
+                pltpu.SemaphoreType.DMA((share // CHUNK_BLOCKS, ranks + 1)),
+            ],
+            compiler_params=params,
+            cost_estimate=pl.CostEstimate(
+                flops=2 * ranks * rows * share * block * width,
+                bytes_accessed=2 * share * block * (width + ranks * rows),
+                transcendentals=0,
+            ),
+        )(weights, *arrays)
+
+    theirs = product(0, other_right, other_left, jnp.bfloat16)
+    back = lax.ppermute(theirs, "rep", across)
+    ours = product(1, mine_right, mine_left, jnp.float32)
+    return (ours + back.astype(jnp.float32)).astype(jnp.bfloat16)
+
+
+def local(tokens, base_weight, delta_codes, delta_scales, replica_variant, block_home):
+    chips = lax.axis_size("rep") // CORES
+    two = chips == 2 and block_home.shape[0] == 2 and lax.axis_size("tp") > 2
+    plan_of = swap_tokens if two else gather_deltas
+    return plan_of(tokens, base_weight, delta_codes, delta_scales, replica_variant, block_home)
+
+
 def solution(mesh):
     in_specs = (
         P(("groups", "rep", "tp"), None),

time: 143 us -> 205 us (1.43)
  Pallas kernels: 11.9 us -> 108 us
  waiting for transfers between devices: 100 us -> 59.4 us
  starting transfers between devices: 15.9 us -> 28.7 us
  local copies, waits for them, and re-layouts: 8.9 us -> 1.06 us
    pallas_call x1 -> x5, Pallas kernels: 11.9 us -> 108 us  [the longest x1 50.2 us: swap_tokens(): pl.pallas_call(functools.partial(split_kernel, dims), out_shape=[half, ha...]
    ppermute x15 -> x17, waiting for transfers between devices: 100 us -> 59.4 us  [the longest x6 43.6 us: left(): lax.ppermute(value, 'tp', [(i, i - 1) for i in range(1, ranks - hop + 1)])]
    ppermute x15 -> x17, starting transfers between devices: 15.9 us -> 28.7 us  [the longest x6 14.4 us: right(): lax.ppermute(value, 'tp', [(i, i + 1) for i in range(hop - 1, ranks - 1)])]
    unnamed x37 -> x17, local copies, waits for them, and re-layouts: 5.09 us -> 0.76 us
    slice x2 -> x0, local copies, waits for them, and re-layouts: 3.51 us -> none  [local(): held = [[delta_codes[cuts[i]:cuts[i + 1]] for i in range(pieces)]]]
  transfers between devices with their start and end apart: 15 -> 17, of which waited for: 6 -> 5; matrix products, arithmetic and copies ran while one was open for 3% -> 1% of each run, Pallas kernels for 0% -> 53%
where the time goes in v3:
time: 205 us
  Pallas kernels  108 us (53%)
  waiting for transfers between devices  59.4 us (29%)
  starting transfers between devices  28.7 us (14%)
  blocking collectives  5.07 us (2%)
    pallas_call x1, Pallas kernels, swap_tokens(): pl.pallas_call(functools.partial(split_kernel, dims), out_shape=[half, ha...  50.2 us
    ppermute x6, waiting for transfers between devices, left(): lax.ppermute(value, 'tp', [(i, i - 1) for i in range(1, ranks - hop + 1)])  43.6 us
    pallas_call x1, Pallas kernels, swap_tokens(): pl.pallas_call(functools.partial(moved_kernel, dims), out_shape=jax.Shape...  35 us
    ppermute x1, waiting for transfers between devices, swap_tokens(): got = lax.ppermute(moved, 'rep', across)  15.8 us
    ppermute x6, starting transfers between devices, right(): lax.ppermute(value, 'tp', [(i, i + 1) for i in range(hop - 1, ranks - 1)])  14.4 us
    pallas_call x1, Pallas kernels, swap_tokens(): pl.pallas_call(functools.partial(merge_kernel, dims + (CHUNK_BLOCKS,)), o...  13.6 us
    pallas_call x2, Pallas kernels, product(): pl.pallas_call(functools.partial(product_kernel, (ranks, part, span)), ou...  9.24 us
    ppermute x6, starting transfers between devices, left(): lax.ppermute(value, 'tp', [(i, i - 1) for i in range(1, ranks - hop + 1)])  7.72 us
  transfers between devices with their start and end apart: 17, of which 5 were waited for; matrix products, arithmetic and copies ran while one was open for 1% of the time, Pallas kernels for 53%

profile of v3, /device:TPU:0, one launch (start us, length us, event | category | flops | bytes accessed | tf_op | source)
XLA Modules:
  0.0 204.5 jit_solution(6432461591285064126)
XLA Ops:
  0.0 0.5 collective-permute-start
  0.5 50.2 %shard_map.64 = (bf16[96,4096]{1,0:T(8,128)(2,1)}, bf16[96,4096]{1,0:T(8,128)(2,1)}) custom-call(s32[4]{0:T(128)} %variant_ref.3, s32[2,64]{1,0:T(2,128)} %home_ref.5, bf16[96,8192]{1,0:T(8,128)(2,1)} %tokens_ref.1), custom_call_target="tpu_custom_call" | custom-call | tf_op jit(solution)/shard_map/pallas_call | solution.py:418
  50.7 2.7 %collective-permute-start.4 = (bf16[96,4096]{1,0:T(8,128)(2,1)}, bf16[96,4096]{1,0:T(8,128)(2,1)S(1)}, u32[]{:S(2)}, u32[]{:S(2)}) collective-permute-start(bf16[96,4096]{1,0:T(8,128)(2,1)} %get-tuple-element.25), channel_id=1, source_target_pairs={{0,8},{4,12},{8,0},{12,4},{1,9},{5,13},{9,1},{13,5},{2,10},{6,14},... | collective-permute-start | bytes 2359304 | tf_op jit(solution)/shard_map/ppermute | solution.py:426
  53.4 3.5 %collective-permute-start.2 = (bf16[96,4096]{1,0:T(8,128)(2,1)}, bf16[96,4096]{1,0:T(8,128)(2,1)S(1)}, u32[]{:S(2)}, u32[]{:S(2)}) collective-permute-start(bf16[96,4096]{1,0:T(8,128)(2,1)} %get-tuple-element.22.refs_0_), channel_id=1, source_target_pairs={{0,1},{1,2},{2,3},{4,5},{5,6},{6,7},{8,9},{9,10},{10,11},{12,13},{... | collective-permute-start | bytes 2359304 | tf_op jit(solution)/shard_map/ppermute | solution.py:412
  56.9 1.3 collective-permute-start.3
  58.2 35.0 %shard_map.65 = bf16[1024,512]{1,0:T(8,128)(2,1)} custom-call(s32[2,64]{1,0:T(2,128)} %home_ref.5, bf16[4096,512]{1,0:T(8,128)(2,1)} %own), custom_call_target="tpu_custom_call" | custom-call | tf_op jit(solution)/shard_map/pallas_call | solution.py:430
  93.2 1.8 collective-permute-start.1
  95.1 0.0 collective-permute-done.4.refs_0_
  95.1 4.6 %collective-permute-start.6 = (bf16[96,4096]{1,0:T(8,128)(2,1)S(1)}, bf16[96,4096]{1,0:T(8,128)(2,1)S(1)}, u32[]{:S(2)}, u32[]{:S(2)}) collective-permute-start(bf16[96,4096]{1,0:T(8,128)(2,1)S(1)} %collective-permute-done.4.refs_0_), channel_id=1, source_target_pairs={{0,1},{1,2},{2,3},{4,5},{5,6},{6,7},{8,9},{9,10},{10,11},{12,13},{... | collective-permute-start | bytes 2359304 | tf_op jit(solution)/shard_map/ppermute | solution.py:412
  99.7 1.3 collective-permute-start.7
  101.0 1.6 collective-permute-start.8
  102.6 15.8 %collective-permute-done.1.got = bf16[1024,512]{1,0:T(8,128)(2,1)S(1)} collective-permute-done((bf16[1024,512]{1,0:T(8,128)(2,1)}, bf16[1024,512]{1,0:T(8,128)(2,1)S(1)}, u32[]{:S(2)}, u32[]{:S(2)}) %collective-permute-start.1) | collective-permute-done | bytes 1048608 | tf_op jit(solution)/shard_map/ppermute | solution.py:438
  118.4 1.3 collective-permute-start.9
  119.7 0.1 collective-permute-done.7.refs_4_
  119.8 1.6 collective-permute-start.12
  121.3 1.3 collective-permute-start.13
  122.6 18.5 %collective-permute-done.9.refs_5_ = bf16[96,4096]{1,0:T(8,128)(2,1)} collective-permute-done((bf16[96,4096]{1,0:T(8,128)(2,1)S(1)}, bf16[96,4096]{1,0:T(8,128)(2,1)}, u32[]{:S(2)}, u32[]{:S(2)}) %collective-permute-start.9) | collective-permute-done | bytes 786464 | tf_op jit(solution)/shard_map/ppermute | solution.py:415
  141.2 16.6 %collective-permute-done.13.refs_5_ = bf16[96,4096]{1,0:T(8,128)(2,1)} collective-permute-done((bf16[96,4096]{1,0:T(8,128)(2,1)S(1)}, bf16[96,4096]{1,0:T(8,128)(2,1)}, u32[]{:S(2)}, u32[]{:S(2)}) %collective-permute-start.13) | collective-permute-done | bytes 786464 | tf_op jit(solution)/shard_map/ppermute | solution.py:415
  157.8 1.6 collective-permute-start.14
  159.4 1.3 collective-permute-start.15
  160.7 1.6 collective-permute-start.10
  162.3 1.3 collective-permute-start.11
  163.6 5.1 %all-gather = bf16[4,32,4]{1,2,0:T(4,128)(2,1)S(1)} all-gather(bf16[1,32,4]{1,2,0:T(4,128)(2,1)S(1)} %bitcast.9), channel_id=1, replica_groups=mesh['groups'=2,'rep'=4,'tp'=4] {'rep'}, dimensions={0}, use_global_device_ids=true | all-gather | bytes 1280 | tf_op jit(solution)/shard_map/all_gather | solution.py:441
  168.6 0.1 copy.11
  168.8 0.2 broadcast_in_dim.3
  168.9 0.7 copy.15
  169.7 13.6 %shard_map.66.weight_ref = bf16[8192,512]{1,0:T(8,128)(2,1)} custom-call(s32[4]{0:T(128)} %variant_ref.3, s32[2,64]{1,0:T(2,128)} %home_ref.5, f32[128,512]{1,0:T(8,128)} %bitcast.6, bf16[8192,512]{1,0:T(8,128)(2,1)} %base_ref.1, bf16[4096,512]{1,0:T(8,128)(2,1)} %own, bf16[4096,512]{1,0:T(8,128)(2,1)} %collective-permute-done.twin, ...), custom_call_target="tpu_custom_call" | custom-call | flops 8388608 | bytes 25165824 | tf_op jit(solution)/shard_map/pallas_call | solution.py:455
  183.3 4.6 %shard_map.68 = bf16[384,512]{1,0:T(8,128)(2,1)} custom-call(bf16[8192,512]{1,0:T(8,128)(2,1)} %shard_map.66.weight_ref, bf16[96,4096]{1,0:T(8,128)(2,1)} %copy-done.4, bf16[96,4096]{1,0:T(8,128)(2,1)} %copy-done.5, bf16[96,4096]{1,0:T(8,128)(2,1)} %collective-permute-done.12.refs_2_, bf16[96,4096]{1,0:T(8,128)(2,1)} %collective-permute-done.14.refs_3_, ...), custom_call_target="tpu_custom_call" | custom-call | flops 1610612736 | bytes 7340032 | tf_op jit(solution)/shard_map/pallas_call | solution.py:476
  187.8 1.6 collective-permute-start.16
  189.4 8.4 %collective-permute-done.11.refs_6_ = bf16[96,4096]{1,0:T(8,128)(2,1)} collective-permute-done((bf16[96,4096]{1,0:T(8,128)(2,1)}, bf16[96,4096]{1,0:T(8,128)(2,1)}, u32[]{:S(2)}, u32[]{:S(2)}) %collective-permute-start.11) | collective-permute-done | bytes 786464 | tf_op jit(solution)/shard_map/ppermute | solution.py:415
  197.8 4.7 %shard_map.67 = f32[384,512]{1,0:T(8,128)} custom-call(bf16[8192,512]{1,0:T(8,128)(2,1)} %shard_map.66.weight_ref, bf16[96,4096]{1,0:T(8,128)(2,1)} %get-tuple-element.22.refs_0_, bf16[96,4096]{1,0:T(8,128)(2,1)} %copy-done.2, bf16[96,4096]{1,0:T(8,128)(2,1)} %collective-permute-done.8.refs_2_, bf16[96,4096]{1,0:T(8,128)(2,1)} %collective-permute-done.10.refs_3_, ...), custom_call_target="tpu_custom_call" | custom-call | flops 1610612736 | bytes 7340032 | tf_op jit(solution)/shard_map/pallas_call | solution.py:476
  202.5 2.0 add_convert_fusion
  (28 shorter events, 0.1 us)
Async XLA Ops:
  0.0 163.6 %copy-start.7 = (bf16[32,4]{0,1:T(4,128)(2,1)S(1)}, bf16[32,4]{0,1:T(4,128)(2,1)}, u32[]{:S(2)}) copy-start(bf16[32,4]{0,1:T(4,128)(2,1)} %param.9) | copy-start | bytes 772
  0.0 141.2 %collective-permute-start = (bf16[4096,512]{1,0:T(8,128)(2,1)}, bf16[4096,512]{1,0:T(8,128)(2,1)}, u32[]{:S(2)}, u32[]{:S(2)}) collective-permute-start(bf16[4096,512]{1,0:T(8,128)(2,1)} %own), channel_id=1, source_target_pairs={{0,4},{4,0},{8,12},{12,8},{1,5},{5,1},{9,13},{13,9},{2,6},{6,2},{1... | collective-permute-start | bytes 12582920 | tf_op jit(solution)/shard_map/ppermute | solution.py:428
  50.7 44.4 %collective-permute-start.4 = (bf16[96,4096]{1,0:T(8,128)(2,1)}, bf16[96,4096]{1,0:T(8,128)(2,1)S(1)}, u32[]{:S(2)}, u32[]{:S(2)}) collective-permute-start(bf16[96,4096]{1,0:T(8,128)(2,1)} %get-tuple-element.25), channel_id=1, source_target_pairs={{0,8},{4,12},{8,0},{12,4},{1,9},{5,13},{9,1},{13,5},{2,10},{6,14},... | collective-permute-start | bytes 2359304 | tf_op jit(solution)/shard_map/ppermute | solution.py:426
  53.4 46.3 %collective-permute-start.2 = (bf16[96,4096]{1,0:T(8,128)(2,1)}, bf16[96,4096]{1,0:T(8,128)(2,1)S(1)}, u32[]{:S(2)}, u32[]{:S(2)}) collective-permute-start(bf16[96,4096]{1,0:T(8,128)(2,1)} %get-tuple-element.22.refs_0_), channel_id=1, source_target_pairs={{0,1},{1,2},{2,3},{4,5},{5,6},{6,7},{8,9},{9,10},{10,11},{12,13},{... | collective-permute-start | bytes 2359304 | tf_op jit(solution)/shard_map/ppermute | solution.py:412
  56.9 44.1 %collective-permute-start.3 = (bf16[96,4096]{1,0:T(8,128)(2,1)}, bf16[96,4096]{1,0:T(8,128)(2,1)S(1)}, u32[]{:S(2)}, u32[]{:S(2)}) collective-permute-start(bf16[96,4096]{1,0:T(8,128)(2,1)} %get-tuple-element.22.refs_0_), channel_id=1, source_target_pairs={{1,0},{2,1},{3,2},{5,4},{6,5},{7,6},{9,8},{10,9},{11,10},{13,12},{... | collective-permute-start | bytes 2359304 | tf_op jit(solution)/shard_map/ppermute | solution.py:415
  93.2 25.2 %collective-permute-start.1 = (bf16[1024,512]{1,0:T(8,128)(2,1)}, bf16[1024,512]{1,0:T(8,128)(2,1)S(1)}, u32[]{:S(2)}, u32[]{:S(2)}) collective-permute-start(bf16[1024,512]{1,0:T(8,128)(2,1)} %shard_map.65), channel_id=1, source_target_pairs={{0,8},{4,12},{8,0},{12,4},{1,9},{5,13},{9,1},{13,5},{2,10},{6,14},... | collective-permute-start | bytes 3145736 | tf_op jit(solution)/shard_map/ppermute | solution.py:438
  95.1 46.1 %copy-start.4 = (bf16[96,4096]{1,0:T(8,128)(2,1)}, bf16[96,4096]{1,0:T(8,128)(2,1)S(1)}, u32[]{:S(2)}) copy-start(bf16[96,4096]{1,0:T(8,128)(2,1)S(1)} %collective-permute-done.4.refs_0_) | copy-start | bytes 2359300
  95.1 23.3 %collective-permute-start.6 = (bf16[96,4096]{1,0:T(8,128)(2,1)S(1)}, bf16[96,4096]{1,0:T(8,128)(2,1)S(1)}, u32[]{:S(2)}, u32[]{:S(2)}) collective-permute-start(bf16[96,4096]{1,0:T(8,128)(2,1)S(1)} %collective-permute-done.4.refs_0_), channel_id=1, source_target_pairs={{0,1},{1,2},{2,3},{4,5},{5,6},{6,7},{8,9},{9,10},{10,11},{12,13},{... | collective-permute-start | bytes 2359304 | tf_op jit(solution)/shard_map/ppermute | solution.py:412
  99.7 83.6 %copy-start.2 = (bf16[96,4096]{1,0:T(8,128)(2,1)}, bf16[96,4096]{1,0:T(8,128)(2,1)S(1)}, u32[]{:S(2)}) copy-start(bf16[96,4096]{1,0:T(8,128)(2,1)S(1)} %collective-permute-done.2.refs_1_) | copy-start | bytes 2359300
  99.7 20.1 %collective-permute-start.7 = (bf16[96,4096]{1,0:T(8,128)(2,1)S(1)}, bf16[96,4096]{1,0:T(8,128)(2,1)S(1)}, u32[]{:S(2)}, u32[]{:S(2)}) collective-permute-start(bf16[96,4096]{1,0:T(8,128)(2,1)S(1)} %collective-permute-done.4.refs_0_), channel_id=1, source_target_pairs={{1,0},{2,1},{3,2},{5,4},{6,5},{7,6},{9,8},{10,9},{11,10},{13,12},{... | collective-permute-start | bytes 2359304 | tf_op jit(solution)/shard_map/ppermute | solution.py:415
  101.0 40.2 %copy-start.3 = (bf16[96,4096]{1,0:T(8,128)(2,1)}, bf16[96,4096]{1,0:T(8,128)(2,1)S(1)}, u32[]{:S(2)}) copy-start(bf16[96,4096]{1,0:T(8,128)(2,1)S(1)} %collective-permute-done.3.refs_4_) | copy-start | bytes 2359300
  101.0 20.3 %collective-permute-start.8 = (bf16[96,4096]{1,0:T(8,128)(2,1)S(1)}, bf16[96,4096]{1,0:T(8,128)(2,1)}, u32[]{:S(2)}, u32[]{:S(2)}) collective-permute-start(bf16[96,4096]{1,0:T(8,128)(2,1)S(1)} %collective-permute-done.2.refs_1_), channel_id=1, source_target_pairs={{1,2},{2,3},{5,6},{6,7},{9,10},{10,11},{13,14},{14,15},{17,18},{18... | collective-permute-start | bytes 2359304 | tf_op jit(solution)/shard_map/ppermute | solution.py:412
  118.4 51.3 %copy-start = (bf16[1024,512]{1,0:T(8,128)(2,1)}, bf16[1024,512]{1,0:T(8,128)(2,1)S(1)}, u32[]{:S(2)}) copy-start(bf16[1024,512]{1,0:T(8,128)(2,1)S(1)} %collective-permute-done.1.got) | copy-start | bytes 3145732
  118.4 22.8 %collective-permute-start.5 = (bf16[1024,512]{1,0:T(8,128)(2,1)S(1)}, bf16[1024,512]{1,0:T(8,128)(2,1)S(1)}, u32[]{:S(2)}, u32[]{:S(2)}) collective-permute-start(bf16[1024,512]{1,0:T(8,128)(2,1)S(1)} %collective-permute-done.1.got), channel_id=1, source_target_pairs={{0,4},{4,0},{8,12},{12,8},{1,5},{5,1},{9,13},{13,9},{2,6},{6,2},{1... | collective-permute-start | bytes 3145736 | tf_op jit(solution)/shard_map/ppermute | solution.py:449
  118.4 22.8 %copy-start.5 = (bf16[96,4096]{1,0:T(8,128)(2,1)}, bf16[96,4096]{1,0:T(8,128)(2,1)S(1)}, u32[]{:S(2)}) copy-start(bf16[96,4096]{1,0:T(8,128)(2,1)S(1)} %collective-permute-done.6.refs_1_) | copy-start | bytes 2359300
  118.4 22.8 %collective-permute-start.9 = (bf16[96,4096]{1,0:T(8,128)(2,1)S(1)}, bf16[96,4096]{1,0:T(8,128)(2,1)}, u32[]{:S(2)}, u32[]{:S(2)}) collective-permute-start(bf16[96,4096]{1,0:T(8,128)(2,1)S(1)} %collective-permute-done.3.refs_4_), channel_id=1, source_target_pairs={{1,0},{2,1},{5,4},{6,5},{9,8},{10,9},{13,12},{14,13},{17,16},{18,1... | collective-permute-start | bytes 2359304 | tf_op jit(solution)/shard_map/ppermute | solution.py:415
  119.8 38.1 %copy-start.6 = (bf16[96,4096]{1,0:T(8,128)(2,1)}, bf16[96,4096]{1,0:T(8,128)(2,1)S(1)}, u32[]{:S(2)}) copy-start(bf16[96,4096]{1,0:T(8,128)(2,1)S(1)} %collective-permute-done.7.refs_4_) | copy-start | bytes 2359300
  119.8 21.4 %collective-permute-start.12 = (bf16[96,4096]{1,0:T(8,128)(2,1)S(1)}, bf16[96,4096]{1,0:T(8,128)(2,1)}, u32[]{:S(2)}, u32[]{:S(2)}) collective-permute-start(bf16[96,4096]{1,0:T(8,128)(2,1)S(1)} %collective-permute-done.6.refs_1_), channel_id=1, source_target_pairs={{1,2},{2,3},{5,6},{6,7},{9,10},{10,11},{13,14},{14,15},{17,18},{18... | collective-permute-start | bytes 2359304 | tf_op jit(solution)/shard_map/ppermute | solution.py:412
  121.3 36.5 %collective-permute-start.13 = (bf16[96,4096]{1,0:T(8,128)(2,1)S(1)}, bf16[96,4096]{1,0:T(8,128)(2,1)}, u32[]{:S(2)}, u32[]{:S(2)}) collective-permute-start(bf16[96,4096]{1,0:T(8,128)(2,1)S(1)} %collective-permute-done.7.refs_4_), channel_id=1, source_target_pairs={{1,0},{2,1},{5,4},{6,5},{9,8},{10,9},{13,12},{14,13},{17,16},{18,1... | collective-permute-start | bytes 2359304 | tf_op jit(solution)/shard_map/ppermute | solution.py:415
  141.2 28.5 %copy-start.1 = (bf16[1024,512]{1,0:T(8,128)(2,1)}, bf16[1024,512]{1,0:T(8,128)(2,1)S(1)}, u32[]{:S(2)}) copy-start(bf16[1024,512]{1,0:T(8,128)(2,1)S(1)} %collective-permute-done.5.got_twin) | copy-start | bytes 3145732
  157.8 25.4 %collective-permute-start.14 = (bf16[96,4096]{1,0:T(8,128)(2,1)}, bf16[96,4096]{1,0:T(8,128)(2,1)}, u32[]{:S(2)}, u32[]{:S(2)}) collective-permute-start(bf16[96,4096]{1,0:T(8,128)(2,1)} %collective-permute-done.12.refs_2_), channel_id=1, source_target_pairs={{2,3},{6,7},{10,11},{14,15},{18,19},{22,23},{26,27},{30,31}} | collective-permute-start | bytes 2359304 | tf_op jit(solution)/shard_map/ppermute | solution.py:412
  159.4 23.9 %collective-permute-start.15 = (bf16[96,4096]{1,0:T(8,128)(2,1)}, bf16[96,4096]{1,0:T(8,128)(2,1)}, u32[]{:S(2)}, u32[]{:S(2)}) collective-permute-start(bf16[96,4096]{1,0:T(8,128)(2,1)} %collective-permute-done.13.refs_5_), channel_id=1, source_target_pairs={{1,0},{5,4},{9,8},{13,12},{17,16},{21,20},{25,24},{29,28}} | collective-permute-start | bytes 2359304 | tf_op jit(solution)/shard_map/ppermute | solution.py:415
  160.7 28.7 %collective-permute-start.10 = (bf16[96,4096]{1,0:T(8,128)(2,1)}, bf16[96,4096]{1,0:T(8,128)(2,1)}, u32[]{:S(2)}, u32[]{:S(2)}) collective-permute-start(bf16[96,4096]{1,0:T(8,128)(2,1)} %collective-permute-done.8.refs_2_), channel_id=1, source_target_pairs={{2,3},{6,7},{10,11},{14,15},{18,19},{22,23},{26,27},{30,31}} | collective-permute-start | bytes 2359304 | tf_op jit(solution)/shard_map/ppermute | solution.py:412
  162.3 35.6 %collective-permute-start.11 = (bf16[96,4096]{1,0:T(8,128)(2,1)}, bf16[96,4096]{1,0:T(8,128)(2,1)}, u32[]{:S(2)}, u32[]{:S(2)}) collective-permute-start(bf16[96,4096]{1,0:T(8,128)(2,1)} %collective-permute-done.9.refs_5_), channel_id=1, source_target_pairs={{1,0},{5,4},{9,8},{13,12},{17,16},{21,20},{25,24},{29,28}} | collective-permute-start | bytes 2359304 | tf_op jit(solution)/shard_map/ppermute | solution.py:415
  187.8 14.7 %collective-permute-start.16 = (bf16[384,512]{1,0:T(8,128)(2,1)}, bf16[384,512]{1,0:T(8,128)(2,1)S(1)}, u32[]{:S(2)}, u32[]{:S(2)}) collective-permute-start(bf16[384,512]{1,0:T(8,128)(2,1)} %shard_map.68), channel_id=1, source_target_pairs={{0,8},{4,12},{8,0},{12,4},{1,9},{5,13},{9,1},{13,5},{2,10},{6,14},... | collective-permute-start | bytes 1179656 | tf_op jit(solution)/shard_map/ppermute | solution.py:496

commit v4 on v1

v4 whole, which is shorter than its diff:
```python
import functools
import jax
import jax.numpy as jnp
from jax import lax
from jax.experimental import pallas as pl
from jax.experimental.pallas import tpu as pltpu
from jax.sharding import PartitionSpec as P

CORES = 2
CHUNK_BLOCKS = 8


CHAINS = 2
SMEM = pl.BlockSpec(memory_space=pltpu.SMEM)
VMEM = pl.BlockSpec(memory_space=pltpu.VMEM)
HBM = pl.BlockSpec(memory_space=pl.ANY)


def kernel(dims, variant_ref, home_ref, scale_ref, base_ref, *refs):
    ranks, reps, block, slots, cuts = dims
    pieces = len(cuts) - 1
    lanes = 2 * ranks - 1
    token_refs = [refs[chain * lanes : (chain + 1) * lanes] for chain in range(CHAINS)]
    store_refs = refs[CHAINS * lanes : CHAINS * lanes + CORES + (reps - CORES) * pieces]
    out_ref, token_buf, base_buf, code_buf, total, sems, code_sems = refs[-7:]
    rows, depth = token_refs[0][0].shape
    span = CHUNK_BLOCKS * block
    chunks = depth // span
    rank, rep = lax.axis_index("tp"), lax.axis_index("rep")
    chips = reps // CORES
    variant = variant_ref[rep]

    def base_copy(chunk):
        at = pl.ds(pl.multiple_of(chunk * span, span), span)
        return pltpu.make_async_copy(base_ref.at[at, :], base_buf.at[at, :], sems.at[chunk, CHAINS * ranks])

    def token_copy(chunk, chain, hop, source):
        at = pl.ds(pl.multiple_of(chunk * span, span), span)
        origin = lax.rem(rank - hop + ranks, ranks)
        row = pl.multiple_of((origin * CHAINS + chain) * rows, rows)
        return pltpu.make_async_copy(
            source.at[:, at], token_buf.at[pl.ds(row, rows), at], sems.at[chunk, chain * ranks + hop]
        )

    def code_copy(chunk, index, source, slot):
        return pltpu.make_async_copy(
            source.at[pl.ds(pl.multiple_of(slot * block, block), block), :],
            code_buf.at[pl.ds(pl.multiple_of((chunk * CHUNK_BLOCKS + index) * block, block), block), :],
            code_sems.at[chunk, index],
        )

    @pl.loop(0, chunks)
    def _(chunk):
        base_copy(chunk).start()
        for chain in range(CHAINS):
            own, rights, lefts = (
                token_refs[chain][0],
                token_refs[chain][1:ranks],
                token_refs[chain][ranks:],
            )
            token_copy(chunk, chain, 0, own).start()
            for hop in range(1, ranks):
                from_left = rank >= hop

                @pl.when(from_left)
                def _():
                    token_copy(chunk, chain, hop, rights[hop - 1]).start()

                @pl.when(jnp.logical_not(from_left))
                def _():
                    token_copy(chunk, chain, hop, lefts[ranks - hop - 1]).start()

        @pl.loop(0, CHUNK_BLOCKS)
        def _(index):
            home = home_ref[variant, chunk * CHUNK_BLOCKS + index]
            holder = lax.div(home, slots)
            slot = home - holder * slots
            away = lax.rem(lax.div(rep, CORES) - lax.div(holder, CORES) + chips, chips)
            turned = lax.rem(lax.rem(rep, CORES) + lax.rem(holder, CORES), CORES)
            for core in range(CORES):

                @pl.when((away == 0) & (turned == core))
                def _():
                    code_copy(chunk, index, store_refs[core], slot).start()

                for hop in range(1, chips):
                    for piece in range(pieces):
                        low, high = cuts[piece] // block, cuts[piece + 1] // block
                        source = store_refs[CORES + ((hop - 1) * CORES + core) * pieces + piece]

                        @pl.when((away == hop) & (turned == core) & (slot >= low) & (slot < high))
                        def _():
                            code_copy(chunk, index, source, slot - low).start()

    total[...] = jnp.zeros_like(total)

    @pl.loop(0, chunks)
    def _(chunk):
        base_copy(chunk).wait()
        for chain in range(CHAINS):
            for hop in range(ranks):
                token_copy(chunk, chain, hop, token_refs[chain][0]).wait()
        for index in range(CHUNK_BLOCKS):
            code_copy(chunk, index, store_refs[0], 0).wait()
        merged = []
        for index in range(CHUNK_BLOCKS):
            at = pl.ds(pl.multiple_of(chunk * span + index * block, block), block)
            home = home_ref[variant, chunk * CHUNK_BLOCKS + index]
            delta = code_buf[at, :].astype(jnp.float32) * scale_ref[pl.ds(home, 1), :]
            merged.append((base_buf[at, :].astype(jnp.float32) + delta).astype(jnp.bfloat16))
        at = pl.ds(pl.multiple_of(chunk * span, span), span)
        total[...] += jnp.dot(
            token_buf[:, at], jnp.concatenate(merged, axis=0), preferred_element_type=jnp.float32
        )

    out_ref[...] = total[...].astype(out_ref.dtype)


def local(tokens, base_weight, delta_codes, delta_scales, replica_variant, block_home):
    ranks, reps = lax.axis_size("tp"), lax.axis_size("rep")
    blocks = block_home.shape[1]
    depth, width = base_weight.shape
    rows = tokens.shape[0] // CHAINS
    block = depth // blocks
    slots = delta_scales.shape[0]
    chips = reps // CORES
    ring = [(i, (i + CORES) % reps) for i in range(reps)]
    swap = [(i, i // CORES * CORES + (i + 1) % CORES) for i in range(reps)]

    def right(value, hop):
        return lax.ppermute(value, "tp", [(i, i + 1) for i in range(hop - 1, ranks - 1)])

    def left(value, hop):
        return lax.ppermute(value, "tp", [(i, i - 1) for i in range(1, ranks - hop + 1)])

    events = [(hop, chain) for hop in range(1, ranks) for chain in range(CHAINS)]
    pieces = max(len(events) // max(chips - 1, 1), CHAINS)
    cuts = [slots * i // pieces * block for i in range(pieces + 1)]
    moves = [(hop, piece) for hop in range(1, chips) for piece in range(pieces)]
    held = [[delta_codes[cuts[i] : cuts[i + 1]] for i in range(pieces)]]
    held += [[None] * pieces for _ in range(chips - 1)]
    twins = [[None] * pieces for _ in range(chips)]
    halves = [tokens[chain * rows : (chain + 1) * rows] for chain in range(CHAINS)]
    rights, lefts = [[half] for half in halves], [[half] for half in halves]
    flight = []
    for chain in range(CHAINS):
        flight.append((right(halves[chain], 1), left(halves[chain], 1)))
    sent = [lax.ppermute(held[0][piece], "rep", ring) for _, piece in moves[:CHAINS]]
    whole_twin = lax.ppermute(delta_codes, "rep", swap)
    swaps, scales = [], delta_scales
    for index in range(max(len(events), len(moves))):
        landing = flight[:1] if index < len(events) else []
        flight = flight[len(landing) :]
        arrived = (landing, sent[:1], swaps, scales)
        sent = sent[1:]
        landing, came, swapped, scales = lax.optimization_barrier(arrived)
        for came_right, came_left in landing:
            hop, chain = events[index]
            rights[chain].append(came_right)
            lefts[chain].append(came_left)
            if hop + 1 < ranks:
                flight.append((right(came_right, hop + 1), left(came_left, hop + 1)))
        for value in swapped:
            hop, piece = moves[index - 1]
            twins[hop][piece] = value
        swaps = []
        for value in came:
            hop, piece = moves[index]
            held[hop][piece] = value
            swaps.append(lax.ppermute(value, "rep", swap))
        if index + CHAINS < len(moves):
            hop, piece = moves[index + CHAINS]
            sent.append(lax.ppermute(held[hop - 1][piece], "rep", ring))
        if index == 1:
            scales = lax.all_gather(scales, "rep", axis=0, tiled=True).astype(jnp.float32)
            scales = jnp.repeat(scales, width // delta_scales.shape[1], axis=1)
    for value in swaps:
        hop, piece = moves[-1]
        twins[hop][piece] = value

    arrays = []
    for chain in range(CHAINS):
        arrays += rights[chain] + lefts[chain][1:]
    arrays += [delta_codes, whole_twin]
    for hop in range(1, chips):
        arrays += held[hop] + twins[hop]
    chunks = blocks // CHUNK_BLOCKS
    total_rows = ranks * CHAINS * rows
    return pl.pallas_call(
        functools.partial(kernel, (ranks, reps, block, slots, tuple(cuts))),
        out_shape=jax.ShapeDtypeStruct((total_rows, width), jnp.bfloat16),
        in_specs=[SMEM, SMEM, VMEM, HBM] + [HBM] * len(arrays),
        out_specs=VMEM,
        scratch_shapes=[
            pltpu.VMEM((total_rows, depth), jnp.bfloat16),
            pltpu.VMEM((depth, width), jnp.bfloat16),
            pltpu.VMEM((depth, width), jnp.bfloat16),
            pltpu.VMEM((total_rows, width), jnp.float32),
            pltpu.SemaphoreType.DMA((chunks, CHAINS * ranks + 1)),
            pltpu.SemaphoreType.DMA((chunks, CHUNK_BLOCKS)),
        ],
        compiler_params=pltpu.CompilerParams(vmem_limit_bytes=56 * 1024 * 1024),
        cost_estimate=pl.CostEstimate(
            flops=2 * total_rows * depth * width,
            bytes_accessed=2 * (2 * depth * width + total_rows * depth),
            transcendentals=0,
        ),
    )(replica_variant, block_home, scales, base_weight, *arrays)


def solution(mesh):
    in_specs = (
        P(("groups", "rep", "tp"), None),
        P(None, "tp"),
        P(("groups", "rep"), "tp"),
        P(("groups", "rep"), "tp"),
        P("groups"),
        P("groups", None),
    )
    out_specs = P(("groups", "rep"), "tp")
    return jax.shard_map(local, mesh=mesh, in_specs=in_specs, out_specs=out_specs, check_vma=False)
```

time: 187 us -> 144 us (0.77)
  waiting for transfers between devices: 154 us -> 79.7 us
  starting transfers between devices: 14.1 us -> 29.8 us
  blocking collectives: 5.28 us -> 12.9 us
  local copies, waits for them, and re-layouts: 1.06 us -> 8.03 us
    ppermute x9 -> x25, waiting for transfers between devices: 154 us -> 79.7 us  [the longest x4 38.7 us: local(): sent.append(lax.ppermute(held[hop - 1][piece], 'rep', ring))]
    ppermute x9 -> x25, starting transfers between devices: 14.1 us -> 29.8 us  [the longest x6 13.7 us: right(): lax.ppermute(value, 'tp', [(i, i + 1) for i in range(hop - 1, ranks - 1)])]
    all_gather x1, blocking collectives: 5.28 us -> 12.9 us  [local(): lax.all_gather(scales, 'rep', axis=0, tiled=True).astype(jnp.float32)]
    slice x0 -> x3, local copies, waits for them, and re-layouts: none -> 4.95 us  [the longest x2 4.84 us: local(): held = [[delta_codes[cuts[i]:cuts[i + 1]] for i in range(pieces)]]]
    unnamed x5 -> x43, local copies, waits for them, and re-layouts: 0.75 us -> 2.78 us
  transfers between devices with their start and end apart: 9 -> 25, of which waited for: 3 -> 13; matrix products, arithmetic and copies ran while one was open for 1% -> 2% of each run, Pallas kernels for 0% -> 0%
where the time goes in v4:
time: 144 us; the launch traced here: 143 us
  waiting for transfers between devices  79.7 us (55%)
  starting transfers between devices  29.8 us (21%)
  blocking collectives  12.9 us (9%)
  Pallas kernels  12.6 us (9%)
  local copies, waits for them, and re-layouts  8.03 us (6%)
    ppermute x4, waiting for transfers between devices, local(): sent.append(lax.ppermute(held[hop - 1][piece], 'rep', ring))  38.7 us
    ppermute x6, waiting for transfers between devices, left(): lax.ppermute(value, 'tp', [(i, i - 1) for i in range(1, ranks - hop + 1)])  30.7 us
    ppermute x6, starting transfers between devices, right(): lax.ppermute(value, 'tp', [(i, i + 1) for i in range(hop - 1, ranks - 1)])  13.7 us
    all_gather x1, blocking collectives, local(): lax.all_gather(scales, 'rep', axis=0, tiled=True).astype(jnp.float32)  12.9 us
    pallas_call x1, Pallas kernels, local(): pl.pallas_call(functools.partial(kernel, (ranks, reps, block, slots, tupl...  12.6 us
    ppermute x6, starting transfers between devices, left(): lax.ppermute(value, 'tp', [(i, i - 1) for i in range(1, ranks - hop + 1)])  7.72 us
    ppermute x2, waiting for transfers between devices, local(): lax.ppermute(held[0][piece], 'rep', ring)  6.96 us
    slice x2, local copies, waits for them, and re-layouts, local(): held = [[delta_codes[cuts[i]:cuts[i + 1]] for i in range(pieces)]]  4.84 us
  transfers between devices with their start and end apart: 25, of which 13 were waited for; matrix products, arithmetic and copies ran while one was open for 2% of the time, Pallas kernels for 0%

profile of v4, /device:TPU:0, one launch (start us, length us, event | category | flops | bytes accessed | tf_op | source)
XLA Modules:
  0.0 143.3 jit_solution(10595334660399359002)
XLA Ops:
  0.0 3.1 %fusion = (bf16[640,512]{1,0:T(8,128)(2,1)}, bf16[640,512]{1,0:T(8,128)(2,1)}, bf16[640,512]{1,0:T(8,128)(2,1)S(1)}, bf16[640,512]{1,0:T(8,128)(2,1)S(1)}) fusion(bf16[4096,512]{1,0:T(8,128)(2,1)} %refs_14_.1), kind=kLoop, calls=%fused_computation.1 | loop fusion | bytes 5242880 | tf_op jit(solution)/shard_map/slice | solution.py:140
  3.1 2.9 %collective-permute-start.5 = (bf16[640,512]{1,0:T(8,128)(2,1)S(1)}, bf16[640,512]{1,0:T(8,128)(2,1)S(1)}, u32[]{:S(2)}, u32[]{:S(2)}) collective-permute-start(bf16[640,512]{1,0:T(8,128)(2,1)S(1)} %get-tuple-element.65), channel_id=1, source_target_pairs={{0,8},{4,12},{8,0},{12,4},{1,9},{5,13},{9,1},{13,5},{2,10},{6,14},... | collective-permute-start | bytes 1966088 | tf_op jit(solution)/shard_map/ppermute | solution.py:148
  6.2 1.3 collective-permute-start.4
  7.5 4.6 %collective-permute-start.3 = (bf16[48,8192]{1,0:T(8,128)(2,1)S(1)}, bf16[48,8192]{1,0:T(8,128)(2,1)S(1)}, u32[]{:S(2)}, u32[]{:S(2)}) collective-permute-start(bf16[48,8192]{1,0:T(8,128)(2,1)S(1)} %get-tuple-element.69.refs_0_), channel_id=1, source_target_pairs={{0,1},{1,2},{2,3},{4,5},{5,6},{6,7},{8,9},{9,10},{10,11},{12,13},{... | collective-permute-start | bytes 2359304 | tf_op jit(solution)/shard_map/ppermute | solution.py:131
  12.1 1.3 collective-permute-start.1
  13.4 5.4 %collective-permute-start = (bf16[48,8192]{1,0:T(8,128)(2,1)S(1)}, bf16[48,8192]{1,0:T(8,128)(2,1)}, u32[]{:S(2)}, u32[]{:S(2)}) collective-permute-start(bf16[48,8192]{1,0:T(8,128)(2,1)S(1)} %get-tuple-element.70.refs_7_), channel_id=1, source_target_pairs={{0,1},{1,2},{2,3},{4,5},{5,6},{6,7},{8,9},{9,10},{10,11},{12,13},{... | collective-permute-start | bytes 2359304 | tf_op jit(solution)/shard_map/ppermute | solution.py:131
  18.8 1.9 %collective-permute-done.5.refs_16_ = bf16[640,512]{1,0:T(8,128)(2,1)S(1)} collective-permute-done((bf16[640,512]{1,0:T(8,128)(2,1)S(1)}, bf16[640,512]{1,0:T(8,128)(2,1)S(1)}, u32[]{:S(2)}, u32[]{:S(2)}) %collective-permute-start.5) | collective-permute-done | bytes 655392 | tf_op jit(solution)/shard_map/ppermute | solution.py:148
  20.8 1.7 %collective-permute-start.2 = (bf16[640,512]{1,0:T(8,128)(2,1)S(1)}, bf16[640,512]{1,0:T(8,128)(2,1)}, u32[]{:S(2)}, u32[]{:S(2)}) collective-permute-start(bf16[640,512]{1,0:T(8,128)(2,1)S(1)} %get-tuple-element.66), channel_id=1, source_target_pairs={{0,8},{4,12},{8,0},{12,4},{1,9},{5,13},{9,1},{13,5},{2,10},{6,14},... | collective-permute-start | bytes 1966088 | tf_op jit(solution)/shard_map/ppermute | solution.py:148
  22.5 6.0 %collective-permute-done.4.refs_4_ = bf16[48,8192]{1,0:T(8,128)(2,1)S(1)} collective-permute-done((bf16[48,8192]{1,0:T(8,128)(2,1)S(1)}, bf16[48,8192]{1,0:T(8,128)(2,1)S(1)}, u32[]{:S(2)}, u32[]{:S(2)}) %collective-permute-start.4) | collective-permute-done | bytes 786464 | tf_op jit(solution)/shard_map/ppermute | solution.py:134
  28.5 1.5 %collective-permute-done.3.refs_1_ = bf16[48,8192]{1,0:T(8,128)(2,1)S(1)} collective-permute-done((bf16[48,8192]{1,0:T(8,128)(2,1)S(1)}, bf16[48,8192]{1,0:T(8,128)(2,1)S(1)}, u32[]{:S(2)}, u32[]{:S(2)}) %collective-permute-start.3) | collective-permute-done | bytes 786464 | tf_op jit(solution)/shard_map/ppermute | solution.py:131
  30.0 1.8 %fusion.1 = (bf16[768,512]{1,0:T(8,128)(2,1)S(1)}, bf16[768,512]{1,0:T(8,128)(2,1)S(1)}) fusion(bf16[4096,512]{1,0:T(8,128)(2,1)} %refs_14_.1), kind=kLoop, calls=%fused_computation.2 | loop fusion | bytes 3145728 | tf_op jit(solution)/shard_map/slice | solution.py:140
  31.8 5.0 %collective-permute-done.2.refs_17_ = bf16[640,512]{1,0:T(8,128)(2,1)} collective-permute-done((bf16[640,512]{1,0:T(8,128)(2,1)S(1)}, bf16[640,512]{1,0:T(8,128)(2,1)}, u32[]{:S(2)}, u32[]{:S(2)}) %collective-permute-start.2) | collective-permute-done | bytes 655392 | tf_op jit(solution)/shard_map/ppermute | solution.py:148
  36.8 1.4 collective-permute-start.12
  38.2 5.8 %collective-permute-done.1.refs_11_ = bf16[48,8192]{1,0:T(8,128)(2,1)} collective-permute-done((bf16[48,8192]{1,0:T(8,128)(2,1)S(1)}, bf16[48,8192]{1,0:T(8,128)(2,1)}, u32[]{:S(2)}, u32[]{:S(2)}) %collective-permute-start.1) | collective-permute-done | bytes 786464 | tf_op jit(solution)/shard_map/ppermute | solution.py:134
  45.1 1.3 collective-permute-start.11
  46.5 8.1 %collective-permute-done.12.refs_18_ = bf16[768,512]{1,0:T(8,128)(2,1)S(1)} collective-permute-done((bf16[768,512]{1,0:T(8,128)(2,1)S(1)}, bf16[768,512]{1,0:T(8,128)(2,1)S(1)}, u32[]{:S(2)}, u32[]{:S(2)}) %collective-permute-start.12) | collective-permute-done | bytes 786464 | tf_op jit(solution)/shard_map/ppermute | solution.py:173
  54.6 1.5 %collective-permute-start.7 = (bf16[48,8192]{1,0:T(8,128)(2,1)}, bf16[48,8192]{1,0:T(8,128)(2,1)}, u32[]{:S(2)}, u32[]{:S(2)}) collective-permute-start(bf16[48,8192]{1,0:T(8,128)(2,1)} %collective-permute-done.refs_8_), channel_id=1, source_target_pairs={{1,2},{2,3},{5,6},{6,7},{9,10},{10,11},{13,14},{14,15},{17,18},{18... | collective-permute-start | bytes 2359304 | tf_op jit(solution)/shard_map/ppermute | solution.py:131
  56.1 1.3 collective-permute-start.8
  57.4 11.4 %collective-permute-done.11.refs_5_ = bf16[48,8192]{1,0:T(8,128)(2,1)S(1)} collective-permute-done((bf16[48,8192]{1,0:T(8,128)(2,1)S(1)}, bf16[48,8192]{1,0:T(8,128)(2,1)S(1)}, u32[]{:S(2)}, u32[]{:S(2)}) %collective-permute-start.11) | collective-permute-done | bytes 786464 | tf_op jit(solution)/shard_map/ppermute | solution.py:134
  69.7 12.9 %all-gather = bf16[4,32,4]{1,2,0:T(4,128)(2,1)S(1)} all-gather(bf16[1,32,4]{1,2,0:T(4,128)(2,1)S(1)} %bitcast.9), channel_id=1, replica_groups=mesh['groups'=2,'rep'=4,'tp'=4] {'rep'}, dimensions={0}, use_global_device_ids=true | all-gather | bytes 1280 | tf_op jit(solution)/shard_map/all_gather | solution.py:175
  83.0 0.7 copy.15
  84.0 0.7 collective-permute-start.18
  84.7 1.3 collective-permute-start.19
  86.7 16.5 %collective-permute-done.20.refs_20_ = bf16[640,512]{1,0:T(8,128)(2,1)S(1)} collective-permute-done((bf16[640,512]{1,0:T(8,128)(2,1)}, bf16[640,512]{1,0:T(8,128)(2,1)S(1)}, u32[]{:S(2)}, u32[]{:S(2)}) %collective-permute-start.20) | collective-permute-done | bytes 655392 | tf_op jit(solution)/shard_map/ppermute | solution.py:173
  104.4 2.1 %collective-permute-done.19.refs_6_ = bf16[48,8192]{1,0:T(8,128)(2,1)S(1)} collective-permute-done((bf16[48,8192]{1,0:T(8,128)(2,1)}, bf16[48,8192]{1,0:T(8,128)(2,1)S(1)}, u32[]{:S(2)}, u32[]{:S(2)}) %collective-permute-start.19) | collective-permute-done | bytes 786464 | tf_op jit(solution)/shard_map/ppermute | solution.py:134
  106.5 1.3 collective-permute-start.16
  107.9 14.1 %collective-permute-done.17.refs_21_ = bf16[768,512]{1,0:T(8,128)(2,1)S(1)} collective-permute-done((bf16[768,512]{1,0:T(8,128)(2,1)S(1)}, bf16[768,512]{1,0:T(8,128)(2,1)S(1)}, u32[]{:S(2)}, u32[]{:S(2)}) %collective-permute-start.17) | collective-permute-done | bytes 786464 | tf_op jit(solution)/shard_map/ppermute | solution.py:173
  122.0 5.4 %collective-permute-done.16.refs_13_ = bf16[48,8192]{1,0:T(8,128)(2,1)S(1)} collective-permute-done((bf16[48,8192]{1,0:T(8,128)(2,1)}, bf16[48,8192]{1,0:T(8,128)(2,1)S(1)}, u32[]{:S(2)}, u32[]{:S(2)}) %collective-permute-start.16) | collective-permute-done | bytes 786464 | tf_op jit(solution)/shard_map/ppermute | solution.py:134
  127.5 0.8 copy-done.19
  128.3 1.5 %collective-permute-done.24.refs_27_ = bf16[768,512]{1,0:T(8,128)(2,1)S(1)} collective-permute-done((bf16[768,512]{1,0:T(8,128)(2,1)S(1)}, bf16[768,512]{1,0:T(8,128)(2,1)S(1)}, u32[]{:S(2)}, u32[]{:S(2)}) %collective-permute-start.24) | collective-permute-done | bytes 786464 | tf_op jit(solution)/shard_map/ppermute | solution.py:170
  129.8 0.9 copy-done.14
  130.7 12.6 %shard_map.64 = bf16[384,512]{1,0:T(8,128)(2,1)} custom-call(s32[4]{0:T(128)} %variant_ref.1, s32[2,64]{1,0:T(2,128)} %home_ref.1, f32[128,512]{1,0:T(8,128)} %bitcast.6, bf16[8192,512]{1,0:T(8,128)(2,1)} %base_ref.1, bf16[48,8192]{1,0:T(8,128)(2,1)} %copy-done, bf16[48,8192]{1,0:T(8,128)(2,1)} %copy-done.4, bf16[48,8192]{1,0:T(8,128)(2,1)} %copy-done.6, ...), custom_call_target="tpu_custom_call" | custom-call | flops 3221225472 | bytes 23068672 | tf_op jit(solution)/shard_map/pallas_call | solution.py:189
  (68 shorter events, 4.9 us)
Async XLA Ops:
  3.1 66.7 %copy-start.20 = (bf16[32,4]{0,1:T(4,128)(2,1)S(1)}, bf16[32,4]{0,1:T(4,128)(2,1)}, u32[]{:S(2)}) copy-start(bf16[32,4]{0,1:T(4,128)(2,1)} %param.9) | copy-start | bytes 772
  3.1 17.7 %collective-permute-start.5 = (bf16[640,512]{1,0:T(8,128)(2,1)S(1)}, bf16[640,512]{1,0:T(8,128)(2,1)S(1)}, u32[]{:S(2)}, u32[]{:S(2)}) collective-permute-start(bf16[640,512]{1,0:T(8,128)(2,1)S(1)} %get-tuple-element.65), channel_id=1, source_target_pairs={{0,8},{4,12},{8,0},{12,4},{1,9},{5,13},{9,1},{13,5},{2,10},{6,14},... | collective-permute-start | bytes 1966088 | tf_op jit(solution)/shard_map/ppermute | solution.py:148
  6.1 123.6 %copy-start = (bf16[48,8192]{1,0:T(8,128)(2,1)}, bf16[48,8192]{1,0:T(8,128)(2,1)S(1)}, u32[]{:S(2)}) copy-start(bf16[48,8192]{1,0:T(8,128)(2,1)S(1)} %get-tuple-element.69.refs_0_) | copy-start | bytes 2359300
  6.2 123.6 %copy-start.1 = (bf16[48,8192]{1,0:T(8,128)(2,1)}, bf16[48,8192]{1,0:T(8,128)(2,1)S(1)}, u32[]{:S(2)}) copy-start(bf16[48,8192]{1,0:T(8,128)(2,1)S(1)} %get-tuple-element.70.refs_7_) | copy-start | bytes 2359300
  6.2 22.4 %collective-permute-start.4 = (bf16[48,8192]{1,0:T(8,128)(2,1)S(1)}, bf16[48,8192]{1,0:T(8,128)(2,1)S(1)}, u32[]{:S(2)}, u32[]{:S(2)}) collective-permute-start(bf16[48,8192]{1,0:T(8,128)(2,1)S(1)} %get-tuple-element.69.refs_0_), channel_id=1, source_target_pairs={{1,0},{2,1},{3,2},{5,4},{6,5},{7,6},{9,8},{10,9},{11,10},{13,12},{... | collective-permute-start | bytes 2359304 | tf_op jit(solution)/shard_map/ppermute | solution.py:134
  7.5 22.5 %collective-permute-start.3 = (bf16[48,8192]{1,0:T(8,128)(2,1)S(1)}, bf16[48,8192]{1,0:T(8,128)(2,1)S(1)}, u32[]{:S(2)}, u32[]{:S(2)}) collective-permute-start(bf16[48,8192]{1,0:T(8,128)(2,1)S(1)} %get-tuple-element.69.refs_0_), channel_id=1, source_target_pairs={{0,1},{1,2},{2,3},{4,5},{5,6},{6,7},{8,9},{9,10},{10,11},{12,13},{... | collective-permute-start | bytes 2359304 | tf_op jit(solution)/shard_map/ppermute | solution.py:131
  12.1 31.9 %collective-permute-start.1 = (bf16[48,8192]{1,0:T(8,128)(2,1)S(1)}, bf16[48,8192]{1,0:T(8,128)(2,1)}, u32[]{:S(2)}, u32[]{:S(2)}) collective-permute-start(bf16[48,8192]{1,0:T(8,128)(2,1)S(1)} %get-tuple-element.70.refs_7_), channel_id=1, source_target_pairs={{1,0},{2,1},{3,2},{5,4},{6,5},{7,6},{9,8},{10,9},{11,10},{13,12},{... | collective-permute-start | bytes 2359304 | tf_op jit(solution)/shard_map/ppermute | solution.py:134
  13.4 31.7 %collective-permute-start = (bf16[48,8192]{1,0:T(8,128)(2,1)S(1)}, bf16[48,8192]{1,0:T(8,128)(2,1)}, u32[]{:S(2)}, u32[]{:S(2)}) collective-permute-start(bf16[48,8192]{1,0:T(8,128)(2,1)S(1)} %get-tuple-element.70.refs_7_), channel_id=1, source_target_pairs={{0,1},{1,2},{2,3},{4,5},{5,6},{6,7},{8,9},{9,10},{10,11},{12,13},{... | collective-permute-start | bytes 2359304 | tf_op jit(solution)/shard_map/ppermute | solution.py:131
  20.8 48.6 %copy-start.15 = (bf16[640,512]{1,0:T(8,128)(2,1)}, bf16[640,512]{1,0:T(8,128)(2,1)S(1)}, u32[]{:S(2)}) copy-start(bf16[640,512]{1,0:T(8,128)(2,1)S(1)} %collective-permute-done.5.refs_16_) | copy-start | bytes 1966084
  20.8 16.0 %collective-permute-start.2 = (bf16[640,512]{1,0:T(8,128)(2,1)S(1)}, bf16[640,512]{1,0:T(8,128)(2,1)}, u32[]{:S(2)}, u32[]{:S(2)}) collective-permute-start(bf16[640,512]{1,0:T(8,128)(2,1)S(1)} %get-tuple-element.66), channel_id=1, source_target_pairs={{0,8},{4,12},{8,0},{12,4},{1,9},{5,13},{9,1},{13,5},{2,10},{6,14},... | collective-permute-start | bytes 1966088 | tf_op jit(solution)/shard_map/ppermute | solution.py:148
  28.5 101.2 %copy-start.3 = (bf16[48,8192]{1,0:T(8,128)(2,1)}, bf16[48,8192]{1,0:T(8,128)(2,1)S(1)}, u32[]{:S(2)}) copy-start(bf16[48,8192]{1,0:T(8,128)(2,1)S(1)} %collective-permute-done.4.refs_4_) | copy-start | bytes 2359300
  28.5 99.0 %collective-permute-start.23 = (bf16[4096,512]{1,0:T(8,128)(2,1)}, bf16[4096,512]{1,0:T(8,128)(2,1)}, u32[]{:S(2)}, u32[]{:S(2)}) collective-permute-start(bf16[4096,512]{1,0:T(8,128)(2,1)} %refs_14_.1), channel_id=1, source_target_pairs={{0,4},{4,0},{8,12},{12,8},{1,5},{5,1},{9,13},{13,9},{2,6},{6,2},{1... | collective-permute-start | bytes 12582920 | tf_op jit(solution)/shard_map/ppermute | solution.py:149
  30.0 38.8 %copy-start.4 = (bf16[48,8192]{1,0:T(8,128)(2,1)}, bf16[48,8192]{1,0:T(8,128)(2,1)S(1)}, u32[]{:S(2)}) copy-start(bf16[48,8192]{1,0:T(8,128)(2,1)S(1)} %collective-permute-done.3.refs_1_) | copy-start | bytes 2359300
  30.0 16.4 %collective-permute-start.6 = (bf16[640,512]{1,0:T(8,128)(2,1)S(1)}, bf16[640,512]{1,0:T(8,128)(2,1)S(1)}, u32[]{:S(2)}, u32[]{:S(2)}) collective-permute-start(bf16[640,512]{1,0:T(8,128)(2,1)S(1)} %collective-permute-done.5.refs_16_), channel_id=1, source_target_pairs={{0,4},{4,0},{8,12},{12,8},{1,5},{5,1},{9,13},{13,9},{2,6},{6,2},{1... | collective-permute-start | bytes 1966088 | tf_op jit(solution)/shard_map/ppermute | solution.py:170
  36.8 17.8 %collective-permute-start.12 = (bf16[768,512]{1,0:T(8,128)(2,1)S(1)}, bf16[768,512]{1,0:T(8,128)(2,1)S(1)}, u32[]{:S(2)}, u32[]{:S(2)}) collective-permute-start(bf16[768,512]{1,0:T(8,128)(2,1)S(1)} %get-tuple-element.68), channel_id=1, source_target_pairs={{0,8},{4,12},{8,0},{12,4},{1,9},{5,13},{9,1},{13,5},{2,10},{6,14},... | collective-permute-start | bytes 2359304 | tf_op jit(solution)/shard_map/ppermute | solution.py:173
  44.0 12.1 %collective-permute-start.10 = (bf16[48,8192]{1,0:T(8,128)(2,1)S(1)}, bf16[48,8192]{1,0:T(8,128)(2,1)S(1)}, u32[]{:S(2)}, u32[]{:S(2)}) collective-permute-start(bf16[48,8192]{1,0:T(8,128)(2,1)S(1)} %collective-permute-done.3.refs_1_), channel_id=1, source_target_pairs={{1,2},{2,3},{5,6},{6,7},{9,10},{10,11},{13,14},{14,15},{17,18},{18... | collective-permute-start | bytes 2359304 | tf_op jit(solution)/shard_map/ppermute | solution.py:131
  45.1 23.7 %collective-permute-start.11 = (bf16[48,8192]{1,0:T(8,128)(2,1)S(1)}, bf16[48,8192]{1,0:T(8,128)(2,1)S(1)}, u32[]{:S(2)}, u32[]{:S(2)}) collective-permute-start(bf16[48,8192]{1,0:T(8,128)(2,1)S(1)} %collective-permute-done.4.refs_4_), channel_id=1, source_target_pairs={{1,0},{2,1},{5,4},{6,5},{9,8},{10,9},{13,12},{14,13},{17,16},{18,1... | collective-permute-start | bytes 2359304 | tf_op jit(solution)/shard_map/ppermute | solution.py:134
  46.4 37.3 %collective-permute-start.13 = (bf16[640,512]{1,0:T(8,128)(2,1)}, bf16[640,512]{1,0:T(8,128)(2,1)}, u32[]{:S(2)}, u32[]{:S(2)}) collective-permute-start(bf16[640,512]{1,0:T(8,128)(2,1)} %collective-permute-done.2.refs_17_), channel_id=1, source_target_pairs={{0,4},{4,0},{8,12},{12,8},{1,5},{5,1},{9,13},{13,9},{2,6},{6,2},{1... | collective-permute-start | bytes 1966088 | tf_op jit(solution)/shard_map/ppermute | solution.py:170
  54.6 30.1 %collective-permute-start.7 = (bf16[48,8192]{1,0:T(8,128)(2,1)}, bf16[48,8192]{1,0:T(8,128)(2,1)}, u32[]{:S(2)}, u32[]{:S(2)}) collective-permute-start(bf16[48,8192]{1,0:T(8,128)(2,1)} %collective-permute-done.refs_8_), channel_id=1, source_target_pairs={{1,2},{2,3},{5,6},{6,7},{9,10},{10,11},{13,14},{14,15},{17,18},{18... | collective-permute-start | bytes 2359304 | tf_op jit(solution)/shard_map/ppermute | solution.py:131
  56.1 29.9 %collective-permute-start.8 = (bf16[48,8192]{1,0:T(8,128)(2,1)}, bf16[48,8192]{1,0:T(8,128)(2,1)}, u32[]{:S(2)}, u32[]{:S(2)}) collective-permute-start(bf16[48,8192]{1,0:T(8,128)(2,1)} %collective-permute-done.1.refs_11_), channel_id=1, source_target_pairs={{1,0},{2,1},{5,4},{6,5},{9,8},{10,9},{13,12},{14,13},{17,16},{18,1... | collective-permute-start | bytes 2359304 | tf_op jit(solution)/shard_map/ppermute | solution.py:134
  68.8 15.2 %collective-permute-start.9 = (bf16[640,512]{1,0:T(8,128)(2,1)}, bf16[640,512]{1,0:T(8,128)(2,1)}, u32[]{:S(2)}, u32[]{:S(2)}) collective-permute-start(bf16[640,512]{1,0:T(8,128)(2,1)} %get-tuple-element.64), channel_id=1, source_target_pairs={{0,8},{4,12},{8,0},{12,4},{1,9},{5,13},{9,1},{13,5},{2,10},{6,14},... | collective-permute-start | bytes 1966088 | tf_op jit(solution)/shard_map/ppermute | solution.py:173
  83.7 3.0 %collective-permute-start.14 = (bf16[768,512]{1,0:T(8,128)(2,1)}, bf16[768,512]{1,0:T(8,128)(2,1)S(1)}, u32[]{:S(2)}, u32[]{:S(2)}) collective-permute-start(bf16[768,512]{1,0:T(8,128)(2,1)} %copy-done.5), channel_id=1, source_target_pairs={{0,4},{4,0},{8,12},{12,8},{1,5},{5,1},{9,13},{13,9},{2,6},{6,2},{1... | collective-permute-start | bytes 2359304 | tf_op jit(solution)/shard_map/ppermute | solution.py:170
  84.0 19.7 %collective-permute-start.18 = (bf16[48,8192]{1,0:T(8,128)(2,1)}, bf16[48,8192]{1,0:T(8,128)(2,1)S(1)}, u32[]{:S(2)}, u32[]{:S(2)}) collective-permute-start(bf16[48,8192]{1,0:T(8,128)(2,1)} %copy-done.6), channel_id=1, source_target_pairs={{2,3},{6,7},{10,11},{14,15},{18,19},{22,23},{26,27},{30,31}} | collective-permute-start | bytes 2359304 | tf_op jit(solution)/shard_map/ppermute | solution.py:131
  84.7 21.7 %collective-permute-start.19 = (bf16[48,8192]{1,0:T(8,128)(2,1)}, bf16[48,8192]{1,0:T(8,128)(2,1)S(1)}, u32[]{:S(2)}, u32[]{:S(2)}) collective-permute-start(bf16[48,8192]{1,0:T(8,128)(2,1)} %copy-done.7), channel_id=1, source_target_pairs={{1,0},{5,4},{9,8},{13,12},{17,16},{21,20},{25,24},{29,28}} | collective-permute-start | bytes 2359304 | tf_op jit(solution)/shard_map/ppermute | solution.py:134
  86.1 17.1 %collective-permute-start.20 = (bf16[640,512]{1,0:T(8,128)(2,1)}, bf16[640,512]{1,0:T(8,128)(2,1)S(1)}, u32[]{:S(2)}, u32[]{:S(2)}) collective-permute-start(bf16[640,512]{1,0:T(8,128)(2,1)} %get-tuple-element.63), channel_id=1, source_target_pairs={{0,8},{4,12},{8,0},{12,4},{1,9},{5,13},{9,1},{13,5},{2,10},{6,14},... | collective-permute-start | bytes 1966088 | tf_op jit(solution)/shard_map/ppermute | solution.py:173
  86.7 43.1 %copy-start.8 = (bf16[768,512]{1,0:T(8,128)(2,1)}, bf16[768,512]{1,0:T(8,128)(2,1)S(1)}, u32[]{:S(2)}) copy-start(bf16[768,512]{1,0:T(8,128)(2,1)S(1)} %collective-permute-done.14.refs_24_) | copy-start | bytes 2359300
  86.7 21.1 %collective-permute-start.21 = (bf16[640,512]{1,0:T(8,128)(2,1)}, bf16[640,512]{1,0:T(8,128)(2,1)S(1)}, u32[]{:S(2)}, u32[]{:S(2)}) collective-permute-start(bf16[640,512]{1,0:T(8,128)(2,1)} %collective-permute-done.9.refs_19_), channel_id=1, source_target_pairs={{0,4},{4,0},{8,12},{12,8},{1,5},{5,1},{9,13},{13,9},{2,6},{6,2},{1... | collective-permute-start | bytes 1966088 | tf_op jit(solution)/shard_map/ppermute | solution.py:170
  103.2 18.8 %collective-permute-start.17 = (bf16[768,512]{1,0:T(8,128)(2,1)S(1)}, bf16[768,512]{1,0:T(8,128)(2,1)S(1)}, u32[]{:S(2)}, u32[]{:S(2)}) collective-permute-start(bf16[768,512]{1,0:T(8,128)(2,1)S(1)} %get-tuple-element.67), channel_id=1, source_target_pairs={{0,8},{4,12},{8,0},{12,4},{1,9},{5,13},{9,1},{13,5},{2,10},{6,14},... | collective-permute-start | bytes 2359304 | tf_op jit(solution)/shard_map/ppermute | solution.py:173
  103.7 18.3 %collective-permute-start.15 = (bf16[48,8192]{1,0:T(8,128)(2,1)}, bf16[48,8192]{1,0:T(8,128)(2,1)S(1)}, u32[]{:S(2)}, u32[]{:S(2)}) collective-permute-start(bf16[48,8192]{1,0:T(8,128)(2,1)} %collective-permute-done.7.refs_9_), channel_id=1, source_target_pairs={{2,3},{6,7},{10,11},{14,15},{18,19},{22,23},{26,27},{30,31}} | collective-permute-start | bytes 2359304 | tf_op jit(solution)/shard_map/ppermute | solution.py:131
  106.5 20.9 %collective-permute-start.16 = (bf16[48,8192]{1,0:T(8,128)(2,1)}, bf16[48,8192]{1,0:T(8,128)(2,1)S(1)}, u32[]{:S(2)}, u32[]{:S(2)}) collective-permute-start(bf16[48,8192]{1,0:T(8,128)(2,1)} %collective-permute-done.8.refs_12_), channel_id=1, source_target_pairs={{1,0},{5,4},{9,8},{13,12},{17,16},{21,20},{25,24},{29,28}} | collective-permute-start | bytes 2359304 | tf_op jit(solution)/shard_map/ppermute | solution.py:134
  107.8 19.6 %collective-permute-start.22 = (bf16[640,512]{1,0:T(8,128)(2,1)S(1)}, bf16[640,512]{1,0:T(8,128)(2,1)S(1)}, u32[]{:S(2)}, u32[]{:S(2)}) collective-permute-start(bf16[640,512]{1,0:T(8,128)(2,1)S(1)} %collective-permute-done.20.refs_20_), channel_id=1, source_target_pairs={{0,4},{4,0},{8,12},{12,8},{1,5},{5,1},{9,13},{13,9},{2,6},{6,2},{1... | collective-permute-start | bytes 1966088 | tf_op jit(solution)/shard_map/ppermute | solution.py:170
  127.4 2.3 %collective-permute-start.24 = (bf16[768,512]{1,0:T(8,128)(2,1)S(1)}, bf16[768,512]{1,0:T(8,128)(2,1)S(1)}, u32[]{:S(2)}, u32[]{:S(2)}) collective-permute-start(bf16[768,512]{1,0:T(8,128)(2,1)S(1)} %collective-permute-done.17.refs_21_), channel_id=1, source_target_pairs={{0,4},{4,0},{8,12},{12,8},{1,5},{5,1},{9,13},{13,9},{2,6},{6,2},{1... | collective-permute-start | bytes 2359304 | tf_op jit(solution)/shard_map/ppermute | solution.py:170
  (14 other events, 170.7 us)

commit v5 on v4

v5 whole, which is shorter than its diff:
```python
import functools
import jax
import jax.numpy as jnp
from jax import lax
from jax.experimental import pallas as pl
from jax.experimental.pallas import tpu as pltpu
from jax.sharding import PartitionSpec as P

CORES = 2
CHUNK_BLOCKS = 8


CHAINS = 2
VMEM_LIMIT = 56 * 1024 * 1024
SMEM = pl.BlockSpec(memory_space=pltpu.SMEM)
VMEM = pl.BlockSpec(memory_space=pltpu.VMEM)
HBM = pl.BlockSpec(memory_space=pl.ANY)
BRIEF = pl.CostEstimate(flops=1, bytes_accessed=1, transcendentals=0)


def merge_kernel(dims, variant_ref, home_ref, scale_ref, base_ref, *refs):
    reps, block, slots, parts = dims
    stores = refs[: len(parts)]
    out_ref, base_buf, code_buf, base_sems, code_sems, out_sems = refs[-6:]
    blocks = home_ref.shape[1]
    chips = reps // CORES
    rep = lax.axis_index("rep")
    variant = variant_ref[rep]

    def rows(index):
        return pl.ds(pl.multiple_of(index * block, block), block)

    def copies(index, store, slot):
        return (
            pltpu.make_async_copy(base_ref.at[rows(index), :], base_buf.at[rows(index), :], base_sems.at[index]),
            pltpu.make_async_copy(store.at[rows(slot), :], code_buf.at[rows(index), :], code_sems.at[index]),
        )

    def result(index):
        return pltpu.make_async_copy(base_buf.at[rows(index), :], out_ref.at[rows(index), :], out_sems.at[index])

    def source(index):
        home = home_ref[variant, index]
        holder = lax.div(home, slots)
        slot = home - holder * slots
        away = lax.rem(lax.div(rep, CORES) - lax.div(holder, CORES) + chips, chips)
        turned = lax.rem(lax.rem(rep, CORES) + lax.rem(holder, CORES), CORES)
        return slot, away, turned

    def chosen(part, slot, away, turned):
        hop, core, low, high = part
        return (away == hop) & (turned == core) & (slot >= low) & (slot < high)

    def any_part(slot, away, turned):
        return functools.reduce(jnp.logical_or, [chosen(part, slot, away, turned) for part in parts])

    @pl.loop(0, blocks)
    def _(index):
        slot, away, turned = source(index)
        for part, store in zip(parts, stores):

            @pl.when(chosen(part, slot, away, turned))
            def _():
                for copy in copies(index, store, slot - part[2]):
                    copy.start()

    @pl.loop(0, blocks)
    def _(index):
        slot, away, turned = source(index)

        @pl.when(any_part(slot, away, turned))
        def _():
            for copy in copies(index, stores[0], 0):
                copy.wait()
            row = (turned * chips + away) * slots + slot
            delta = code_buf[rows(index), :].astype(jnp.float32) * scale_ref[pl.ds(row, 1), :]
            merged = base_buf[rows(index), :].astype(jnp.float32) + delta
            base_buf[rows(index), :] = merged.astype(jnp.bfloat16)
            result(index).start()

    @pl.loop(0, blocks)
    def _(index):
        slot, away, turned = source(index)

        @pl.when(any_part(slot, away, turned))
        def _():
            result(index).wait()


def product_kernel(dims, weight_ref, *refs):
    ranks, span = dims
    lanes = 2 * ranks - 1
    token_refs = [refs[chain * lanes : (chain + 1) * lanes] for chain in range(CHAINS)]
    out_ref, token_buf, weight_buf, total, sems = refs[-5:]
    rows, depth = token_refs[0][0].shape
    chunks = depth // span
    rank = lax.axis_index("tp")

    def weight_copy(chunk):
        at = pl.ds(pl.multiple_of(chunk * span, span), span)
        return pltpu.make_async_copy(weight_ref.at[at, :], weight_buf.at[at, :], sems.at[chunk, CHAINS * ranks])

    def token_copy(chunk, chain, hop, source):
        at = pl.ds(pl.multiple_of(chunk * span, span), span)
        origin = lax.rem(rank - hop + ranks, ranks)
        row = pl.multiple_of((origin * CHAINS + chain) * rows, rows)
        return pltpu.make_async_copy(
            source.at[:, at], token_buf.at[pl.ds(row, rows), at], sems.at[chunk, chain * ranks + hop]
        )

    @pl.loop(0, chunks)
    def _(chunk):
        weight_copy(chunk).start()
        for chain in range(CHAINS):
            own, rights, lefts = (
                token_refs[chain][0],
                token_refs[chain][1:ranks],
                token_refs[chain][ranks:],
            )
            token_copy(chunk, chain, 0, own).start()
            for hop in range(1, ranks):
                from_left = rank >= hop

                @pl.when(from_left)
                def _():
                    token_copy(chunk, chain, hop, rights[hop - 1]).start()

                @pl.when(jnp.logical_not(from_left))
                def _():
                    token_copy(chunk, chain, hop, lefts[ranks - hop - 1]).start()

    total[...] = jnp.zeros_like(total)

    @pl.loop(0, chunks)
    def _(chunk):
        weight_copy(chunk).wait()
        for chain in range(CHAINS):
            for hop in range(ranks):
                token_copy(chunk, chain, hop, token_refs[chain][0]).wait()
        at = pl.ds(pl.multiple_of(chunk * span, span), span)
        total[...] += jnp.dot(token_buf[:, at], weight_buf[at, :], preferred_element_type=jnp.float32)

    out_ref[...] = total[...].astype(out_ref.dtype)


def local(tokens, base_weight, delta_codes, delta_scales, replica_variant, block_home):
    ranks, reps = lax.axis_size("tp"), lax.axis_size("rep")
    blocks = block_home.shape[1]
    depth, width = base_weight.shape
    rows = tokens.shape[0] // CHAINS
    block = depth // blocks
    slots, col_blocks = delta_scales.shape
    chips = reps // CORES
    ring = [(i, (i + CORES) % reps) for i in range(reps)]
    swap = [(i, i // CORES * CORES + (i + 1) % CORES) for i in range(reps)]

    def tie(values):
        return lax.optimization_barrier(values)

    def right(value, hop):
        return lax.ppermute(value, "tp", [(i, i + 1) for i in range(hop - 1, ranks - 1)])

    def left(value, hop):
        return lax.ppermute(value, "tp", [(i, i - 1) for i in range(1, ranks - hop + 1)])

    def step(chain, hop):
        return right(rights[chain][-1], hop), left(lefts[chain][-1], hop)

    halves = [tokens[chain * rows : (chain + 1) * rows] for chain in range(CHAINS)]
    rights, lefts = [[half] for half in halves], [[half] for half in halves]
    events = [(hop, chain) for hop in range(1, ranks) for chain in range(CHAINS)]
    most = slots * 3 // 4
    tail_cuts = [most, (most + slots) // 2, slots]
    tails = list(zip(tail_cuts[:-1], tail_cuts[1:]))
    near_last = len(events) - 3
    turns = [near_last * hop // (chips - 1) for hop in range(1, chips)]

    def cut(store, low, high):
        return store[low * block : high * block]

    def across(store):
        return lax.ppermute(store, "rep", ring)

    def turn(store):
        return lax.ppermute(store, "rep", swap)

    flight = [step(chain, 1) for chain in range(CHAINS)]
    bounds = [slots] * (chips - 2) + [most]
    heads, head_twins, source = [], [], delta_codes
    sent = [across(cut(source, 0, bounds[0]))]
    own_twin = turn(delta_codes)
    scale_parts = [delta_scales]
    for _ in range(1, chips):
        scale_parts.append(across(scale_parts[-1]))
    near = jnp.concatenate(scale_parts, axis=0)
    near_twin = turn(near)

    for index, (hop, chain) in enumerate(events[: near_last + 1]):
        came = sent if index in turns else []
        rights[chain].append(flight[0][0])
        lefts[chain].append(flight[0][1])
        flight = flight[1:]
        if index == 1:
            near, near_twin, rights, lefts = tie((near, near_twin, rights, lefts))
        came, rights, lefts = tie((came, rights, lefts))
        if hop + 1 < ranks:
            flight.append(step(chain, hop + 1))
        if index == near_last:
            source, rights, lefts = tie((source, rights, lefts))
        if came:
            heads.append(came[0])
            if len(heads) < chips - 1:
                source = came[0]
                sent = [across(cut(source, 0, bounds[len(heads)]))]
            else:
                sent = [across(cut(source, *ends)) for ends in tails]
            head_twins.append(turn(came[0]))

    near, near_twin = near.astype(jnp.float32), near_twin.astype(jnp.float32)
    both = jnp.concatenate([near, near_twin], axis=0)
    scales = jnp.repeat(both, width // col_blocks, axis=1)

    def merge(weight, parts, stores):
        inputs = [replica_variant, block_home, scales, base_weight] + stores
        given = [] if weight is None else [weight]
        return pl.pallas_call(
            functools.partial(merge_kernel, (reps, block, slots, tuple(parts))),
            out_shape=jax.ShapeDtypeStruct((depth, width), jnp.bfloat16),
            in_specs=[SMEM, SMEM, VMEM] + [HBM] * (1 + len(stores) + len(given)),
            out_specs=HBM,
            scratch_shapes=[
                pltpu.VMEM((depth, width), jnp.bfloat16),
                pltpu.VMEM((depth, width), jnp.bfloat16),
                pltpu.SemaphoreType.DMA((blocks,)),
                pltpu.SemaphoreType.DMA((blocks,)),
                pltpu.SemaphoreType.DMA((blocks,)),
            ],
            input_output_aliases={len(inputs): 0} if given else {},
            compiler_params=pltpu.CompilerParams(vmem_limit_bytes=VMEM_LIMIT),
            cost_estimate=BRIEF,
        )(*inputs, *given)

    parts = [(0, core, 0, slots) for core in range(CORES)]
    own_twin, rights, lefts = tie((own_twin, rights, lefts))
    weight = merge(None, parts, [delta_codes, own_twin])
    sent, weight = tie((sent, weight))
    came = sent
    came_twins = [turn(value) for value in came]
    parts = [(hop, core, 0, high) for core in range(CORES) for hop, high in enumerate(bounds, 1)]
    weight = merge(weight, parts, heads + head_twins)
    parts = [(chips - 1, core, low, high) for core in range(CORES) for low, high in tails]
    weight = merge(weight, parts, came + came_twins)
    flight, weight = tie((flight, weight))
    for (hop, chain), landing in zip(events[near_last + 1 :], flight):
        rights[chain].append(landing[0])
        lefts[chain].append(landing[1])

    arrays = []
    for chain in range(CHAINS):
        arrays += rights[chain] + lefts[chain][1:]
    total_rows = ranks * CHAINS * rows
    chunks = blocks // CHUNK_BLOCKS
    return pl.pallas_call(
        functools.partial(product_kernel, (ranks, CHUNK_BLOCKS * block)),
        out_shape=jax.ShapeDtypeStruct((total_rows, width), jnp.bfloat16),
        in_specs=[HBM] * (1 + len(arrays)),
        out_specs=VMEM,
        scratch_shapes=[
            pltpu.VMEM((total_rows, depth), jnp.bfloat16),
            pltpu.VMEM((depth, width), jnp.bfloat16),
            pltpu.VMEM((total_rows, width), jnp.float32),
            pltpu.SemaphoreType.DMA((chunks, CHAINS * ranks + 1)),
        ],
        compiler_params=pltpu.CompilerParams(vmem_limit_bytes=VMEM_LIMIT),
        cost_estimate=BRIEF,
    )(weight, *arrays)


def solution(mesh):
    in_specs = (
        P(("groups", "rep", "tp"), None),
        P(None, "tp"),
        P(("groups", "rep"), "tp"),
        P(("groups", "rep"), "tp"),
        P("groups"),
        P("groups", None),
    )
    out_specs = P(("groups", "rep"), "tp")
    return jax.shard_map(local, mesh=mesh, in_specs=in_specs, out_specs=out_specs, check_vma=False)
```

time: 144 us -> 208 us (1.44)
  waiting for transfers between devices: 79.7 us -> 138 us
  Pallas kernels: 12.6 us -> 36.7 us
  blocking collectives: 12.9 us -> 0 us
  starting transfers between devices: 29.8 us -> 24.2 us
    ppermute x13 -> x9, waiting for transfers between devices: 47.1 us -> 75.2 us  [the longest x4 74.1 us: across(): return lax.ppermute(store, 'rep', ring)]
    pallas_call x1 -> x4, Pallas kernels: 12.6 us -> 36.7 us  [the longest x3 29.2 us: merge(): pl.pallas_call(functools.partial(merge_kernel, (reps, block, slots, tuple...]
    ppermute x6, waiting for transfers between devices: 30.7 us -> 50.4 us  [left(): lax.ppermute(value, 'tp', [(i, i - 1) for i in range(1, ranks - hop + 1)])]
    all_gather x1 -> x0, blocking collectives: 12.9 us -> none  [local(): lax.all_gather(scales, 'rep', axis=0, tiled=True).astype(jnp.float32)]
    ppermute x6, waiting for transfers between devices: 1.85 us -> 12.6 us  [right(): lax.ppermute(value, 'tp', [(i, i + 1) for i in range(hop - 1, ranks - 1)])]
    ppermute x6, starting transfers between devices: 13.7 us -> 10.1 us  [right(): lax.ppermute(value, 'tp', [(i, i + 1) for i in range(hop - 1, ranks - 1)])]
    ppermute x13 -> x9, starting transfers between devices: 8.37 us -> 6.31 us  [the longest x4 5.63 us: across(): return lax.ppermute(store, 'rep', ring)]
  transfers between devices with their start and end apart: 25 -> 21, of which waited for: 13 -> 9; matrix products, arithmetic and copies ran while one was open for 2% -> 2% of each run, Pallas kernels for 0% -> 14%
where the time goes in v5:
time: 208 us
  waiting for transfers between devices  138 us (66%)
  Pallas kernels  36.7 us (18%)
  starting transfers between devices  24.2 us (12%)
  local copies, waits for them, and re-layouts  8.2 us (4%)
    ppermute x4, waiting for transfers between devices, across(): return lax.ppermute(store, 'rep', ring)  74.1 us
    ppermute x6, waiting for transfers between devices, left(): lax.ppermute(value, 'tp', [(i, i - 1) for i in range(1, ranks - hop + 1)])  50.4 us
    pallas_call x3, Pallas kernels, merge(): pl.pallas_call(functools.partial(merge_kernel, (reps, block, slots, tuple...  29.2 us
    ppermute x6, waiting for transfers between devices, right(): lax.ppermute(value, 'tp', [(i, i + 1) for i in range(hop - 1, ranks - 1)])  12.6 us
    ppermute x6, starting transfers between devices, right(): lax.ppermute(value, 'tp', [(i, i + 1) for i in range(hop - 1, ranks - 1)])  10.1 us
    ppermute x6, starting transfers between devices, left(): lax.ppermute(value, 'tp', [(i, i - 1) for i in range(1, ranks - hop + 1)])  7.74 us
    pallas_call x1, Pallas kernels, local(): pl.pallas_call(functools.partial(product_kernel, (ranks, CHUNK_BLOCKS * b...  7.51 us
    ppermute x4, starting transfers between devices, across(): return lax.ppermute(store, 'rep', ring)  5.63 us
  transfers between devices with their start and end apart: 21, of which 9 were waited for; matrix products, arithmetic and copies ran while one was open for 2% of the time, Pallas kernels for 14%

profile of v5, /device:TPU:0, one launch (start us, length us, event | category | flops | bytes accessed | tf_op | source)
XLA Modules:
  0.0 207.8 jit_solution(941416379966944107)
XLA Ops:
  0.0 2.2 %slice.17 = bf16[3072,512]{1,0:T(8,128)(2,1)S(1)} slice(bf16[4096,512]{1,0:T(8,128)(2,1)} %refs_0_.1), slice={[0:3072], [0:512]} | slice | bytes 6291456 | tf_op jit(solution)/shard_map/slice | solution.py:179
  2.2 3.0 %collective-permute-start.10 = (bf16[3072,512]{1,0:T(8,128)(2,1)S(1)}, bf16[3072,512]{1,0:T(8,128)(2,1)}, u32[]{:S(2)}, u32[]{:S(2)}) collective-permute-start(bf16[3072,512]{1,0:T(8,128)(2,1)S(1)} %slice.17), channel_id=1, source_target_pairs={{0,8},{4,12},{8,0},{12,4},{1,9},{5,13},{9,1},{13,5},{2,10},{6,14},... | collective-permute-start | bytes 9437192 | tf_op jit(solution)/shard_map/ppermute | solution.py:182
  5.4 3.5 %collective-permute-start.2 = (bf16[48,8192]{1,0:T(8,128)(2,1)S(1)}, bf16[48,8192]{1,0:T(8,128)(2,1)S(1)}, u32[]{:S(2)}, u32[]{:S(2)}) collective-permute-start(bf16[48,8192]{1,0:T(8,128)(2,1)S(1)} %get-tuple-element.125.refs_0_), channel_id=1, source_target_pairs={{0,1},{1,2},{2,3},{4,5},{5,6},{6,7},{8,9},{9,10},{10,11},{12,13},{... | collective-permute-start | bytes 2359304 | tf_op jit(solution)/shard_map/ppermute | solution.py:161
  8.9 1.3 collective-permute-start.3
  10.9 62.6 %collective-permute-done = bf16[32,4]{0,1:T(4,128)(2,1)S(1)} collective-permute-done((bf16[32,4]{0,1:T(4,128)(2,1)S(1)}, bf16[32,4]{0,1:T(4,128)(2,1)S(1)}, u32[]{:S(2)}, u32[]{:S(2)}) %collective-permute-start) | collective-permute-done | bytes 288 | tf_op jit(solution)/shard_map/ppermute | solution.py:182
  73.4 3.8 %collective-permute-start.4 = (bf16[48,8192]{1,0:T(8,128)(2,1)S(1)}, bf16[48,8192]{1,0:T(8,128)(2,1)S(1)}, u32[]{:S(2)}, u32[]{:S(2)}) collective-permute-start(bf16[48,8192]{1,0:T(8,128)(2,1)S(1)} %get-tuple-element.132.refs_7_), channel_id=1, source_target_pairs={{0,1},{1,2},{2,3},{4,5},{5,6},{6,7},{8,9},{9,10},{10,11},{12,13},{... | collective-permute-start | bytes 2359304 | tf_op jit(solution)/shard_map/ppermute | solution.py:161
  77.2 1.3 collective-permute-start.5
  78.7 1.1 collective-permute-done.1
  79.8 0.7 collective-permute-start.6
  80.5 12.6 %collective-permute-done.4.refs_8_ = bf16[48,8192]{1,0:T(8,128)(2,1)S(1)} collective-permute-done((bf16[48,8192]{1,0:T(8,128)(2,1)S(1)}, bf16[48,8192]{1,0:T(8,128)(2,1)S(1)}, u32[]{:S(2)}, u32[]{:S(2)}) %collective-permute-start.4) | collective-permute-done | bytes 786464 | tf_op jit(solution)/shard_map/ppermute | solution.py:161
  93.1 1.3 collective-permute-start.7
  94.4 3.7 %collective-permute-done.5.refs_11_ = bf16[48,8192]{1,0:T(8,128)(2,1)S(1)} collective-permute-done((bf16[48,8192]{1,0:T(8,128)(2,1)S(1)}, bf16[48,8192]{1,0:T(8,128)(2,1)S(1)}, u32[]{:S(2)}, u32[]{:S(2)}) %collective-permute-start.5) | collective-permute-done | bytes 786464 | tf_op jit(solution)/shard_map/ppermute | solution.py:164
  98.1 0.7 collective-permute-start.11
  98.8 1.3 collective-permute-start.12
  100.1 15.7 %collective-permute-done.7.refs_5_ = bf16[48,8192]{1,0:T(8,128)(2,1)S(1)} collective-permute-done((bf16[48,8192]{1,0:T(8,128)(2,1)S(1)}, bf16[48,8192]{1,0:T(8,128)(2,1)S(1)}, u32[]{:S(2)}, u32[]{:S(2)}) %collective-permute-start.7) | collective-permute-done | bytes 786464 | tf_op jit(solution)/shard_map/ppermute | solution.py:164
  115.9 15.1 %collective-permute-done.12.refs_12_ = bf16[48,8192]{1,0:T(8,128)(2,1)S(1)} collective-permute-done((bf16[48,8192]{1,0:T(8,128)(2,1)S(1)}, bf16[48,8192]{1,0:T(8,128)(2,1)S(1)}, u32[]{:S(2)}, u32[]{:S(2)}) %collective-permute-start.12) | collective-permute-done | bytes 786464 | tf_op jit(solution)/shard_map/ppermute | solution.py:164
  131.0 0.8 copy-done.13
  131.9 2.3 %fusion = (bf16[512,512]{1,0:T(8,128)(2,1)}, bf16[512,512]{1,0:T(8,128)(2,1)}) fusion(bf16[4096,512]{1,0:T(8,128)(2,1)} %refs_0_.1), kind=kLoop, calls=%fused_computation.3 | loop fusion | bytes 2097152 | tf_op jit(solution)/shard_map/slice | solution.py:179
  134.1 1.5 collective-permute-start.15
  136.5 0.7 copy.12
  137.3 11.1 %shard_map.64.refs_2_ = bf16[8192,512]{1,0:T(8,128)(2,1)} custom-call(s32[4]{0:T(128)} %variant_ref.5, s32[2,64]{1,0:T(2,128)} %home_ref.5, f32[128,512]{1,0:T(8,128)} %bitcast.4, bf16[8192,512]{1,0:T(8,128)(2,1)} %base_ref.5, bf16[4096,512]{1,0:T(8,128)(2,1)} %refs_0_.1, bf16[4096,512]{1,0:T(8,128)(2,1)} %collective-permute-done.17.refs_1_), custom_call_target="tpu_custom_call" | custom-call | flops 1 | bytes 1 | tf_op jit(solution)/shard_map/pallas_call | solution.py:226
  149.2 10.9 %collective-permute-done.16.refs_1_ = bf16[512,512]{1,0:T(8,128)(2,1)} collective-permute-done((bf16[512,512]{1,0:T(8,128)(2,1)}, bf16[512,512]{1,0:T(8,128)(2,1)}, u32[]{:S(2)}, u32[]{:S(2)}) %collective-permute-start.16) | collective-permute-done | bytes 524320 | tf_op jit(solution)/shard_map/ppermute | solution.py:182
  160.0 0.7 collective-permute-start.8
  160.7 1.3 collective-permute-start.9
  162.0 0.7 collective-permute-start.13
  162.8 1.3 collective-permute-start.14
  164.7 8.7 %shard_map.65.refs_4_ = bf16[8192,512]{1,0:T(8,128)(2,1)} custom-call(s32[4]{0:T(128)} %variant_ref.5, s32[2,64]{1,0:T(2,128)} %home_ref.5, f32[128,512]{1,0:T(8,128)} %bitcast.5, bf16[8192,512]{1,0:T(8,128)(2,1)} %base_ref.5, bf16[3072,512]{1,0:T(8,128)(2,1)} %collective-permute-done.10.refs_0_, ...), custom_call_target="tpu_custom_call", output_to_operand_aliasing={{}: (6, {})} | custom-call | flops 1 | bytes 1 | tf_op jit(solution)/shard_map/pallas_call | solution.py:226
  173.4 0.8 copy-done.20
  174.2 9.3 %shard_map.66.weight_ref = bf16[8192,512]{1,0:T(8,128)(2,1)} custom-call(s32[4]{0:T(128)} %variant_ref.5, s32[2,64]{1,0:T(2,128)} %home_ref.5, f32[128,512]{1,0:T(8,128)} %bitcast.6, bf16[8192,512]{1,0:T(8,128)(2,1)} %base_ref.5, bf16[512,512]{1,0:T(8,128)(2,1)} %collective-permute-done.15.refs_0_, ...), custom_call_target="tpu_custom_call", output_to_operand_aliasing={{}: (8, {})} | custom-call | flops 1 | bytes 1 | tf_op jit(solution)/shard_map/pallas_call | solution.py:226
  183.6 15.8 %collective-permute-done.14.refs_13_ = bf16[48,8192]{1,0:T(8,128)(2,1)S(1)} collective-permute-done((bf16[48,8192]{1,0:T(8,128)(2,1)S(1)}, bf16[48,8192]{1,0:T(8,128)(2,1)S(1)}, u32[]{:S(2)}, u32[]{:S(2)}) %collective-permute-start.14) | collective-permute-done | bytes 786464 | tf_op jit(solution)/shard_map/ppermute | solution.py:164
  199.5 0.9 copy-done.18
  200.3 7.5 %shard_map.67 = bf16[384,512]{1,0:T(8,128)(2,1)} custom-call(bf16[8192,512]{1,0:T(8,128)(2,1)} %shard_map.66.weight_ref, bf16[48,8192]{1,0:T(8,128)(2,1)} %copy-done.1, bf16[48,8192]{1,0:T(8,128)(2,1)} %copy-done.3, bf16[48,8192]{1,0:T(8,128)(2,1)} %copy-done.7, bf16[48,8192]{1,0:T(8,128)(2,1)} %copy-done.15, bf16[48,8192]{1,0:T(8,128)(2,1)} %copy-done.4, ...), custom_call_target="tpu_custom_call" | custom-call | flops 1 | bytes 1 | tf_op jit(solution)/shard_map/pallas_call | solution.py:263
  (66 shorter events, 3.2 us)
Async XLA Ops:
  2.2 128.8 %collective-permute-start.10 = (bf16[3072,512]{1,0:T(8,128)(2,1)S(1)}, bf16[3072,512]{1,0:T(8,128)(2,1)}, u32[]{:S(2)}, u32[]{:S(2)}) collective-permute-start(bf16[3072,512]{1,0:T(8,128)(2,1)S(1)} %slice.17), channel_id=1, source_target_pairs={{0,8},{4,12},{8,0},{12,4},{1,9},{5,13},{9,1},{13,5},{2,10},{6,14},... | collective-permute-start | bytes 9437192 | tf_op jit(solution)/shard_map/ppermute | solution.py:182
  5.3 143.1 %copy-start = (bf16[48,8192]{1,0:T(8,128)(2,1)}, bf16[48,8192]{1,0:T(8,128)(2,1)S(1)}, u32[]{:S(2)}) copy-start(bf16[48,8192]{1,0:T(8,128)(2,1)S(1)} %get-tuple-element.132.refs_7_) | copy-start | bytes 2359300
  5.3 143.1 %copy-start.1 = (bf16[48,8192]{1,0:T(8,128)(2,1)}, bf16[48,8192]{1,0:T(8,128)(2,1)S(1)}, u32[]{:S(2)}) copy-start(bf16[48,8192]{1,0:T(8,128)(2,1)S(1)} %get-tuple-element.125.refs_0_) | copy-start | bytes 2359300
  5.4 71.9 %collective-permute-start.2 = (bf16[48,8192]{1,0:T(8,128)(2,1)S(1)}, bf16[48,8192]{1,0:T(8,128)(2,1)S(1)}, u32[]{:S(2)}, u32[]{:S(2)}) collective-permute-start(bf16[48,8192]{1,0:T(8,128)(2,1)S(1)} %get-tuple-element.125.refs_0_), channel_id=1, source_target_pairs={{0,1},{1,2},{2,3},{4,5},{5,6},{6,7},{8,9},{9,10},{10,11},{12,13},{... | collective-permute-start | bytes 2359304 | tf_op jit(solution)/shard_map/ppermute | solution.py:161
  8.9 69.7 %collective-permute-start.3 = (bf16[48,8192]{1,0:T(8,128)(2,1)S(1)}, bf16[48,8192]{1,0:T(8,128)(2,1)S(1)}, u32[]{:S(2)}, u32[]{:S(2)}) collective-permute-start(bf16[48,8192]{1,0:T(8,128)(2,1)S(1)} %get-tuple-element.125.refs_0_), channel_id=1, source_target_pairs={{1,0},{2,1},{3,2},{5,4},{6,5},{7,6},{9,8},{10,9},{11,10},{13,12},{... | collective-permute-start | bytes 2359304 | tf_op jit(solution)/shard_map/ppermute | solution.py:164
  10.2 127.1 %collective-permute-start.17 = (bf16[4096,512]{1,0:T(8,128)(2,1)}, bf16[4096,512]{1,0:T(8,128)(2,1)}, u32[]{:S(2)}, u32[]{:S(2)}) collective-permute-start(bf16[4096,512]{1,0:T(8,128)(2,1)} %refs_0_.1), channel_id=1, source_target_pairs={{0,4},{4,0},{8,12},{12,8},{1,5},{5,1},{9,13},{13,9},{2,6},{6,2},{1... | collective-permute-start | bytes 12582920 | tf_op jit(solution)/shard_map/ppermute | solution.py:185
  10.3 63.2 %collective-permute-start = (bf16[32,4]{0,1:T(4,128)(2,1)S(1)}, bf16[32,4]{0,1:T(4,128)(2,1)S(1)}, u32[]{:S(2)}, u32[]{:S(2)}) collective-permute-start(bf16[32,4]{0,1:T(4,128)(2,1)S(1)} %copy-done.21), channel_id=1, source_target_pairs={{0,8},{4,12},{8,0},{12,4},{1,9},{5,13},{9,1},{13,5},{2,10},{6,14},... | collective-permute-start | bytes 776 | tf_op jit(solution)/shard_map/ppermute | solution.py:182
  73.4 19.6 %collective-permute-start.4 = (bf16[48,8192]{1,0:T(8,128)(2,1)S(1)}, bf16[48,8192]{1,0:T(8,128)(2,1)S(1)}, u32[]{:S(2)}, u32[]{:S(2)}) collective-permute-start(bf16[48,8192]{1,0:T(8,128)(2,1)S(1)} %get-tuple-element.132.refs_7_), channel_id=1, source_target_pairs={{0,1},{1,2},{2,3},{4,5},{5,6},{6,7},{8,9},{9,10},{10,11},{12,13},{... | collective-permute-start | bytes 2359304 | tf_op jit(solution)/shard_map/ppermute | solution.py:161
  77.2 71.2 %copy-start.3 = (bf16[48,8192]{1,0:T(8,128)(2,1)}, bf16[48,8192]{1,0:T(8,128)(2,1)S(1)}, u32[]{:S(2)}) copy-start(bf16[48,8192]{1,0:T(8,128)(2,1)S(1)} %collective-permute-done.2.refs_1_) | copy-start | bytes 2359300
  77.2 20.9 %collective-permute-start.5 = (bf16[48,8192]{1,0:T(8,128)(2,1)S(1)}, bf16[48,8192]{1,0:T(8,128)(2,1)S(1)}, u32[]{:S(2)}, u32[]{:S(2)}) collective-permute-start(bf16[48,8192]{1,0:T(8,128)(2,1)S(1)} %get-tuple-element.132.refs_7_), channel_id=1, source_target_pairs={{1,0},{2,1},{3,2},{5,4},{6,5},{7,6},{9,8},{10,9},{11,10},{13,12},{... | collective-permute-start | bytes 2359304 | tf_op jit(solution)/shard_map/ppermute | solution.py:164
  78.6 69.8 %copy-start.4 = (bf16[48,8192]{1,0:T(8,128)(2,1)}, bf16[48,8192]{1,0:T(8,128)(2,1)S(1)}, u32[]{:S(2)}) copy-start(bf16[48,8192]{1,0:T(8,128)(2,1)S(1)} %collective-permute-done.3.refs_4_) | copy-start | bytes 2359300
  78.6 1.2 collective-permute-start.1
  79.8 19.0 %collective-permute-start.6 = (bf16[48,8192]{1,0:T(8,128)(2,1)S(1)}, bf16[48,8192]{1,0:T(8,128)(2,1)S(1)}, u32[]{:S(2)}, u32[]{:S(2)}) collective-permute-start(bf16[48,8192]{1,0:T(8,128)(2,1)S(1)} %collective-permute-done.2.refs_1_), channel_id=1, source_target_pairs={{1,2},{2,3},{5,6},{6,7},{9,10},{10,11},{13,14},{14,15},{17,18},{18... | collective-permute-start | bytes 2359304 | tf_op jit(solution)/shard_map/ppermute | solution.py:161
  93.1 37.9 %copy-start.5 = (bf16[48,8192]{1,0:T(8,128)(2,1)}, bf16[48,8192]{1,0:T(8,128)(2,1)S(1)}, u32[]{:S(2)}) copy-start(bf16[48,8192]{1,0:T(8,128)(2,1)S(1)} %collective-permute-done.4.refs_8_) | copy-start | bytes 2359300
  93.1 22.8 %collective-permute-start.7 = (bf16[48,8192]{1,0:T(8,128)(2,1)S(1)}, bf16[48,8192]{1,0:T(8,128)(2,1)S(1)}, u32[]{:S(2)}, u32[]{:S(2)}) collective-permute-start(bf16[48,8192]{1,0:T(8,128)(2,1)S(1)} %collective-permute-done.3.refs_4_), channel_id=1, source_target_pairs={{1,0},{2,1},{5,4},{6,5},{9,8},{10,9},{13,12},{14,13},{17,16},{18,1... | collective-permute-start | bytes 2359304 | tf_op jit(solution)/shard_map/ppermute | solution.py:164
  98.1 32.9 %copy-start.6 = (bf16[48,8192]{1,0:T(8,128)(2,1)}, bf16[48,8192]{1,0:T(8,128)(2,1)S(1)}, u32[]{:S(2)}) copy-start(bf16[48,8192]{1,0:T(8,128)(2,1)S(1)} %collective-permute-done.5.refs_11_) | copy-start | bytes 2359300
  98.1 17.8 %collective-permute-start.11 = (bf16[48,8192]{1,0:T(8,128)(2,1)S(1)}, bf16[48,8192]{1,0:T(8,128)(2,1)S(1)}, u32[]{:S(2)}, u32[]{:S(2)}) collective-permute-start(bf16[48,8192]{1,0:T(8,128)(2,1)S(1)} %collective-permute-done.4.refs_8_), channel_id=1, source_target_pairs={{1,2},{2,3},{5,6},{6,7},{9,10},{10,11},{13,14},{14,15},{17,18},{18... | collective-permute-start | bytes 2359304 | tf_op jit(solution)/shard_map/ppermute | solution.py:161
  98.8 32.2 %copy-start.7 = (bf16[48,8192]{1,0:T(8,128)(2,1)}, bf16[48,8192]{1,0:T(8,128)(2,1)S(1)}, u32[]{:S(2)}) copy-start(bf16[48,8192]{1,0:T(8,128)(2,1)S(1)} %collective-permute-done.6.refs_2_) | copy-start | bytes 2359300
  98.8 32.1 %collective-permute-start.12 = (bf16[48,8192]{1,0:T(8,128)(2,1)S(1)}, bf16[48,8192]{1,0:T(8,128)(2,1)S(1)}, u32[]{:S(2)}, u32[]{:S(2)}) collective-permute-start(bf16[48,8192]{1,0:T(8,128)(2,1)S(1)} %collective-permute-done.5.refs_11_), channel_id=1, source_target_pairs={{1,0},{2,1},{5,4},{6,5},{9,8},{10,9},{13,12},{14,13},{17,16},{18,1... | collective-permute-start | bytes 2359304 | tf_op jit(solution)/shard_map/ppermute | solution.py:164
  131.9 32.2 %collective-permute-start.20 = (bf16[3072,512]{1,0:T(8,128)(2,1)}, bf16[3072,512]{1,0:T(8,128)(2,1)}, u32[]{:S(2)}, u32[]{:S(2)}) collective-permute-start(bf16[3072,512]{1,0:T(8,128)(2,1)} %collective-permute-done.10.refs_0_), channel_id=1, source_target_pairs={{0,4},{4,0},{8,12},{12,8},{1,5},{5,1},{9,13},{13,9},{2,6},{6,2},{1... | collective-permute-start | bytes 9437192 | tf_op jit(solution)/shard_map/ppermute | solution.py:185
  134.1 15.0 %collective-permute-start.15 = (bf16[512,512]{1,0:T(8,128)(2,1)}, bf16[512,512]{1,0:T(8,128)(2,1)}, u32[]{:S(2)}, u32[]{:S(2)}) collective-permute-start(bf16[512,512]{1,0:T(8,128)(2,1)} %get-tuple-element.140), channel_id=1, source_target_pairs={{0,8},{4,12},{8,0},{12,4},{1,9},{5,13},{9,1},{13,5},{2,10},{6,14},... | collective-permute-start | bytes 1572872 | tf_op jit(solution)/shard_map/ppermute | solution.py:182
  135.6 24.4 %collective-permute-start.16 = (bf16[512,512]{1,0:T(8,128)(2,1)}, bf16[512,512]{1,0:T(8,128)(2,1)}, u32[]{:S(2)}, u32[]{:S(2)}) collective-permute-start(bf16[512,512]{1,0:T(8,128)(2,1)} %get-tuple-element.139), channel_id=1, source_target_pairs={{0,8},{4,12},{8,0},{12,4},{1,9},{5,13},{9,1},{13,5},{2,10},{6,14},... | collective-permute-start | bytes 1572872 | tf_op jit(solution)/shard_map/ppermute | solution.py:182
  137.3 22.7 %copy-start.8 = (bf16[48,8192]{1,0:T(8,128)(2,1)S(1)}, bf16[48,8192]{1,0:T(8,128)(2,1)}, u32[]{:S(2)}) copy-start(bf16[48,8192]{1,0:T(8,128)(2,1)} %copy-done.7) | copy-start | bytes 2359300
  137.3 23.5 %copy-start.10 = (bf16[48,8192]{1,0:T(8,128)(2,1)S(1)}, bf16[48,8192]{1,0:T(8,128)(2,1)}, u32[]{:S(2)}) copy-start(bf16[48,8192]{1,0:T(8,128)(2,1)} %copy-done.9) | copy-start | bytes 2359300
  137.3 24.8 %copy-start.12 = (bf16[48,8192]{1,0:T(8,128)(2,1)S(1)}, bf16[48,8192]{1,0:T(8,128)(2,1)}, u32[]{:S(2)}) copy-start(bf16[48,8192]{1,0:T(8,128)(2,1)} %copy-done.11) | copy-start | bytes 2359300
  137.3 25.5 %copy-start.14 = (bf16[48,8192]{1,0:T(8,128)(2,1)S(1)}, bf16[48,8192]{1,0:T(8,128)(2,1)}, u32[]{:S(2)}) copy-start(bf16[48,8192]{1,0:T(8,128)(2,1)} %copy-done.13) | copy-start | bytes 2359300
  160.0 2.8 %collective-permute-start.18 = (bf16[512,512]{1,0:T(8,128)(2,1)}, bf16[512,512]{1,0:T(8,128)(2,1)S(1)}, u32[]{:S(2)}, u32[]{:S(2)}) collective-permute-start(bf16[512,512]{1,0:T(8,128)(2,1)} %collective-permute-done.15.refs_0_), channel_id=1, source_target_pairs={{0,4},{4,0},{8,12},{12,8},{1,5},{5,1},{9,13},{13,9},{2,6},{6,2},{1... | collective-permute-start | bytes 1572872 | tf_op jit(solution)/shard_map/ppermute | solution.py:185
  160.0 23.5 %collective-permute-start.8 = (bf16[48,8192]{1,0:T(8,128)(2,1)S(1)}, bf16[48,8192]{1,0:T(8,128)(2,1)S(1)}, u32[]{:S(2)}, u32[]{:S(2)}) collective-permute-start(bf16[48,8192]{1,0:T(8,128)(2,1)S(1)} %copy-done.8), channel_id=1, source_target_pairs={{2,3},{6,7},{10,11},{14,15},{18,19},{22,23},{26,27},{30,31}} | collective-permute-start | bytes 2359304 | tf_op jit(solution)/shard_map/ppermute | solution.py:161
  160.7 22.8 %collective-permute-start.9 = (bf16[48,8192]{1,0:T(8,128)(2,1)S(1)}, bf16[48,8192]{1,0:T(8,128)(2,1)S(1)}, u32[]{:S(2)}, u32[]{:S(2)}) collective-permute-start(bf16[48,8192]{1,0:T(8,128)(2,1)S(1)} %copy-done.10), channel_id=1, source_target_pairs={{1,0},{5,4},{9,8},{13,12},{17,16},{21,20},{25,24},{29,28}} | collective-permute-start | bytes 2359304 | tf_op jit(solution)/shard_map/ppermute | solution.py:164
  162.0 21.5 %collective-permute-start.13 = (bf16[48,8192]{1,0:T(8,128)(2,1)S(1)}, bf16[48,8192]{1,0:T(8,128)(2,1)S(1)}, u32[]{:S(2)}, u32[]{:S(2)}) collective-permute-start(bf16[48,8192]{1,0:T(8,128)(2,1)S(1)} %copy-done.12), channel_id=1, source_target_pairs={{2,3},{6,7},{10,11},{14,15},{18,19},{22,23},{26,27},{30,31}} | collective-permute-start | bytes 2359304 | tf_op jit(solution)/shard_map/ppermute | solution.py:161
  162.8 36.6 %collective-permute-start.14 = (bf16[48,8192]{1,0:T(8,128)(2,1)S(1)}, bf16[48,8192]{1,0:T(8,128)(2,1)S(1)}, u32[]{:S(2)}, u32[]{:S(2)}) collective-permute-start(bf16[48,8192]{1,0:T(8,128)(2,1)S(1)} %copy-done.14), channel_id=1, source_target_pairs={{1,0},{5,4},{9,8},{13,12},{17,16},{21,20},{25,24},{29,28}} | collective-permute-start | bytes 2359304 | tf_op jit(solution)/shard_map/ppermute | solution.py:164
  164.1 9.3 %collective-permute-start.19 = (bf16[512,512]{1,0:T(8,128)(2,1)}, bf16[512,512]{1,0:T(8,128)(2,1)S(1)}, u32[]{:S(2)}, u32[]{:S(2)}) collective-permute-start(bf16[512,512]{1,0:T(8,128)(2,1)} %collective-permute-done.16.refs_1_), channel_id=1, source_target_pairs={{0,4},{4,0},{8,12},{12,8},{1,5},{5,1},{9,13},{13,9},{2,6},{6,2},{1... | collective-permute-start | bytes 1572872 | tf_op jit(solution)/shard_map/ppermute | solution.py:185
  (11 other events, 106.6 us)

commit v6 on v0

v6 whole, which is shorter than its diff:
```python
import functools
import jax
import jax.numpy as jnp
from jax import lax
from jax.experimental import pallas as pl
from jax.experimental.pallas import tpu as pltpu
from jax.sharding import PartitionSpec as P

CORES = 2
CHUNK_BLOCKS = 8


CHAINS = 2
VMEM_LIMIT = 56 * 1024 * 1024
SMEM = pl.BlockSpec(memory_space=pltpu.SMEM)
VMEM = pl.BlockSpec(memory_space=pltpu.VMEM)
HBM = pl.BlockSpec(memory_space=pl.ANY)
BRIEF = pl.CostEstimate(flops=1, bytes_accessed=1, transcendentals=0)


def scale_kernel(block, scale_ref, codes_ref, *out_refs):
    col_blocks = scale_ref.shape[1]
    wide = codes_ref.shape[1] // col_blocks
    first = 0
    for out_ref in out_refs:
        count = out_ref.shape[0] // block

        @pl.loop(0, count)
        def _(index):
            source = pl.ds(pl.multiple_of((first + index) * block, block), block)
            target = pl.ds(pl.multiple_of(index * block, block), block)
            for col in range(col_blocks):
                at = pl.ds(col * wide, wide)
                delta = codes_ref[source, at].astype(jnp.float32) * scale_ref[first + index, col]
                out_ref[target, at] = delta.astype(jnp.bfloat16)

        first += count


def merge_kernel(block, parts, row_ref, base_ref, *refs):
    stores = refs[: len(parts)]
    out_ref, base_buf, delta_buf, base_sems, delta_sems, out_sems = refs[-6:]
    blocks = row_ref.shape[0]

    def rows(index):
        return pl.ds(pl.multiple_of(index * block, block), block)

    def copies(index, store, slot):
        return (
            pltpu.make_async_copy(base_ref.at[rows(index), :], base_buf.at[rows(index), :], base_sems.at[index]),
            pltpu.make_async_copy(store.at[rows(slot), :], delta_buf.at[rows(index), :], delta_sems.at[index]),
        )

    def result(index):
        return pltpu.make_async_copy(base_buf.at[rows(index), :], out_ref.at[rows(index), :], out_sems.at[index])

    def inside(row, part):
        return (row >= part[0]) & (row < part[1])

    def present(index):
        row = row_ref[index]
        return functools.reduce(jnp.logical_or, [inside(row, part) for part in parts])

    @pl.loop(0, blocks)
    def _(index):
        row = row_ref[index]
        for part, store in zip(parts, stores):

            @pl.when(inside(row, part))
            def _():
                for copy in copies(index, store, row - part[0]):
                    copy.start()

    @pl.loop(0, blocks)
    def _(index):
        @pl.when(present(index))
        def _():
            for copy in copies(index, stores[0], 0):
                copy.wait()
            merged = base_buf[rows(index), :].astype(jnp.float32) + delta_buf[rows(index), :].astype(jnp.float32)
            base_buf[rows(index), :] = merged.astype(jnp.bfloat16)
            result(index).start()

    @pl.loop(0, blocks)
    def _(index):
        @pl.when(present(index))
        def _():
            result(index).wait()


def product_kernel(ranks, span, weight_ref, *refs):
    gathered = refs[:CHAINS]
    out_ref, token_buf, weight_buf, total, sems = refs[CHAINS:]
    height, depth = gathered[0].shape
    rows = height // ranks
    chunks = depth // span

    def copies(chunk):
        at = pl.ds(pl.multiple_of(chunk * span, span), span)
        yield pltpu.make_async_copy(weight_ref.at[at, :], weight_buf.at[at, :], sems.at[chunk, CHAINS])
        for chain, source in enumerate(gathered):
            target = token_buf.at[pl.ds(chain * height, height), at]
            yield pltpu.make_async_copy(source.at[:, at], target, sems.at[chunk, chain])

    @pl.loop(0, chunks)
    def _(chunk):
        for copy in copies(chunk):
            copy.start()

    total[...] = jnp.zeros_like(total)

    @pl.loop(0, chunks)
    def _(chunk):
        for copy in copies(chunk):
            copy.wait()
        at = pl.ds(pl.multiple_of(chunk * span, span), span)
        total[...] += jnp.dot(token_buf[:, at], weight_buf[at, :], preferred_element_type=jnp.float32)

    for chain in range(CHAINS):
        for origin in range(ranks):
            source = pl.ds(chain * height + origin * rows, rows)
            out_ref[pl.ds((origin * CHAINS + chain) * rows, rows), :] = total[source, :].astype(out_ref.dtype)


def local(tokens, base_weight, delta_codes, delta_scales, replica_variant, block_home):
    ranks, reps = lax.axis_size("tp"), lax.axis_size("rep")
    blocks = block_home.shape[1]
    depth, width = base_weight.shape
    rows = tokens.shape[0] // CHAINS
    block = depth // blocks
    slots = delta_scales.shape[0]
    rep = lax.axis_index("rep")
    chips = reps // CORES
    ring = [(i, (i + CORES) % reps) for i in range(reps)]
    swap = [(i, i // CORES * CORES + (i + 1) % CORES) for i in range(reps)]

    halves = [tokens[chain * rows : (chain + 1) * rows] for chain in range(CHAINS)]
    gathered = [lax.all_gather(half, "tp", axis=0, tiled=True) for half in halves]
    cuts = [0, slots * 3 // 4, slots]
    pieces = len(cuts) - 1

    def across(store):
        return lax.ppermute(store, "rep", ring)

    def turn(store):
        return lax.ppermute(store, "rep", swap)

    homes = block_home[replica_variant[rep]]
    holder = homes // slots
    away = (rep // CORES - holder // CORES + chips) % chips
    turned = (rep % CORES + holder % CORES) % CORES
    row_of = (turned * chips + away) * slots + homes % slots

    deltas = pl.pallas_call(
        functools.partial(scale_kernel, block),
        out_shape=[
            jax.ShapeDtypeStruct(((high - low) * block, width), jnp.bfloat16)
            for low, high in zip(cuts[:-1], cuts[1:])
        ],
        in_specs=[SMEM, VMEM],
        out_specs=[VMEM] * pieces,
        compiler_params=pltpu.CompilerParams(vmem_limit_bytes=VMEM_LIMIT),
        cost_estimate=BRIEF,
    )(delta_scales.astype(jnp.float32), delta_codes)
    held, twins = [deltas], [[turn(delta) for delta in deltas]]
    for _ in range(1, chips):
        held.append([across(value) for value in held[-1]])
        twins.append([turn(value) for value in held[-1]])

    def merge(weight, chosen):
        parts, stores = [], []
        for core, kept in enumerate((held, twins)):
            for hop, piece in chosen:
                place = (core * chips + hop) * slots
                parts.append((place + cuts[piece], place + cuts[piece + 1]))
                stores.append(kept[hop][piece])
        inputs = [row_of, base_weight] + stores
        given = [] if weight is None else [weight]
        return pl.pallas_call(
            functools.partial(merge_kernel, block, tuple(parts)),
            out_shape=jax.ShapeDtypeStruct((depth, width), jnp.bfloat16),
            in_specs=[SMEM] + [HBM] * (1 + len(stores) + len(given)),
            out_specs=HBM,
            scratch_shapes=[
                pltpu.VMEM((depth, width), jnp.bfloat16),
                pltpu.VMEM((depth, width), jnp.bfloat16),
                pltpu.SemaphoreType.DMA((blocks,)),
                pltpu.SemaphoreType.DMA((blocks,)),
                pltpu.SemaphoreType.DMA((blocks,)),
            ],
            input_output_aliases={len(inputs): 0} if given else {},
            compiler_params=pltpu.CompilerParams(vmem_limit_bytes=VMEM_LIMIT),
            cost_estimate=BRIEF,
        )(*inputs, *given)

    last = [(chips - 1, piece) for piece in range(1, pieces)]
    early = [(hop, piece) for hop in range(chips) for piece in range(pieces) if (hop, piece) not in last]
    weight = merge(merge(None, early), last)
    gathered, weight = lax.optimization_barrier((gathered, weight))
    total_rows = ranks * CHAINS * rows
    chunks = blocks // CHUNK_BLOCKS
    return pl.pallas_call(
        functools.partial(product_kernel, ranks, CHUNK_BLOCKS * block),
        out_shape=jax.ShapeDtypeStruct((total_rows, width), jnp.bfloat16),
        in_specs=[HBM] * (1 + CHAINS),
        out_specs=VMEM,
        scratch_shapes=[
            pltpu.VMEM((total_rows, depth), jnp.bfloat16),
            pltpu.VMEM((depth, width), jnp.bfloat16),
            pltpu.VMEM((total_rows, width), jnp.float32),
            pltpu.SemaphoreType.DMA((chunks, CHAINS + 1)),
        ],
        compiler_params=pltpu.CompilerParams(vmem_limit_bytes=VMEM_LIMIT),
        cost_estimate=BRIEF,
    )(weight, *gathered)


def solution(mesh):
    in_specs = (
        P(("groups", "rep", "tp"), None),
        P(None, "tp"),
        P(("groups", "rep"), "tp"),
        P(("groups", "rep"), "tp"),
        P("groups"),
        P("groups", None),
    )
    out_specs = P(("groups", "rep"), "tp")
    return jax.shard_map(local, mesh=mesh, in_specs=in_specs, out_specs=out_specs, check_vma=False)
```

time: 221 us -> 153 us (0.69)
  waiting for transfers between devices: 137 us -> 99.1 us
  Pallas kernels: 0 us -> 29.1 us
  local copies, waits for them, and re-layouts: 28.6 us -> 3.94 us
  matrix products: 17.1 us -> 0 us
  other arithmetic: 13.4 us -> 0.55 us
  starting transfers between devices: 10.6 us -> 5.03 us
    all_to_all x2 -> x0, waiting for transfers between devices: 137 us -> none  [the longest x1 137 us: local(): lax.all_to_all(send_codes, 'rep', split_axis=0, concat_axis=0, tiled=True)]
    ppermute x0 -> x6, waiting for transfers between devices: none -> 92.1 us  [the longest x2 92.1 us: across(): return lax.ppermute(store, 'rep', ring)]
    pallas_call x0 -> x4, Pallas kernels: none -> 29.1 us  [the longest x2 16.9 us: merge(): pl.pallas_call(functools.partial(merge_kernel, block, tuple(parts)), out_...]
    gather x4 -> x0, local copies, waits for them, and re-layouts: 20.5 us -> none  [the longest x1 10.1 us: local(): got_codes.reshape(holders * capacity, block_size, width)[source]]
    dot_general x1 -> x0, matrix products: 17.1 us -> none  [local(): jnp.dot(lax.all_gather(tokens, 'tp', axis=0, tiled=True), merged, preferr...]
    select_n x5 -> x0, other arithmetic: 11.3 us -> none  [the longest x1 10.7 us: local(): jnp.where(valid[:, :, None, None], send_codes, jnp.zeros_like(send_codes))]
    all_to_all x2 -> x0, starting transfers between devices: 10.5 us -> none  [the longest x1 6.33 us: local(): lax.all_to_all(send_codes, 'rep', split_axis=0, concat_axis=0, tiled=True)]
    all_gather x1 -> x2, waiting for transfers between devices: 0.01 us -> 6.96 us  [local(): lax.all_gather(half, 'tp', axis=0, tiled=True)]
  transfers between devices with their start and end apart: 3 -> 8, of which waited for: 1 -> 3; matrix products, arithmetic and copies ran while one was open for 14% -> 1% of each run, Pallas kernels for 0% -> 14%
where the time goes in v6:
time: 153 us
  waiting for transfers between devices  99.1 us (65%)
  Pallas kernels  29.1 us (19%)
  between operations  15.5 us (10%)
  starting transfers between devices  5.03 us (3%)
  local copies, waits for them, and re-layouts  3.94 us (3%)
    ppermute x2, waiting for transfers between devices, across(): return lax.ppermute(store, 'rep', ring)  92.1 us
    pallas_call x2, Pallas kernels, merge(): pl.pallas_call(functools.partial(merge_kernel, block, tuple(parts)), out_...  16.9 us
    pallas_call x1, Pallas kernels, local(): pl.pallas_call(functools.partial(product_kernel, ranks, CHUNK_BLOCKS * bl...  7.02 us
    all_gather x2, waiting for transfers between devices, local(): lax.all_gather(half, 'tp', axis=0, tiled=True)  6.96 us
    pallas_call x1, Pallas kernels, local(): pl.pallas_call(functools.partial(scale_kernel, block), out_shape=[jax.Sha...  5.22 us
    ppermute x2, starting transfers between devices, across(): return lax.ppermute(store, 'rep', ring)  4.68 us
  transfers between devices with their start and end apart: 8, of which 3 were waited for; matrix products, arithmetic and copies ran while one was open for 1% of the time, Pallas kernels for 14%

profile of v6, /device:TPU:0, one launch (start us, length us, event | category | flops | bytes accessed | tf_op | source)
XLA Modules:
  0.0 153.2 jit_solution(11500631126549697496)
XLA Ops:
  6.5 0.0 copy-start.1
  6.5 0.0 all-gather.3.cloned.1.call-start
  6.5 2.6 %fusion.6 = (bf16[48,8192]{1,0:T(8,128)(2,1)}, bf16[48,8192]{1,0:T(8,128)(2,1)}) fusion(bf16[96,8192]{1,0:T(8,128)(2,1)} %param.6), kind=kLoop, calls=%fused_computation.23 | loop fusion | bytes 3145728 | tf_op jit(solution)/shard_map/slice | solution.py:137
  9.2 0.0 copy-start.3
  9.2 0.0 all-gather.3.cloned.1.call-update
  9.2 0.0 all-gather.5.cloned.1.call-start
  9.3 0.0 copy-done.1
  9.3 0.7 copy.9.scale_ref
  10.0 5.2 %shard_map.64 = (bf16[3072,512]{1,0:T(8,128)(2,1)}, bf16[1024,512]{1,0:T(8,128)(2,1)}) custom-call(f32[32,4]{1,0:T(8,128)} %copy.9.scale_ref, bf16[4096,512]{1,0:T(8,128)(2,1)} %codes_ref.1), custom_call_target="tpu_custom_call" | custom-call | flops 1 | bytes 1 | tf_op jit(solution)/shard_map/pallas_call | solution.py:154
  15.2 2.9 %collective-permute-start.2 = (bf16[3072,512]{1,0:T(8,128)(2,1)}, bf16[3072,512]{1,0:T(8,128)(2,1)S(1)}, u32[]{:S(2)}, u32[]{:S(2)}) collective-permute-start(bf16[3072,512]{1,0:T(8,128)(2,1)} %get-tuple-element.11.refs_0_), channel_id=1, source_target_pairs={{0,8},{4,12},{8,0},{12,4},{1,9},{5,13},{9,1},{13,5},{2,10},{6,14},... | collective-permute-start | bytes 9437192 | tf_op jit(solution)/shard_map/ppermute | solution.py:143
  18.1 0.0 all-gather.5.cloned.1.call-update
  18.2 0.1 collective-permute-start.3
  18.2 68.2 %collective-permute-done.2.refs_2_ = bf16[3072,512]{1,0:T(8,128)(2,1)S(1)} collective-permute-done((bf16[3072,512]{1,0:T(8,128)(2,1)}, bf16[3072,512]{1,0:T(8,128)(2,1)S(1)}, u32[]{:S(2)}, u32[]{:S(2)}) %collective-permute-start.2) | collective-permute-done | bytes 3145760 | tf_op jit(solution)/shard_map/ppermute | solution.py:143
  86.4 0.0 collective-permute-start.5
  86.4 1.7 %collective-permute-start = (bf16[1024,512]{1,0:T(8,128)(2,1)}, bf16[1024,512]{1,0:T(8,128)(2,1)}, u32[]{:S(2)}, u32[]{:S(2)}) collective-permute-start(bf16[1024,512]{1,0:T(8,128)(2,1)} %get-tuple-element.10.refs_1_), channel_id=1, source_target_pairs={{0,8},{4,12},{8,0},{12,4},{1,9},{5,13},{9,1},{13,5},{2,10},{6,14},... | collective-permute-start | bytes 3145736 | tf_op jit(solution)/shard_map/ppermute | solution.py:143
  88.2 0.2 collective-permute-start.4
  88.4 23.9 %collective-permute-done.refs_0_ = bf16[1024,512]{1,0:T(8,128)(2,1)} collective-permute-done((bf16[1024,512]{1,0:T(8,128)(2,1)}, bf16[1024,512]{1,0:T(8,128)(2,1)}, u32[]{:S(2)}, u32[]{:S(2)}) %collective-permute-start) | collective-permute-done | bytes 1048608 | tf_op jit(solution)/shard_map/ppermute | solution.py:143
  112.3 0.0 collective-permute-start.1
  112.3 0.0 copy-done.3
  112.3 0.6 dynamic_slice.6
  114.9 0.0 copy-done.2
  114.9 0.5 fusion.1.row_ref
  115.4 0.0 collective-permute-done.4.refs_4_
  115.4 0.0 collective-permute-done.3.refs_3_
  115.5 0.0 collective-permute-done.5.refs_5_
  115.5 0.0 copy-done
  115.5 11.4 %shard_map.65.refs_2_ = bf16[8192,512]{1,0:T(8,128)(2,1)} custom-call(s32[64]{0:T(128)} %fusion.1.row_ref, bf16[8192,512]{1,0:T(8,128)(2,1)} %base_ref.3, bf16[3072,512]{1,0:T(8,128)(2,1)} %get-tuple-element.11.refs_0_, bf16[1024,512]{1,0:T(8,128)(2,1)} %get-tuple-element.10.refs_1_, bf16[3072,512]{1,0:T(8,128)(2,1)} %copy-done, ...), custom_call_target="tpu_custom_call" | custom-call | flops 1 | bytes 1 | tf_op jit(solution)/shard_map/pallas_call | solution.py:179
  126.9 0.0 collective-permute-done.1.refs_1_
  126.9 5.4 %shard_map.66.weight_ref = bf16[8192,512]{1,0:T(8,128)(2,1)} custom-call(s32[64]{0:T(128)} %fusion.1.row_ref, bf16[8192,512]{1,0:T(8,128)(2,1)} %base_ref.3, bf16[1024,512]{1,0:T(8,128)(2,1)} %collective-permute-done.refs_0_, bf16[1024,512]{1,0:T(8,128)(2,1)} %collective-permute-done.1.refs_1_, ...), custom_call_target="tpu_custom_call", output_to_operand_aliasing={{}: (4, {})} | custom-call | flops 1 | bytes 1 | tf_op jit(solution)/shard_map/pallas_call | solution.py:179
  132.4 0.0 all-gather.3.cloned.1.call-done.refs_0_
  132.4 6.9 %all-gather.5.cloned.1.call-done.refs_1_ = bf16[192,8192]{1,0:T(8,128)(2,1)} async-done(((bf16[48,8192]{1,0:T(8,128)(2,1)}), bf16[192,8192]{1,0:T(8,128)(2,1)}) %all-gather.5.cloned.1.call-update) | async-done | bytes 3145744 | tf_op jit(solution)/shard_map/all_gather | solution.py:138
  139.3 7.0 %shard_map.67 = bf16[384,512]{1,0:T(8,128)(2,1)} custom-call(bf16[8192,512]{1,0:T(8,128)(2,1)} %shard_map.66.weight_ref, bf16[192,8192]{1,0:T(8,128)(2,1)} %all-gather.3.cloned.1.call-done.refs_0_, bf16[192,8192]{1,0:T(8,128)(2,1)} %all-gather.5.cloned.1.call-done.refs_1_), custom_call_target="tpu_custom_call" | custom-call | flops 1 | bytes 1 | tf_op jit(solution)/shard_map/pallas_call | solution.py:202
  (2 shorter events, 0.0 us)
Async XLA Ops:
  6.5 2.7 %copy-start.1 = (bf16[32,4]{0,1:T(4,128)(2,1)S(1)}, bf16[32,4]{0,1:T(4,128)(2,1)}, u32[]{:S(2)}) copy-start(bf16[32,4]{0,1:T(4,128)(2,1)} %param.9) | copy-start | bytes 772
  6.5 125.8 %all-gather.3.cloned.1.call-start = ((), (), s32[]{:S(2)}) async-start(), calls=%async_computation | async-start | bytes 3932160 | tf_op jit(solution)/shard_map/all_gather | solution.py:138
  9.2 103.2 %copy-start.3 = (s32[4]{0:T(128)S(1)}, s32[4]{0:T(128)}, u32[]{:S(2)}) copy-start(s32[4]{0:T(128)} %param.10) | copy-start | bytes 52
  9.2 105.7 %copy-start.2 = (s32[2,64]{1,0:T(2,128)S(1)}, s32[2,64]{1,0:T(2,128)}, u32[]{:S(2)}) copy-start(s32[2,64]{1,0:T(2,128)} %param.11) | copy-start | bytes 1540
  9.2 130.1 %all-gather.5.cloned.1.call-start = ((), (), s32[]{:S(2)}) async-start(), calls=%async_computation.1 | async-start | bytes 3932160 | tf_op jit(solution)/shard_map/all_gather | solution.py:138
  15.2 71.2 %collective-permute-start.2 = (bf16[3072,512]{1,0:T(8,128)(2,1)}, bf16[3072,512]{1,0:T(8,128)(2,1)S(1)}, u32[]{:S(2)}, u32[]{:S(2)}) collective-permute-start(bf16[3072,512]{1,0:T(8,128)(2,1)} %get-tuple-element.11.refs_0_), channel_id=1, source_target_pairs={{0,8},{4,12},{8,0},{12,4},{1,9},{5,13},{9,1},{13,5},{2,10},{6,14},... | collective-permute-start | bytes 9437192 | tf_op jit(solution)/shard_map/ppermute | solution.py:143
  18.2 97.3 %collective-permute-start.3 = (bf16[3072,512]{1,0:T(8,128)(2,1)}, bf16[3072,512]{1,0:T(8,128)(2,1)}, u32[]{:S(2)}, u32[]{:S(2)}) collective-permute-start(bf16[3072,512]{1,0:T(8,128)(2,1)} %get-tuple-element.11.refs_0_), channel_id=1, source_target_pairs={{0,4},{4,0},{8,12},{12,8},{1,5},{5,1},{9,13},{13,9},{2,6},{6,2},{1... | collective-permute-start | bytes 9437192 | tf_op jit(solution)/shard_map/ppermute | solution.py:146
  86.4 29.0 %copy-start = (bf16[3072,512]{1,0:T(8,128)(2,1)}, bf16[3072,512]{1,0:T(8,128)(2,1)S(1)}, u32[]{:S(2)}) copy-start(bf16[3072,512]{1,0:T(8,128)(2,1)S(1)} %collective-permute-done.2.refs_2_) | copy-start | bytes 9437188
  86.4 29.0 %collective-permute-start.5 = (bf16[3072,512]{1,0:T(8,128)(2,1)S(1)}, bf16[3072,512]{1,0:T(8,128)(2,1)}, u32[]{:S(2)}, u32[]{:S(2)}) collective-permute-start(bf16[3072,512]{1,0:T(8,128)(2,1)S(1)} %collective-permute-done.2.refs_2_), channel_id=1, source_target_pairs={{0,4},{4,0},{8,12},{12,8},{1,5},{5,1},{9,13},{13,9},{2,6},{6,2},{1... | collective-permute-start | bytes 9437192 | tf_op jit(solution)/shard_map/ppermute | solution.py:146
  86.4 25.9 %collective-permute-start = (bf16[1024,512]{1,0:T(8,128)(2,1)}, bf16[1024,512]{1,0:T(8,128)(2,1)}, u32[]{:S(2)}, u32[]{:S(2)}) collective-permute-start(bf16[1024,512]{1,0:T(8,128)(2,1)} %get-tuple-element.10.refs_1_), channel_id=1, source_target_pairs={{0,8},{4,12},{8,0},{12,4},{1,9},{5,13},{9,1},{13,5},{2,10},{6,14},... | collective-permute-start | bytes 3145736 | tf_op jit(solution)/shard_map/ppermute | solution.py:143
  88.2 27.3 %collective-permute-start.4 = (bf16[1024,512]{1,0:T(8,128)(2,1)}, bf16[1024,512]{1,0:T(8,128)(2,1)}, u32[]{:S(2)}, u32[]{:S(2)}) collective-permute-start(bf16[1024,512]{1,0:T(8,128)(2,1)} %get-tuple-element.10.refs_1_), channel_id=1, source_target_pairs={{0,4},{4,0},{8,12},{12,8},{1,5},{5,1},{9,13},{13,9},{2,6},{6,2},{1... | collective-permute-start | bytes 3145736 | tf_op jit(solution)/shard_map/ppermute | solution.py:146
  112.3 14.6 %collective-permute-start.1 = (bf16[1024,512]{1,0:T(8,128)(2,1)}, bf16[1024,512]{1,0:T(8,128)(2,1)}, u32[]{:S(2)}, u32[]{:S(2)}) collective-permute-start(bf16[1024,512]{1,0:T(8,128)(2,1)} %collective-permute-done.refs_0_), channel_id=1, source_target_pairs={{0,4},{4,0},{8,12},{12,8},{1,5},{5,1},{9,13},{13,9},{2,6},{6,2},{1... | collective-permute-start | bytes 3145736 | tf_op jit(solution)/shard_map/ppermute | solution.py:146
Sparse Core Ops, SparseCore 0:
  9.3 66.1 all-gather.2
  77.1 62.1 all-gather.4

commit v7 on v6

--- a/solution.py
+++ b/solution.py
@@ -10,7 +10,7 @@
 CHUNK_BLOCKS = 8
 
 
-CHAINS = 2
+CHAINS = 1
 VMEM_LIMIT = 56 * 1024 * 1024
 SMEM = pl.BlockSpec(memory_space=pltpu.SMEM)
 VMEM = pl.BlockSpec(memory_space=pltpu.VMEM)
@@ -88,38 +88,60 @@
             result(index).wait()
 
 
-def product_kernel(ranks, span, weight_ref, *refs):
-    gathered = refs[:CHAINS]
-    out_ref, token_buf, weight_buf, total, sems = refs[CHAINS:]
-    height, depth = gathered[0].shape
-    rows = height // ranks
+def product_kernel(dims, weight_ref, *refs):
+    ranks, span = dims
+    lanes = 2 * ranks - 1
+    token_refs = [refs[chain * lanes : (chain + 1) * lanes] for chain in range(CHAINS)]
+    out_ref, token_buf, weight_buf, total, sems = refs[-5:]
+    rows, depth = token_refs[0][0].shape
     chunks = depth // span
-
-    def copies(chunk):
+    rank = lax.axis_index("tp")
+
+    def weight_copy(chunk):
         at = pl.ds(pl.multiple_of(chunk * span, span), span)
-        yield pltpu.make_async_copy(weight_ref.at[at, :], weight_buf.at[at, :], sems.at[chunk, CHAINS])
-        for chain, source in enumerate(gathered):
-            target = token_buf.at[pl.ds(chain * height, height), at]
-            yield pltpu.make_async_copy(source.at[:, at], target, sems.at[chunk, chain])
+        return pltpu.make_async_copy(weight_ref.at[at, :], weight_buf.at[at, :], sems.at[chunk, CHAINS * ranks])
+
+    def token_copy(chunk, chain, hop, source):
+        at = pl.ds(pl.multiple_of(chunk * span, span), span)
+        origin = lax.rem(rank - hop + ranks, ranks)
+        row = pl.multiple_of((origin * CHAINS + chain) * rows, rows)
+        return pltpu.make_async_copy(
+            source.at[:, at], token_buf.at[pl.ds(row, rows), at], sems.at[chunk, chain * ranks + hop]
+        )
 
     @pl.loop(0, chunks)
     def _(chunk):
-        for copy in copies(chunk):
-            copy.start()
+        weight_copy(chunk).start()
+        for chain in range(CHAINS):
+            own, rights, lefts = (
+                token_refs[chain][0],
+                token_refs[chain][1:ranks],
+                token_refs[chain][ranks:],
+            )
+            token_copy(chunk, chain, 0, own).start()
+            for hop in range(1, ranks):
+                from_left = rank >= hop
+
+                @pl.when(from_left)
+                def _():
+                    token_copy(chunk, chain, hop, rights[hop - 1]).start()
+
+                @pl.when(jnp.logical_not(from_left))
+                def _():
+                    token_copy(chunk, chain, hop, lefts[ranks - hop - 1]).start()
 
     total[...] = jnp.zeros_like(total)
 
     @pl.loop(0, chunks)
     def _(chunk):
-        for copy in copies(chunk):
-            copy.wait()
+        weight_copy(chunk).wait()
+        for chain in range(CHAINS):
+            for hop in range(ranks):
+                token_copy(chunk, chain, hop, token_refs[chain][0]).wait()
         at = pl.ds(pl.multiple_of(chunk * span, span), span)
         total[...] += jnp.dot(token_buf[:, at], weight_buf[at, :], preferred_element_type=jnp.float32)
 
-    for chain in range(CHAINS):
-        for origin in range(ranks):
-            source = pl.ds(chain * height + origin * rows, rows)
-            out_ref[pl.ds((origin * CHAINS + chain) * rows, rows), :] = total[source, :].astype(out_ref.dtype)
+    out_ref[...] = total[...].astype(out_ref.dtype)
 
 
 def local(tokens, base_weight, delta_codes, delta_scales, replica_variant, block_home):
@@ -134,10 +156,26 @@
     ring = [(i, (i + CORES) % reps) for i in range(reps)]
     swap = [(i, i // CORES * CORES + (i + 1) % CORES) for i in range(reps)]
 
+    def tie(values):
+        return lax.optimization_barrier(values)
+
+    def right(value, hop):
+        return lax.ppermute(value, "tp", [(i, i + 1) for i in range(hop - 1, ranks - 1)])
+
+    def left(value, hop):
+        return lax.ppermute(value, "tp", [(i, i - 1) for i in range(1, ranks - hop + 1)])
+
+    def step(chain, hop):
+        return right(rights[chain][-1], hop), left(lefts[chain][-1], hop)
+
     halves = [tokens[chain * rows : (chain + 1) * rows] for chain in range(CHAINS)]
-    gathered = [lax.all_gather(half, "tp", axis=0, tiled=True) for half in halves]
-    cuts = [0, slots * 3 // 4, slots]
+    rights, lefts = [[half] for half in halves], [[half] for half in halves]
+    events = [(hop, chain) for hop in range(1, ranks) for chain in range(CHAINS)]
+    most = slots * 3 // 4
+    cuts = [0, most, slots]
     pieces = len(cuts) - 1
+    near_last = len(events) - 2
+    turns = [near_last * hop // (chips - 1) for hop in range(1, chips)]
 
     def across(store):
         return lax.ppermute(store, "rep", ring)
@@ -151,6 +189,7 @@
     turned = (rep % CORES + holder % CORES) % CORES
     row_of = (turned * chips + away) * slots + homes % slots
 
+    flight = [step(chain, 1) for chain in range(CHAINS)]
     deltas = pl.pallas_call(
         functools.partial(scale_kernel, block),
         out_shape=[
@@ -163,9 +202,23 @@
         cost_estimate=BRIEF,
     )(delta_scales.astype(jnp.float32), delta_codes)
     held, twins = [deltas], [[turn(delta) for delta in deltas]]
-    for _ in range(1, chips):
-        held.append([across(value) for value in held[-1]])
-        twins.append([turn(value) for value in held[-1]])
+    sent = [across(delta) for delta in deltas]
+    for index, (hop, chain) in enumerate(events[: near_last + 1]):
+        rights[chain].append(flight[0][0])
+        lefts[chain].append(flight[0][1])
+        flight = flight[1:]
+        if index in turns:
+            taken = pieces if len(held) < chips - 1 else 1
+            came, twins, rights, lefts = tie((sent[:taken], twins, rights, lefts))
+        else:
+            taken = 0
+            rights, lefts = tie((rights, lefts))
+        if hop + 1 < ranks:
+            flight.append(step(chain, hop + 1))
+        if taken:
+            held.append(came)
+            twins.append([turn(value) for value in came])
+            sent = [across(value) for value in came] if taken == pieces else sent[1:]
 
     def merge(weight, chosen):
         parts, stores = [], []
@@ -193,26 +246,36 @@
             cost_estimate=BRIEF,
         )(*inputs, *given)
 
-    last = [(chips - 1, piece) for piece in range(1, pieces)]
-    early = [(hop, piece) for hop in range(chips) for piece in range(pieces) if (hop, piece) not in last]
-    weight = merge(merge(None, early), last)
-    gathered, weight = lax.optimization_barrier((gathered, weight))
+    there = [(hop, piece) for hop, values in enumerate(held) for piece in range(len(values))]
+    weight = merge(None, there)
+    sent, weight = tie((sent, weight))
+    held[-1] = held[-1] + sent
+    twins[-1] = twins[-1] + [turn(value) for value in sent]
+    weight = merge(weight, [(chips - 1, piece) for piece in range(1, pieces)])
+    flight, weight = tie((flight, weight))
+    for (hop, chain), landing in zip(events[near_last + 1 :], flight):
+        rights[chain].append(landing[0])
+        lefts[chain].append(landing[1])
+
+    arrays = []
+    for chain in range(CHAINS):
+        arrays += rights[chain] + lefts[chain][1:]
     total_rows = ranks * CHAINS * rows
     chunks = blocks // CHUNK_BLOCKS
     return pl.pallas_call(
-        functools.partial(product_kernel, ranks, CHUNK_BLOCKS * block),
+        functools.partial(product_kernel, (ranks, CHUNK_BLOCKS * block)),
         out_shape=jax.ShapeDtypeStruct((total_rows, width), jnp.bfloat16),
-        in_specs=[HBM] * (1 + CHAINS),
+        in_specs=[HBM] * (1 + len(arrays)),
         out_specs=VMEM,
         scratch_shapes=[
             pltpu.VMEM((total_rows, depth), jnp.bfloat16),
             pltpu.VMEM((depth, width), jnp.bfloat16),
             pltpu.VMEM((total_rows, width), jnp.float32),
-            pltpu.SemaphoreType.DMA((chunks, CHAINS + 1)),
+            pltpu.SemaphoreType.DMA((chunks, CHAINS * ranks + 1)),
         ],
         compiler_params=pltpu.CompilerParams(vmem_limit_bytes=VMEM_LIMIT),
         cost_estimate=BRIEF,
-    )(weight, *gathered)
+    )(weight, *arrays)
 
 
 def solution(mesh):

time: 153 us -> 135 us (0.88)
  waiting for transfers between devices: 99.1 us -> 81.7 us
  between operations: 15.5 us -> 2.07 us
  starting transfers between devices: 5.03 us -> 16.9 us
    ppermute x2, waiting for transfers between devices: 92.1 us -> 40.6 us  [across(): return lax.ppermute(store, 'rep', ring)]
    ppermute x0 -> x6, waiting for transfers between devices: none -> 35.5 us  [the longest x3 23.5 us: right(): lax.ppermute(value, 'tp', [(i, i + 1) for i in range(hop - 1, ranks - 1)])]
    ppermute x0 -> x6, starting transfers between devices: none -> 13.8 us  [the longest x3 9.94 us: right(): lax.ppermute(value, 'tp', [(i, i + 1) for i in range(hop - 1, ranks - 1)])]
    all_gather x2 -> x0, waiting for transfers between devices: 6.96 us -> none  [local(): lax.all_gather(half, 'tp', axis=0, tiled=True)]
    ppermute x4, waiting for transfers between devices: 0.01 us -> 5.73 us  [turn(): return lax.ppermute(store, 'rep', swap)]
    slice x1 -> x0, local copies, waits for them, and re-layouts: 2.64 us -> none  [local(): tokens[chain * rows:(chain + 1) * rows]]
    unnamed x8 -> x12, local copies, waits for them, and re-layouts: 0.01 us -> 2.64 us
    ppermute x2, starting transfers between devices: 4.68 us -> 3.05 us  [across(): return lax.ppermute(store, 'rep', ring)]
  transfers between devices with their start and end apart: 8 -> 12, of which waited for: 3 -> 7; matrix products, arithmetic and copies ran while one was open for 1% -> 2% of each run, Pallas kernels for 14% -> 16%
where the time goes in v7:
time: 135 us
  waiting for transfers between devices  81.7 us (61%)
  Pallas kernels  28.8 us (21%)
  starting transfers between devices  16.9 us (13%)
  local copies, waits for them, and re-layouts  4.6 us (3%)
  between operations  2.07 us (2%)
    ppermute x2, waiting for transfers between devices, across(): return lax.ppermute(store, 'rep', ring)  40.6 us
    ppermute x3, waiting for transfers between devices, right(): lax.ppermute(value, 'tp', [(i, i + 1) for i in range(hop - 1, ranks - 1)])  23.5 us
    pallas_call x2, Pallas kernels, merge(): pl.pallas_call(functools.partial(merge_kernel, block, tuple(parts)), out_...  16.5 us
    ppermute x3, waiting for transfers between devices, left(): lax.ppermute(value, 'tp', [(i, i - 1) for i in range(1, ranks - hop + 1)])  12 us
    ppermute x3, starting transfers between devices, right(): lax.ppermute(value, 'tp', [(i, i + 1) for i in range(hop - 1, ranks - 1)])  9.94 us
    pallas_call x1, Pallas kernels, local(): pl.pallas_call(functools.partial(product_kernel, (ranks, CHUNK_BLOCKS * b...  7.18 us
    ppermute x4, waiting for transfers between devices, turn(): return lax.ppermute(store, 'rep', swap)  5.73 us
    pallas_call x1, Pallas kernels, local(): pl.pallas_call(functools.partial(scale_kernel, block), out_shape=[jax.Sha...  5.13 us
  transfers between devices with their start and end apart: 12, of which 7 were waited for; matrix products, arithmetic and copies ran while one was open for 2% of the time, Pallas kernels for 16%

profile of v7, /device:TPU:0, one launch (start us, length us, event | category | flops | bytes accessed | tf_op | source)
XLA Modules:
  0.0 134.7 jit_solution(13294587147319930316)
XLA Ops:
  0.0 6.3 %collective-permute-start.3 = (bf16[96,8192]{1,0:T(8,128)(2,1)}, bf16[96,8192]{1,0:T(8,128)(2,1)}, u32[]{:S(2)}, u32[]{:S(2)}) collective-permute-start(bf16[96,8192]{1,0:T(8,128)(2,1)} %refs_0_), channel_id=1, source_target_pairs={{0,1},{1,2},{2,3},{4,5},{5,6},{6,7},{8,9},{9,10},{10,11},{12,13},{... | collective-permute-start | bytes 4718600 | tf_op jit(solution)/shard_map/ppermute | solution.py:163
  6.3 1.3 collective-permute-start.4
  7.5 1.4 %copy.9.scale_ref = f32[32,4]{1,0:T(8,128)} copy(bf16[32,4]{0,1:T(4,128)(2,1)} %param.9) | data formatting | bytes 768 | tf_op jit(solution)/shard_map/convert_element_type | solution.py:203
  8.9 5.1 %shard_map.64 = (bf16[3072,512]{1,0:T(8,128)(2,1)}, bf16[1024,512]{1,0:T(8,128)(2,1)}) custom-call(f32[32,4]{1,0:T(8,128)} %copy.9.scale_ref, bf16[4096,512]{1,0:T(8,128)(2,1)} %codes_ref.1), custom_call_target="tpu_custom_call" | custom-call | flops 1 | bytes 1 | tf_op jit(solution)/shard_map/pallas_call | solution.py:193
  14.1 1.5 %collective-permute-start = (bf16[3072,512]{1,0:T(8,128)(2,1)}, bf16[3072,512]{1,0:T(8,128)(2,1)S(1)}, u32[]{:S(2)}, u32[]{:S(2)}) collective-permute-start(bf16[3072,512]{1,0:T(8,128)(2,1)} %get-tuple-element.23.refs_0_), channel_id=1, source_target_pairs={{0,8},{4,12},{8,0},{12,4},{1,9},{5,13},{9,1},{13,5},{2,10},{6,14},... | collective-permute-start | bytes 9437192 | tf_op jit(solution)/shard_map/ppermute | solution.py:181
  15.5 0.0 collective-permute-start.1
  15.5 23.5 %collective-permute-done.3.refs_1_ = bf16[96,8192]{1,0:T(8,128)(2,1)} collective-permute-done((bf16[96,8192]{1,0:T(8,128)(2,1)}, bf16[96,8192]{1,0:T(8,128)(2,1)}, u32[]{:S(2)}, u32[]{:S(2)}) %collective-permute-start.3) | collective-permute-done | bytes 1572896 | tf_op jit(solution)/shard_map/ppermute | solution.py:163
  39.0 5.3 %collective-permute-done.4.refs_4_ = bf16[96,8192]{1,0:T(8,128)(2,1)} collective-permute-done((bf16[96,8192]{1,0:T(8,128)(2,1)}, bf16[96,8192]{1,0:T(8,128)(2,1)}, u32[]{:S(2)}, u32[]{:S(2)}) %collective-permute-start.4) | collective-permute-done | bytes 1572896 | tf_op jit(solution)/shard_map/ppermute | solution.py:166
  44.3 1.9 %collective-permute-start.5 = (bf16[96,8192]{1,0:T(8,128)(2,1)}, bf16[96,8192]{1,0:T(8,128)(2,1)}, u32[]{:S(2)}, u32[]{:S(2)}) collective-permute-start(bf16[96,8192]{1,0:T(8,128)(2,1)} %collective-permute-done.3.refs_1_), channel_id=1, source_target_pairs={{1,2},{2,3},{5,6},{6,7},{9,10},{10,11},{13,14},{14,15},{17,18},{18... | collective-permute-start | bytes 4718600 | tf_op jit(solution)/shard_map/ppermute | solution.py:163
  46.2 1.3 collective-permute-start.6
  47.5 0.1 collective-permute-start.2
  47.6 2.9 %collective-permute-done.2.refs_4_ = bf16[1024,512]{1,0:T(8,128)(2,1)S(1)} collective-permute-done((bf16[1024,512]{1,0:T(8,128)(2,1)}, bf16[1024,512]{1,0:T(8,128)(2,1)S(1)}, u32[]{:S(2)}, u32[]{:S(2)}) %collective-permute-start.2) | collective-permute-done | bytes 1048608 | tf_op jit(solution)/shard_map/ppermute | solution.py:184
  50.4 33.4 %collective-permute-done.refs_2_ = bf16[3072,512]{1,0:T(8,128)(2,1)S(1)} collective-permute-done((bf16[3072,512]{1,0:T(8,128)(2,1)}, bf16[3072,512]{1,0:T(8,128)(2,1)S(1)}, u32[]{:S(2)}, u32[]{:S(2)}) %collective-permute-start) | collective-permute-done | bytes 3145760 | tf_op jit(solution)/shard_map/ppermute | solution.py:181
  83.8 0.0 collective-permute-done.1.refs_3_
  83.8 0.0 collective-permute-done.5.refs_2_
  83.8 1.7 %copy-done.1 = bf16[3072,512]{1,0:T(8,128)(2,1)} copy-done((bf16[3072,512]{1,0:T(8,128)(2,1)}, bf16[3072,512]{1,0:T(8,128)(2,1)S(1)}, u32[]{:S(2)}) %copy-start.1) | copy-done | bytes 3145752
  85.5 0.0 collective-permute-done.6.refs_5_
  85.5 0.0 collective-permute-start.10
  85.5 1.6 %collective-permute-start.9 = (bf16[1024,512]{1,0:T(8,128)(2,1)}, bf16[1024,512]{1,0:T(8,128)(2,1)}, u32[]{:S(2)}, u32[]{:S(2)}) collective-permute-start(bf16[1024,512]{1,0:T(8,128)(2,1)} %get-tuple-element.24.refs_1_), channel_id=1, source_target_pairs={{0,8},{4,12},{8,0},{12,4},{1,9},{5,13},{9,1},{13,5},{2,10},{6,14},... | collective-permute-start | bytes 3145736 | tf_op jit(solution)/shard_map/ppermute | solution.py:181
  87.1 1.8 %collective-permute-start.7 = (bf16[96,8192]{1,0:T(8,128)(2,1)}, bf16[96,8192]{1,0:T(8,128)(2,1)}, u32[]{:S(2)}, u32[]{:S(2)}) collective-permute-start(bf16[96,8192]{1,0:T(8,128)(2,1)} %collective-permute-done.5.refs_2_), channel_id=1, source_target_pairs={{2,3},{6,7},{10,11},{14,15},{18,19},{22,23},{26,27},{30,31}} | collective-permute-start | bytes 4718600 | tf_op jit(solution)/shard_map/ppermute | solution.py:163
  88.9 1.3 collective-permute-start.8
  90.2 0.6 dynamic_slice.6
  92.7 0.5 fusion.1.row_ref
  93.3 0.0 collective-permute-done.10.refs_5_
  93.3 10.9 %shard_map.65.refs_2_ = bf16[8192,512]{1,0:T(8,128)(2,1)} custom-call(s32[64]{0:T(128)} %fusion.1.row_ref, bf16[8192,512]{1,0:T(8,128)(2,1)} %base_ref.3, bf16[3072,512]{1,0:T(8,128)(2,1)} %get-tuple-element.23.refs_0_, bf16[1024,512]{1,0:T(8,128)(2,1)} %get-tuple-element.24.refs_1_, bf16[3072,512]{1,0:T(8,128)(2,1)} %copy-done, ...), custom_call_target="tpu_custom_call" | custom-call | flops 1 | bytes 1 | tf_op jit(solution)/shard_map/pallas_call | solution.py:232
  104.2 7.2 %collective-permute-done.9.refs_0_ = bf16[1024,512]{1,0:T(8,128)(2,1)} collective-permute-done((bf16[1024,512]{1,0:T(8,128)(2,1)}, bf16[1024,512]{1,0:T(8,128)(2,1)}, u32[]{:S(2)}, u32[]{:S(2)}) %collective-permute-start.9) | collective-permute-done | bytes 1048608 | tf_op jit(solution)/shard_map/ppermute | solution.py:181
  111.4 2.9 %collective-permute-done.11.refs_1_ = bf16[1024,512]{1,0:T(8,128)(2,1)S(1)} collective-permute-done((bf16[1024,512]{1,0:T(8,128)(2,1)}, bf16[1024,512]{1,0:T(8,128)(2,1)S(1)}, u32[]{:S(2)}, u32[]{:S(2)}) %collective-permute-start.11) | collective-permute-done | bytes 1048608 | tf_op jit(solution)/shard_map/ppermute | solution.py:184
  114.3 1.0 copy-done.3
  115.2 5.6 %shard_map.66.weight_ref = bf16[8192,512]{1,0:T(8,128)(2,1)} custom-call(s32[64]{0:T(128)} %fusion.1.row_ref, bf16[8192,512]{1,0:T(8,128)(2,1)} %base_ref.3, bf16[1024,512]{1,0:T(8,128)(2,1)} %collective-permute-done.9.refs_0_, bf16[1024,512]{1,0:T(8,128)(2,1)} %copy-done.3, bf16[8192,512]{1,0:T(8,128)(2,1)} %shard_map.65.refs_2_), custom_call_target="tpu_custom_call", output_to_operand_aliasing={{}: (4, {})} | custom-call | flops 1 | bytes 1 | tf_op jit(solution)/shard_map/pallas_call | solution.py:232
  120.8 0.0 collective-permute-done.7.refs_3_
  120.9 6.7 %collective-permute-done.8.refs_6_ = bf16[96,8192]{1,0:T(8,128)(2,1)} collective-permute-done((bf16[96,8192]{1,0:T(8,128)(2,1)}, bf16[96,8192]{1,0:T(8,128)(2,1)}, u32[]{:S(2)}, u32[]{:S(2)}) %collective-permute-start.8) | collective-permute-done | bytes 1572896 | tf_op jit(solution)/shard_map/ppermute | solution.py:166
  127.5 7.2 %shard_map.67 = bf16[384,512]{1,0:T(8,128)(2,1)} custom-call(bf16[8192,512]{1,0:T(8,128)(2,1)} %shard_map.66.weight_ref, bf16[96,8192]{1,0:T(8,128)(2,1)} %refs_0_, bf16[96,8192]{1,0:T(8,128)(2,1)} %collective-permute-done.3.refs_1_, bf16[96,8192]{1,0:T(8,128)(2,1)} %collective-permute-done.5.refs_2_, bf16[96,8192]{1,0:T(8,128)(2,1)} %collective-permute-done.7.refs_3_, ...), custom_call_target="tpu_custom_call" | custom-call | flops 1 | bytes 1 | tf_op jit(solution)/shard_map/pallas_call | solution.py:265
  (11 shorter events, 0.0 us)
Async XLA Ops:
  0.0 90.2 %copy-start.5 = (s32[4]{0:T(128)S(1)}, s32[4]{0:T(128)}, u32[]{:S(2)}) copy-start(s32[4]{0:T(128)} %param.10) | copy-start | bytes 52
  0.0 92.7 %copy-start.4 = (s32[2,64]{1,0:T(2,128)S(1)}, s32[2,64]{1,0:T(2,128)}, u32[]{:S(2)}) copy-start(s32[2,64]{1,0:T(2,128)} %param.11) | copy-start | bytes 1540
  0.0 39.0 %collective-permute-start.3 = (bf16[96,8192]{1,0:T(8,128)(2,1)}, bf16[96,8192]{1,0:T(8,128)(2,1)}, u32[]{:S(2)}, u32[]{:S(2)}) collective-permute-start(bf16[96,8192]{1,0:T(8,128)(2,1)} %refs_0_), channel_id=1, source_target_pairs={{0,1},{1,2},{2,3},{4,5},{5,6},{6,7},{8,9},{9,10},{10,11},{12,13},{... | collective-permute-start | bytes 4718600 | tf_op jit(solution)/shard_map/ppermute | solution.py:163
  6.3 38.1 %collective-permute-start.4 = (bf16[96,8192]{1,0:T(8,128)(2,1)}, bf16[96,8192]{1,0:T(8,128)(2,1)}, u32[]{:S(2)}, u32[]{:S(2)}) collective-permute-start(bf16[96,8192]{1,0:T(8,128)(2,1)} %refs_0_), channel_id=1, source_target_pairs={{1,0},{2,1},{3,2},{5,4},{6,5},{7,6},{9,8},{10,9},{11,10},{13,12},{... | collective-permute-start | bytes 4718600 | tf_op jit(solution)/shard_map/ppermute | solution.py:166
  14.1 69.8 %collective-permute-start = (bf16[3072,512]{1,0:T(8,128)(2,1)}, bf16[3072,512]{1,0:T(8,128)(2,1)S(1)}, u32[]{:S(2)}, u32[]{:S(2)}) collective-permute-start(bf16[3072,512]{1,0:T(8,128)(2,1)} %get-tuple-element.23.refs_0_), channel_id=1, source_target_pairs={{0,8},{4,12},{8,0},{12,4},{1,9},{5,13},{9,1},{13,5},{2,10},{6,14},... | collective-permute-start | bytes 9437192 | tf_op jit(solution)/shard_map/ppermute | solution.py:181
  15.5 68.3 %collective-permute-start.1 = (bf16[3072,512]{1,0:T(8,128)(2,1)}, bf16[3072,512]{1,0:T(8,128)(2,1)S(1)}, u32[]{:S(2)}, u32[]{:S(2)}) collective-permute-start(bf16[3072,512]{1,0:T(8,128)(2,1)} %get-tuple-element.23.refs_0_), channel_id=1, source_target_pairs={{0,4},{4,0},{8,12},{12,8},{1,5},{5,1},{9,13},{13,9},{2,6},{6,2},{1... | collective-permute-start | bytes 9437192 | tf_op jit(solution)/shard_map/ppermute | solution.py:184
  44.3 39.5 %collective-permute-start.5 = (bf16[96,8192]{1,0:T(8,128)(2,1)}, bf16[96,8192]{1,0:T(8,128)(2,1)}, u32[]{:S(2)}, u32[]{:S(2)}) collective-permute-start(bf16[96,8192]{1,0:T(8,128)(2,1)} %collective-permute-done.3.refs_1_), channel_id=1, source_target_pairs={{1,2},{2,3},{5,6},{6,7},{9,10},{10,11},{13,14},{14,15},{17,18},{18... | collective-permute-start | bytes 4718600 | tf_op jit(solution)/shard_map/ppermute | solution.py:163
  46.2 39.3 %collective-permute-start.6 = (bf16[96,8192]{1,0:T(8,128)(2,1)}, bf16[96,8192]{1,0:T(8,128)(2,1)}, u32[]{:S(2)}, u32[]{:S(2)}) collective-permute-start(bf16[96,8192]{1,0:T(8,128)(2,1)} %collective-permute-done.4.refs_4_), channel_id=1, source_target_pairs={{1,0},{2,1},{5,4},{6,5},{9,8},{10,9},{13,12},{14,13},{17,16},{18,1... | collective-permute-start | bytes 4718600 | tf_op jit(solution)/shard_map/ppermute | solution.py:166
  47.5 2.9 %collective-permute-start.2 = (bf16[1024,512]{1,0:T(8,128)(2,1)}, bf16[1024,512]{1,0:T(8,128)(2,1)S(1)}, u32[]{:S(2)}, u32[]{:S(2)}) collective-permute-start(bf16[1024,512]{1,0:T(8,128)(2,1)} %get-tuple-element.24.refs_1_), channel_id=1, source_target_pairs={{0,4},{4,0},{8,12},{12,8},{1,5},{5,1},{9,13},{13,9},{2,6},{6,2},{1... | collective-permute-start | bytes 3145736 | tf_op jit(solution)/shard_map/ppermute | solution.py:184
  50.4 35.1 %copy-start.2 = (bf16[1024,512]{1,0:T(8,128)(2,1)}, bf16[1024,512]{1,0:T(8,128)(2,1)S(1)}, u32[]{:S(2)}) copy-start(bf16[1024,512]{1,0:T(8,128)(2,1)S(1)} %collective-permute-done.2.refs_4_) | copy-start | bytes 3145732
  83.8 9.5 %copy-start = (bf16[3072,512]{1,0:T(8,128)(2,1)}, bf16[3072,512]{1,0:T(8,128)(2,1)S(1)}, u32[]{:S(2)}) copy-start(bf16[3072,512]{1,0:T(8,128)(2,1)S(1)} %collective-permute-done.refs_2_) | copy-start | bytes 9437188
  83.8 1.7 %copy-start.1 = (bf16[3072,512]{1,0:T(8,128)(2,1)}, bf16[3072,512]{1,0:T(8,128)(2,1)S(1)}, u32[]{:S(2)}) copy-start(bf16[3072,512]{1,0:T(8,128)(2,1)S(1)} %collective-permute-done.1.refs_3_) | copy-start | bytes 9437188
  85.5 7.8 %collective-permute-start.10 = (bf16[3072,512]{1,0:T(8,128)(2,1)S(1)}, bf16[3072,512]{1,0:T(8,128)(2,1)}, u32[]{:S(2)}, u32[]{:S(2)}) collective-permute-start(bf16[3072,512]{1,0:T(8,128)(2,1)S(1)} %collective-permute-done.refs_2_), channel_id=1, source_target_pairs={{0,4},{4,0},{8,12},{12,8},{1,5},{5,1},{9,13},{13,9},{2,6},{6,2},{1... | collective-permute-start | bytes 9437192 | tf_op jit(solution)/shard_map/ppermute | solution.py:184
  85.5 25.9 %collective-permute-start.9 = (bf16[1024,512]{1,0:T(8,128)(2,1)}, bf16[1024,512]{1,0:T(8,128)(2,1)}, u32[]{:S(2)}, u32[]{:S(2)}) collective-permute-start(bf16[1024,512]{1,0:T(8,128)(2,1)} %get-tuple-element.24.refs_1_), channel_id=1, source_target_pairs={{0,8},{4,12},{8,0},{12,4},{1,9},{5,13},{9,1},{13,5},{2,10},{6,14},... | collective-permute-start | bytes 3145736 | tf_op jit(solution)/shard_map/ppermute | solution.py:181
  87.1 33.8 %collective-permute-start.7 = (bf16[96,8192]{1,0:T(8,128)(2,1)}, bf16[96,8192]{1,0:T(8,128)(2,1)}, u32[]{:S(2)}, u32[]{:S(2)}) collective-permute-start(bf16[96,8192]{1,0:T(8,128)(2,1)} %collective-permute-done.5.refs_2_), channel_id=1, source_target_pairs={{2,3},{6,7},{10,11},{14,15},{18,19},{22,23},{26,27},{30,31}} | collective-permute-start | bytes 4718600 | tf_op jit(solution)/shard_map/ppermute | solution.py:163
  88.9 38.7 %collective-permute-start.8 = (bf16[96,8192]{1,0:T(8,128)(2,1)}, bf16[96,8192]{1,0:T(8,128)(2,1)}, u32[]{:S(2)}, u32[]{:S(2)}) collective-permute-start(bf16[96,8192]{1,0:T(8,128)(2,1)} %collective-permute-done.6.refs_5_), channel_id=1, source_target_pairs={{1,0},{5,4},{9,8},{13,12},{17,16},{21,20},{25,24},{29,28}} | collective-permute-start | bytes 4718600 | tf_op jit(solution)/shard_map/ppermute | solution.py:166
  111.4 2.9 %collective-permute-start.11 = (bf16[1024,512]{1,0:T(8,128)(2,1)}, bf16[1024,512]{1,0:T(8,128)(2,1)S(1)}, u32[]{:S(2)}, u32[]{:S(2)}) collective-permute-start(bf16[1024,512]{1,0:T(8,128)(2,1)} %collective-permute-done.9.refs_0_), channel_id=1, source_target_pairs={{0,4},{4,0},{8,12},{12,8},{1,5},{5,1},{9,13},{13,9},{2,6},{6,2},{1... | collective-permute-start | bytes 3145736 | tf_op jit(solution)/shard_map/ppermute | solution.py:184
  114.3 1.0 copy-start.3

commit v8 on v7

--- a/solution.py
+++ b/solution.py
@@ -10,31 +10,29 @@
 CHUNK_BLOCKS = 8
 
 
-CHAINS = 1
-VMEM_LIMIT = 56 * 1024 * 1024
+CHAINS = 2
+VMEM_LIMIT = 60 * 1024 * 1024
 SMEM = pl.BlockSpec(memory_space=pltpu.SMEM)
 VMEM = pl.BlockSpec(memory_space=pltpu.VMEM)
 HBM = pl.BlockSpec(memory_space=pl.ANY)
 BRIEF = pl.CostEstimate(flops=1, bytes_accessed=1, transcendentals=0)
 
 
-def scale_kernel(block, scale_ref, codes_ref, *out_refs):
+def scale_kernel(block, edges, scale_ref, codes_ref, *out_refs):
     col_blocks = scale_ref.shape[1]
     wide = codes_ref.shape[1] // col_blocks
-    first = 0
-    for out_ref in out_refs:
-        count = out_ref.shape[0] // block
-
-        @pl.loop(0, count)
-        def _(index):
-            source = pl.ds(pl.multiple_of((first + index) * block, block), block)
-            target = pl.ds(pl.multiple_of(index * block, block), block)
-            for col in range(col_blocks):
-                at = pl.ds(col * wide, wide)
-                delta = codes_ref[source, at].astype(jnp.float32) * scale_ref[first + index, col]
-                out_ref[target, at] = delta.astype(jnp.bfloat16)
-
-        first += count
+    count = codes_ref.shape[0] // block
+    grid_step = pl.program_id(0)
+    for out_ref, low, high in zip(out_refs, edges[:-1], edges[1:]):
+
+        @pl.when((grid_step >= low) & (grid_step < high))
+        def _():
+            for index in range(count):
+                rows = pl.ds(index * block, block)
+                for col in range(col_blocks):
+                    at = pl.ds(col * wide, wide)
+                    delta = codes_ref[rows, at].astype(jnp.float32) * scale_ref[grid_step * count + index, col]
+                    out_ref[rows, at] = delta.astype(jnp.bfloat16)
 
 
 def merge_kernel(block, parts, row_ref, base_ref, *refs):
@@ -89,46 +87,47 @@
 
 
 def product_kernel(dims, weight_ref, *refs):
-    ranks, span = dims
-    lanes = 2 * ranks - 1
-    token_refs = [refs[chain * lanes : (chain + 1) * lanes] for chain in range(CHAINS)]
+    ranks, joint, span = dims
     out_ref, token_buf, weight_buf, total, sems = refs[-5:]
-    rows, depth = token_refs[0][0].shape
+    lanes = 2 * joint - 1
+    half_refs = [refs[chain * lanes : (chain + 1) * lanes] for chain in range(CHAINS)]
+    joint_refs = refs[CHAINS * lanes : -5]
+    rows, depth = half_refs[0][0].shape
     chunks = depth // span
     rank = lax.axis_index("tp")
+
+    def source(chain, hop, left):
+        if hop >= joint:
+            return joint_refs[hop - joint].at[pl.ds(chain * rows, rows), :]
+        return half_refs[chain][hop + joint - 1 if left else hop]
 
     def weight_copy(chunk):
         at = pl.ds(pl.multiple_of(chunk * span, span), span)
         return pltpu.make_async_copy(weight_ref.at[at, :], weight_buf.at[at, :], sems.at[chunk, CHAINS * ranks])
 
-    def token_copy(chunk, chain, hop, source):
+    def token_copy(chunk, chain, hop, given):
         at = pl.ds(pl.multiple_of(chunk * span, span), span)
         origin = lax.rem(rank - hop + ranks, ranks)
         row = pl.multiple_of((origin * CHAINS + chain) * rows, rows)
         return pltpu.make_async_copy(
-            source.at[:, at], token_buf.at[pl.ds(row, rows), at], sems.at[chunk, chain * ranks + hop]
+            given.at[:, at], token_buf.at[pl.ds(row, rows), at], sems.at[chunk, chain * ranks + hop]
         )
 
     @pl.loop(0, chunks)
     def _(chunk):
         weight_copy(chunk).start()
         for chain in range(CHAINS):
-            own, rights, lefts = (
-                token_refs[chain][0],
-                token_refs[chain][1:ranks],
-                token_refs[chain][ranks:],
-            )
-            token_copy(chunk, chain, 0, own).start()
+            token_copy(chunk, chain, 0, half_refs[chain][0]).start()
             for hop in range(1, ranks):
                 from_left = rank >= hop
 
                 @pl.when(from_left)
                 def _():
-                    token_copy(chunk, chain, hop, rights[hop - 1]).start()
+                    token_copy(chunk, chain, hop, source(chain, hop, False)).start()
 
                 @pl.when(jnp.logical_not(from_left))
                 def _():
-                    token_copy(chunk, chain, hop, lefts[ranks - hop - 1]).start()
+                    token_copy(chunk, chain, hop, source(chain, ranks - hop, True)).start()
 
     total[...] = jnp.zeros_like(total)
 
@@ -137,7 +136,7 @@
         weight_copy(chunk).wait()
         for chain in range(CHAINS):
             for hop in range(ranks):
-                token_copy(chunk, chain, hop, token_refs[chain][0]).wait()
+                token_copy(chunk, chain, hop, half_refs[chain][0]).wait()
         at = pl.ds(pl.multiple_of(chunk * span, span), span)
         total[...] += jnp.dot(token_buf[:, at], weight_buf[at, :], preferred_element_type=jnp.float32)
 
@@ -170,11 +169,12 @@
 
     halves = [tokens[chain * rows : (chain + 1) * rows] for chain in range(CHAINS)]
     rights, lefts = [[half] for half in halves], [[half] for half in halves]
-    events = [(hop, chain) for hop in range(1, ranks) for chain in range(CHAINS)]
+    joint = ranks // 2 + 1
+    events = [(hop, chain) for hop in range(1, joint) for chain in range(CHAINS)]
     most = slots * 3 // 4
     cuts = [0, most, slots]
     pieces = len(cuts) - 1
-    near_last = len(events) - 2
+    near_last = len(events) - 1
     turns = [near_last * hop // (chips - 1) for hop in range(1, chips)]
 
     def across(store):
@@ -190,14 +190,21 @@
     row_of = (turned * chips + away) * slots + homes % slots
 
     flight = [step(chain, 1) for chain in range(CHAINS)]
+    count = slots // 8
+    edges = [cut // count for cut in cuts]
+
+    def piece_spec(low, high):
+        return pl.BlockSpec((count * block, width), lambda i: (jnp.clip(i, low, high - 1) - low, 0))
+
     deltas = pl.pallas_call(
-        functools.partial(scale_kernel, block),
+        functools.partial(scale_kernel, block, tuple(edges)),
+        grid=(slots // count,),
         out_shape=[
             jax.ShapeDtypeStruct(((high - low) * block, width), jnp.bfloat16)
             for low, high in zip(cuts[:-1], cuts[1:])
         ],
-        in_specs=[SMEM, VMEM],
-        out_specs=[VMEM] * pieces,
+        in_specs=[SMEM, pl.BlockSpec((count * block, width), lambda i: (i, 0))],
+        out_specs=[piece_spec(low, high) for low, high in zip(edges[:-1], edges[1:])],
         compiler_params=pltpu.CompilerParams(vmem_limit_bytes=VMEM_LIMIT),
         cost_estimate=BRIEF,
     )(delta_scales.astype(jnp.float32), delta_codes)
@@ -213,12 +220,27 @@
         else:
             taken = 0
             rights, lefts = tie((rights, lefts))
-        if hop + 1 < ranks:
+        if hop + 1 < joint:
             flight.append(step(chain, hop + 1))
         if taken:
             held.append(came)
             twins.append([turn(value) for value in came])
             sent = [across(value) for value in came] if taken == pieces else sent[1:]
+
+    pairs = [
+        [(i, i + 1) for i in range(hop - 1, ranks - 1)] + [(i, i - 1) for i in range(1, ranks - hop + 1)]
+        for hop in range(joint, ranks)
+    ]
+    from_left = lax.axis_index("tp") >= joint - 1
+    whole = jnp.where(
+        from_left,
+        jnp.concatenate([values[-1] for values in rights], axis=0),
+        jnp.concatenate([values[-1] for values in lefts], axis=0),
+    )
+    whole_steps = []
+    for pair in pairs:
+        whole = lax.ppermute(whole, "tp", pair)
+        whole_steps.append(whole)
 
     def merge(weight, chosen):
         parts, stores = [], []
@@ -252,18 +274,15 @@
     held[-1] = held[-1] + sent
     twins[-1] = twins[-1] + [turn(value) for value in sent]
     weight = merge(weight, [(chips - 1, piece) for piece in range(1, pieces)])
-    flight, weight = tie((flight, weight))
-    for (hop, chain), landing in zip(events[near_last + 1 :], flight):
-        rights[chain].append(landing[0])
-        lefts[chain].append(landing[1])
-
+    whole_steps, weight = tie((whole_steps, weight))
     arrays = []
     for chain in range(CHAINS):
         arrays += rights[chain] + lefts[chain][1:]
+    arrays += whole_steps
     total_rows = ranks * CHAINS * rows
     chunks = blocks // CHUNK_BLOCKS
     return pl.pallas_call(
-        functools.partial(product_kernel, (ranks, CHUNK_BLOCKS * block)),
+        functools.partial(product_kernel, (ranks, joint, CHUNK_BLOCKS * block)),
         out_shape=jax.ShapeDtypeStruct((total_rows, width), jnp.bfloat16),
         in_specs=[HBM] * (1 + len(arrays)),
         out_specs=VMEM,

time: 135 us -> 139 us (1.030)
  waiting for transfers between devices: 81.7 us -> 78.3 us
  starting transfers between devices: 16.9 us -> 19.6 us
  Pallas kernels: 28.8 us -> 31.4 us
  other arithmetic: 0.55 us -> 2.05 us
    ppermute x2, waiting for transfers between devices: 40.6 us -> 8.14 us  [across(): return lax.ppermute(store, 'rep', ring)]
    ppermute x3 -> x4, waiting for transfers between devices: 12 us -> 37.9 us  [left(): lax.ppermute(value, 'tp', [(i, i - 1) for i in range(1, ranks - hop + 1)])]
    ppermute x0 -> x1, waiting for transfers between devices: none -> 5.52 us  [local(): whole = lax.ppermute(whole, 'tp', pair)]
    ppermute x4, waiting for transfers between devices: 5.73 us -> 2.88 us  [turn(): return lax.ppermute(store, 'rep', swap)]
    pallas_call x2, Pallas kernels: 12.3 us -> 14.7 us  [the longest x1 7.51 us: local(): pl.pallas_call(functools.partial(product_kernel, (ranks, joint, CHUNK_BLO...]
    select_n x0 -> x1, other arithmetic: none -> 1.5 us  [local(): jnp.where(from_left, jnp.concatenate([values[-1] for values in rights], a...]
    ppermute x3 -> x4, starting transfers between devices: 3.84 us -> 5.14 us  [left(): lax.ppermute(value, 'tp', [(i, i - 1) for i in range(1, ranks - hop + 1)])]
    ppermute x3 -> x4, waiting for transfers between devices: 23.5 us -> 23.9 us  [right(): lax.ppermute(value, 'tp', [(i, i + 1) for i in range(hop - 1, ranks - 1)])]
  transfers between devices with their start and end apart: 12 -> 15, of which waited for: 7 -> 9; matrix products, arithmetic and copies ran while one was open for 2% -> 2% of each run, Pallas kernels for 16% -> 12%
where the time goes in v8:
time: 139 us
  waiting for transfers between devices  78.3 us (56%)
  Pallas kernels  31.4 us (23%)
  starting transfers between devices  19.6 us (14%)
  local copies, waits for them, and re-layouts  4.99 us (4%)
  between operations  2.25 us (2%)
  other arithmetic  2.05 us (1%)
    ppermute x4, waiting for transfers between devices, left(): lax.ppermute(value, 'tp', [(i, i - 1) for i in range(1, ranks - hop + 1)])  37.9 us
    ppermute x4, waiting for transfers between devices, right(): lax.ppermute(value, 'tp', [(i, i + 1) for i in range(hop - 1, ranks - 1)])  23.9 us
    pallas_call x2, Pallas kernels, merge(): pl.pallas_call(functools.partial(merge_kernel, block, tuple(parts)), out_...  16.7 us
    ppermute x4, starting transfers between devices, right(): lax.ppermute(value, 'tp', [(i, i + 1) for i in range(hop - 1, ranks - 1)])  9.66 us
    ppermute x2, waiting for transfers between devices, across(): return lax.ppermute(store, 'rep', ring)  8.14 us
    pallas_call x1, Pallas kernels, local(): pl.pallas_call(functools.partial(product_kernel, (ranks, joint, CHUNK_BLO...  7.51 us
    pallas_call x1, Pallas kernels, local(): pl.pallas_call(functools.partial(scale_kernel, block, tuple(edges)), grid...  7.16 us
    ppermute x1, waiting for transfers between devices, local(): whole = lax.ppermute(whole, 'tp', pair)  5.52 us
  transfers between devices with their start and end apart: 15, of which 9 were waited for; matrix products, arithmetic and copies ran while one was open for 2% of the time, Pallas kernels for 12%

profile of v8, /device:TPU:0, one launch (start us, length us, event | category | flops | bytes accessed | tf_op | source)
XLA Modules:
  0.0 138.5 jit_solution(6732778245677068795)
XLA Ops:
  0.0 1.5 %copy.9.scale_ref = f32[32,4]{1,0:T(8,128)} copy(bf16[32,4]{0,1:T(4,128)(2,1)} %param.9) | data formatting | bytes 768 | tf_op jit(solution)/shard_map/convert_element_type | solution.py:210
  1.5 7.2 %shard_map.64 = (bf16[3072,512]{1,0:T(8,128)(2,1)}, bf16[1024,512]{1,0:T(8,128)(2,1)}) custom-call(f32[32,4]{1,0:T(8,128)} %copy.9.scale_ref, bf16[4096,512]{1,0:T(8,128)(2,1)} %codes_ref.1), custom_call_target="tpu_custom_call" | custom-call | flops 1 | bytes 1 | tf_op jit(solution)/shard_map/pallas_call | solution.py:199
  8.7 2.9 %collective-permute-start = (bf16[3072,512]{1,0:T(8,128)(2,1)}, bf16[3072,512]{1,0:T(8,128)(2,1)}, u32[]{:S(2)}, u32[]{:S(2)}) collective-permute-start(bf16[3072,512]{1,0:T(8,128)(2,1)} %get-tuple-element.42.refs_0_), channel_id=1, source_target_pairs={{0,8},{4,12},{8,0},{12,4},{1,9},{5,13},{9,1},{13,5},{2,10},{6,14},... | collective-permute-start | bytes 9437192 | tf_op jit(solution)/shard_map/ppermute | solution.py:181
  11.6 0.1 fusion.6
  11.7 0.0 copy-start.14
  11.8 3.7 %collective-permute-start.3 = (bf16[48,8192]{1,0:T(8,128)(2,1)S(1)}, bf16[48,8192]{1,0:T(8,128)(2,1)S(1)}, u32[]{:S(2)}, u32[]{:S(2)}) collective-permute-start(bf16[48,8192]{1,0:T(8,128)(2,1)S(1)} %get-tuple-element.72.refs_0_), channel_id=1, source_target_pairs={{0,1},{1,2},{2,3},{4,5},{5,6},{6,7},{8,9},{9,10},{10,11},{12,13},{... | collective-permute-start | bytes 2359304 | tf_op jit(solution)/shard_map/ppermute | solution.py:162
  15.4 1.3 collective-permute-start.4
  16.7 4.6 %collective-permute-start.5 = (bf16[48,8192]{1,0:T(8,128)(2,1)S(1)}, bf16[48,8192]{1,0:T(8,128)(2,1)S(1)}, u32[]{:S(2)}, u32[]{:S(2)}) collective-permute-start(bf16[48,8192]{1,0:T(8,128)(2,1)S(1)} %get-tuple-element.75.refs_5_), channel_id=1, source_target_pairs={{0,1},{1,2},{2,3},{4,5},{5,6},{6,7},{8,9},{9,10},{10,11},{12,13},{... | collective-permute-start | bytes 2359304 | tf_op jit(solution)/shard_map/ppermute | solution.py:162
  21.3 11.9 %collective-permute-done.3.refs_1_ = bf16[48,8192]{1,0:T(8,128)(2,1)S(1)} collective-permute-done((bf16[48,8192]{1,0:T(8,128)(2,1)S(1)}, bf16[48,8192]{1,0:T(8,128)(2,1)S(1)}, u32[]{:S(2)}, u32[]{:S(2)}) %collective-permute-start.3) | collective-permute-done | bytes 786464 | tf_op jit(solution)/shard_map/ppermute | solution.py:162
  33.2 1.3 collective-permute-start.6
  34.5 2.5 %collective-permute-done.4.refs_3_ = bf16[48,8192]{1,0:T(8,128)(2,1)S(1)} collective-permute-done((bf16[48,8192]{1,0:T(8,128)(2,1)S(1)}, bf16[48,8192]{1,0:T(8,128)(2,1)S(1)}, u32[]{:S(2)}, u32[]{:S(2)}) %collective-permute-start.4) | collective-permute-done | bytes 786464 | tf_op jit(solution)/shard_map/ppermute | solution.py:165
  37.0 0.7 collective-permute-start.7
  37.7 12.0 %collective-permute-done.5.refs_6_ = bf16[48,8192]{1,0:T(8,128)(2,1)S(1)} collective-permute-done((bf16[48,8192]{1,0:T(8,128)(2,1)S(1)}, bf16[48,8192]{1,0:T(8,128)(2,1)S(1)}, u32[]{:S(2)}, u32[]{:S(2)}) %collective-permute-start.5) | collective-permute-done | bytes 786464 | tf_op jit(solution)/shard_map/ppermute | solution.py:162
  49.7 1.3 collective-permute-start.8
  51.0 3.8 %collective-permute-done.6.refs_8_ = bf16[48,8192]{1,0:T(8,128)(2,1)S(1)} collective-permute-done((bf16[48,8192]{1,0:T(8,128)(2,1)S(1)}, bf16[48,8192]{1,0:T(8,128)(2,1)S(1)}, u32[]{:S(2)}, u32[]{:S(2)}) %collective-permute-start.6) | collective-permute-done | bytes 786464 | tf_op jit(solution)/shard_map/ppermute | solution.py:165
  54.8 1.3 collective-permute-start.10
  56.1 16.4 %collective-permute-done.8.refs_4_ = bf16[48,8192]{1,0:T(8,128)(2,1)S(1)} collective-permute-done((bf16[48,8192]{1,0:T(8,128)(2,1)S(1)}, bf16[48,8192]{1,0:T(8,128)(2,1)S(1)}, u32[]{:S(2)}, u32[]{:S(2)}) %collective-permute-start.8) | collective-permute-done | bytes 786464 | tf_op jit(solution)/shard_map/ppermute | solution.py:165
  72.4 0.7 collective-permute-start.9
  73.2 15.3 %collective-permute-done.10.refs_9_ = bf16[48,8192]{1,0:T(8,128)(2,1)S(1)} collective-permute-done((bf16[48,8192]{1,0:T(8,128)(2,1)S(1)}, bf16[48,8192]{1,0:T(8,128)(2,1)S(1)}, u32[]{:S(2)}, u32[]{:S(2)}) %collective-permute-start.10) | collective-permute-done | bytes 786464 | tf_op jit(solution)/shard_map/ppermute | solution.py:165
  88.5 1.7 %copy-done.6 = bf16[3072,512]{1,0:T(8,128)(2,1)} copy-done((bf16[3072,512]{1,0:T(8,128)(2,1)}, bf16[3072,512]{1,0:T(8,128)(2,1)S(1)}, u32[]{:S(2)}) %copy-start.6) | copy-done | bytes 3145752
  90.2 0.5 collective-permute-start.12
  90.7 1.5 %maximum_select_fusion = bf16[96,8192]{1,0:T(8,128)(2,1)} fusion(bf16[48,8192]{1,0:T(8,128)(2,1)S(1)} %collective-permute-done.9.refs_7_, bf16[48,8192]{1,0:T(8,128)(2,1)S(1)} %collective-permute-done.7.refs_2_, bf16[48,8192]{1,0:T(8,128)(2,1)S(1)} %collective-permute-done.10.refs_9_, bf16[48,8192]{1,0:T(8,128)(2,1)S(1)} %collective-permute-done.8.refs_4_, ...), kind=kLoop, calls=%fused_computation | loop fusion | flops 7077888 | bytes 4718593 | tf_op jit(solution)/shard_map/jit(_where)/select_n | solution.py:235
  92.2 1.3 collective-permute-start.11
  93.6 0.6 dynamic_slice.6
  96.1 0.5 fusion.1.row_ref
  96.7 11.2 %shard_map.65.refs_2_ = bf16[8192,512]{1,0:T(8,128)(2,1)} custom-call(s32[64]{0:T(128)} %fusion.1.row_ref, bf16[8192,512]{1,0:T(8,128)(2,1)} %base_ref.3, bf16[3072,512]{1,0:T(8,128)(2,1)} %get-tuple-element.42.refs_0_, bf16[1024,512]{1,0:T(8,128)(2,1)} %get-tuple-element.43.refs_1_, bf16[3072,512]{1,0:T(8,128)(2,1)} %collective-permute-done.refs_2_, ...), custom_call_target="tpu_custom_call" | custom-call | flops 1 | bytes 1 | tf_op jit(solution)/shard_map/pallas_call | solution.py:254
  107.9 8.1 %collective-permute-done.12.refs_0_ = bf16[1024,512]{1,0:T(8,128)(2,1)} collective-permute-done((bf16[1024,512]{1,0:T(8,128)(2,1)}, bf16[1024,512]{1,0:T(8,128)(2,1)}, u32[]{:S(2)}, u32[]{:S(2)}) %collective-permute-start.12) | collective-permute-done | bytes 1048608 | tf_op jit(solution)/shard_map/ppermute | solution.py:181
  116.1 2.9 %collective-permute-done.14.refs_1_ = bf16[1024,512]{1,0:T(8,128)(2,1)S(1)} collective-permute-done((bf16[1024,512]{1,0:T(8,128)(2,1)}, bf16[1024,512]{1,0:T(8,128)(2,1)S(1)}, u32[]{:S(2)}, u32[]{:S(2)}) %collective-permute-start.14) | collective-permute-done | bytes 1048608 | tf_op jit(solution)/shard_map/ppermute | solution.py:184
  119.0 1.1 copy-done.9
  120.0 5.5 %shard_map.66.weight_ref = bf16[8192,512]{1,0:T(8,128)(2,1)} custom-call(s32[64]{0:T(128)} %fusion.1.row_ref, bf16[8192,512]{1,0:T(8,128)(2,1)} %base_ref.3, bf16[1024,512]{1,0:T(8,128)(2,1)} %collective-permute-done.12.refs_0_, bf16[1024,512]{1,0:T(8,128)(2,1)} %copy-done.9, bf16[8192,512]{1,0:T(8,128)(2,1)} %shard_map.65.refs_2_), custom_call_target="tpu_custom_call", output_to_operand_aliasing={{}: (4, {})} | custom-call | flops 1 | bytes 1 | tf_op jit(solution)/shard_map/pallas_call | solution.py:254
  125.5 5.5 %collective-permute-done.11.refs_10_ = bf16[96,8192]{1,0:T(8,128)(2,1)} collective-permute-done((bf16[96,8192]{1,0:T(8,128)(2,1)}, bf16[96,8192]{1,0:T(8,128)(2,1)}, u32[]{:S(2)}, u32[]{:S(2)}) %collective-permute-start.11) | collective-permute-done | bytes 1572896 | tf_op jit(solution)/shard_map/ppermute | solution.py:242
  131.0 7.5 %shard_map.67 = bf16[384,512]{1,0:T(8,128)(2,1)} custom-call(bf16[8192,512]{1,0:T(8,128)(2,1)} %shard_map.66.weight_ref, bf16[48,8192]{1,0:T(8,128)(2,1)} %copy-done.5, bf16[48,8192]{1,0:T(8,128)(2,1)} %copy-done.10, bf16[48,8192]{1,0:T(8,128)(2,1)} %copy-done, bf16[48,8192]{1,0:T(8,128)(2,1)} %copy-done.11, bf16[48,8192]{1,0:T(8,128)(2,1)} %copy-done.1, ...), custom_call_target="tpu_custom_call" | custom-call | flops 1 | bytes 1 | tf_op jit(solution)/shard_map/pallas_call | solution.py:284
  (39 shorter events, 0.1 us)
Async XLA Ops:
  0.0 11.6 %copy-start.7 = (bf16[96,8192]{1,0:T(8,128)(2,1)S(1)}, bf16[96,8192]{1,0:T(8,128)(2,1)}, u32[]{:S(2)}) copy-start(bf16[96,8192]{1,0:T(8,128)(2,1)} %param.6) | copy-start | bytes 4718596
  8.7 79.8 %collective-permute-start = (bf16[3072,512]{1,0:T(8,128)(2,1)}, bf16[3072,512]{1,0:T(8,128)(2,1)}, u32[]{:S(2)}, u32[]{:S(2)}) collective-permute-start(bf16[3072,512]{1,0:T(8,128)(2,1)} %get-tuple-element.42.refs_0_), channel_id=1, source_target_pairs={{0,8},{4,12},{8,0},{12,4},{1,9},{5,13},{9,1},{13,5},{2,10},{6,14},... | collective-permute-start | bytes 9437192 | tf_op jit(solution)/shard_map/ppermute | solution.py:181
  11.6 76.9 %collective-permute-start.1 = (bf16[3072,512]{1,0:T(8,128)(2,1)}, bf16[3072,512]{1,0:T(8,128)(2,1)S(1)}, u32[]{:S(2)}, u32[]{:S(2)}) collective-permute-start(bf16[3072,512]{1,0:T(8,128)(2,1)} %get-tuple-element.42.refs_0_), channel_id=1, source_target_pairs={{0,4},{4,0},{8,12},{12,8},{1,5},{5,1},{9,13},{13,9},{2,6},{6,2},{1... | collective-permute-start | bytes 9437192 | tf_op jit(solution)/shard_map/ppermute | solution.py:184
  11.7 76.7 %copy-start.4 = (bf16[48,8192]{1,0:T(8,128)(2,1)}, bf16[48,8192]{1,0:T(8,128)(2,1)S(1)}, u32[]{:S(2)}) copy-start(bf16[48,8192]{1,0:T(8,128)(2,1)S(1)} %get-tuple-element.75.refs_5_) | copy-start | bytes 2359300
  11.7 76.8 %copy-start.5 = (bf16[48,8192]{1,0:T(8,128)(2,1)}, bf16[48,8192]{1,0:T(8,128)(2,1)S(1)}, u32[]{:S(2)}) copy-start(bf16[48,8192]{1,0:T(8,128)(2,1)S(1)} %get-tuple-element.72.refs_0_) | copy-start | bytes 2359300
  11.7 81.8 %copy-start.15 = (s32[4]{0:T(128)S(1)}, s32[4]{0:T(128)}, u32[]{:S(2)}) copy-start(s32[4]{0:T(128)} %param.10) | copy-start | bytes 52
  11.7 84.4 %copy-start.14 = (s32[2,64]{1,0:T(2,128)S(1)}, s32[2,64]{1,0:T(2,128)}, u32[]{:S(2)}) copy-start(s32[2,64]{1,0:T(2,128)} %param.11) | copy-start | bytes 1540
  11.8 21.5 %collective-permute-start.3 = (bf16[48,8192]{1,0:T(8,128)(2,1)S(1)}, bf16[48,8192]{1,0:T(8,128)(2,1)S(1)}, u32[]{:S(2)}, u32[]{:S(2)}) collective-permute-start(bf16[48,8192]{1,0:T(8,128)(2,1)S(1)} %get-tuple-element.72.refs_0_), channel_id=1, source_target_pairs={{0,1},{1,2},{2,3},{4,5},{5,6},{6,7},{8,9},{9,10},{10,11},{12,13},{... | collective-permute-start | bytes 2359304 | tf_op jit(solution)/shard_map/ppermute | solution.py:162
  15.4 21.6 %collective-permute-start.4 = (bf16[48,8192]{1,0:T(8,128)(2,1)S(1)}, bf16[48,8192]{1,0:T(8,128)(2,1)S(1)}, u32[]{:S(2)}, u32[]{:S(2)}) collective-permute-start(bf16[48,8192]{1,0:T(8,128)(2,1)S(1)} %get-tuple-element.72.refs_0_), channel_id=1, source_target_pairs={{1,0},{2,1},{3,2},{5,4},{6,5},{7,6},{9,8},{10,9},{11,10},{13,12},{... | collective-permute-start | bytes 2359304 | tf_op jit(solution)/shard_map/ppermute | solution.py:165
  16.7 33.0 %collective-permute-start.5 = (bf16[48,8192]{1,0:T(8,128)(2,1)S(1)}, bf16[48,8192]{1,0:T(8,128)(2,1)S(1)}, u32[]{:S(2)}, u32[]{:S(2)}) collective-permute-start(bf16[48,8192]{1,0:T(8,128)(2,1)S(1)} %get-tuple-element.75.refs_5_), channel_id=1, source_target_pairs={{0,1},{1,2},{2,3},{4,5},{5,6},{6,7},{8,9},{9,10},{10,11},{12,13},{... | collective-permute-start | bytes 2359304 | tf_op jit(solution)/shard_map/ppermute | solution.py:162
  33.2 57.5 %copy-start.10 = (bf16[48,8192]{1,0:T(8,128)(2,1)}, bf16[48,8192]{1,0:T(8,128)(2,1)S(1)}, u32[]{:S(2)}) copy-start(bf16[48,8192]{1,0:T(8,128)(2,1)S(1)} %collective-permute-done.3.refs_1_) | copy-start | bytes 2359300
  33.2 21.5 %collective-permute-start.6 = (bf16[48,8192]{1,0:T(8,128)(2,1)S(1)}, bf16[48,8192]{1,0:T(8,128)(2,1)S(1)}, u32[]{:S(2)}, u32[]{:S(2)}) collective-permute-start(bf16[48,8192]{1,0:T(8,128)(2,1)S(1)} %get-tuple-element.75.refs_5_), channel_id=1, source_target_pairs={{1,0},{2,1},{3,2},{5,4},{6,5},{7,6},{9,8},{10,9},{11,10},{13,12},{... | collective-permute-start | bytes 2359304 | tf_op jit(solution)/shard_map/ppermute | solution.py:165
  37.0 53.7 %copy-start.11 = (bf16[48,8192]{1,0:T(8,128)(2,1)}, bf16[48,8192]{1,0:T(8,128)(2,1)S(1)}, u32[]{:S(2)}) copy-start(bf16[48,8192]{1,0:T(8,128)(2,1)S(1)} %collective-permute-done.4.refs_3_) | copy-start | bytes 2359300
  37.0 17.8 %collective-permute-start.7 = (bf16[48,8192]{1,0:T(8,128)(2,1)S(1)}, bf16[48,8192]{1,0:T(8,128)(2,1)S(1)}, u32[]{:S(2)}, u32[]{:S(2)}) collective-permute-start(bf16[48,8192]{1,0:T(8,128)(2,1)S(1)} %collective-permute-done.3.refs_1_), channel_id=1, source_target_pairs={{1,2},{2,3},{5,6},{6,7},{9,10},{10,11},{13,14},{14,15},{17,18},{18... | collective-permute-start | bytes 2359304 | tf_op jit(solution)/shard_map/ppermute | solution.py:162
  49.7 41.0 %copy-start.12 = (bf16[48,8192]{1,0:T(8,128)(2,1)}, bf16[48,8192]{1,0:T(8,128)(2,1)S(1)}, u32[]{:S(2)}) copy-start(bf16[48,8192]{1,0:T(8,128)(2,1)S(1)} %collective-permute-done.5.refs_6_) | copy-start | bytes 2359300
  49.7 22.7 %collective-permute-start.8 = (bf16[48,8192]{1,0:T(8,128)(2,1)S(1)}, bf16[48,8192]{1,0:T(8,128)(2,1)S(1)}, u32[]{:S(2)}, u32[]{:S(2)}) collective-permute-start(bf16[48,8192]{1,0:T(8,128)(2,1)S(1)} %collective-permute-done.4.refs_3_), channel_id=1, source_target_pairs={{1,0},{2,1},{5,4},{6,5},{9,8},{10,9},{13,12},{14,13},{17,16},{18,1... | collective-permute-start | bytes 2359304 | tf_op jit(solution)/shard_map/ppermute | solution.py:165
  54.7 36.0 %copy-start.13 = (bf16[48,8192]{1,0:T(8,128)(2,1)}, bf16[48,8192]{1,0:T(8,128)(2,1)S(1)}, u32[]{:S(2)}) copy-start(bf16[48,8192]{1,0:T(8,128)(2,1)S(1)} %collective-permute-done.6.refs_8_) | copy-start | bytes 2359300
  54.7 18.4 %collective-permute-start.2 = (bf16[1024,512]{1,0:T(8,128)(2,1)}, bf16[1024,512]{1,0:T(8,128)(2,1)S(1)}, u32[]{:S(2)}, u32[]{:S(2)}) collective-permute-start(bf16[1024,512]{1,0:T(8,128)(2,1)} %get-tuple-element.43.refs_1_), channel_id=1, source_target_pairs={{0,4},{4,0},{8,12},{12,8},{1,5},{5,1},{9,13},{13,9},{2,6},{6,2},{1... | collective-permute-start | bytes 3145736 | tf_op jit(solution)/shard_map/ppermute | solution.py:184
  54.8 53.2 %copy-start = (bf16[48,8192]{1,0:T(8,128)(2,1)}, bf16[48,8192]{1,0:T(8,128)(2,1)S(1)}, u32[]{:S(2)}) copy-start(bf16[48,8192]{1,0:T(8,128)(2,1)S(1)} %collective-permute-done.7.refs_2_) | copy-start | bytes 2359300
  54.8 33.7 %collective-permute-start.10 = (bf16[48,8192]{1,0:T(8,128)(2,1)S(1)}, bf16[48,8192]{1,0:T(8,128)(2,1)S(1)}, u32[]{:S(2)}, u32[]{:S(2)}) collective-permute-start(bf16[48,8192]{1,0:T(8,128)(2,1)S(1)} %collective-permute-done.6.refs_8_), channel_id=1, source_target_pairs={{1,0},{2,1},{5,4},{6,5},{9,8},{10,9},{13,12},{14,13},{17,16},{18,1... | collective-permute-start | bytes 2359304 | tf_op jit(solution)/shard_map/ppermute | solution.py:165
  72.4 35.5 %copy-start.1 = (bf16[48,8192]{1,0:T(8,128)(2,1)}, bf16[48,8192]{1,0:T(8,128)(2,1)S(1)}, u32[]{:S(2)}) copy-start(bf16[48,8192]{1,0:T(8,128)(2,1)S(1)} %collective-permute-done.8.refs_4_) | copy-start | bytes 2359300
  72.4 16.0 %collective-permute-start.9 = (bf16[48,8192]{1,0:T(8,128)(2,1)S(1)}, bf16[48,8192]{1,0:T(8,128)(2,1)S(1)}, u32[]{:S(2)}, u32[]{:S(2)}) collective-permute-start(bf16[48,8192]{1,0:T(8,128)(2,1)S(1)} %collective-permute-done.5.refs_6_), channel_id=1, source_target_pairs={{1,2},{2,3},{5,6},{6,7},{9,10},{10,11},{13,14},{14,15},{17,18},{18... | collective-permute-start | bytes 2359304 | tf_op jit(solution)/shard_map/ppermute | solution.py:162
  73.2 17.0 %copy-start.8 = (bf16[1024,512]{1,0:T(8,128)(2,1)}, bf16[1024,512]{1,0:T(8,128)(2,1)S(1)}, u32[]{:S(2)}) copy-start(bf16[1024,512]{1,0:T(8,128)(2,1)S(1)} %collective-permute-done.2.refs_4_) | copy-start | bytes 3145732
  88.4 19.5 %copy-start.2 = (bf16[48,8192]{1,0:T(8,128)(2,1)}, bf16[48,8192]{1,0:T(8,128)(2,1)S(1)}, u32[]{:S(2)}) copy-start(bf16[48,8192]{1,0:T(8,128)(2,1)S(1)} %collective-permute-done.10.refs_9_) | copy-start | bytes 2359300
  88.5 19.5 %copy-start.3 = (bf16[48,8192]{1,0:T(8,128)(2,1)}, bf16[48,8192]{1,0:T(8,128)(2,1)S(1)}, u32[]{:S(2)}) copy-start(bf16[48,8192]{1,0:T(8,128)(2,1)S(1)} %collective-permute-done.9.refs_7_) | copy-start | bytes 2359300
  88.5 1.7 %copy-start.6 = (bf16[3072,512]{1,0:T(8,128)(2,1)}, bf16[3072,512]{1,0:T(8,128)(2,1)S(1)}, u32[]{:S(2)}) copy-start(bf16[3072,512]{1,0:T(8,128)(2,1)S(1)} %collective-permute-done.1.refs_3_) | copy-start | bytes 9437188
  90.2 6.5 %collective-permute-start.13 = (bf16[3072,512]{1,0:T(8,128)(2,1)}, bf16[3072,512]{1,0:T(8,128)(2,1)}, u32[]{:S(2)}, u32[]{:S(2)}) collective-permute-start(bf16[3072,512]{1,0:T(8,128)(2,1)} %collective-permute-done.refs_2_), channel_id=1, source_target_pairs={{0,4},{4,0},{8,12},{12,8},{1,5},{5,1},{9,13},{13,9},{2,6},{6,2},{1... | collective-permute-start | bytes 9437192 | tf_op jit(solution)/shard_map/ppermute | solution.py:184
  90.2 25.9 %collective-permute-start.12 = (bf16[1024,512]{1,0:T(8,128)(2,1)}, bf16[1024,512]{1,0:T(8,128)(2,1)}, u32[]{:S(2)}, u32[]{:S(2)}) collective-permute-start(bf16[1024,512]{1,0:T(8,128)(2,1)} %get-tuple-element.43.refs_1_), channel_id=1, source_target_pairs={{0,8},{4,12},{8,0},{12,4},{1,9},{5,13},{9,1},{13,5},{2,10},{6,14},... | collective-permute-start | bytes 3145736 | tf_op jit(solution)/shard_map/ppermute | solution.py:181
  92.2 38.8 %collective-permute-start.11 = (bf16[96,8192]{1,0:T(8,128)(2,1)}, bf16[96,8192]{1,0:T(8,128)(2,1)}, u32[]{:S(2)}, u32[]{:S(2)}) collective-permute-start(bf16[96,8192]{1,0:T(8,128)(2,1)} %maximum_select_fusion), channel_id=1, source_target_pairs={{2,3},{1,0},{6,7},{5,4},{10,11},{9,8},{14,15},{13,12},{18,19},{17,... | collective-permute-start | bytes 4718600 | tf_op jit(solution)/shard_map/ppermute | solution.py:242
  116.1 2.9 %collective-permute-start.14 = (bf16[1024,512]{1,0:T(8,128)(2,1)}, bf16[1024,512]{1,0:T(8,128)(2,1)S(1)}, u32[]{:S(2)}, u32[]{:S(2)}) collective-permute-start(bf16[1024,512]{1,0:T(8,128)(2,1)} %collective-permute-done.12.refs_0_), channel_id=1, source_target_pairs={{0,4},{4,0},{8,12},{12,8},{1,5},{5,1},{9,13},{13,9},{2,6},{6,2},{1... | collective-permute-start | bytes 3145736 | tf_op jit(solution)/shard_map/ppermute | solution.py:184
  119.0 1.1 copy-start.9

commit v9 on v6

v9 whole, which is shorter than its diff:
```python
import functools
import jax
import jax.numpy as jnp
from jax import lax
from jax.experimental import pallas as pl
from jax.experimental.pallas import tpu as pltpu
from jax.sharding import PartitionSpec as P

CORES = 2
CHUNK_BLOCKS = 8


VMEM_LIMIT = 60 * 1024 * 1024
SMEM = pl.BlockSpec(memory_space=pltpu.SMEM)
VMEM = pl.BlockSpec(memory_space=pltpu.VMEM)
HBM = pl.BlockSpec(memory_space=pl.ANY)
BRIEF = pl.CostEstimate(flops=1, bytes_accessed=1, transcendentals=0)


def scale_kernel(block, scale_ref, codes_ref, *out_refs):
    col_blocks = scale_ref.shape[1]
    wide = codes_ref.shape[1] // col_blocks
    first = 0
    for out_ref in out_refs:
        count = out_ref.shape[0] // block

        @pl.loop(0, count)
        def _(index):
            source = pl.ds(pl.multiple_of((first + index) * block, block), block)
            target = pl.ds(pl.multiple_of(index * block, block), block)
            for col in range(col_blocks):
                at = pl.ds(col * wide, wide)
                delta = codes_ref[source, at].astype(jnp.float32) * scale_ref[first + index, col]
                out_ref[target, at] = delta.astype(jnp.bfloat16)

        first += count


def merge_kernel(block, parts, block_ref, base_ref, *refs):
    stores = refs[: len(parts)]
    out_ref, base_buf, delta_buf, base_sems, delta_sems, out_sems = refs[-6:]

    def rows(index):
        return pl.ds(pl.multiple_of(index * block, block), block)

    def copies(index, store, slot):
        return (
            pltpu.make_async_copy(base_ref.at[rows(index), :], base_buf.at[rows(index), :], base_sems.at[index]),
            pltpu.make_async_copy(store.at[rows(slot), :], delta_buf.at[rows(index), :], delta_sems.at[index]),
        )

    def result(index):
        return pltpu.make_async_copy(base_buf.at[rows(index), :], out_ref.at[rows(index), :], out_sems.at[index])

    def each(visit):
        for (low, high), store in zip(parts, stores):

            @pl.loop(low, high)
            def _(row):
                index = block_ref[row]

                @pl.when(index >= 0)
                def _():
                    visit(index, store, row - low)

    def fetch(index, store, slot):
        for copy in copies(index, store, slot):
            copy.start()

    def merge(index, store, slot):
        for copy in copies(index, store, slot):
            copy.wait()
        merged = base_buf[rows(index), :].astype(jnp.float32) + delta_buf[rows(index), :].astype(jnp.float32)
        base_buf[rows(index), :] = merged.astype(jnp.bfloat16)
        result(index).start()

    each(fetch)
    each(merge)
    each(lambda index, store, slot: result(index).wait())


def product_kernel(dims, weight_ref, *refs):
    ranks, span, last = dims
    given = 2 * ranks - 1 if last else 2 * ranks - 3
    own, rights = refs[0], refs[1 : (given + 1) // 2]
    lefts = refs[(given + 1) // 2 : given]
    out_ref, token_buf, weight_buf, total, sems = refs[-5:] if not last else refs[-6:-1]
    rows, depth = own.shape
    chunks = depth // span
    rank = lax.axis_index("tp")
    star = lax.rem(2 * rank + 1, ranks)

    def columns(chunk):
        return pl.ds(pl.multiple_of(chunk * span, span), span)

    def origin_rows(hop):
        return pl.ds(pl.multiple_of(lax.rem(rank - hop + ranks, ranks) * rows, rows), rows)

    def slot_rows(hop):
        slot = 0 if last else hop - (star < hop).astype(jnp.int32)
        return pl.ds(pl.multiple_of(slot * rows, rows), rows)

    def weight_copy(chunk):
        at = columns(chunk)
        return pltpu.make_async_copy(weight_ref.at[at, :], weight_buf.at[at, :], sems.at[chunk, ranks])

    def token_copy(chunk, hop, source):
        at = columns(chunk)
        return pltpu.make_async_copy(source.at[:, at], token_buf.at[slot_rows(hop), at], sems.at[chunk, hop])

    def each(visit):
        for hop in range(ranks):

            @pl.when((star == hop) if last else (star != hop))
            def _():
                visit(hop)

    def fetch(chunk, hop):
        if hop == 0:
            token_copy(chunk, hop, own).start()
            return
        if hop <= len(rights):

            @pl.when(rank >= hop)
            def _():
                token_copy(chunk, hop, rights[hop - 1]).start()

        if ranks - hop <= len(lefts):

            @pl.when(rank < hop)
            def _():
                token_copy(chunk, hop, lefts[ranks - hop - 1]).start()

    @pl.loop(0, chunks)
    def _(chunk):
        weight_copy(chunk).start()
        each(functools.partial(fetch, chunk))

    total[...] = jnp.zeros_like(total)

    @pl.loop(0, chunks)
    def _(chunk):
        weight_copy(chunk).wait()
        each(lambda hop: token_copy(chunk, hop, own).wait())
        at = columns(chunk)
        total[...] += jnp.dot(token_buf[:, at], weight_buf[at, :], preferred_element_type=jnp.float32)

    if last:
        result = refs[-1]
        result[...] = total[...].astype(result.dtype)

        def store(hop):
            pltpu.sync_copy(result, out_ref.at[origin_rows(hop), :])

    else:

        def store(hop):
            out_ref[origin_rows(hop), :] = total[slot_rows(hop), :].astype(out_ref.dtype)

    each(store)


def local(tokens, base_weight, delta_codes, delta_scales, replica_variant, block_home):
    ranks, reps = lax.axis_size("tp"), lax.axis_size("rep")
    blocks = block_home.shape[1]
    depth, width = base_weight.shape
    rows = tokens.shape[0]
    block = depth // blocks
    slots = delta_scales.shape[0]
    rep = lax.axis_index("rep")
    chips = reps // CORES
    ring = [(i, (i + CORES) % reps) for i in range(reps)]
    swap = [(i, i // CORES * CORES + (i + 1) % CORES) for i in range(reps)]

    def tie(values):
        return lax.optimization_barrier(values)

    def right(value, hop):
        return lax.ppermute(value, "tp", [(i, i + 1) for i in range(hop - 1, ranks - 1)])

    def left(value, hop):
        return lax.ppermute(value, "tp", [(i, i - 1) for i in range(1, ranks - hop + 1)])

    rights, lefts = [tokens], [tokens]
    cuts = [0, slots * 3 // 4, slots]
    pieces = len(cuts) - 1

    def across(store):
        return lax.ppermute(store, "rep", ring)

    def turn(store):
        return lax.ppermute(store, "rep", swap)

    homes = block_home[replica_variant[rep]]
    holder = homes // slots
    away = (rep // CORES - holder // CORES + chips) % chips
    turned = (rep % CORES + holder % CORES) % CORES
    row_of = (turned * chips + away) * slots + homes % slots
    here = row_of[None, :] == jnp.arange(reps * slots, dtype=jnp.int32)[:, None]
    block_of = jnp.max(jnp.where(here, jnp.arange(blocks, dtype=jnp.int32)[None, :], -1), axis=1)

    deltas = pl.pallas_call(
        functools.partial(scale_kernel, block),
        out_shape=[
            jax.ShapeDtypeStruct(((high - low) * block, width), jnp.bfloat16)
            for low, high in zip(cuts[:-1], cuts[1:])
        ],
        in_specs=[SMEM, VMEM],
        out_specs=[VMEM] * pieces,
        compiler_params=pltpu.CompilerParams(vmem_limit_bytes=VMEM_LIMIT),
        cost_estimate=BRIEF,
    )(delta_scales.astype(jnp.float32), delta_codes)
    held, twins = [deltas], [[turn(delta) for delta in deltas]]
    sent = [across(delta) for delta in deltas]
    turns = [(ranks - 2) * hop // (chips - 1) for hop in range(1, chips)]
    for hop in range(1, ranks):
        came_right, came_left = right(rights[-1], hop), left(lefts[-1], hop)
        if hop == ranks - 1:
            break
        taken = 0
        if hop in turns:
            taken = pieces if len(held) < chips - 1 else 1
        if taken:
            came, twins, came_right, came_left = tie((sent[:taken], twins, came_right, came_left))
        else:
            came_right, came_left = tie((came_right, came_left))
        rights.append(came_right)
        lefts.append(came_left)
        if taken:
            held.append(came)
            twins.append([turn(value) for value in came])
            sent = [across(value) for value in came] if taken == pieces else sent[taken:]

    def merge(weight, chosen):
        parts, stores = [], []
        for core, kept in enumerate((held, twins)):
            for hop, piece in chosen:
                place = (core * chips + hop) * slots
                parts.append((place + cuts[piece], place + cuts[piece + 1]))
                stores.append(kept[hop][piece])
        inputs = [block_of, base_weight] + stores
        given = [] if weight is None else [weight]
        return pl.pallas_call(
            functools.partial(merge_kernel, block, tuple(parts)),
            out_shape=jax.ShapeDtypeStruct((depth, width), jnp.bfloat16),
            in_specs=[SMEM] + [HBM] * (1 + len(stores) + len(given)),
            out_specs=HBM,
            scratch_shapes=[
                pltpu.VMEM((depth, width), jnp.bfloat16),
                pltpu.VMEM((depth, width), jnp.bfloat16),
                pltpu.SemaphoreType.DMA((blocks,)),
                pltpu.SemaphoreType.DMA((blocks,)),
                pltpu.SemaphoreType.DMA((blocks,)),
            ],
            input_output_aliases={len(inputs): 0} if given else {},
            compiler_params=pltpu.CompilerParams(vmem_limit_bytes=VMEM_LIMIT),
            cost_estimate=BRIEF,
        )(*inputs, *given)

    there = [(hop, piece) for hop, values in enumerate(held) for piece in range(len(values))]
    weight = merge(None, there)
    sent, weight = tie((sent, weight))
    held[-1] = held[-1] + sent
    twins[-1] = twins[-1] + [turn(value) for value in sent]
    weight = merge(weight, [(chips - 1, piece) for piece in range(1, pieces)])
    chunks = blocks // CHUNK_BLOCKS

    def product(arrays, prior):
        last = prior is not None
        count = 1 if last else ranks - 1
        inputs = [weight] + arrays + ([prior] if last else [])
        scratch = [
            pltpu.VMEM((count * rows, depth), jnp.bfloat16),
            pltpu.VMEM((depth, width), jnp.bfloat16),
            pltpu.VMEM((count * rows, width), jnp.float32),
            pltpu.SemaphoreType.DMA((chunks, ranks + 1)),
        ]
        return pl.pallas_call(
            functools.partial(product_kernel, (ranks, CHUNK_BLOCKS * block, last)),
            out_shape=jax.ShapeDtypeStruct((ranks * rows, width), jnp.bfloat16),
            in_specs=[HBM] * len(inputs),
            out_specs=HBM if last else VMEM,
            scratch_shapes=scratch + ([pltpu.VMEM((rows, width), jnp.bfloat16)] if last else []),
            input_output_aliases={len(inputs) - 1: 0} if last else {},
            compiler_params=pltpu.CompilerParams(vmem_limit_bytes=VMEM_LIMIT),
            cost_estimate=BRIEF,
        )(*inputs)

    early = product(rights + lefts[1:], None)
    (came_right, came_left), early = tie(((came_right, came_left), early))
    return product(rights + [came_right] + lefts[1:] + [came_left], early)


def solution(mesh):
    in_specs = (
        P(("groups", "rep", "tp"), None),
        P(None, "tp"),
        P(("groups", "rep"), "tp"),
        P(("groups", "rep"), "tp"),
        P("groups"),
        P("groups", None),
    )
    out_specs = P(("groups", "rep"), "tp")
    return jax.shard_map(local, mesh=mesh, in_specs=in_specs, out_specs=out_specs, check_vma=False)
```

time: 153 us -> 132 us (0.86)
  waiting for transfers between devices: 99.1 us -> 77.4 us
  between operations: 15.5 us -> 2.1 us
  starting transfers between devices: 5.03 us -> 15.7 us
  Pallas kernels: 29.1 us -> 32.6 us
    ppermute x2, waiting for transfers between devices: 92.1 us -> 40.4 us  [across(): return lax.ppermute(store, 'rep', ring)]
    ppermute x0 -> x6, waiting for transfers between devices: none -> 31.3 us  [the longest x3 24.5 us: right(): lax.ppermute(value, 'tp', [(i, i + 1) for i in range(hop - 1, ranks - 1)])]
    ppermute x0 -> x6, starting transfers between devices: none -> 12.6 us  [the longest x3 8.79 us: right(): lax.ppermute(value, 'tp', [(i, i + 1) for i in range(hop - 1, ranks - 1)])]
    all_gather x2 -> x0, waiting for transfers between devices: 6.96 us -> none  [local(): lax.all_gather(half, 'tp', axis=0, tiled=True)]
    ppermute x4, waiting for transfers between devices: 0.01 us -> 5.73 us  [turn(): return lax.ppermute(store, 'rep', swap)]
    pallas_call x1 -> x2, Pallas kernels: 7.02 us -> 11.5 us  [product(): pl.pallas_call(functools.partial(product_kernel, (ranks, CHUNK_BLOCKS * b...]
    slice x1 -> x0, local copies, waits for them, and re-layouts: 2.64 us -> none  [local(): tokens[chain * rows:(chain + 1) * rows]]
    ppermute x2, starting transfers between devices: 4.68 us -> 2.98 us  [across(): return lax.ppermute(store, 'rep', ring)]
  transfers between devices with their start and end apart: 8 -> 12, of which waited for: 3 -> 8; matrix products, arithmetic and copies ran while one was open for 1% -> 2% of each run, Pallas kernels for 14% -> 21%
where the time goes in v9:
time: 132 us
  waiting for transfers between devices  77.4 us (59%)
  Pallas kernels  32.6 us (25%)
  starting transfers between devices  15.7 us (12%)
  local copies, waits for them, and re-layouts  3.17 us (2%)
  between operations  2.1 us (2%)
    ppermute x2, waiting for transfers between devices, across(): return lax.ppermute(store, 'rep', ring)  40.4 us
    ppermute x3, waiting for transfers between devices, right(): lax.ppermute(value, 'tp', [(i, i + 1) for i in range(hop - 1, ranks - 1)])  24.5 us
    pallas_call x2, Pallas kernels, merge(): pl.pallas_call(functools.partial(merge_kernel, block, tuple(parts)), out_...  15.9 us
    pallas_call x2, Pallas kernels, product(): pl.pallas_call(functools.partial(product_kernel, (ranks, CHUNK_BLOCKS * b...  11.5 us
    ppermute x3, starting transfers between devices, right(): lax.ppermute(value, 'tp', [(i, i + 1) for i in range(hop - 1, ranks - 1)])  8.79 us
    ppermute x3, waiting for transfers between devices, left(): lax.ppermute(value, 'tp', [(i, i - 1) for i in range(1, ranks - hop + 1)])  6.74 us
    ppermute x4, waiting for transfers between devices, turn(): return lax.ppermute(store, 'rep', swap)  5.73 us
    pallas_call x1, Pallas kernels, local(): pl.pallas_call(functools.partial(scale_kernel, block), out_shape=[jax.Sha...  5.16 us
  transfers between devices with their start and end apart: 12, of which 8 were waited for; matrix products, arithmetic and copies ran while one was open for 2% of the time, Pallas kernels for 21%

profile of v9, /device:TPU:0, one launch (start us, length us, event | category | flops | bytes accessed | tf_op | source)
XLA Modules:
  0.0 131.7 jit_solution(1452816351381837179)
XLA Ops:
  0.0 5.1 %collective-permute-start.4 = (bf16[96,8192]{1,0:T(8,128)(2,1)}, bf16[96,8192]{1,0:T(8,128)(2,1)S(1)}, u32[]{:S(2)}, u32[]{:S(2)}) collective-permute-start(bf16[96,8192]{1,0:T(8,128)(2,1)} %refs_0_.3), channel_id=1, source_target_pairs={{0,1},{1,2},{2,3},{4,5},{5,6},{6,7},{8,9},{9,10},{10,11},{12,13},{... | collective-permute-start | bytes 4718600 | tf_op jit(solution)/shard_map/ppermute | solution.py:179
  5.2 1.3 collective-permute-start.5
  6.5 1.4 %copy.11.scale_ref = f32[32,4]{1,0:T(8,128)} copy(bf16[32,4]{0,1:T(4,128)(2,1)} %param.9) | data formatting | bytes 768 | tf_op jit(solution)/shard_map/convert_element_type | solution.py:212
  7.8 5.2 %shard_map.64 = (bf16[3072,512]{1,0:T(8,128)(2,1)}, bf16[1024,512]{1,0:T(8,128)(2,1)}) custom-call(f32[32,4]{1,0:T(8,128)} %copy.11.scale_ref, bf16[4096,512]{1,0:T(8,128)(2,1)} %codes_ref.1), custom_call_target="tpu_custom_call" | custom-call | flops 1 | bytes 1 | tf_op jit(solution)/shard_map/pallas_call | solution.py:202
  13.0 1.5 %collective-permute-start.1 = (bf16[3072,512]{1,0:T(8,128)(2,1)}, bf16[3072,512]{1,0:T(8,128)(2,1)}, u32[]{:S(2)}, u32[]{:S(2)}) collective-permute-start(bf16[3072,512]{1,0:T(8,128)(2,1)} %get-tuple-element.20.refs_0_), channel_id=1, source_target_pairs={{0,8},{4,12},{8,0},{12,4},{1,9},{5,13},{9,1},{13,5},{2,10},{6,14},... | collective-permute-start | bytes 9437192 | tf_op jit(solution)/shard_map/ppermute | solution.py:189
  14.5 0.0 collective-permute-start.2
  14.5 24.5 %collective-permute-done.4.refs_1_ = bf16[96,8192]{1,0:T(8,128)(2,1)S(1)} collective-permute-done((bf16[96,8192]{1,0:T(8,128)(2,1)}, bf16[96,8192]{1,0:T(8,128)(2,1)S(1)}, u32[]{:S(2)}, u32[]{:S(2)}) %collective-permute-start.4) | collective-permute-done | bytes 1572896 | tf_op jit(solution)/shard_map/ppermute | solution.py:179
  39.0 4.1 %collective-permute-done.5.refs_3_.refs_4_ = bf16[96,8192]{1,0:T(8,128)(2,1)S(1)} collective-permute-done((bf16[96,8192]{1,0:T(8,128)(2,1)}, bf16[96,8192]{1,0:T(8,128)(2,1)S(1)}, u32[]{:S(2)}, u32[]{:S(2)}) %collective-permute-start.5) | collective-permute-done | bytes 1572896 | tf_op jit(solution)/shard_map/ppermute | solution.py:182
  43.1 1.8 %collective-permute-start.6 = (bf16[96,8192]{1,0:T(8,128)(2,1)S(1)}, bf16[96,8192]{1,0:T(8,128)(2,1)}, u32[]{:S(2)}, u32[]{:S(2)}) collective-permute-start(bf16[96,8192]{1,0:T(8,128)(2,1)S(1)} %collective-permute-done.4.refs_1_), channel_id=1, source_target_pairs={{1,2},{2,3},{5,6},{6,7},{9,10},{10,11},{13,14},{14,15},{17,18},{18... | collective-permute-start | bytes 4718600 | tf_op jit(solution)/shard_map/ppermute | solution.py:179
  45.0 1.3 collective-permute-start.7
  46.2 0.1 collective-permute-start.3
  46.3 2.9 %collective-permute-done.3.refs_4_ = bf16[1024,512]{1,0:T(8,128)(2,1)S(1)} collective-permute-done((bf16[1024,512]{1,0:T(8,128)(2,1)}, bf16[1024,512]{1,0:T(8,128)(2,1)S(1)}, u32[]{:S(2)}, u32[]{:S(2)}) %collective-permute-start.3) | collective-permute-done | bytes 1048608 | tf_op jit(solution)/shard_map/ppermute | solution.py:192
  49.2 33.7 %collective-permute-done.1.refs_2_ = bf16[3072,512]{1,0:T(8,128)(2,1)} collective-permute-done((bf16[3072,512]{1,0:T(8,128)(2,1)}, bf16[3072,512]{1,0:T(8,128)(2,1)}, u32[]{:S(2)}, u32[]{:S(2)}) %collective-permute-start.1) | collective-permute-done | bytes 3145760 | tf_op jit(solution)/shard_map/ppermute | solution.py:189
  82.9 0.0 collective-permute-done.2.refs_3_
  82.9 0.0 collective-permute-done.6.refs_2_
  82.9 1.4 %collective-permute-done.7.refs_4_.refs_5_ = bf16[96,8192]{1,0:T(8,128)(2,1)} collective-permute-done((bf16[96,8192]{1,0:T(8,128)(2,1)S(1)}, bf16[96,8192]{1,0:T(8,128)(2,1)}, u32[]{:S(2)}, u32[]{:S(2)}) %collective-permute-start.7) | collective-permute-done | bytes 1572896 | tf_op jit(solution)/shard_map/ppermute | solution.py:182
  84.3 0.2 copy-done.2
  84.5 0.0 collective-permute-start.8
  84.5 1.5 %collective-permute-start = (bf16[1024,512]{1,0:T(8,128)(2,1)}, bf16[1024,512]{1,0:T(8,128)(2,1)}, u32[]{:S(2)}, u32[]{:S(2)}) collective-permute-start(bf16[1024,512]{1,0:T(8,128)(2,1)} %get-tuple-element.19.refs_1_), channel_id=1, source_target_pairs={{0,8},{4,12},{8,0},{12,4},{1,9},{5,13},{9,1},{13,5},{2,10},{6,14},... | collective-permute-start | bytes 3145736 | tf_op jit(solution)/shard_map/ppermute | solution.py:189
  86.0 1.8 %collective-permute-start.10 = (bf16[96,8192]{1,0:T(8,128)(2,1)}, bf16[96,8192]{1,0:T(8,128)(2,1)}, u32[]{:S(2)}, u32[]{:S(2)}) collective-permute-start(bf16[96,8192]{1,0:T(8,128)(2,1)} %collective-permute-done.6.refs_2_), channel_id=1, source_target_pairs={{2,3},{6,7},{10,11},{14,15},{18,19},{22,23},{26,27},{30,31}} | collective-permute-start | bytes 4718600 | tf_op jit(solution)/shard_map/ppermute | solution.py:179
  87.8 1.3 collective-permute-start.11
  89.1 0.6 dynamic_slice.6
  91.7 0.6 select_reduce_fusion.block_ref
  92.3 11.3 %shard_map.65.refs_2_ = bf16[8192,512]{1,0:T(8,128)(2,1)} custom-call(s32[128]{0:T(128)} %select_reduce_fusion.block_ref, bf16[8192,512]{1,0:T(8,128)(2,1)} %base_ref.3, bf16[3072,512]{1,0:T(8,128)(2,1)} %get-tuple-element.20.refs_0_, bf16[1024,512]{1,0:T(8,128)(2,1)} %get-tuple-element.19.refs_1_, bf16[3072,512]{1,0:T(8,128)(2,1)} %collective-permute-done.1.refs_2_, ...), custom_call_target="tpu_custom_call" | custom-call | flops 1 | bytes 1 | tf_op jit(solution)/shard_map/pallas_call | solution.py:243
  103.7 6.7 %collective-permute-done.refs_0_ = bf16[1024,512]{1,0:T(8,128)(2,1)} collective-permute-done((bf16[1024,512]{1,0:T(8,128)(2,1)}, bf16[1024,512]{1,0:T(8,128)(2,1)}, u32[]{:S(2)}, u32[]{:S(2)}) %collective-permute-start) | collective-permute-done | bytes 1048608 | tf_op jit(solution)/shard_map/ppermute | solution.py:189
  110.4 2.9 %collective-permute-done.9.refs_1_ = bf16[1024,512]{1,0:T(8,128)(2,1)S(1)} collective-permute-done((bf16[1024,512]{1,0:T(8,128)(2,1)}, bf16[1024,512]{1,0:T(8,128)(2,1)S(1)}, u32[]{:S(2)}, u32[]{:S(2)}) %collective-permute-start.9) | collective-permute-done | bytes 1048608 | tf_op jit(solution)/shard_map/ppermute | solution.py:192
  113.3 1.0 copy-done.4
  114.2 4.6 %shard_map.66.weight_ref = bf16[8192,512]{1,0:T(8,128)(2,1)} custom-call(s32[128]{0:T(128)} %select_reduce_fusion.block_ref, bf16[8192,512]{1,0:T(8,128)(2,1)} %base_ref.3, bf16[1024,512]{1,0:T(8,128)(2,1)} %collective-permute-done.refs_0_, bf16[1024,512]{1,0:T(8,128)(2,1)} %copy-done.4, ...), custom_call_target="tpu_custom_call", output_to_operand_aliasing={{}: (4, {})} | custom-call | flops 1 | bytes 1 | tf_op jit(solution)/shard_map/pallas_call | solution.py:243
  118.9 6.4 %shard_map.67.refs_7_ = bf16[384,512]{1,0:T(8,128)(2,1)} custom-call(bf16[8192,512]{1,0:T(8,128)(2,1)} %shard_map.66.weight_ref, bf16[96,8192]{1,0:T(8,128)(2,1)} %refs_0_.3, bf16[96,8192]{1,0:T(8,128)(2,1)} %copy-done, bf16[96,8192]{1,0:T(8,128)(2,1)} %collective-permute-done.6.refs_2_, bf16[96,8192]{1,0:T(8,128)(2,1)} %copy-done.1, ...), custom_call_target="tpu_custom_call" | custom-call | flops 1 | bytes 1 | tf_op jit(solution)/shard_map/pallas_call | solution.py:278
  125.3 0.0 collective-permute-done.10.refs_3_
  125.3 1.2 collective-permute-done.11.refs_6_
  126.6 5.1 %shard_map.68 = bf16[384,512]{1,0:T(8,128)(2,1)} custom-call(bf16[8192,512]{1,0:T(8,128)(2,1)} %shard_map.66.weight_ref, bf16[96,8192]{1,0:T(8,128)(2,1)} %refs_0_.3, bf16[96,8192]{1,0:T(8,128)(2,1)} %copy-done, bf16[96,8192]{1,0:T(8,128)(2,1)} %collective-permute-done.6.refs_2_, ...), custom_call_target="tpu_custom_call", output_to_operand_aliasing={{}: (8, {})} | custom-call | flops 1 | bytes 1 | tf_op jit(solution)/shard_map/pallas_call | solution.py:278
  (15 shorter events, 0.1 us)
Async XLA Ops:
  0.0 89.1 %copy-start.6 = (s32[4]{0:T(128)S(1)}, s32[4]{0:T(128)}, u32[]{:S(2)}) copy-start(s32[4]{0:T(128)} %param.10) | copy-start | bytes 52
  0.0 91.7 %copy-start.5 = (s32[2,64]{1,0:T(2,128)S(1)}, s32[2,64]{1,0:T(2,128)}, u32[]{:S(2)}) copy-start(s32[2,64]{1,0:T(2,128)} %param.11) | copy-start | bytes 1540
  0.0 39.0 %collective-permute-start.4 = (bf16[96,8192]{1,0:T(8,128)(2,1)}, bf16[96,8192]{1,0:T(8,128)(2,1)S(1)}, u32[]{:S(2)}, u32[]{:S(2)}) collective-permute-start(bf16[96,8192]{1,0:T(8,128)(2,1)} %refs_0_.3), channel_id=1, source_target_pairs={{0,1},{1,2},{2,3},{4,5},{5,6},{6,7},{8,9},{9,10},{10,11},{12,13},{... | collective-permute-start | bytes 4718600 | tf_op jit(solution)/shard_map/ppermute | solution.py:179
  5.2 38.0 %collective-permute-start.5 = (bf16[96,8192]{1,0:T(8,128)(2,1)}, bf16[96,8192]{1,0:T(8,128)(2,1)S(1)}, u32[]{:S(2)}, u32[]{:S(2)}) collective-permute-start(bf16[96,8192]{1,0:T(8,128)(2,1)} %refs_0_.3), channel_id=1, source_target_pairs={{1,0},{2,1},{3,2},{5,4},{6,5},{7,6},{9,8},{10,9},{11,10},{13,12},{... | collective-permute-start | bytes 4718600 | tf_op jit(solution)/shard_map/ppermute | solution.py:182
  13.0 69.9 %collective-permute-start.1 = (bf16[3072,512]{1,0:T(8,128)(2,1)}, bf16[3072,512]{1,0:T(8,128)(2,1)}, u32[]{:S(2)}, u32[]{:S(2)}) collective-permute-start(bf16[3072,512]{1,0:T(8,128)(2,1)} %get-tuple-element.20.refs_0_), channel_id=1, source_target_pairs={{0,8},{4,12},{8,0},{12,4},{1,9},{5,13},{9,1},{13,5},{2,10},{6,14},... | collective-permute-start | bytes 9437192 | tf_op jit(solution)/shard_map/ppermute | solution.py:189
  14.5 68.4 %collective-permute-start.2 = (bf16[3072,512]{1,0:T(8,128)(2,1)}, bf16[3072,512]{1,0:T(8,128)(2,1)S(1)}, u32[]{:S(2)}, u32[]{:S(2)}) collective-permute-start(bf16[3072,512]{1,0:T(8,128)(2,1)} %get-tuple-element.20.refs_0_), channel_id=1, source_target_pairs={{0,4},{4,0},{8,12},{12,8},{1,5},{5,1},{9,13},{13,9},{2,6},{6,2},{1... | collective-permute-start | bytes 9437192 | tf_op jit(solution)/shard_map/ppermute | solution.py:192
  39.0 64.6 %copy-start = (bf16[96,8192]{1,0:T(8,128)(2,1)}, bf16[96,8192]{1,0:T(8,128)(2,1)S(1)}, u32[]{:S(2)}) copy-start(bf16[96,8192]{1,0:T(8,128)(2,1)S(1)} %collective-permute-done.4.refs_1_) | copy-start | bytes 4718596
  43.1 60.5 %copy-start.1 = (bf16[96,8192]{1,0:T(8,128)(2,1)}, bf16[96,8192]{1,0:T(8,128)(2,1)S(1)}, u32[]{:S(2)}) copy-start(bf16[96,8192]{1,0:T(8,128)(2,1)S(1)} %collective-permute-done.5.refs_3_.refs_4_) | copy-start | bytes 4718596
  43.1 39.8 %collective-permute-start.6 = (bf16[96,8192]{1,0:T(8,128)(2,1)S(1)}, bf16[96,8192]{1,0:T(8,128)(2,1)}, u32[]{:S(2)}, u32[]{:S(2)}) collective-permute-start(bf16[96,8192]{1,0:T(8,128)(2,1)S(1)} %collective-permute-done.4.refs_1_), channel_id=1, source_target_pairs={{1,2},{2,3},{5,6},{6,7},{9,10},{10,11},{13,14},{14,15},{17,18},{18... | collective-permute-start | bytes 4718600 | tf_op jit(solution)/shard_map/ppermute | solution.py:179
  45.0 39.3 %collective-permute-start.7 = (bf16[96,8192]{1,0:T(8,128)(2,1)S(1)}, bf16[96,8192]{1,0:T(8,128)(2,1)}, u32[]{:S(2)}, u32[]{:S(2)}) collective-permute-start(bf16[96,8192]{1,0:T(8,128)(2,1)S(1)} %collective-permute-done.5.refs_3_.refs_4_), channel_id=1, source_target_pairs={{1,0},{2,1},{5,4},{6,5},{9,8},{10,9},{13,12},{14,13},{17,16},{18,1... | collective-permute-start | bytes 4718600 | tf_op jit(solution)/shard_map/ppermute | solution.py:182
  46.2 2.9 %collective-permute-start.3 = (bf16[1024,512]{1,0:T(8,128)(2,1)}, bf16[1024,512]{1,0:T(8,128)(2,1)S(1)}, u32[]{:S(2)}, u32[]{:S(2)}) collective-permute-start(bf16[1024,512]{1,0:T(8,128)(2,1)} %get-tuple-element.19.refs_1_), channel_id=1, source_target_pairs={{0,4},{4,0},{8,12},{12,8},{1,5},{5,1},{9,13},{13,9},{2,6},{6,2},{1... | collective-permute-start | bytes 3145736 | tf_op jit(solution)/shard_map/ppermute | solution.py:192
  49.2 35.3 %copy-start.3 = (bf16[1024,512]{1,0:T(8,128)(2,1)}, bf16[1024,512]{1,0:T(8,128)(2,1)S(1)}, u32[]{:S(2)}) copy-start(bf16[1024,512]{1,0:T(8,128)(2,1)S(1)} %collective-permute-done.3.refs_4_) | copy-start | bytes 3145732
  82.9 1.7 %copy-start.2 = (bf16[3072,512]{1,0:T(8,128)(2,1)}, bf16[3072,512]{1,0:T(8,128)(2,1)S(1)}, u32[]{:S(2)}) copy-start(bf16[3072,512]{1,0:T(8,128)(2,1)S(1)} %collective-permute-done.2.refs_3_) | copy-start | bytes 9437188
  84.5 7.8 %collective-permute-start.8 = (bf16[3072,512]{1,0:T(8,128)(2,1)}, bf16[3072,512]{1,0:T(8,128)(2,1)}, u32[]{:S(2)}, u32[]{:S(2)}) collective-permute-start(bf16[3072,512]{1,0:T(8,128)(2,1)} %collective-permute-done.1.refs_2_), channel_id=1, source_target_pairs={{0,4},{4,0},{8,12},{12,8},{1,5},{5,1},{9,13},{13,9},{2,6},{6,2},{1... | collective-permute-start | bytes 9437192 | tf_op jit(solution)/shard_map/ppermute | solution.py:192
  84.5 25.9 %collective-permute-start = (bf16[1024,512]{1,0:T(8,128)(2,1)}, bf16[1024,512]{1,0:T(8,128)(2,1)}, u32[]{:S(2)}, u32[]{:S(2)}) collective-permute-start(bf16[1024,512]{1,0:T(8,128)(2,1)} %get-tuple-element.19.refs_1_), channel_id=1, source_target_pairs={{0,8},{4,12},{8,0},{12,4},{1,9},{5,13},{9,1},{13,5},{2,10},{6,14},... | collective-permute-start | bytes 3145736 | tf_op jit(solution)/shard_map/ppermute | solution.py:189
  86.0 39.3 %collective-permute-start.10 = (bf16[96,8192]{1,0:T(8,128)(2,1)}, bf16[96,8192]{1,0:T(8,128)(2,1)}, u32[]{:S(2)}, u32[]{:S(2)}) collective-permute-start(bf16[96,8192]{1,0:T(8,128)(2,1)} %collective-permute-done.6.refs_2_), channel_id=1, source_target_pairs={{2,3},{6,7},{10,11},{14,15},{18,19},{22,23},{26,27},{30,31}} | collective-permute-start | bytes 4718600 | tf_op jit(solution)/shard_map/ppermute | solution.py:179
  87.8 38.7 %collective-permute-start.11 = (bf16[96,8192]{1,0:T(8,128)(2,1)}, bf16[96,8192]{1,0:T(8,128)(2,1)}, u32[]{:S(2)}, u32[]{:S(2)}) collective-permute-start(bf16[96,8192]{1,0:T(8,128)(2,1)} %collective-permute-done.7.refs_4_.refs_5_), channel_id=1, source_target_pairs={{1,0},{5,4},{9,8},{13,12},{17,16},{21,20},{25,24},{29,28}} | collective-permute-start | bytes 4718600 | tf_op jit(solution)/shard_map/ppermute | solution.py:182
  110.4 2.9 %collective-permute-start.9 = (bf16[1024,512]{1,0:T(8,128)(2,1)}, bf16[1024,512]{1,0:T(8,128)(2,1)S(1)}, u32[]{:S(2)}, u32[]{:S(2)}) collective-permute-start(bf16[1024,512]{1,0:T(8,128)(2,1)} %collective-permute-done.refs_0_), channel_id=1, source_target_pairs={{0,4},{4,0},{8,12},{12,8},{1,5},{5,1},{9,13},{13,9},{2,6},{6,2},{1... | collective-permute-start | bytes 3145736 | tf_op jit(solution)/shard_map/ppermute | solution.py:192
  113.3 1.0 copy-start.4

commit v10 on v9

--- a/solution.py
+++ b/solution.py
@@ -182,7 +182,7 @@
         return lax.ppermute(value, "tp", [(i, i - 1) for i in range(1, ranks - hop + 1)])
 
     rights, lefts = [tokens], [tokens]
-    cuts = [0, slots * 3 // 4, slots]
+    cuts = [-(-slots * i // 3) for i in range(4)]
     pieces = len(cuts) - 1
 
     def across(store):
@@ -210,26 +210,33 @@
         compiler_params=pltpu.CompilerParams(vmem_limit_bytes=VMEM_LIMIT),
         cost_estimate=BRIEF,
     )(delta_scales.astype(jnp.float32), delta_codes)
-    held, twins = [deltas], [[turn(delta) for delta in deltas]]
-    sent = [across(delta) for delta in deltas]
-    turns = [(ranks - 2) * hop // (chips - 1) for hop in range(1, chips)]
+    held = [deltas] + [[] for _ in range(1, chips)]
+    twins = [[turn(delta) for delta in deltas]] + [[] for _ in range(1, chips)]
+    moves = [(hop, piece) for hop in range(1, chips) for piece in range(pieces)]
+    flying = {(1, piece): across(delta) for piece, delta in enumerate(deltas)}
+
+    def take(move, value):
+        hop, piece = move
+        held[hop].append(value)
+        twins[hop].append(turn(value))
+        if hop + 1 < chips:
+            flying[hop + 1, piece] = across(value)
+
+    done = 0
     for hop in range(1, ranks):
         came_right, came_left = right(rights[-1], hop), left(lefts[-1], hop)
         if hop == ranks - 1:
             break
-        taken = 0
-        if hop in turns:
-            taken = pieces if len(held) < chips - 1 else 1
-        if taken:
-            came, twins, came_right, came_left = tie((sent[:taken], twins, came_right, came_left))
-        else:
-            came_right, came_left = tie((came_right, came_left))
+        batch = moves[done : (len(moves) - 1) * hop // (ranks - 2)]
+        came = [flying.pop(move) for move in batch]
+        done += len(batch)
+        came, came_right, came_left = tie((came, came_right, came_left))
+        if hop == ranks - 2:
+            twins[0], came_right, came_left = tie((twins[0], came_right, came_left))
         rights.append(came_right)
         lefts.append(came_left)
-        if taken:
-            held.append(came)
-            twins.append([turn(value) for value in came])
-            sent = [across(value) for value in came] if taken == pieces else sent[taken:]
+        for move, value in zip(batch, came):
+            take(move, value)
 
     def merge(weight, chosen):
         parts, stores = [], []
@@ -257,12 +264,10 @@
             cost_estimate=BRIEF,
         )(*inputs, *given)
 
-    there = [(hop, piece) for hop, values in enumerate(held) for piece in range(len(values))]
-    weight = merge(None, there)
-    sent, weight = tie((sent, weight))
-    held[-1] = held[-1] + sent
-    twins[-1] = twins[-1] + [turn(value) for value in sent]
-    weight = merge(weight, [(chips - 1, piece) for piece in range(1, pieces)])
+    weight = merge(None, [(hop, piece) for hop in range(chips) for piece in range(len(held[hop]))])
+    came, weight = tie((flying.pop(moves[-1]), weight))
+    take(moves[-1], came)
+    weight = merge(weight, moves[-1:])
     chunks = blocks // CHUNK_BLOCKS
 
     def product(arrays, prior):

time: 132 us -> 141 us (1.068)
  waiting for transfers between devices: 77.4 us -> 84.8 us
  starting transfers between devices: 15.7 us -> 17.4 us
    ppermute x2 -> x3, waiting for transfers between devices: 40.4 us -> 71.4 us  [across(): return lax.ppermute(store, 'rep', ring)]
    ppermute x3, waiting for transfers between devices: 24.5 us -> 0.01 us  [right(): lax.ppermute(value, 'tp', [(i, i + 1) for i in range(hop - 1, ranks - 1)])]
    ppermute x3, waiting for transfers between devices: 6.74 us -> 10.2 us  [left(): lax.ppermute(value, 'tp', [(i, i - 1) for i in range(1, ranks - hop + 1)])]
    ppermute x4 -> x6, waiting for transfers between devices: 5.73 us -> 3.26 us  [turn(): return lax.ppermute(store, 'rep', swap)]
    ppermute x2 -> x3, starting transfers between devices: 2.98 us -> 3.52 us  [across(): return lax.ppermute(store, 'rep', ring)]
  transfers between devices with their start and end apart: 12 -> 15, of which waited for: 8 -> 5; matrix products, arithmetic and copies ran while one was open for 2% -> 2% of each run, Pallas kernels for 21% -> 19%
where the time goes in v10:
time: 141 us; the launch traced here: 140 us
  waiting for transfers between devices  84.8 us (60%)
  Pallas kernels  32.3 us (23%)
  starting transfers between devices  17.4 us (12%)
  local copies, waits for them, and re-layouts  3.06 us (2%)
  between operations  2.11 us (1%)
    ppermute x3, waiting for transfers between devices, across(): return lax.ppermute(store, 'rep', ring)  71.4 us
    pallas_call x2, Pallas kernels, merge(): pl.pallas_call(functools.partial(merge_kernel, block, tuple(parts)), out_...  15.6 us
    pallas_call x2, Pallas kernels, product(): pl.pallas_call(functools.partial(product_kernel, (ranks, CHUNK_BLOCKS * b...  11.6 us
    ppermute x3, waiting for transfers between devices, left(): lax.ppermute(value, 'tp', [(i, i - 1) for i in range(1, ranks - hop + 1)])  10.2 us
    ppermute x3, starting transfers between devices, right(): lax.ppermute(value, 'tp', [(i, i + 1) for i in range(hop - 1, ranks - 1)])  8.99 us
    pallas_call x1, Pallas kernels, local(): pl.pallas_call(functools.partial(scale_kernel, block), out_shape=[jax.Sha...  5.2 us
    ppermute x3, starting transfers between devices, left(): lax.ppermute(value, 'tp', [(i, i - 1) for i in range(1, ranks - hop + 1)])  3.85 us
    ppermute x3, starting transfers between devices, across(): return lax.ppermute(store, 'rep', ring)  3.52 us
  transfers between devices with their start and end apart: 15, of which 5 were waited for; matrix products, arithmetic and copies ran while one was open for 2% of the time, Pallas kernels for 19%

profile of v10, /device:TPU:0, one launch (start us, length us, event | category | flops | bytes accessed | tf_op | source)
XLA Modules:
  0.0 140.4 jit_solution(6234220233814894048)
XLA Ops:
  0.0 5.0 %collective-permute-start.2 = (bf16[96,8192]{1,0:T(8,128)(2,1)}, bf16[96,8192]{1,0:T(8,128)(2,1)S(1)}, u32[]{:S(2)}, u32[]{:S(2)}) collective-permute-start(bf16[96,8192]{1,0:T(8,128)(2,1)} %refs_0_.3), channel_id=1, source_target_pairs={{0,1},{1,2},{2,3},{4,5},{5,6},{6,7},{8,9},{9,10},{10,11},{12,13},{... | collective-permute-start | bytes 4718600 | tf_op jit(solution)/shard_map/ppermute | solution.py:179
  5.0 1.3 collective-permute-start.3
  6.3 1.4 copy.11.scale_ref
  7.7 5.2 %shard_map.64 = (bf16[1408,512]{1,0:T(8,128)(2,1)}, bf16[1408,512]{1,0:T(8,128)(2,1)}, bf16[1280,512]{1,0:T(8,128)(2,1)}) custom-call(f32[32,4]{1,0:T(8,128)} %copy.11.scale_ref, bf16[4096,512]{1,0:T(8,128)(2,1)} %codes_ref.1), custom_call_target="tpu_custom_call" | custom-call | flops 1 | bytes 1 | tf_op jit(solution)/shard_map/pallas_call | solution.py:202
  12.9 1.5 %collective-permute-start.1 = (bf16[1408,512]{1,0:T(8,128)(2,1)}, bf16[1408,512]{1,0:T(8,128)(2,1)}, u32[]{:S(2)}, u32[]{:S(2)}) collective-permute-start(bf16[1408,512]{1,0:T(8,128)(2,1)} %get-tuple-element.25.refs_0_), channel_id=1, source_target_pairs={{0,8},{4,12},{8,0},{12,4},{1,9},{5,13},{9,1},{13,5},{2,10},{6,14},... | collective-permute-start | bytes 4325384 | tf_op jit(solution)/shard_map/ppermute | solution.py:189
  14.4 0.5 collective-permute-start.4
  14.9 32.8 %collective-permute-done.1.refs_3_ = bf16[1408,512]{1,0:T(8,128)(2,1)} collective-permute-done((bf16[1408,512]{1,0:T(8,128)(2,1)}, bf16[1408,512]{1,0:T(8,128)(2,1)}, u32[]{:S(2)}, u32[]{:S(2)}) %collective-permute-start.1) | collective-permute-done | bytes 1441824 | tf_op jit(solution)/shard_map/ppermute | solution.py:189
  47.7 2.1 %collective-permute-start.5 = (bf16[96,8192]{1,0:T(8,128)(2,1)S(1)}, bf16[96,8192]{1,0:T(8,128)(2,1)}, u32[]{:S(2)}, u32[]{:S(2)}) collective-permute-start(bf16[96,8192]{1,0:T(8,128)(2,1)S(1)} %collective-permute-done.2.refs_1_), channel_id=1, source_target_pairs={{1,2},{2,3},{5,6},{6,7},{9,10},{10,11},{13,14},{14,15},{17,18},{18... | collective-permute-start | bytes 4718600 | tf_op jit(solution)/shard_map/ppermute | solution.py:179
  49.9 1.3 collective-permute-start.6
  51.2 0.1 collective-permute-start.9
  51.3 0.5 collective-permute-start.7
  51.8 25.4 %collective-permute-done.4.refs_4_ = bf16[1408,512]{1,0:T(8,128)(2,1)} collective-permute-done((bf16[1408,512]{1,0:T(8,128)(2,1)}, bf16[1408,512]{1,0:T(8,128)(2,1)}, u32[]{:S(2)}, u32[]{:S(2)}) %collective-permute-start.4) | collective-permute-done | bytes 1441824 | tf_op jit(solution)/shard_map/ppermute | solution.py:189
  77.2 0.0 collective-permute-start.8
  77.2 0.0 collective-permute-done.5.refs_2_
  77.2 0.5 collective-permute-start.10
  77.7 10.1 %collective-permute-done.6.refs_4_.refs_5_ = bf16[96,8192]{1,0:T(8,128)(2,1)} collective-permute-done((bf16[96,8192]{1,0:T(8,128)(2,1)S(1)}, bf16[96,8192]{1,0:T(8,128)(2,1)}, u32[]{:S(2)}, u32[]{:S(2)}) %collective-permute-start.6) | collective-permute-done | bytes 1572896 | tf_op jit(solution)/shard_map/ppermute | solution.py:182
  87.8 1.5 %collective-permute-start = (bf16[1280,512]{1,0:T(8,128)(2,1)}, bf16[1280,512]{1,0:T(8,128)(2,1)}, u32[]{:S(2)}, u32[]{:S(2)}) collective-permute-start(bf16[1280,512]{1,0:T(8,128)(2,1)} %get-tuple-element.24.refs_2_), channel_id=1, source_target_pairs={{0,8},{4,12},{8,0},{12,4},{1,9},{5,13},{9,1},{13,5},{2,10},{6,14},... | collective-permute-start | bytes 3932168 | tf_op jit(solution)/shard_map/ppermute | solution.py:189
  89.3 0.0 collective-permute-done.7.refs_5_
  89.3 0.0 collective-permute-done.8.refs_6_
  89.3 1.8 %collective-permute-start.13 = (bf16[96,8192]{1,0:T(8,128)(2,1)}, bf16[96,8192]{1,0:T(8,128)(2,1)}, u32[]{:S(2)}, u32[]{:S(2)}) collective-permute-start(bf16[96,8192]{1,0:T(8,128)(2,1)} %collective-permute-done.5.refs_2_), channel_id=1, source_target_pairs={{2,3},{6,7},{10,11},{14,15},{18,19},{22,23},{26,27},{30,31}} | collective-permute-start | bytes 4718600 | tf_op jit(solution)/shard_map/ppermute | solution.py:179
  91.2 1.3 collective-permute-start.14
  92.5 0.6 dynamic_slice.6
  95.1 0.6 select_reduce_fusion.block_ref
  95.7 0.0 collective-permute-done.11.refs_9_
  95.7 10.4 %shard_map.65.refs_2_ = bf16[8192,512]{1,0:T(8,128)(2,1)} custom-call(s32[128]{0:T(128)} %select_reduce_fusion.block_ref, bf16[8192,512]{1,0:T(8,128)(2,1)} %base_ref.3, bf16[1408,512]{1,0:T(8,128)(2,1)} %get-tuple-element.25.refs_0_, bf16[1408,512]{1,0:T(8,128)(2,1)} %get-tuple-element.26.refs_1_, bf16[1280,512]{1,0:T(8,128)(2,1)} %get-tuple-element.24.refs_2_, ...), custom_call_target="tpu_custom_call" | custom-call | flops 1 | bytes 1 | tf_op jit(solution)/shard_map/pallas_call | solution.py:250
  106.1 13.2 %collective-permute-done.refs_0_ = bf16[1280,512]{1,0:T(8,128)(2,1)} collective-permute-done((bf16[1280,512]{1,0:T(8,128)(2,1)}, bf16[1280,512]{1,0:T(8,128)(2,1)}, u32[]{:S(2)}, u32[]{:S(2)}) %collective-permute-start) | collective-permute-done | bytes 1310752 | tf_op jit(solution)/shard_map/ppermute | solution.py:189
  119.3 0.0 collective-permute-start.12
  119.3 3.2 %collective-permute-done.12.refs_1_ = bf16[1280,512]{1,0:T(8,128)(2,1)S(1)} collective-permute-done((bf16[1280,512]{1,0:T(8,128)(2,1)}, bf16[1280,512]{1,0:T(8,128)(2,1)S(1)}, u32[]{:S(2)}, u32[]{:S(2)}) %collective-permute-start.12) | collective-permute-done | bytes 1310752 | tf_op jit(solution)/shard_map/ppermute | solution.py:192
  122.6 1.1 copy-done.2
  123.7 5.2 %shard_map.66.weight_ref = bf16[8192,512]{1,0:T(8,128)(2,1)} custom-call(s32[128]{0:T(128)} %select_reduce_fusion.block_ref, bf16[8192,512]{1,0:T(8,128)(2,1)} %base_ref.3, bf16[1280,512]{1,0:T(8,128)(2,1)} %collective-permute-done.refs_0_, bf16[1280,512]{1,0:T(8,128)(2,1)} %copy-done.2, ...), custom_call_target="tpu_custom_call", output_to_operand_aliasing={{}: (4, {})} | custom-call | flops 1 | bytes 1 | tf_op jit(solution)/shard_map/pallas_call | solution.py:250
  128.8 6.4 %shard_map.67.refs_7_ = bf16[384,512]{1,0:T(8,128)(2,1)} custom-call(bf16[8192,512]{1,0:T(8,128)(2,1)} %shard_map.66.weight_ref, bf16[96,8192]{1,0:T(8,128)(2,1)} %refs_0_.3, bf16[96,8192]{1,0:T(8,128)(2,1)} %copy-done, bf16[96,8192]{1,0:T(8,128)(2,1)} %collective-permute-done.5.refs_2_, bf16[96,8192]{1,0:T(8,128)(2,1)} %copy-done.1, ...), custom_call_target="tpu_custom_call" | custom-call | flops 1 | bytes 1 | tf_op jit(solution)/shard_map/pallas_call | solution.py:283
  135.3 5.2 %shard_map.68 = bf16[384,512]{1,0:T(8,128)(2,1)} custom-call(bf16[8192,512]{1,0:T(8,128)(2,1)} %shard_map.66.weight_ref, bf16[96,8192]{1,0:T(8,128)(2,1)} %refs_0_.3, bf16[96,8192]{1,0:T(8,128)(2,1)} %copy-done, bf16[96,8192]{1,0:T(8,128)(2,1)} %collective-permute-done.5.refs_2_, ...), custom_call_target="tpu_custom_call", output_to_operand_aliasing={{}: (8, {})} | custom-call | flops 1 | bytes 1 | tf_op jit(solution)/shard_map/pallas_call | solution.py:283
  (17 shorter events, 0.1 us)
Async XLA Ops:
  0.0 47.7 %collective-permute-start.2 = (bf16[96,8192]{1,0:T(8,128)(2,1)}, bf16[96,8192]{1,0:T(8,128)(2,1)S(1)}, u32[]{:S(2)}, u32[]{:S(2)}) collective-permute-start(bf16[96,8192]{1,0:T(8,128)(2,1)} %refs_0_.3), channel_id=1, source_target_pairs={{0,1},{1,2},{2,3},{4,5},{5,6},{6,7},{8,9},{9,10},{10,11},{12,13},{... | collective-permute-start | bytes 4718600 | tf_op jit(solution)/shard_map/ppermute | solution.py:179
  5.0 42.7 %collective-permute-start.3 = (bf16[96,8192]{1,0:T(8,128)(2,1)}, bf16[96,8192]{1,0:T(8,128)(2,1)S(1)}, u32[]{:S(2)}, u32[]{:S(2)}) collective-permute-start(bf16[96,8192]{1,0:T(8,128)(2,1)} %refs_0_.3), channel_id=1, source_target_pairs={{1,0},{2,1},{3,2},{5,4},{6,5},{7,6},{9,8},{10,9},{11,10},{13,12},{... | collective-permute-start | bytes 4718600 | tf_op jit(solution)/shard_map/ppermute | solution.py:182
  7.7 84.8 %copy-start.4 = (s32[4]{0:T(128)S(1)}, s32[4]{0:T(128)}, u32[]{:S(2)}) copy-start(s32[4]{0:T(128)} %param.10) | copy-start | bytes 52
  7.7 87.3 %copy-start.3 = (s32[2,64]{1,0:T(2,128)S(1)}, s32[2,64]{1,0:T(2,128)}, u32[]{:S(2)}) copy-start(s32[2,64]{1,0:T(2,128)} %param.11) | copy-start | bytes 1540
  12.9 34.8 %collective-permute-start.1 = (bf16[1408,512]{1,0:T(8,128)(2,1)}, bf16[1408,512]{1,0:T(8,128)(2,1)}, u32[]{:S(2)}, u32[]{:S(2)}) collective-permute-start(bf16[1408,512]{1,0:T(8,128)(2,1)} %get-tuple-element.25.refs_0_), channel_id=1, source_target_pairs={{0,8},{4,12},{8,0},{12,4},{1,9},{5,13},{9,1},{13,5},{2,10},{6,14},... | collective-permute-start | bytes 4325384 | tf_op jit(solution)/shard_map/ppermute | solution.py:189
  14.4 62.8 %collective-permute-start.4 = (bf16[1408,512]{1,0:T(8,128)(2,1)}, bf16[1408,512]{1,0:T(8,128)(2,1)}, u32[]{:S(2)}, u32[]{:S(2)}) collective-permute-start(bf16[1408,512]{1,0:T(8,128)(2,1)} %get-tuple-element.26.refs_1_), channel_id=1, source_target_pairs={{0,8},{4,12},{8,0},{12,4},{1,9},{5,13},{9,1},{13,5},{2,10},{6,14},... | collective-permute-start | bytes 4325384 | tf_op jit(solution)/shard_map/ppermute | solution.py:189
  47.7 58.4 %copy-start = (bf16[96,8192]{1,0:T(8,128)(2,1)}, bf16[96,8192]{1,0:T(8,128)(2,1)S(1)}, u32[]{:S(2)}) copy-start(bf16[96,8192]{1,0:T(8,128)(2,1)S(1)} %collective-permute-done.2.refs_1_) | copy-start | bytes 4718596
  47.7 58.4 %copy-start.1 = (bf16[96,8192]{1,0:T(8,128)(2,1)}, bf16[96,8192]{1,0:T(8,128)(2,1)S(1)}, u32[]{:S(2)}) copy-start(bf16[96,8192]{1,0:T(8,128)(2,1)S(1)} %collective-permute-done.3.refs_3_.refs_4_) | copy-start | bytes 4718596
  47.7 29.4 %collective-permute-start.5 = (bf16[96,8192]{1,0:T(8,128)(2,1)S(1)}, bf16[96,8192]{1,0:T(8,128)(2,1)}, u32[]{:S(2)}, u32[]{:S(2)}) collective-permute-start(bf16[96,8192]{1,0:T(8,128)(2,1)S(1)} %collective-permute-done.2.refs_1_), channel_id=1, source_target_pairs={{1,2},{2,3},{5,6},{6,7},{9,10},{10,11},{13,14},{14,15},{17,18},{18... | collective-permute-start | bytes 4718600 | tf_op jit(solution)/shard_map/ppermute | solution.py:179
  49.9 37.9 %collective-permute-start.6 = (bf16[96,8192]{1,0:T(8,128)(2,1)S(1)}, bf16[96,8192]{1,0:T(8,128)(2,1)}, u32[]{:S(2)}, u32[]{:S(2)}) collective-permute-start(bf16[96,8192]{1,0:T(8,128)(2,1)S(1)} %collective-permute-done.3.refs_3_.refs_4_), channel_id=1, source_target_pairs={{1,0},{2,1},{5,4},{6,5},{9,8},{10,9},{13,12},{14,13},{17,16},{18,1... | collective-permute-start | bytes 4718600 | tf_op jit(solution)/shard_map/ppermute | solution.py:182
  51.2 36.6 %collective-permute-start.9 = (bf16[1280,512]{1,0:T(8,128)(2,1)}, bf16[1280,512]{1,0:T(8,128)(2,1)}, u32[]{:S(2)}, u32[]{:S(2)}) collective-permute-start(bf16[1280,512]{1,0:T(8,128)(2,1)} %get-tuple-element.24.refs_2_), channel_id=1, source_target_pairs={{0,4},{4,0},{8,12},{12,8},{1,5},{5,1},{9,13},{13,9},{2,6},{6,2},{1... | collective-permute-start | bytes 3932168 | tf_op jit(solution)/shard_map/ppermute | solution.py:192
  51.3 38.1 %collective-permute-start.7 = (bf16[1408,512]{1,0:T(8,128)(2,1)}, bf16[1408,512]{1,0:T(8,128)(2,1)}, u32[]{:S(2)}, u32[]{:S(2)}) collective-permute-start(bf16[1408,512]{1,0:T(8,128)(2,1)} %get-tuple-element.25.refs_0_), channel_id=1, source_target_pairs={{0,4},{4,0},{8,12},{12,8},{1,5},{5,1},{9,13},{13,9},{2,6},{6,2},{1... | collective-permute-start | bytes 4325384 | tf_op jit(solution)/shard_map/ppermute | solution.py:192
  77.2 12.2 %collective-permute-start.8 = (bf16[1408,512]{1,0:T(8,128)(2,1)}, bf16[1408,512]{1,0:T(8,128)(2,1)}, u32[]{:S(2)}, u32[]{:S(2)}) collective-permute-start(bf16[1408,512]{1,0:T(8,128)(2,1)} %get-tuple-element.26.refs_1_), channel_id=1, source_target_pairs={{0,4},{4,0},{8,12},{12,8},{1,5},{5,1},{9,13},{13,9},{2,6},{6,2},{1... | collective-permute-start | bytes 4325384 | tf_op jit(solution)/shard_map/ppermute | solution.py:192
  77.2 18.5 %collective-permute-start.10 = (bf16[1408,512]{1,0:T(8,128)(2,1)}, bf16[1408,512]{1,0:T(8,128)(2,1)}, u32[]{:S(2)}, u32[]{:S(2)}) collective-permute-start(bf16[1408,512]{1,0:T(8,128)(2,1)} %collective-permute-done.1.refs_3_), channel_id=1, source_target_pairs={{0,4},{4,0},{8,12},{12,8},{1,5},{5,1},{9,13},{13,9},{2,6},{6,2},{1... | collective-permute-start | bytes 4325384 | tf_op jit(solution)/shard_map/ppermute | solution.py:192
  87.8 7.9 %collective-permute-start.11 = (bf16[1408,512]{1,0:T(8,128)(2,1)}, bf16[1408,512]{1,0:T(8,128)(2,1)}, u32[]{:S(2)}, u32[]{:S(2)}) collective-permute-start(bf16[1408,512]{1,0:T(8,128)(2,1)} %collective-permute-done.4.refs_4_), channel_id=1, source_target_pairs={{0,4},{4,0},{8,12},{12,8},{1,5},{5,1},{9,13},{13,9},{2,6},{6,2},{1... | collective-permute-start | bytes 4325384 | tf_op jit(solution)/shard_map/ppermute | solution.py:192
  87.8 31.5 %collective-permute-start = (bf16[1280,512]{1,0:T(8,128)(2,1)}, bf16[1280,512]{1,0:T(8,128)(2,1)}, u32[]{:S(2)}, u32[]{:S(2)}) collective-permute-start(bf16[1280,512]{1,0:T(8,128)(2,1)} %get-tuple-element.24.refs_2_), channel_id=1, source_target_pairs={{0,8},{4,12},{8,0},{12,4},{1,9},{5,13},{9,1},{13,5},{2,10},{6,14},... | collective-permute-start | bytes 3932168 | tf_op jit(solution)/shard_map/ppermute | solution.py:189
  89.3 45.9 %collective-permute-start.13 = (bf16[96,8192]{1,0:T(8,128)(2,1)}, bf16[96,8192]{1,0:T(8,128)(2,1)}, u32[]{:S(2)}, u32[]{:S(2)}) collective-permute-start(bf16[96,8192]{1,0:T(8,128)(2,1)} %collective-permute-done.5.refs_2_), channel_id=1, source_target_pairs={{2,3},{6,7},{10,11},{14,15},{18,19},{22,23},{26,27},{30,31}} | collective-permute-start | bytes 4718600 | tf_op jit(solution)/shard_map/ppermute | solution.py:179
  91.2 44.1 %collective-permute-start.14 = (bf16[96,8192]{1,0:T(8,128)(2,1)}, bf16[96,8192]{1,0:T(8,128)(2,1)}, u32[]{:S(2)}, u32[]{:S(2)}) collective-permute-start(bf16[96,8192]{1,0:T(8,128)(2,1)} %collective-permute-done.6.refs_4_.refs_5_), channel_id=1, source_target_pairs={{1,0},{5,4},{9,8},{13,12},{17,16},{21,20},{25,24},{29,28}} | collective-permute-start | bytes 4718600 | tf_op jit(solution)/shard_map/ppermute | solution.py:182
  119.3 3.2 %collective-permute-start.12 = (bf16[1280,512]{1,0:T(8,128)(2,1)}, bf16[1280,512]{1,0:T(8,128)(2,1)S(1)}, u32[]{:S(2)}, u32[]{:S(2)}) collective-permute-start(bf16[1280,512]{1,0:T(8,128)(2,1)} %collective-permute-done.refs_0_), channel_id=1, source_target_pairs={{0,4},{4,0},{8,12},{12,8},{1,5},{5,1},{9,13},{13,9},{2,6},{6,2},{1... | collective-permute-start | bytes 3932168 | tf_op jit(solution)/shard_map/ppermute | solution.py:192
  122.6 1.1 copy-start.2

commit v11 on v9

--- a/solution.py
+++ b/solution.py
@@ -10,6 +10,7 @@
 CHUNK_BLOCKS = 8
 
 
+ALL, EARLY, LAST = 0, 1, 2
 VMEM_LIMIT = 60 * 1024 * 1024
 SMEM = pl.BlockSpec(memory_space=pltpu.SMEM)
 VMEM = pl.BlockSpec(memory_space=pltpu.VMEM)
@@ -80,8 +81,9 @@
 
 
 def product_kernel(dims, weight_ref, *refs):
-    ranks, span, last = dims
-    given = 2 * ranks - 1 if last else 2 * ranks - 3
+    ranks, span, which = dims
+    last = which == LAST
+    given = 2 * ranks - 3 if which == EARLY else 2 * ranks - 1
     own, rights = refs[0], refs[1 : (given + 1) // 2]
     lefts = refs[(given + 1) // 2 : given]
     out_ref, token_buf, weight_buf, total, sems = refs[-5:] if not last else refs[-6:-1]
@@ -97,7 +99,7 @@
         return pl.ds(pl.multiple_of(lax.rem(rank - hop + ranks, ranks) * rows, rows), rows)
 
     def slot_rows(hop):
-        slot = 0 if last else hop - (star < hop).astype(jnp.int32)
+        slot = {ALL: hop, EARLY: hop - (star < hop).astype(jnp.int32), LAST: 0}[which]
         return pl.ds(pl.multiple_of(slot * rows, rows), rows)
 
     def weight_copy(chunk):
@@ -111,7 +113,7 @@
     def each(visit):
         for hop in range(ranks):
 
-            @pl.when((star == hop) if last else (star != hop))
+            @pl.when({ALL: hop >= 0, EARLY: star != hop, LAST: star == hop}[which])
             def _():
                 visit(hop)
 
@@ -182,7 +184,7 @@
         return lax.ppermute(value, "tp", [(i, i - 1) for i in range(1, ranks - hop + 1)])
 
     rights, lefts = [tokens], [tokens]
-    cuts = [0, slots * 3 // 4, slots]
+    cuts = [0, slots * 3 // 8, slots * 11 // 16, slots]
     pieces = len(cuts) - 1
 
     def across(store):
@@ -217,19 +219,17 @@
         came_right, came_left = right(rights[-1], hop), left(lefts[-1], hop)
         if hop == ranks - 1:
             break
-        taken = 0
+        came_right, came_left = tie((came_right, came_left))
+        if hop == 1:
+            twins[0], came_right, came_left = tie((twins[0], came_right, came_left))
         if hop in turns:
             taken = pieces if len(held) < chips - 1 else 1
-        if taken:
-            came, twins, came_right, came_left = tie((sent[:taken], twins, came_right, came_left))
-        else:
-            came_right, came_left = tie((came_right, came_left))
-        rights.append(came_right)
-        lefts.append(came_left)
-        if taken:
+            came, rights, lefts = tie((sent[:taken], rights, lefts))
             held.append(came)
             twins.append([turn(value) for value in came])
             sent = [across(value) for value in came] if taken == pieces else sent[taken:]
+        rights.append(came_right)
+        lefts.append(came_left)
 
     def merge(weight, chosen):
         parts, stores = [], []
@@ -257,17 +257,16 @@
             cost_estimate=BRIEF,
         )(*inputs, *given)
 
-    there = [(hop, piece) for hop, values in enumerate(held) for piece in range(len(values))]
-    weight = merge(None, there)
+    weight = merge(None, [(hop, piece) for hop in range(chips) for piece in range(len(held[hop]))])
     sent, weight = tie((sent, weight))
     held[-1] = held[-1] + sent
     twins[-1] = twins[-1] + [turn(value) for value in sent]
     weight = merge(weight, [(chips - 1, piece) for piece in range(1, pieces)])
     chunks = blocks // CHUNK_BLOCKS
 
-    def product(arrays, prior):
-        last = prior is not None
-        count = 1 if last else ranks - 1
+    def product(which, arrays, prior=None):
+        last = which == LAST
+        count = {ALL: ranks, EARLY: ranks - 1, LAST: 1}[which]
         inputs = [weight] + arrays + ([prior] if last else [])
         scratch = [
             pltpu.VMEM((count * rows, depth), jnp.bfloat16),
@@ -276,7 +275,7 @@
             pltpu.SemaphoreType.DMA((chunks, ranks + 1)),
         ]
         return pl.pallas_call(
-            functools.partial(product_kernel, (ranks, CHUNK_BLOCKS * block, last)),
+            functools.partial(product_kernel, (ranks, CHUNK_BLOCKS * block, which)),
             out_shape=jax.ShapeDtypeStruct((ranks * rows, width), jnp.bfloat16),
             in_specs=[HBM] * len(inputs),
             out_specs=HBM if last else VMEM,
@@ -286,9 +285,8 @@
             cost_estimate=BRIEF,
         )(*inputs)
 
-    early = product(rights + lefts[1:], None)
-    (came_right, came_left), early = tie(((came_right, came_left), early))
-    return product(rights + [came_right] + lefts[1:] + [came_left], early)
+    (came_right, came_left), weight = tie(((came_right, came_left), weight))
+    return product(ALL, rights + [came_right] + lefts[1:] + [came_left])
 
 
 def solution(mesh):

time: 132 us -> 133 us (level)
  Pallas kernels: 32.6 us -> 28.3 us
  waiting for transfers between devices: 77.4 us -> 80.9 us
  starting transfers between devices: 15.7 us -> 17.4 us
    ppermute x3, waiting for transfers between devices: 6.74 us -> 40.7 us  [left(): lax.ppermute(value, 'tp', [(i, i - 1) for i in range(1, ranks - hop + 1)])]
    ppermute x2 -> x3, waiting for transfers between devices: 40.4 us -> 11.4 us  [across(): return lax.ppermute(store, 'rep', ring)]
    pallas_call x2 -> x1, Pallas kernels: 11.5 us -> 7.18 us  [product(): pl.pallas_call(functools.partial(product_kernel, (ranks, CHUNK_BLOCKS * b...]
    ppermute x4 -> x6, waiting for transfers between devices: 5.73 us -> 4.62 us  [turn(): return lax.ppermute(store, 'rep', swap)]
    ppermute x2 -> x3, starting transfers between devices: 2.98 us -> 3.52 us  [across(): return lax.ppermute(store, 'rep', ring)]
  transfers between devices with their start and end apart: 12 -> 15, of which waited for: 8 -> 8; matrix products, arithmetic and copies ran while one was open for 2% -> 2% of each run, Pallas kernels for 21% -> 16%
where the time goes in v11:
time: 133 us; the launch traced here: 132 us
  waiting for transfers between devices  80.9 us (61%)
  Pallas kernels  28.3 us (21%)
  starting transfers between devices  17.4 us (13%)
  local copies, waits for them, and re-layouts  3.04 us (2%)
  between operations  2.13 us (2%)
    ppermute x3, waiting for transfers between devices, left(): lax.ppermute(value, 'tp', [(i, i - 1) for i in range(1, ranks - hop + 1)])  40.7 us
    ppermute x3, waiting for transfers between devices, right(): lax.ppermute(value, 'tp', [(i, i + 1) for i in range(hop - 1, ranks - 1)])  24.2 us
    pallas_call x2, Pallas kernels, merge(): pl.pallas_call(functools.partial(merge_kernel, block, tuple(parts)), out_...  15.9 us
    ppermute x3, waiting for transfers between devices, across(): return lax.ppermute(store, 'rep', ring)  11.4 us
    ppermute x3, starting transfers between devices, right(): lax.ppermute(value, 'tp', [(i, i + 1) for i in range(hop - 1, ranks - 1)])  9.28 us
    pallas_call x1, Pallas kernels, product(): pl.pallas_call(functools.partial(product_kernel, (ranks, CHUNK_BLOCKS * b...  7.18 us
    pallas_call x1, Pallas kernels, local(): pl.pallas_call(functools.partial(scale_kernel, block), out_shape=[jax.Sha...  5.24 us
    ppermute x6, waiting for transfers between devices, turn(): return lax.ppermute(store, 'rep', swap)  4.62 us
  transfers between devices with their start and end apart: 15, of which 8 were waited for; matrix products, arithmetic and copies ran while one was open for 2% of the time, Pallas kernels for 16%

profile of v11, /device:TPU:0, one launch (start us, length us, event | category | flops | bytes accessed | tf_op | source)
XLA Modules:
  0.0 132.4 jit_solution(288765025230974032)
XLA Ops:
  0.0 5.0 %collective-permute-start.3 = (bf16[96,8192]{1,0:T(8,128)(2,1)}, bf16[96,8192]{1,0:T(8,128)(2,1)S(1)}, u32[]{:S(2)}, u32[]{:S(2)}) collective-permute-start(bf16[96,8192]{1,0:T(8,128)(2,1)} %refs_0_), channel_id=1, source_target_pairs={{0,1},{1,2},{2,3},{4,5},{5,6},{6,7},{8,9},{9,10},{10,11},{12,13},{... | collective-permute-start | bytes 4718600 | tf_op jit(solution)/shard_map/ppermute | solution.py:181
  5.0 1.3 collective-permute-start.4
  6.3 1.4 %copy.10.scale_ref = f32[32,4]{1,0:T(8,128)} copy(bf16[32,4]{0,1:T(4,128)(2,1)} %param.9) | data formatting | bytes 768 | tf_op jit(solution)/shard_map/convert_element_type | solution.py:214
  7.7 5.2 %shard_map.64 = (bf16[1536,512]{1,0:T(8,128)(2,1)}, bf16[1280,512]{1,0:T(8,128)(2,1)}, bf16[1280,512]{1,0:T(8,128)(2,1)}) custom-call(f32[32,4]{1,0:T(8,128)} %copy.10.scale_ref, bf16[4096,512]{1,0:T(8,128)(2,1)} %codes_ref.1), custom_call_target="tpu_custom_call" | custom-call | flops 1 | bytes 1 | tf_op jit(solution)/shard_map/pallas_call | solution.py:204
  12.9 1.5 %collective-permute-start.11 = (bf16[1536,512]{1,0:T(8,128)(2,1)}, bf16[1536,512]{1,0:T(8,128)(2,1)}, u32[]{:S(2)}, u32[]{:S(2)}) collective-permute-start(bf16[1536,512]{1,0:T(8,128)(2,1)} %get-tuple-element.27.refs_0_), channel_id=1, source_target_pairs={{0,8},{4,12},{8,0},{12,4},{1,9},{5,13},{9,1},{13,5},{2,10},{6,14},... | collective-permute-start | bytes 4718600 | tf_op jit(solution)/shard_map/ppermute | solution.py:191
  14.4 0.2 collective-permute-start.1
  14.7 24.2 %collective-permute-done.3.refs_1_ = bf16[96,8192]{1,0:T(8,128)(2,1)S(1)} collective-permute-done((bf16[96,8192]{1,0:T(8,128)(2,1)}, bf16[96,8192]{1,0:T(8,128)(2,1)S(1)}, u32[]{:S(2)}, u32[]{:S(2)}) %collective-permute-start.3) | collective-permute-done | bytes 1572896 | tf_op jit(solution)/shard_map/ppermute | solution.py:181
  38.9 0.0 collective-permute-start.2
  38.9 4.1 %collective-permute-done.4.refs_4_ = bf16[96,8192]{1,0:T(8,128)(2,1)S(1)} collective-permute-done((bf16[96,8192]{1,0:T(8,128)(2,1)}, bf16[96,8192]{1,0:T(8,128)(2,1)S(1)}, u32[]{:S(2)}, u32[]{:S(2)}) %collective-permute-start.4) | collective-permute-done | bytes 1572896 | tf_op jit(solution)/shard_map/ppermute | solution.py:184
  43.0 0.0 collective-permute-done.1.refs_5_
  43.0 0.0 collective-permute-done.refs_4_
  43.0 2.5 %collective-permute-start.5 = (bf16[96,8192]{1,0:T(8,128)(2,1)S(1)}, bf16[96,8192]{1,0:T(8,128)(2,1)}, u32[]{:S(2)}, u32[]{:S(2)}) collective-permute-start(bf16[96,8192]{1,0:T(8,128)(2,1)S(1)} %collective-permute-done.3.refs_1_), channel_id=1, source_target_pairs={{1,2},{2,3},{5,6},{6,7},{9,10},{10,11},{13,14},{14,15},{17,18},{18... | collective-permute-start | bytes 4718600 | tf_op jit(solution)/shard_map/ppermute | solution.py:181
  45.5 1.3 collective-permute-start.6
  46.8 3.3 %collective-permute-done.11.refs_3_ = bf16[1536,512]{1,0:T(8,128)(2,1)} collective-permute-done((bf16[1536,512]{1,0:T(8,128)(2,1)}, bf16[1536,512]{1,0:T(8,128)(2,1)}, u32[]{:S(2)}, u32[]{:S(2)}) %collective-permute-start.11) | collective-permute-done | bytes 1572896 | tf_op jit(solution)/shard_map/ppermute | solution.py:191
  50.1 1.5 %collective-permute-start.10 = (bf16[1280,512]{1,0:T(8,128)(2,1)}, bf16[1280,512]{1,0:T(8,128)(2,1)}, u32[]{:S(2)}, u32[]{:S(2)}) collective-permute-start(bf16[1280,512]{1,0:T(8,128)(2,1)} %get-tuple-element.29.refs_2_), channel_id=1, source_target_pairs={{0,8},{4,12},{8,0},{12,4},{1,9},{5,13},{9,1},{13,5},{2,10},{6,14},... | collective-permute-start | bytes 3932168 | tf_op jit(solution)/shard_map/ppermute | solution.py:191
  51.6 0.5 collective-permute-start.9
  52.1 33.5 %collective-permute-done.6.refs_5_ = bf16[96,8192]{1,0:T(8,128)(2,1)} collective-permute-done((bf16[96,8192]{1,0:T(8,128)(2,1)S(1)}, bf16[96,8192]{1,0:T(8,128)(2,1)}, u32[]{:S(2)}, u32[]{:S(2)}) %collective-permute-start.6) | collective-permute-done | bytes 1572896 | tf_op jit(solution)/shard_map/ppermute | solution.py:184
  85.7 1.8 %collective-permute-start.7 = (bf16[96,8192]{1,0:T(8,128)(2,1)}, bf16[96,8192]{1,0:T(8,128)(2,1)}, u32[]{:S(2)}, u32[]{:S(2)}) collective-permute-start(bf16[96,8192]{1,0:T(8,128)(2,1)} %collective-permute-done.5.refs_2_), channel_id=1, source_target_pairs={{2,3},{6,7},{10,11},{14,15},{18,19},{22,23},{26,27},{30,31}} | collective-permute-start | bytes 4718600 | tf_op jit(solution)/shard_map/ppermute | solution.py:181
  87.5 1.3 collective-permute-start.8
  88.8 0.6 dynamic_slice.6
  91.4 0.6 select_reduce_fusion.block_ref
  92.0 9.6 %shard_map.65.refs_4_ = bf16[8192,512]{1,0:T(8,128)(2,1)} custom-call(s32[128]{0:T(128)} %select_reduce_fusion.block_ref, bf16[8192,512]{1,0:T(8,128)(2,1)} %base_ref.3, bf16[1536,512]{1,0:T(8,128)(2,1)} %get-tuple-element.27.refs_0_, bf16[1280,512]{1,0:T(8,128)(2,1)} %get-tuple-element.28.refs_1_, bf16[1280,512]{1,0:T(8,128)(2,1)} %get-tuple-element.29.refs_2_, ...), custom_call_target="tpu_custom_call" | custom-call | flops 1 | bytes 1 | tf_op jit(solution)/shard_map/pallas_call | solution.py:243
  101.6 0.0 collective-permute-done.10.refs_1_
  101.6 8.1 %collective-permute-done.9.refs_0_ = bf16[1280,512]{1,0:T(8,128)(2,1)} collective-permute-done((bf16[1280,512]{1,0:T(8,128)(2,1)}, bf16[1280,512]{1,0:T(8,128)(2,1)}, u32[]{:S(2)}, u32[]{:S(2)}) %collective-permute-start.9) | collective-permute-done | bytes 1310752 | tf_op jit(solution)/shard_map/ppermute | solution.py:191
  109.7 0.0 collective-permute-start.13
  109.7 0.5 collective-permute-start.14
  110.2 2.7 %collective-permute-done.13.refs_2_ = bf16[1280,512]{1,0:T(8,128)(2,1)S(1)} collective-permute-done((bf16[1280,512]{1,0:T(8,128)(2,1)}, bf16[1280,512]{1,0:T(8,128)(2,1)S(1)}, u32[]{:S(2)}, u32[]{:S(2)}) %collective-permute-start.13) | collective-permute-done | bytes 1310752 | tf_op jit(solution)/shard_map/ppermute | solution.py:194
  112.9 1.9 %collective-permute-done.14.refs_3_ = bf16[1280,512]{1,0:T(8,128)(2,1)S(1)} collective-permute-done((bf16[1280,512]{1,0:T(8,128)(2,1)}, bf16[1280,512]{1,0:T(8,128)(2,1)S(1)}, u32[]{:S(2)}, u32[]{:S(2)}) %collective-permute-start.14) | collective-permute-done | bytes 1310752 | tf_op jit(solution)/shard_map/ppermute | solution.py:194
  114.8 1.1 copy-done.4
  115.9 6.3 %shard_map.66.weight_ref = bf16[8192,512]{1,0:T(8,128)(2,1)} custom-call(s32[128]{0:T(128)} %select_reduce_fusion.block_ref, bf16[8192,512]{1,0:T(8,128)(2,1)} %base_ref.3, bf16[1280,512]{1,0:T(8,128)(2,1)} %collective-permute-done.9.refs_0_, bf16[1280,512]{1,0:T(8,128)(2,1)} %collective-permute-done.10.refs_1_, ...), custom_call_target="tpu_custom_call", output_to_operand_aliasing={{}: (6, {})} | custom-call | flops 1 | bytes 1 | tf_op jit(solution)/shard_map/pallas_call | solution.py:243
  122.2 3.1 %collective-permute-done.8.refs_6_ = bf16[96,8192]{1,0:T(8,128)(2,1)} collective-permute-done((bf16[96,8192]{1,0:T(8,128)(2,1)}, bf16[96,8192]{1,0:T(8,128)(2,1)}, u32[]{:S(2)}, u32[]{:S(2)}) %collective-permute-start.8) | collective-permute-done | bytes 1572896 | tf_op jit(solution)/shard_map/ppermute | solution.py:184
  125.2 7.2 %shard_map.67 = bf16[384,512]{1,0:T(8,128)(2,1)} custom-call(bf16[8192,512]{1,0:T(8,128)(2,1)} %shard_map.66.weight_ref, bf16[96,8192]{1,0:T(8,128)(2,1)} %refs_0_, bf16[96,8192]{1,0:T(8,128)(2,1)} %copy-done, bf16[96,8192]{1,0:T(8,128)(2,1)} %collective-permute-done.5.refs_2_, bf16[96,8192]{1,0:T(8,128)(2,1)} %collective-permute-done.7.refs_3_, ...), custom_call_target="tpu_custom_call" | custom-call | flops 1 | bytes 1 | tf_op jit(solution)/shard_map/pallas_call | solution.py:277
  (24 shorter events, 0.1 us)
Async XLA Ops:
  0.0 38.9 %collective-permute-start.3 = (bf16[96,8192]{1,0:T(8,128)(2,1)}, bf16[96,8192]{1,0:T(8,128)(2,1)S(1)}, u32[]{:S(2)}, u32[]{:S(2)}) collective-permute-start(bf16[96,8192]{1,0:T(8,128)(2,1)} %refs_0_), channel_id=1, source_target_pairs={{0,1},{1,2},{2,3},{4,5},{5,6},{6,7},{8,9},{9,10},{10,11},{12,13},{... | collective-permute-start | bytes 4718600 | tf_op jit(solution)/shard_map/ppermute | solution.py:181
  5.0 38.0 %collective-permute-start.4 = (bf16[96,8192]{1,0:T(8,128)(2,1)}, bf16[96,8192]{1,0:T(8,128)(2,1)S(1)}, u32[]{:S(2)}, u32[]{:S(2)}) collective-permute-start(bf16[96,8192]{1,0:T(8,128)(2,1)} %refs_0_), channel_id=1, source_target_pairs={{1,0},{2,1},{3,2},{5,4},{6,5},{7,6},{9,8},{10,9},{11,10},{13,12},{... | collective-permute-start | bytes 4718600 | tf_op jit(solution)/shard_map/ppermute | solution.py:184
  7.7 81.1 %copy-start.8 = (s32[4]{0:T(128)S(1)}, s32[4]{0:T(128)}, u32[]{:S(2)}) copy-start(s32[4]{0:T(128)} %param.10) | copy-start | bytes 52
  7.7 83.6 %copy-start.7 = (s32[2,64]{1,0:T(2,128)S(1)}, s32[2,64]{1,0:T(2,128)}, u32[]{:S(2)}) copy-start(s32[2,64]{1,0:T(2,128)} %param.11) | copy-start | bytes 1540
  12.9 30.1 %collective-permute-start = (bf16[1536,512]{1,0:T(8,128)(2,1)}, bf16[1536,512]{1,0:T(8,128)(2,1)S(1)}, u32[]{:S(2)}, u32[]{:S(2)}) collective-permute-start(bf16[1536,512]{1,0:T(8,128)(2,1)} %get-tuple-element.27.refs_0_), channel_id=1, source_target_pairs={{0,4},{4,0},{8,12},{12,8},{1,5},{5,1},{9,13},{13,9},{2,6},{6,2},{1... | collective-permute-start | bytes 4718600 | tf_op jit(solution)/shard_map/ppermute | solution.py:194
  12.9 37.1 %collective-permute-start.11 = (bf16[1536,512]{1,0:T(8,128)(2,1)}, bf16[1536,512]{1,0:T(8,128)(2,1)}, u32[]{:S(2)}, u32[]{:S(2)}) collective-permute-start(bf16[1536,512]{1,0:T(8,128)(2,1)} %get-tuple-element.27.refs_0_), channel_id=1, source_target_pairs={{0,8},{4,12},{8,0},{12,4},{1,9},{5,13},{9,1},{13,5},{2,10},{6,14},... | collective-permute-start | bytes 4718600 | tf_op jit(solution)/shard_map/ppermute | solution.py:191
  14.4 28.6 %collective-permute-start.1 = (bf16[1280,512]{1,0:T(8,128)(2,1)}, bf16[1280,512]{1,0:T(8,128)(2,1)S(1)}, u32[]{:S(2)}, u32[]{:S(2)}) collective-permute-start(bf16[1280,512]{1,0:T(8,128)(2,1)} %get-tuple-element.28.refs_1_), channel_id=1, source_target_pairs={{0,4},{4,0},{8,12},{12,8},{1,5},{5,1},{9,13},{13,9},{2,6},{6,2},{1... | collective-permute-start | bytes 3932168 | tf_op jit(solution)/shard_map/ppermute | solution.py:194
  38.9 62.7 %copy-start = (bf16[96,8192]{1,0:T(8,128)(2,1)}, bf16[96,8192]{1,0:T(8,128)(2,1)S(1)}, u32[]{:S(2)}) copy-start(bf16[96,8192]{1,0:T(8,128)(2,1)S(1)} %collective-permute-done.3.refs_1_) | copy-start | bytes 4718596
  38.9 4.1 %collective-permute-start.2 = (bf16[1280,512]{1,0:T(8,128)(2,1)}, bf16[1280,512]{1,0:T(8,128)(2,1)S(1)}, u32[]{:S(2)}, u32[]{:S(2)}) collective-permute-start(bf16[1280,512]{1,0:T(8,128)(2,1)} %get-tuple-element.29.refs_2_), channel_id=1, source_target_pairs={{0,4},{4,0},{8,12},{12,8},{1,5},{5,1},{9,13},{13,9},{2,6},{6,2},{1... | collective-permute-start | bytes 3932168 | tf_op jit(solution)/shard_map/ppermute | solution.py:194
  43.0 58.6 %copy-start.1 = (bf16[96,8192]{1,0:T(8,128)(2,1)}, bf16[96,8192]{1,0:T(8,128)(2,1)S(1)}, u32[]{:S(2)}) copy-start(bf16[96,8192]{1,0:T(8,128)(2,1)S(1)} %collective-permute-done.4.refs_4_) | copy-start | bytes 4718596
  43.0 44.5 %copy-start.5 = (bf16[1280,512]{1,0:T(8,128)(2,1)}, bf16[1280,512]{1,0:T(8,128)(2,1)S(1)}, u32[]{:S(2)}) copy-start(bf16[1280,512]{1,0:T(8,128)(2,1)S(1)} %collective-permute-done.1.refs_5_) | copy-start | bytes 3932164
  43.0 45.8 %copy-start.6 = (bf16[1280,512]{1,0:T(8,128)(2,1)}, bf16[1280,512]{1,0:T(8,128)(2,1)S(1)}, u32[]{:S(2)}) copy-start(bf16[1280,512]{1,0:T(8,128)(2,1)S(1)} %collective-permute-done.2.refs_6_) | copy-start | bytes 3932164
  43.0 42.6 %copy-start.2 = (bf16[1536,512]{1,0:T(8,128)(2,1)}, bf16[1536,512]{1,0:T(8,128)(2,1)S(1)}, u32[]{:S(2)}) copy-start(bf16[1536,512]{1,0:T(8,128)(2,1)S(1)} %collective-permute-done.refs_4_) | copy-start | bytes 4718596
  43.0 9.1 %collective-permute-start.5 = (bf16[96,8192]{1,0:T(8,128)(2,1)S(1)}, bf16[96,8192]{1,0:T(8,128)(2,1)}, u32[]{:S(2)}, u32[]{:S(2)}) collective-permute-start(bf16[96,8192]{1,0:T(8,128)(2,1)S(1)} %collective-permute-done.3.refs_1_), channel_id=1, source_target_pairs={{1,2},{2,3},{5,6},{6,7},{9,10},{10,11},{13,14},{14,15},{17,18},{18... | collective-permute-start | bytes 4718600 | tf_op jit(solution)/shard_map/ppermute | solution.py:181
  45.5 40.2 %collective-permute-start.6 = (bf16[96,8192]{1,0:T(8,128)(2,1)S(1)}, bf16[96,8192]{1,0:T(8,128)(2,1)}, u32[]{:S(2)}, u32[]{:S(2)}) collective-permute-start(bf16[96,8192]{1,0:T(8,128)(2,1)S(1)} %collective-permute-done.4.refs_4_), channel_id=1, source_target_pairs={{1,0},{2,1},{5,4},{6,5},{9,8},{10,9},{13,12},{14,13},{17,16},{18,1... | collective-permute-start | bytes 4718600 | tf_op jit(solution)/shard_map/ppermute | solution.py:184
  50.1 41.9 %collective-permute-start.12 = (bf16[1536,512]{1,0:T(8,128)(2,1)}, bf16[1536,512]{1,0:T(8,128)(2,1)}, u32[]{:S(2)}, u32[]{:S(2)}) collective-permute-start(bf16[1536,512]{1,0:T(8,128)(2,1)} %collective-permute-done.11.refs_3_), channel_id=1, source_target_pairs={{0,4},{4,0},{8,12},{12,8},{1,5},{5,1},{9,13},{13,9},{2,6},{6,2},{1... | collective-permute-start | bytes 4718600 | tf_op jit(solution)/shard_map/ppermute | solution.py:194
  50.1 51.5 %collective-permute-start.10 = (bf16[1280,512]{1,0:T(8,128)(2,1)}, bf16[1280,512]{1,0:T(8,128)(2,1)}, u32[]{:S(2)}, u32[]{:S(2)}) collective-permute-start(bf16[1280,512]{1,0:T(8,128)(2,1)} %get-tuple-element.29.refs_2_), channel_id=1, source_target_pairs={{0,8},{4,12},{8,0},{12,4},{1,9},{5,13},{9,1},{13,5},{2,10},{6,14},... | collective-permute-start | bytes 3932168 | tf_op jit(solution)/shard_map/ppermute | solution.py:191
  51.6 58.1 %collective-permute-start.9 = (bf16[1280,512]{1,0:T(8,128)(2,1)}, bf16[1280,512]{1,0:T(8,128)(2,1)}, u32[]{:S(2)}, u32[]{:S(2)}) collective-permute-start(bf16[1280,512]{1,0:T(8,128)(2,1)} %get-tuple-element.28.refs_1_), channel_id=1, source_target_pairs={{0,8},{4,12},{8,0},{12,4},{1,9},{5,13},{9,1},{13,5},{2,10},{6,14},... | collective-permute-start | bytes 3932168 | tf_op jit(solution)/shard_map/ppermute | solution.py:191
  85.7 36.5 %collective-permute-start.7 = (bf16[96,8192]{1,0:T(8,128)(2,1)}, bf16[96,8192]{1,0:T(8,128)(2,1)}, u32[]{:S(2)}, u32[]{:S(2)}) collective-permute-start(bf16[96,8192]{1,0:T(8,128)(2,1)} %collective-permute-done.5.refs_2_), channel_id=1, source_target_pairs={{2,3},{6,7},{10,11},{14,15},{18,19},{22,23},{26,27},{30,31}} | collective-permute-start | bytes 4718600 | tf_op jit(solution)/shard_map/ppermute | solution.py:181
  87.5 37.8 %collective-permute-start.8 = (bf16[96,8192]{1,0:T(8,128)(2,1)}, bf16[96,8192]{1,0:T(8,128)(2,1)}, u32[]{:S(2)}, u32[]{:S(2)}) collective-permute-start(bf16[96,8192]{1,0:T(8,128)(2,1)} %collective-permute-done.6.refs_5_), channel_id=1, source_target_pairs={{1,0},{5,4},{9,8},{13,12},{17,16},{21,20},{25,24},{29,28}} | collective-permute-start | bytes 4718600 | tf_op jit(solution)/shard_map/ppermute | solution.py:184
  109.7 3.2 %collective-permute-start.13 = (bf16[1280,512]{1,0:T(8,128)(2,1)}, bf16[1280,512]{1,0:T(8,128)(2,1)S(1)}, u32[]{:S(2)}, u32[]{:S(2)}) collective-permute-start(bf16[1280,512]{1,0:T(8,128)(2,1)} %collective-permute-done.9.refs_0_), channel_id=1, source_target_pairs={{0,4},{4,0},{8,12},{12,8},{1,5},{5,1},{9,13},{13,9},{2,6},{6,2},{1... | collective-permute-start | bytes 3932168 | tf_op jit(solution)/shard_map/ppermute | solution.py:194
  109.7 5.1 %collective-permute-start.14 = (bf16[1280,512]{1,0:T(8,128)(2,1)}, bf16[1280,512]{1,0:T(8,128)(2,1)S(1)}, u32[]{:S(2)}, u32[]{:S(2)}) collective-permute-start(bf16[1280,512]{1,0:T(8,128)(2,1)} %collective-permute-done.10.refs_1_), channel_id=1, source_target_pairs={{0,4},{4,0},{8,12},{12,8},{1,5},{5,1},{9,13},{13,9},{2,6},{6,2},{1... | collective-permute-start | bytes 3932168 | tf_op jit(solution)/shard_map/ppermute | solution.py:194
  112.9 1.9 %copy-start.3 = (bf16[1280,512]{1,0:T(8,128)(2,1)}, bf16[1280,512]{1,0:T(8,128)(2,1)S(1)}, u32[]{:S(2)}) copy-start(bf16[1280,512]{1,0:T(8,128)(2,1)S(1)} %collective-permute-done.13.refs_2_) | copy-start | bytes 3932164
  114.8 1.1 copy-start.4

commit v12 on v9

--- a/solution.py
+++ b/solution.py
@@ -217,16 +217,12 @@
         came_right, came_left = right(rights[-1], hop), left(lefts[-1], hop)
         if hop == ranks - 1:
             break
-        taken = 0
+        rights.append(came_right)
+        lefts.append(came_left)
         if hop in turns:
             taken = pieces if len(held) < chips - 1 else 1
-        if taken:
-            came, twins, came_right, came_left = tie((sent[:taken], twins, came_right, came_left))
-        else:
-            came_right, came_left = tie((came_right, came_left))
-        rights.append(came_right)
-        lefts.append(came_left)
-        if taken:
+            came, twins, tied_right, tied_left = tie((sent[:taken], twins, came_right, came_left))
+            kept = [tied_right, tied_left]
             held.append(came)
             twins.append([turn(value) for value in came])
             sent = [across(value) for value in came] if taken == pieces else sent[taken:]
@@ -286,7 +282,7 @@
             cost_estimate=BRIEF,
         )(*inputs)
 
-    early = product(rights + lefts[1:], None)
+    early = product(rights[:-1] + kept[:1] + lefts[1:-1] + kept[1:], None)
     (came_right, came_left), early = tie(((came_right, came_left), early))
     return product(rights + [came_right] + lefts[1:] + [came_left], early)
 

time: 132 us -> 130 us (0.985)
    ppermute x2, waiting for transfers between devices: 40.4 us -> 8.82 us  [across(): return lax.ppermute(store, 'rep', ring)]
    ppermute x3, waiting for transfers between devices: 6.74 us -> 37.2 us  [left(): lax.ppermute(value, 'tp', [(i, i - 1) for i in range(1, ranks - hop + 1)])]
where the time goes in v12:
time: 130 us
  waiting for transfers between devices  76.3 us (59%)
  Pallas kernels  32.4 us (25%)
  starting transfers between devices  15.7 us (12%)
  local copies, waits for them, and re-layouts  2.94 us (2%)
  between operations  2.1 us (2%)
    ppermute x3, waiting for transfers between devices, left(): lax.ppermute(value, 'tp', [(i, i - 1) for i in range(1, ranks - hop + 1)])  37.2 us
    ppermute x3, waiting for transfers between devices, right(): lax.ppermute(value, 'tp', [(i, i + 1) for i in range(hop - 1, ranks - 1)])  24.5 us
    pallas_call x2, Pallas kernels, merge(): pl.pallas_call(functools.partial(merge_kernel, block, tuple(parts)), out_...  15.7 us
    pallas_call x2, Pallas kernels, product(): pl.pallas_call(functools.partial(product_kernel, (ranks, CHUNK_BLOCKS * b...  11.5 us
    ppermute x2, waiting for transfers between devices, across(): return lax.ppermute(store, 'rep', ring)  8.82 us
    ppermute x3, starting transfers between devices, right(): lax.ppermute(value, 'tp', [(i, i + 1) for i in range(hop - 1, ranks - 1)])  8.78 us
    ppermute x4, waiting for transfers between devices, turn(): return lax.ppermute(store, 'rep', swap)  5.73 us
    pallas_call x1, Pallas kernels, local(): pl.pallas_call(functools.partial(scale_kernel, block), out_shape=[jax.Sha...  5.18 us
  transfers between devices with their start and end apart: 12, of which 8 were waited for; matrix products, arithmetic and copies ran while one was open for 2% of the time, Pallas kernels for 21%

profile of v12, /device:TPU:0, one launch (start us, length us, event | category | flops | bytes accessed | tf_op | source)
XLA Modules:
  0.0 130.0 jit_solution(16086149211751118512)
XLA Ops:
  0.0 5.1 %collective-permute-start.4 = (bf16[96,8192]{1,0:T(8,128)(2,1)}, bf16[96,8192]{1,0:T(8,128)(2,1)S(1)}, u32[]{:S(2)}, u32[]{:S(2)}) collective-permute-start(bf16[96,8192]{1,0:T(8,128)(2,1)} %refs_0_.3), channel_id=1, source_target_pairs={{0,1},{1,2},{2,3},{4,5},{5,6},{6,7},{8,9},{9,10},{10,11},{12,13},{... | collective-permute-start | bytes 4718600 | tf_op jit(solution)/shard_map/ppermute | solution.py:179
  5.2 1.3 collective-permute-start.6
  6.5 1.4 %copy.11.scale_ref = f32[32,4]{1,0:T(8,128)} copy(bf16[32,4]{0,1:T(4,128)(2,1)} %param.9) | data formatting | bytes 768 | tf_op jit(solution)/shard_map/convert_element_type | solution.py:212
  7.8 5.2 %shard_map.64 = (bf16[3072,512]{1,0:T(8,128)(2,1)}, bf16[1024,512]{1,0:T(8,128)(2,1)}) custom-call(f32[32,4]{1,0:T(8,128)} %copy.11.scale_ref, bf16[4096,512]{1,0:T(8,128)(2,1)} %codes_ref.1), custom_call_target="tpu_custom_call" | custom-call | flops 1 | bytes 1 | tf_op jit(solution)/shard_map/pallas_call | solution.py:202
  13.0 1.5 %collective-permute-start.1 = (bf16[3072,512]{1,0:T(8,128)(2,1)}, bf16[3072,512]{1,0:T(8,128)(2,1)}, u32[]{:S(2)}, u32[]{:S(2)}) collective-permute-start(bf16[3072,512]{1,0:T(8,128)(2,1)} %get-tuple-element.18.refs_0_), channel_id=1, source_target_pairs={{0,8},{4,12},{8,0},{12,4},{1,9},{5,13},{9,1},{13,5},{2,10},{6,14},... | collective-permute-start | bytes 9437192 | tf_op jit(solution)/shard_map/ppermute | solution.py:189
  14.5 0.0 collective-permute-start.2
  14.5 24.5 %collective-permute-done.4.refs_1_ = bf16[96,8192]{1,0:T(8,128)(2,1)S(1)} collective-permute-done((bf16[96,8192]{1,0:T(8,128)(2,1)}, bf16[96,8192]{1,0:T(8,128)(2,1)S(1)}, u32[]{:S(2)}, u32[]{:S(2)}) %collective-permute-start.4) | collective-permute-done | bytes 1572896 | tf_op jit(solution)/shard_map/ppermute | solution.py:179
  39.0 1.8 %collective-permute-start.5 = (bf16[96,8192]{1,0:T(8,128)(2,1)S(1)}, bf16[96,8192]{1,0:T(8,128)(2,1)}, u32[]{:S(2)}, u32[]{:S(2)}) collective-permute-start(bf16[96,8192]{1,0:T(8,128)(2,1)S(1)} %collective-permute-done.4.refs_1_), channel_id=1, source_target_pairs={{1,2},{2,3},{5,6},{6,7},{9,10},{10,11},{13,14},{14,15},{17,18},{18... | collective-permute-start | bytes 4718600 | tf_op jit(solution)/shard_map/ppermute | solution.py:179
  40.8 2.3 %collective-permute-done.6.refs_3_.refs_4_ = bf16[96,8192]{1,0:T(8,128)(2,1)S(1)} collective-permute-done((bf16[96,8192]{1,0:T(8,128)(2,1)}, bf16[96,8192]{1,0:T(8,128)(2,1)S(1)}, u32[]{:S(2)}, u32[]{:S(2)}) %collective-permute-start.6) | collective-permute-done | bytes 1572896 | tf_op jit(solution)/shard_map/ppermute | solution.py:182
  43.1 1.3 collective-permute-start.7
  44.4 0.1 collective-permute-start.3
  44.5 2.9 %collective-permute-done.3.refs_4_ = bf16[1024,512]{1,0:T(8,128)(2,1)S(1)} collective-permute-done((bf16[1024,512]{1,0:T(8,128)(2,1)}, bf16[1024,512]{1,0:T(8,128)(2,1)S(1)}, u32[]{:S(2)}, u32[]{:S(2)}) %collective-permute-start.3) | collective-permute-done | bytes 1048608 | tf_op jit(solution)/shard_map/ppermute | solution.py:192
  47.4 0.0 collective-permute-done.5.refs_2_
  47.4 34.0 %collective-permute-done.7.refs_4_.refs_5_ = bf16[96,8192]{1,0:T(8,128)(2,1)} collective-permute-done((bf16[96,8192]{1,0:T(8,128)(2,1)S(1)}, bf16[96,8192]{1,0:T(8,128)(2,1)}, u32[]{:S(2)}, u32[]{:S(2)}) %collective-permute-start.7) | collective-permute-done | bytes 1572896 | tf_op jit(solution)/shard_map/ppermute | solution.py:182
  81.4 1.5 %collective-permute-done.1.refs_2_ = bf16[3072,512]{1,0:T(8,128)(2,1)} collective-permute-done((bf16[3072,512]{1,0:T(8,128)(2,1)}, bf16[3072,512]{1,0:T(8,128)(2,1)}, u32[]{:S(2)}, u32[]{:S(2)}) %collective-permute-start.1) | collective-permute-done | bytes 3145760 | tf_op jit(solution)/shard_map/ppermute | solution.py:189
  82.9 0.0 collective-permute-done.2.refs_3_
  82.9 0.0 collective-permute-start.8
  82.9 1.5 %collective-permute-start = (bf16[1024,512]{1,0:T(8,128)(2,1)}, bf16[1024,512]{1,0:T(8,128)(2,1)}, u32[]{:S(2)}, u32[]{:S(2)}) collective-permute-start(bf16[1024,512]{1,0:T(8,128)(2,1)} %get-tuple-element.17.refs_1_), channel_id=1, source_target_pairs={{0,8},{4,12},{8,0},{12,4},{1,9},{5,13},{9,1},{13,5},{2,10},{6,14},... | collective-permute-start | bytes 3145736 | tf_op jit(solution)/shard_map/ppermute | solution.py:189
  84.4 1.8 %collective-permute-start.10 = (bf16[96,8192]{1,0:T(8,128)(2,1)}, bf16[96,8192]{1,0:T(8,128)(2,1)}, u32[]{:S(2)}, u32[]{:S(2)}) collective-permute-start(bf16[96,8192]{1,0:T(8,128)(2,1)} %collective-permute-done.5.refs_2_), channel_id=1, source_target_pairs={{2,3},{6,7},{10,11},{14,15},{18,19},{22,23},{26,27},{30,31}} | collective-permute-start | bytes 4718600 | tf_op jit(solution)/shard_map/ppermute | solution.py:179
  86.2 1.3 collective-permute-start.11
  87.5 0.6 dynamic_slice.6
  90.1 0.6 select_reduce_fusion.block_ref
  90.7 0.0 collective-permute-done.8.refs_5_
  90.7 10.7 %shard_map.65.refs_2_ = bf16[8192,512]{1,0:T(8,128)(2,1)} custom-call(s32[128]{0:T(128)} %select_reduce_fusion.block_ref, bf16[8192,512]{1,0:T(8,128)(2,1)} %base_ref.3, bf16[3072,512]{1,0:T(8,128)(2,1)} %get-tuple-element.18.refs_0_, bf16[1024,512]{1,0:T(8,128)(2,1)} %get-tuple-element.17.refs_1_, bf16[3072,512]{1,0:T(8,128)(2,1)} %collective-permute-done.1.refs_2_, ...), custom_call_target="tpu_custom_call" | custom-call | flops 1 | bytes 1 | tf_op jit(solution)/shard_map/pallas_call | solution.py:239
  101.5 7.3 %collective-permute-done.refs_0_ = bf16[1024,512]{1,0:T(8,128)(2,1)} collective-permute-done((bf16[1024,512]{1,0:T(8,128)(2,1)}, bf16[1024,512]{1,0:T(8,128)(2,1)}, u32[]{:S(2)}, u32[]{:S(2)}) %collective-permute-start) | collective-permute-done | bytes 1048608 | tf_op jit(solution)/shard_map/ppermute | solution.py:189
  108.8 0.0 collective-permute-start.9
  108.8 2.9 %collective-permute-done.9.refs_1_ = bf16[1024,512]{1,0:T(8,128)(2,1)S(1)} collective-permute-done((bf16[1024,512]{1,0:T(8,128)(2,1)}, bf16[1024,512]{1,0:T(8,128)(2,1)S(1)}, u32[]{:S(2)}, u32[]{:S(2)}) %collective-permute-start.9) | collective-permute-done | bytes 1048608 | tf_op jit(solution)/shard_map/ppermute | solution.py:192
  111.7 1.0 copy-done.3
  112.6 4.9 %shard_map.66.weight_ref = bf16[8192,512]{1,0:T(8,128)(2,1)} custom-call(s32[128]{0:T(128)} %select_reduce_fusion.block_ref, bf16[8192,512]{1,0:T(8,128)(2,1)} %base_ref.3, bf16[1024,512]{1,0:T(8,128)(2,1)} %collective-permute-done.refs_0_, bf16[1024,512]{1,0:T(8,128)(2,1)} %copy-done.3, ...), custom_call_target="tpu_custom_call", output_to_operand_aliasing={{}: (4, {})} | custom-call | flops 1 | bytes 1 | tf_op jit(solution)/shard_map/pallas_call | solution.py:239
  117.6 6.4 %shard_map.67.refs_7_ = bf16[384,512]{1,0:T(8,128)(2,1)} custom-call(bf16[8192,512]{1,0:T(8,128)(2,1)} %shard_map.66.weight_ref, bf16[96,8192]{1,0:T(8,128)(2,1)} %refs_0_.3, bf16[96,8192]{1,0:T(8,128)(2,1)} %copy-done, bf16[96,8192]{1,0:T(8,128)(2,1)} %collective-permute-done.5.refs_2_, bf16[96,8192]{1,0:T(8,128)(2,1)} %copy-done.1, ...), custom_call_target="tpu_custom_call" | custom-call | flops 1 | bytes 1 | tf_op jit(solution)/shard_map/pallas_call | solution.py:274
  124.0 0.9 collective-permute-done.11.refs_6_
  124.9 5.1 %shard_map.68 = bf16[384,512]{1,0:T(8,128)(2,1)} custom-call(bf16[8192,512]{1,0:T(8,128)(2,1)} %shard_map.66.weight_ref, bf16[96,8192]{1,0:T(8,128)(2,1)} %refs_0_.3, bf16[96,8192]{1,0:T(8,128)(2,1)} %copy-done, bf16[96,8192]{1,0:T(8,128)(2,1)} %collective-permute-done.5.refs_2_, ...), custom_call_target="tpu_custom_call", output_to_operand_aliasing={{}: (8, {})} | custom-call | flops 1 | bytes 1 | tf_op jit(solution)/shard_map/pallas_call | solution.py:274
  (13 shorter events, 0.1 us)
Async XLA Ops:
  0.0 87.5 %copy-start.5 = (s32[4]{0:T(128)S(1)}, s32[4]{0:T(128)}, u32[]{:S(2)}) copy-start(s32[4]{0:T(128)} %param.10) | copy-start | bytes 52
  0.0 90.1 %copy-start.4 = (s32[2,64]{1,0:T(2,128)S(1)}, s32[2,64]{1,0:T(2,128)}, u32[]{:S(2)}) copy-start(s32[2,64]{1,0:T(2,128)} %param.11) | copy-start | bytes 1540
  0.0 39.0 %collective-permute-start.4 = (bf16[96,8192]{1,0:T(8,128)(2,1)}, bf16[96,8192]{1,0:T(8,128)(2,1)S(1)}, u32[]{:S(2)}, u32[]{:S(2)}) collective-permute-start(bf16[96,8192]{1,0:T(8,128)(2,1)} %refs_0_.3), channel_id=1, source_target_pairs={{0,1},{1,2},{2,3},{4,5},{5,6},{6,7},{8,9},{9,10},{10,11},{12,13},{... | collective-permute-start | bytes 4718600 | tf_op jit(solution)/shard_map/ppermute | solution.py:179
  5.2 38.0 %collective-permute-start.6 = (bf16[96,8192]{1,0:T(8,128)(2,1)}, bf16[96,8192]{1,0:T(8,128)(2,1)S(1)}, u32[]{:S(2)}, u32[]{:S(2)}) collective-permute-start(bf16[96,8192]{1,0:T(8,128)(2,1)} %refs_0_.3), channel_id=1, source_target_pairs={{1,0},{2,1},{3,2},{5,4},{6,5},{7,6},{9,8},{10,9},{11,10},{13,12},{... | collective-permute-start | bytes 4718600 | tf_op jit(solution)/shard_map/ppermute | solution.py:182
  13.0 69.9 %collective-permute-start.1 = (bf16[3072,512]{1,0:T(8,128)(2,1)}, bf16[3072,512]{1,0:T(8,128)(2,1)}, u32[]{:S(2)}, u32[]{:S(2)}) collective-permute-start(bf16[3072,512]{1,0:T(8,128)(2,1)} %get-tuple-element.18.refs_0_), channel_id=1, source_target_pairs={{0,8},{4,12},{8,0},{12,4},{1,9},{5,13},{9,1},{13,5},{2,10},{6,14},... | collective-permute-start | bytes 9437192 | tf_op jit(solution)/shard_map/ppermute | solution.py:189
  14.5 68.4 %collective-permute-start.2 = (bf16[3072,512]{1,0:T(8,128)(2,1)}, bf16[3072,512]{1,0:T(8,128)(2,1)}, u32[]{:S(2)}, u32[]{:S(2)}) collective-permute-start(bf16[3072,512]{1,0:T(8,128)(2,1)} %get-tuple-element.18.refs_0_), channel_id=1, source_target_pairs={{0,4},{4,0},{8,12},{12,8},{1,5},{5,1},{9,13},{13,9},{2,6},{6,2},{1... | collective-permute-start | bytes 9437192 | tf_op jit(solution)/shard_map/ppermute | solution.py:192
  39.0 62.4 %copy-start = (bf16[96,8192]{1,0:T(8,128)(2,1)}, bf16[96,8192]{1,0:T(8,128)(2,1)S(1)}, u32[]{:S(2)}) copy-start(bf16[96,8192]{1,0:T(8,128)(2,1)S(1)} %collective-permute-done.4.refs_1_) | copy-start | bytes 4718596
  39.0 8.3 %collective-permute-start.5 = (bf16[96,8192]{1,0:T(8,128)(2,1)S(1)}, bf16[96,8192]{1,0:T(8,128)(2,1)}, u32[]{:S(2)}, u32[]{:S(2)}) collective-permute-start(bf16[96,8192]{1,0:T(8,128)(2,1)S(1)} %collective-permute-done.4.refs_1_), channel_id=1, source_target_pairs={{1,2},{2,3},{5,6},{6,7},{9,10},{10,11},{13,14},{14,15},{17,18},{18... | collective-permute-start | bytes 4718600 | tf_op jit(solution)/shard_map/ppermute | solution.py:179
  43.1 58.3 %copy-start.1 = (bf16[96,8192]{1,0:T(8,128)(2,1)}, bf16[96,8192]{1,0:T(8,128)(2,1)S(1)}, u32[]{:S(2)}) copy-start(bf16[96,8192]{1,0:T(8,128)(2,1)S(1)} %collective-permute-done.6.refs_3_.refs_4_) | copy-start | bytes 4718596
  43.1 38.3 %collective-permute-start.7 = (bf16[96,8192]{1,0:T(8,128)(2,1)S(1)}, bf16[96,8192]{1,0:T(8,128)(2,1)}, u32[]{:S(2)}, u32[]{:S(2)}) collective-permute-start(bf16[96,8192]{1,0:T(8,128)(2,1)S(1)} %collective-permute-done.6.refs_3_.refs_4_), channel_id=1, source_target_pairs={{1,0},{2,1},{5,4},{6,5},{9,8},{10,9},{13,12},{14,13},{17,16},{18,1... | collective-permute-start | bytes 4718600 | tf_op jit(solution)/shard_map/ppermute | solution.py:182
  44.4 2.9 %collective-permute-start.3 = (bf16[1024,512]{1,0:T(8,128)(2,1)}, bf16[1024,512]{1,0:T(8,128)(2,1)S(1)}, u32[]{:S(2)}, u32[]{:S(2)}) collective-permute-start(bf16[1024,512]{1,0:T(8,128)(2,1)} %get-tuple-element.17.refs_1_), channel_id=1, source_target_pairs={{0,4},{4,0},{8,12},{12,8},{1,5},{5,1},{9,13},{13,9},{2,6},{6,2},{1... | collective-permute-start | bytes 3145736 | tf_op jit(solution)/shard_map/ppermute | solution.py:192
  47.4 34.0 %copy-start.2 = (bf16[1024,512]{1,0:T(8,128)(2,1)}, bf16[1024,512]{1,0:T(8,128)(2,1)S(1)}, u32[]{:S(2)}) copy-start(bf16[1024,512]{1,0:T(8,128)(2,1)S(1)} %collective-permute-done.3.refs_4_) | copy-start | bytes 3145732
  82.9 7.8 %collective-permute-start.8 = (bf16[3072,512]{1,0:T(8,128)(2,1)}, bf16[3072,512]{1,0:T(8,128)(2,1)}, u32[]{:S(2)}, u32[]{:S(2)}) collective-permute-start(bf16[3072,512]{1,0:T(8,128)(2,1)} %collective-permute-done.1.refs_2_), channel_id=1, source_target_pairs={{0,4},{4,0},{8,12},{12,8},{1,5},{5,1},{9,13},{13,9},{2,6},{6,2},{1... | collective-permute-start | bytes 9437192 | tf_op jit(solution)/shard_map/ppermute | solution.py:192
  82.9 25.9 %collective-permute-start = (bf16[1024,512]{1,0:T(8,128)(2,1)}, bf16[1024,512]{1,0:T(8,128)(2,1)}, u32[]{:S(2)}, u32[]{:S(2)}) collective-permute-start(bf16[1024,512]{1,0:T(8,128)(2,1)} %get-tuple-element.17.refs_1_), channel_id=1, source_target_pairs={{0,8},{4,12},{8,0},{12,4},{1,9},{5,13},{9,1},{13,5},{2,10},{6,14},... | collective-permute-start | bytes 3145736 | tf_op jit(solution)/shard_map/ppermute | solution.py:189
  84.4 39.6 %collective-permute-start.10 = (bf16[96,8192]{1,0:T(8,128)(2,1)}, bf16[96,8192]{1,0:T(8,128)(2,1)}, u32[]{:S(2)}, u32[]{:S(2)}) collective-permute-start(bf16[96,8192]{1,0:T(8,128)(2,1)} %collective-permute-done.5.refs_2_), channel_id=1, source_target_pairs={{2,3},{6,7},{10,11},{14,15},{18,19},{22,23},{26,27},{30,31}} | collective-permute-start | bytes 4718600 | tf_op jit(solution)/shard_map/ppermute | solution.py:179
  86.2 38.7 %collective-permute-start.11 = (bf16[96,8192]{1,0:T(8,128)(2,1)}, bf16[96,8192]{1,0:T(8,128)(2,1)}, u32[]{:S(2)}, u32[]{:S(2)}) collective-permute-start(bf16[96,8192]{1,0:T(8,128)(2,1)} %collective-permute-done.7.refs_4_.refs_5_), channel_id=1, source_target_pairs={{1,0},{5,4},{9,8},{13,12},{17,16},{21,20},{25,24},{29,28}} | collective-permute-start | bytes 4718600 | tf_op jit(solution)/shard_map/ppermute | solution.py:182
  108.8 2.9 %collective-permute-start.9 = (bf16[1024,512]{1,0:T(8,128)(2,1)}, bf16[1024,512]{1,0:T(8,128)(2,1)S(1)}, u32[]{:S(2)}, u32[]{:S(2)}) collective-permute-start(bf16[1024,512]{1,0:T(8,128)(2,1)} %collective-permute-done.refs_0_), channel_id=1, source_target_pairs={{0,4},{4,0},{8,12},{12,8},{1,5},{5,1},{9,13},{13,9},{2,6},{6,2},{1... | collective-permute-start | bytes 3145736 | tf_op jit(solution)/shard_map/ppermute | solution.py:192
  111.7 1.0 copy-start.3

commit v13 on v12

--- a/solution.py
+++ b/solution.py
@@ -84,7 +84,8 @@
     given = 2 * ranks - 1 if last else 2 * ranks - 3
     own, rights = refs[0], refs[1 : (given + 1) // 2]
     lefts = refs[(given + 1) // 2 : given]
-    out_ref, token_buf, weight_buf, total, sems = refs[-5:] if not last else refs[-6:-1]
+    out_ref, token_buf, total, sems = refs[-5:-1] if last else refs[-4:]
+    result = refs[-1]
     rows, depth = own.shape
     chunks = depth // span
     rank = lax.axis_index("tp")
@@ -99,10 +100,6 @@
     def slot_rows(hop):
         slot = 0 if last else hop - (star < hop).astype(jnp.int32)
         return pl.ds(pl.multiple_of(slot * rows, rows), rows)
-
-    def weight_copy(chunk):
-        at = columns(chunk)
-        return pltpu.make_async_copy(weight_ref.at[at, :], weight_buf.at[at, :], sems.at[chunk, ranks])
 
     def token_copy(chunk, hop, source):
         at = columns(chunk)
@@ -133,20 +130,17 @@
 
     @pl.loop(0, chunks)
     def _(chunk):
-        weight_copy(chunk).start()
         each(functools.partial(fetch, chunk))
 
     total[...] = jnp.zeros_like(total)
 
     @pl.loop(0, chunks)
     def _(chunk):
-        weight_copy(chunk).wait()
         each(lambda hop: token_copy(chunk, hop, own).wait())
         at = columns(chunk)
-        total[...] += jnp.dot(token_buf[:, at], weight_buf[at, :], preferred_element_type=jnp.float32)
+        total[...] += jnp.dot(token_buf[:, at], weight_ref[at, :], preferred_element_type=jnp.float32)
 
     if last:
-        result = refs[-1]
         result[...] = total[...].astype(result.dtype)
 
         def store(hop):
@@ -265,20 +259,18 @@
         last = prior is not None
         count = 1 if last else ranks - 1
         inputs = [weight] + arrays + ([prior] if last else [])
-        scratch = [
-            pltpu.VMEM((count * rows, depth), jnp.bfloat16),
-            pltpu.VMEM((depth, width), jnp.bfloat16),
-            pltpu.VMEM((count * rows, width), jnp.float32),
-            pltpu.SemaphoreType.DMA((chunks, ranks + 1)),
-        ]
+        need = 2 * (count * rows + width) * depth + 12 * count * rows * width + 6 * 1024 * 1024
+        buffers = [pltpu.VMEM((count * rows, depth), jnp.bfloat16)]
+        buffers += [pltpu.VMEM((count * rows, width), jnp.float32), pltpu.SemaphoreType.DMA((chunks, ranks + 1))]
+        buffers += [pltpu.VMEM((rows, width), jnp.bfloat16)] if last else []
         return pl.pallas_call(
             functools.partial(product_kernel, (ranks, CHUNK_BLOCKS * block, last)),
             out_shape=jax.ShapeDtypeStruct((ranks * rows, width), jnp.bfloat16),
-            in_specs=[HBM] * len(inputs),
+            in_specs=[VMEM] + [HBM] * (len(inputs) - 1),
             out_specs=HBM if last else VMEM,
-            scratch_shapes=scratch + ([pltpu.VMEM((rows, width), jnp.bfloat16)] if last else []),
+            scratch_shapes=buffers,
             input_output_aliases={len(inputs) - 1: 0} if last else {},
-            compiler_params=pltpu.CompilerParams(vmem_limit_bytes=VMEM_LIMIT),
+            compiler_params=pltpu.CompilerParams(vmem_limit_bytes=need),
             cost_estimate=BRIEF,
         )(*inputs)
 

time: 130 us -> 132 us (1.015); the launches traced: 130 us -> 131 us
  local copies, waits for them, and re-layouts: 2.94 us -> 5.36 us
    unnamed x12, local copies, waits for them, and re-layouts: 0.98 us -> 3.4 us
  transfers between devices with their start and end apart: 12 -> 12, of which waited for: 8 -> 7; matrix products, arithmetic and copies ran while one was open for 2% -> 2% of each run, Pallas kernels for 21% -> 21%
where the time goes in v13:
time: 132 us; the launch traced here: 131 us
  waiting for transfers between devices  75.5 us (57%)
  Pallas kernels  31.4 us (24%)
  starting transfers between devices  15.7 us (12%)
  local copies, waits for them, and re-layouts  5.36 us (4%)
  between operations  2.12 us (2%)
    ppermute x3, waiting for transfers between devices, left(): lax.ppermute(value, 'tp', [(i, i - 1) for i in range(1, ranks - hop + 1)])  36.5 us
    ppermute x3, waiting for transfers between devices, right(): lax.ppermute(value, 'tp', [(i, i + 1) for i in range(hop - 1, ranks - 1)])  24.5 us
    pallas_call x2, Pallas kernels, merge(): pl.pallas_call(functools.partial(merge_kernel, block, tuple(parts)), out_...  15.6 us
    pallas_call x2, Pallas kernels, product(): pl.pallas_call(functools.partial(product_kernel, (ranks, CHUNK_BLOCKS * b...  10.6 us
    ppermute x3, starting transfers between devices, right(): lax.ppermute(value, 'tp', [(i, i + 1) for i in range(hop - 1, ranks - 1)])  8.78 us
    ppermute x2, waiting for transfers between devices, across(): return lax.ppermute(store, 'rep', ring)  8.61 us
    ppermute x4, waiting for transfers between devices, turn(): return lax.ppermute(store, 'rep', swap)  5.86 us
    pallas_call x1, Pallas kernels, local(): pl.pallas_call(functools.partial(scale_kernel, block), out_shape=[jax.Sha...  5.16 us
  transfers between devices with their start and end apart: 12, of which 7 were waited for; matrix products, arithmetic and copies ran while one was open for 2% of the time, Pallas kernels for 21%

profile of v13, /device:TPU:0, one launch (start us, length us, event | category | flops | bytes accessed | tf_op | source)
XLA Modules:
  0.0 130.7 jit_solution(8217701931978349841)
XLA Ops:
  0.0 5.1 %collective-permute-start.4 = (bf16[96,8192]{1,0:T(8,128)(2,1)}, bf16[96,8192]{1,0:T(8,128)(2,1)S(1)}, u32[]{:S(2)}, u32[]{:S(2)}) collective-permute-start(bf16[96,8192]{1,0:T(8,128)(2,1)} %refs_0_.3), channel_id=1, source_target_pairs={{0,1},{1,2},{2,3},{4,5},{5,6},{6,7},{8,9},{9,10},{10,11},{12,13},{... | collective-permute-start | bytes 4718600 | tf_op jit(solution)/shard_map/ppermute | solution.py:173
  5.2 1.3 collective-permute-start.6
  6.5 1.4 %copy.11.scale_ref = f32[32,4]{1,0:T(8,128)} copy(bf16[32,4]{0,1:T(4,128)(2,1)} %param.9) | data formatting | bytes 768 | tf_op jit(solution)/shard_map/convert_element_type | solution.py:206
  7.8 5.2 %shard_map.64 = (bf16[3072,512]{1,0:T(8,128)(2,1)}, bf16[1024,512]{1,0:T(8,128)(2,1)}) custom-call(f32[32,4]{1,0:T(8,128)} %copy.11.scale_ref, bf16[4096,512]{1,0:T(8,128)(2,1)} %codes_ref.1), custom_call_target="tpu_custom_call" | custom-call | flops 1 | bytes 1 | tf_op jit(solution)/shard_map/pallas_call | solution.py:196
  13.0 1.5 %collective-permute-start.1 = (bf16[3072,512]{1,0:T(8,128)(2,1)}, bf16[3072,512]{1,0:T(8,128)(2,1)}, u32[]{:S(2)}, u32[]{:S(2)}) collective-permute-start(bf16[3072,512]{1,0:T(8,128)(2,1)} %get-tuple-element.18.refs_0_), channel_id=1, source_target_pairs={{0,8},{4,12},{8,0},{12,4},{1,9},{5,13},{9,1},{13,5},{2,10},{6,14},... | collective-permute-start | bytes 9437192 | tf_op jit(solution)/shard_map/ppermute | solution.py:183
  14.5 0.0 collective-permute-start.2
  14.5 24.5 %collective-permute-done.4.refs_1_ = bf16[96,8192]{1,0:T(8,128)(2,1)S(1)} collective-permute-done((bf16[96,8192]{1,0:T(8,128)(2,1)}, bf16[96,8192]{1,0:T(8,128)(2,1)S(1)}, u32[]{:S(2)}, u32[]{:S(2)}) %collective-permute-start.4) | collective-permute-done | bytes 1572896 | tf_op jit(solution)/shard_map/ppermute | solution.py:173
  39.0 1.8 %collective-permute-start.5 = (bf16[96,8192]{1,0:T(8,128)(2,1)S(1)}, bf16[96,8192]{1,0:T(8,128)(2,1)}, u32[]{:S(2)}, u32[]{:S(2)}) collective-permute-start(bf16[96,8192]{1,0:T(8,128)(2,1)S(1)} %collective-permute-done.4.refs_1_), channel_id=1, source_target_pairs={{1,2},{2,3},{5,6},{6,7},{9,10},{10,11},{13,14},{14,15},{17,18},{18... | collective-permute-start | bytes 4718600 | tf_op jit(solution)/shard_map/ppermute | solution.py:173
  40.8 2.4 %collective-permute-done.6.refs_3_.refs_4_ = bf16[96,8192]{1,0:T(8,128)(2,1)} collective-permute-done((bf16[96,8192]{1,0:T(8,128)(2,1)}, bf16[96,8192]{1,0:T(8,128)(2,1)}, u32[]{:S(2)}, u32[]{:S(2)}) %collective-permute-start.6) | collective-permute-done | bytes 1572896 | tf_op jit(solution)/shard_map/ppermute | solution.py:176
  43.2 1.3 collective-permute-start.7
  44.5 0.1 collective-permute-start.3
  44.6 2.9 %collective-permute-done.3.refs_4_ = bf16[1024,512]{1,0:T(8,128)(2,1)S(1)} collective-permute-done((bf16[1024,512]{1,0:T(8,128)(2,1)}, bf16[1024,512]{1,0:T(8,128)(2,1)S(1)}, u32[]{:S(2)}, u32[]{:S(2)}) %collective-permute-start.3) | collective-permute-done | bytes 1048608 | tf_op jit(solution)/shard_map/ppermute | solution.py:186
  47.5 34.1 %collective-permute-done.7.refs_4_.refs_5_ = bf16[96,8192]{1,0:T(8,128)(2,1)} collective-permute-done((bf16[96,8192]{1,0:T(8,128)(2,1)}, bf16[96,8192]{1,0:T(8,128)(2,1)}, u32[]{:S(2)}, u32[]{:S(2)}) %collective-permute-start.7) | collective-permute-done | bytes 1572896 | tf_op jit(solution)/shard_map/ppermute | solution.py:176
  81.6 1.3 collective-permute-done.1.refs_2_
  82.9 0.0 collective-permute-done.2.refs_3_
  82.9 0.0 collective-permute-start.8
  82.9 1.5 %collective-permute-start = (bf16[1024,512]{1,0:T(8,128)(2,1)}, bf16[1024,512]{1,0:T(8,128)(2,1)}, u32[]{:S(2)}, u32[]{:S(2)}) collective-permute-start(bf16[1024,512]{1,0:T(8,128)(2,1)} %get-tuple-element.17.refs_1_), channel_id=1, source_target_pairs={{0,8},{4,12},{8,0},{12,4},{1,9},{5,13},{9,1},{13,5},{2,10},{6,14},... | collective-permute-start | bytes 3145736 | tf_op jit(solution)/shard_map/ppermute | solution.py:183
  84.4 1.8 %collective-permute-start.10 = (bf16[96,8192]{1,0:T(8,128)(2,1)}, bf16[96,8192]{1,0:T(8,128)(2,1)}, u32[]{:S(2)}, u32[]{:S(2)}) collective-permute-start(bf16[96,8192]{1,0:T(8,128)(2,1)} %collective-permute-done.5.refs_2_), channel_id=1, source_target_pairs={{2,3},{6,7},{10,11},{14,15},{18,19},{22,23},{26,27},{30,31}} | collective-permute-start | bytes 4718600 | tf_op jit(solution)/shard_map/ppermute | solution.py:173
  86.2 1.3 collective-permute-start.11
  87.5 0.6 dynamic_slice.6
  90.1 0.6 select_reduce_fusion.block_ref
  90.7 0.0 collective-permute-done.8.refs_5_
  90.7 10.7 %shard_map.65.refs_2_ = bf16[8192,512]{1,0:T(8,128)(2,1)} custom-call(s32[128]{0:T(128)} %select_reduce_fusion.block_ref, bf16[8192,512]{1,0:T(8,128)(2,1)} %base_ref.3, bf16[3072,512]{1,0:T(8,128)(2,1)} %get-tuple-element.18.refs_0_, bf16[1024,512]{1,0:T(8,128)(2,1)} %get-tuple-element.17.refs_1_, bf16[3072,512]{1,0:T(8,128)(2,1)} %collective-permute-done.1.refs_2_, ...), custom_call_target="tpu_custom_call" | custom-call | flops 1 | bytes 1 | tf_op jit(solution)/shard_map/pallas_call | solution.py:233
  101.4 0.0 copy-start.2
  101.4 7.3 %collective-permute-done.refs_0_ = bf16[1024,512]{1,0:T(8,128)(2,1)} collective-permute-done((bf16[1024,512]{1,0:T(8,128)(2,1)}, bf16[1024,512]{1,0:T(8,128)(2,1)}, u32[]{:S(2)}, u32[]{:S(2)}) %collective-permute-start) | collective-permute-done | bytes 1048608 | tf_op jit(solution)/shard_map/ppermute | solution.py:183
  108.8 0.0 collective-permute-start.9
  108.8 3.0 %collective-permute-done.9.refs_1_ = bf16[1024,512]{1,0:T(8,128)(2,1)} collective-permute-done((bf16[1024,512]{1,0:T(8,128)(2,1)}, bf16[1024,512]{1,0:T(8,128)(2,1)}, u32[]{:S(2)}, u32[]{:S(2)}) %collective-permute-start.9) | collective-permute-done | bytes 1048608 | tf_op jit(solution)/shard_map/ppermute | solution.py:186
  111.8 4.9 %shard_map.66.weight_ref = bf16[8192,512]{1,0:T(8,128)(2,1)} custom-call(s32[128]{0:T(128)} %select_reduce_fusion.block_ref, bf16[8192,512]{1,0:T(8,128)(2,1)} %base_ref.3, bf16[1024,512]{1,0:T(8,128)(2,1)} %collective-permute-done.refs_0_, bf16[1024,512]{1,0:T(8,128)(2,1)} %collective-permute-done.9.refs_1_, ...), custom_call_target="tpu_custom_call", output_to_operand_aliasing={{}: (4, {})} | custom-call | flops 1 | bytes 1 | tf_op jit(solution)/shard_map/pallas_call | solution.py:233
  116.7 3.4 %copy-done = bf16[8192,512]{1,0:T(8,128)(2,1)S(1)} copy-done((bf16[8192,512]{1,0:T(8,128)(2,1)S(1)}, bf16[8192,512]{1,0:T(8,128)(2,1)}, u32[]{:S(2)}) %copy-start) | copy-done | bytes 8388632
  120.1 6.2 %shard_map.67.refs_7_ = bf16[384,512]{1,0:T(8,128)(2,1)} custom-call(bf16[8192,512]{1,0:T(8,128)(2,1)S(1)} %copy-done, bf16[96,8192]{1,0:T(8,128)(2,1)S(1)} %copy-done.2, bf16[96,8192]{1,0:T(8,128)(2,1)S(1)} %collective-permute-done.4.refs_1_, bf16[96,8192]{1,0:T(8,128)(2,1)} %collective-permute-done.5.refs_2_, ...), custom_call_target="tpu_custom_call" | custom-call | flops 1 | bytes 1 | tf_op jit(solution)/shard_map/pallas_call | solution.py:266
  126.3 0.0 collective-permute-done.10.refs_3_
  126.3 4.4 %shard_map.68 = bf16[384,512]{1,0:T(8,128)(2,1)} custom-call(bf16[8192,512]{1,0:T(8,128)(2,1)S(1)} %copy-done.1, bf16[96,8192]{1,0:T(8,128)(2,1)S(1)} %copy-done.2, bf16[96,8192]{1,0:T(8,128)(2,1)S(1)} %collective-permute-done.4.refs_1_, bf16[96,8192]{1,0:T(8,128)(2,1)} %collective-permute-done.5.refs_2_, ...), custom_call_target="tpu_custom_call", output_to_operand_aliasing={{}: (8, {})} | custom-call | flops 1 | bytes 1 | tf_op jit(solution)/shard_map/pallas_call | solution.py:266
  (13 shorter events, 0.1 us)
Async XLA Ops:
  0.0 87.5 %copy-start.5 = (s32[4]{0:T(128)S(1)}, s32[4]{0:T(128)}, u32[]{:S(2)}) copy-start(s32[4]{0:T(128)} %param.10) | copy-start | bytes 52
  0.0 90.1 %copy-start.4 = (s32[2,64]{1,0:T(2,128)S(1)}, s32[2,64]{1,0:T(2,128)}, u32[]{:S(2)}) copy-start(s32[2,64]{1,0:T(2,128)} %param.11) | copy-start | bytes 1540
  0.0 39.0 %collective-permute-start.4 = (bf16[96,8192]{1,0:T(8,128)(2,1)}, bf16[96,8192]{1,0:T(8,128)(2,1)S(1)}, u32[]{:S(2)}, u32[]{:S(2)}) collective-permute-start(bf16[96,8192]{1,0:T(8,128)(2,1)} %refs_0_.3), channel_id=1, source_target_pairs={{0,1},{1,2},{2,3},{4,5},{5,6},{6,7},{8,9},{9,10},{10,11},{12,13},{... | collective-permute-start | bytes 4718600 | tf_op jit(solution)/shard_map/ppermute | solution.py:173
  5.2 38.1 %collective-permute-start.6 = (bf16[96,8192]{1,0:T(8,128)(2,1)}, bf16[96,8192]{1,0:T(8,128)(2,1)}, u32[]{:S(2)}, u32[]{:S(2)}) collective-permute-start(bf16[96,8192]{1,0:T(8,128)(2,1)} %refs_0_.3), channel_id=1, source_target_pairs={{1,0},{2,1},{3,2},{5,4},{6,5},{7,6},{9,8},{10,9},{11,10},{13,12},{... | collective-permute-start | bytes 4718600 | tf_op jit(solution)/shard_map/ppermute | solution.py:176
  13.0 69.9 %collective-permute-start.1 = (bf16[3072,512]{1,0:T(8,128)(2,1)}, bf16[3072,512]{1,0:T(8,128)(2,1)}, u32[]{:S(2)}, u32[]{:S(2)}) collective-permute-start(bf16[3072,512]{1,0:T(8,128)(2,1)} %get-tuple-element.18.refs_0_), channel_id=1, source_target_pairs={{0,8},{4,12},{8,0},{12,4},{1,9},{5,13},{9,1},{13,5},{2,10},{6,14},... | collective-permute-start | bytes 9437192 | tf_op jit(solution)/shard_map/ppermute | solution.py:183
  14.5 68.4 %collective-permute-start.2 = (bf16[3072,512]{1,0:T(8,128)(2,1)}, bf16[3072,512]{1,0:T(8,128)(2,1)}, u32[]{:S(2)}, u32[]{:S(2)}) collective-permute-start(bf16[3072,512]{1,0:T(8,128)(2,1)} %get-tuple-element.18.refs_0_), channel_id=1, source_target_pairs={{0,4},{4,0},{8,12},{12,8},{1,5},{5,1},{9,13},{13,9},{2,6},{6,2},{1... | collective-permute-start | bytes 9437192 | tf_op jit(solution)/shard_map/ppermute | solution.py:186
  39.0 8.4 %collective-permute-start.5 = (bf16[96,8192]{1,0:T(8,128)(2,1)S(1)}, bf16[96,8192]{1,0:T(8,128)(2,1)}, u32[]{:S(2)}, u32[]{:S(2)}) collective-permute-start(bf16[96,8192]{1,0:T(8,128)(2,1)S(1)} %collective-permute-done.4.refs_1_), channel_id=1, source_target_pairs={{1,2},{2,3},{5,6},{6,7},{9,10},{10,11},{13,14},{14,15},{17,18},{18... | collective-permute-start | bytes 4718600 | tf_op jit(solution)/shard_map/ppermute | solution.py:173
  43.2 38.4 %collective-permute-start.7 = (bf16[96,8192]{1,0:T(8,128)(2,1)}, bf16[96,8192]{1,0:T(8,128)(2,1)}, u32[]{:S(2)}, u32[]{:S(2)}) collective-permute-start(bf16[96,8192]{1,0:T(8,128)(2,1)} %collective-permute-done.6.refs_3_.refs_4_), channel_id=1, source_target_pairs={{1,0},{2,1},{5,4},{6,5},{9,8},{10,9},{13,12},{14,13},{17,16},{18,1... | collective-permute-start | bytes 4718600 | tf_op jit(solution)/shard_map/ppermute | solution.py:176
  44.5 2.9 %collective-permute-start.3 = (bf16[1024,512]{1,0:T(8,128)(2,1)}, bf16[1024,512]{1,0:T(8,128)(2,1)S(1)}, u32[]{:S(2)}, u32[]{:S(2)}) collective-permute-start(bf16[1024,512]{1,0:T(8,128)(2,1)} %get-tuple-element.17.refs_1_), channel_id=1, source_target_pairs={{0,4},{4,0},{8,12},{12,8},{1,5},{5,1},{9,13},{13,9},{2,6},{6,2},{1... | collective-permute-start | bytes 3145736 | tf_op jit(solution)/shard_map/ppermute | solution.py:186
  47.5 43.3 %copy-start.3 = (bf16[1024,512]{1,0:T(8,128)(2,1)}, bf16[1024,512]{1,0:T(8,128)(2,1)S(1)}, u32[]{:S(2)}) copy-start(bf16[1024,512]{1,0:T(8,128)(2,1)S(1)} %collective-permute-done.3.refs_4_) | copy-start | bytes 3145732
  82.9 7.8 %collective-permute-start.8 = (bf16[3072,512]{1,0:T(8,128)(2,1)}, bf16[3072,512]{1,0:T(8,128)(2,1)}, u32[]{:S(2)}, u32[]{:S(2)}) collective-permute-start(bf16[3072,512]{1,0:T(8,128)(2,1)} %collective-permute-done.1.refs_2_), channel_id=1, source_target_pairs={{0,4},{4,0},{8,12},{12,8},{1,5},{5,1},{9,13},{13,9},{2,6},{6,2},{1... | collective-permute-start | bytes 9437192 | tf_op jit(solution)/shard_map/ppermute | solution.py:186
  82.9 25.9 %collective-permute-start = (bf16[1024,512]{1,0:T(8,128)(2,1)}, bf16[1024,512]{1,0:T(8,128)(2,1)}, u32[]{:S(2)}, u32[]{:S(2)}) collective-permute-start(bf16[1024,512]{1,0:T(8,128)(2,1)} %get-tuple-element.17.refs_1_), channel_id=1, source_target_pairs={{0,8},{4,12},{8,0},{12,4},{1,9},{5,13},{9,1},{13,5},{2,10},{6,14},... | collective-permute-start | bytes 3145736 | tf_op jit(solution)/shard_map/ppermute | solution.py:183
  84.4 41.9 %collective-permute-start.10 = (bf16[96,8192]{1,0:T(8,128)(2,1)}, bf16[96,8192]{1,0:T(8,128)(2,1)}, u32[]{:S(2)}, u32[]{:S(2)}) collective-permute-start(bf16[96,8192]{1,0:T(8,128)(2,1)} %collective-permute-done.5.refs_2_), channel_id=1, source_target_pairs={{2,3},{6,7},{10,11},{14,15},{18,19},{22,23},{26,27},{30,31}} | collective-permute-start | bytes 4718600 | tf_op jit(solution)/shard_map/ppermute | solution.py:173
  86.2 40.1 %collective-permute-start.11 = (bf16[96,8192]{1,0:T(8,128)(2,1)}, bf16[96,8192]{1,0:T(8,128)(2,1)}, u32[]{:S(2)}, u32[]{:S(2)}) collective-permute-start(bf16[96,8192]{1,0:T(8,128)(2,1)} %collective-permute-done.7.refs_4_.refs_5_), channel_id=1, source_target_pairs={{1,0},{5,4},{9,8},{13,12},{17,16},{21,20},{25,24},{29,28}} | collective-permute-start | bytes 4718600 | tf_op jit(solution)/shard_map/ppermute | solution.py:176
  101.4 15.3 %copy-start.2 = (bf16[96,8192]{1,0:T(8,128)(2,1)S(1)}, bf16[96,8192]{1,0:T(8,128)(2,1)}, u32[]{:S(2)}) copy-start(bf16[96,8192]{1,0:T(8,128)(2,1)} %refs_0_.3) | copy-start | bytes 4718596
  108.8 3.0 %collective-permute-start.9 = (bf16[1024,512]{1,0:T(8,128)(2,1)}, bf16[1024,512]{1,0:T(8,128)(2,1)}, u32[]{:S(2)}, u32[]{:S(2)}) collective-permute-start(bf16[1024,512]{1,0:T(8,128)(2,1)} %collective-permute-done.refs_0_), channel_id=1, source_target_pairs={{0,4},{4,0},{8,12},{12,8},{1,5},{5,1},{9,13},{13,9},{2,6},{6,2},{1... | collective-permute-start | bytes 3145736 | tf_op jit(solution)/shard_map/ppermute | solution.py:186
  116.7 3.4 %copy-start = (bf16[8192,512]{1,0:T(8,128)(2,1)S(1)}, bf16[8192,512]{1,0:T(8,128)(2,1)}, u32[]{:S(2)}) copy-start(bf16[8192,512]{1,0:T(8,128)(2,1)} %shard_map.66.weight_ref) | copy-start | bytes 25165828
  120.1 6.2 %copy-start.1 = (bf16[8192,512]{1,0:T(8,128)(2,1)S(1)}, bf16[8192,512]{1,0:T(8,128)(2,1)}, u32[]{:S(2)}) copy-start(bf16[8192,512]{1,0:T(8,128)(2,1)} %shard_map.66.weight_ref) | copy-start | bytes 25165828

commit v14 on v12

--- a/solution.py
+++ b/solution.py
@@ -18,21 +18,19 @@
 
 
 def scale_kernel(block, scale_ref, codes_ref, *out_refs):
-    col_blocks = scale_ref.shape[1]
+    scales = scale_ref[...].astype(jnp.float32)
+    col_blocks = scales.shape[0]
     wide = codes_ref.shape[1] // col_blocks
     first = 0
     for out_ref in out_refs:
         count = out_ref.shape[0] // block
-
-        @pl.loop(0, count)
-        def _(index):
-            source = pl.ds(pl.multiple_of((first + index) * block, block), block)
-            target = pl.ds(pl.multiple_of(index * block, block), block)
+        for index in range(count):
+            slot = first + index
             for col in range(col_blocks):
                 at = pl.ds(col * wide, wide)
-                delta = codes_ref[source, at].astype(jnp.float32) * scale_ref[first + index, col]
-                out_ref[target, at] = delta.astype(jnp.bfloat16)
-
+                delta = codes_ref[pl.ds(slot * block, block), at].astype(jnp.float32)
+                delta = delta * scales[col : col + 1, slot : slot + 1]
+                out_ref[pl.ds(index * block, block), at] = delta.astype(jnp.bfloat16)
         first += count
 
 
@@ -205,11 +203,11 @@
             jax.ShapeDtypeStruct(((high - low) * block, width), jnp.bfloat16)
             for low, high in zip(cuts[:-1], cuts[1:])
         ],
-        in_specs=[SMEM, VMEM],
+        in_specs=[VMEM, VMEM],
         out_specs=[VMEM] * pieces,
         compiler_params=pltpu.CompilerParams(vmem_limit_bytes=VMEM_LIMIT),
         cost_estimate=BRIEF,
-    )(delta_scales.astype(jnp.float32), delta_codes)
+    )(delta_scales.T, delta_codes)
     held, twins = [deltas], [[turn(delta) for delta in deltas]]
     sent = [across(delta) for delta in deltas]
     turns = [(ranks - 2) * hop // (chips - 1) for hop in range(1, chips)]

time: 130 us -> 129 us (level)
  local copies, waits for them, and re-layouts: 2.94 us -> 1.57 us
    ppermute x2, waiting for transfers between devices: 8.82 us -> 6.53 us  [across(): return lax.ppermute(store, 'rep', ring)]
    ppermute x3, waiting for transfers between devices: 24.5 us -> 26.1 us  [right(): lax.ppermute(value, 'tp', [(i, i + 1) for i in range(hop - 1, ranks - 1)])]
    convert_element_type x1 -> x0, local copies, waits for them, and re-layouts: 1.37 us -> none  [local(): delta_scales.astype(jnp.float32)]
  transfers between devices with their start and end apart: 12 -> 12, of which waited for: 8 -> 7; matrix products, arithmetic and copies ran while one was open for 2% -> 1% of each run, Pallas kernels for 21% -> 21%
where the time goes in v14:
time: 129 us
  waiting for transfers between devices  76 us (59%)
  Pallas kernels  32.4 us (25%)
  starting transfers between devices  15.8 us (12%)
  between operations  2.1 us (2%)
  local copies, waits for them, and re-layouts  1.57 us (1%)
    ppermute x3, waiting for transfers between devices, left(): lax.ppermute(value, 'tp', [(i, i - 1) for i in range(1, ranks - hop + 1)])  37.6 us
    ppermute x3, waiting for transfers between devices, right(): lax.ppermute(value, 'tp', [(i, i + 1) for i in range(hop - 1, ranks - 1)])  26.1 us
    pallas_call x2, Pallas kernels, merge(): pl.pallas_call(functools.partial(merge_kernel, block, tuple(parts)), out_...  16 us
    pallas_call x2, Pallas kernels, product(): pl.pallas_call(functools.partial(product_kernel, (ranks, CHUNK_BLOCKS * b...  11.5 us
    ppermute x3, starting transfers between devices, right(): lax.ppermute(value, 'tp', [(i, i + 1) for i in range(hop - 1, ranks - 1)])  8.78 us
    ppermute x2, waiting for transfers between devices, across(): return lax.ppermute(store, 'rep', ring)  6.53 us
    ppermute x4, waiting for transfers between devices, turn(): return lax.ppermute(store, 'rep', swap)  5.73 us
    pallas_call x1, Pallas kernels, local(): pl.pallas_call(functools.partial(scale_kernel, block), out_shape=[jax.Sha...  4.92 us
  transfers between devices with their start and end apart: 12, of which 7 were waited for; matrix products, arithmetic and copies ran while one was open for 1% of the time, Pallas kernels for 21%

profile of v14, /device:TPU:0, one launch (start us, length us, event | category | flops | bytes accessed | tf_op | source)
XLA Modules:
  0.0 128.6 jit_solution(6182742739212717929)
XLA Ops:
  0.0 5.1 %collective-permute-start.4 = (bf16[96,8192]{1,0:T(8,128)(2,1)}, bf16[96,8192]{1,0:T(8,128)(2,1)S(1)}, u32[]{:S(2)}, u32[]{:S(2)}) collective-permute-start(bf16[96,8192]{1,0:T(8,128)(2,1)} %refs_0_.3), channel_id=1, source_target_pairs={{0,1},{1,2},{2,3},{4,5},{5,6},{6,7},{8,9},{9,10},{10,11},{12,13},{... | collective-permute-start | bytes 4718600 | tf_op jit(solution)/shard_map/ppermute | solution.py:177
  5.2 1.3 %collective-permute-start.6 = (bf16[96,8192]{1,0:T(8,128)(2,1)}, bf16[96,8192]{1,0:T(8,128)(2,1)S(1)}, u32[]{:S(2)}, u32[]{:S(2)}) collective-permute-start(bf16[96,8192]{1,0:T(8,128)(2,1)} %refs_0_.3), channel_id=1, source_target_pairs={{1,0},{2,1},{3,2},{5,4},{6,5},{7,6},{9,8},{10,9},{11,10},{13,12},{... | collective-permute-start | bytes 4718600 | tf_op jit(solution)/shard_map/ppermute | solution.py:180
  6.5 4.9 %shard_map.64 = (bf16[3072,512]{1,0:T(8,128)(2,1)}, bf16[1024,512]{1,0:T(8,128)(2,1)}) custom-call(bf16[4,32]{1,0:T(4,128)(2,1)} %bitcast.4, bf16[4096,512]{1,0:T(8,128)(2,1)} %codes_ref.1), custom_call_target="tpu_custom_call" | custom-call | flops 1 | bytes 1 | tf_op jit(solution)/shard_map/pallas_call | solution.py:200
  11.4 1.5 %collective-permute-start.1 = (bf16[3072,512]{1,0:T(8,128)(2,1)}, bf16[3072,512]{1,0:T(8,128)(2,1)}, u32[]{:S(2)}, u32[]{:S(2)}) collective-permute-start(bf16[3072,512]{1,0:T(8,128)(2,1)} %get-tuple-element.18.refs_0_), channel_id=1, source_target_pairs={{0,8},{4,12},{8,0},{12,4},{1,9},{5,13},{9,1},{13,5},{2,10},{6,14},... | collective-permute-start | bytes 9437192 | tf_op jit(solution)/shard_map/ppermute | solution.py:187
  12.9 0.0 collective-permute-start.2
  12.9 26.1 %collective-permute-done.4.refs_1_ = bf16[96,8192]{1,0:T(8,128)(2,1)S(1)} collective-permute-done((bf16[96,8192]{1,0:T(8,128)(2,1)}, bf16[96,8192]{1,0:T(8,128)(2,1)S(1)}, u32[]{:S(2)}, u32[]{:S(2)}) %collective-permute-start.4) | collective-permute-done | bytes 1572896 | tf_op jit(solution)/shard_map/ppermute | solution.py:177
  39.0 1.8 %collective-permute-start.5 = (bf16[96,8192]{1,0:T(8,128)(2,1)S(1)}, bf16[96,8192]{1,0:T(8,128)(2,1)}, u32[]{:S(2)}, u32[]{:S(2)}) collective-permute-start(bf16[96,8192]{1,0:T(8,128)(2,1)S(1)} %collective-permute-done.4.refs_1_), channel_id=1, source_target_pairs={{1,2},{2,3},{5,6},{6,7},{9,10},{10,11},{13,14},{14,15},{17,18},{18... | collective-permute-start | bytes 4718600 | tf_op jit(solution)/shard_map/ppermute | solution.py:177
  40.8 2.3 %collective-permute-done.6.refs_3_.refs_4_ = bf16[96,8192]{1,0:T(8,128)(2,1)S(1)} collective-permute-done((bf16[96,8192]{1,0:T(8,128)(2,1)}, bf16[96,8192]{1,0:T(8,128)(2,1)S(1)}, u32[]{:S(2)}, u32[]{:S(2)}) %collective-permute-start.6) | collective-permute-done | bytes 1572896 | tf_op jit(solution)/shard_map/ppermute | solution.py:180
  43.1 1.3 collective-permute-start.7
  44.4 0.1 collective-permute-start.3
  44.5 2.9 %collective-permute-done.3.refs_4_ = bf16[1024,512]{1,0:T(8,128)(2,1)S(1)} collective-permute-done((bf16[1024,512]{1,0:T(8,128)(2,1)}, bf16[1024,512]{1,0:T(8,128)(2,1)S(1)}, u32[]{:S(2)}, u32[]{:S(2)}) %collective-permute-start.3) | collective-permute-done | bytes 1048608 | tf_op jit(solution)/shard_map/ppermute | solution.py:190
  47.4 0.0 collective-permute-done.5.refs_2_
  47.4 34.0 %collective-permute-done.7.refs_4_.refs_5_ = bf16[96,8192]{1,0:T(8,128)(2,1)} collective-permute-done((bf16[96,8192]{1,0:T(8,128)(2,1)S(1)}, bf16[96,8192]{1,0:T(8,128)(2,1)}, u32[]{:S(2)}, u32[]{:S(2)}) %collective-permute-start.7) | collective-permute-done | bytes 1572896 | tf_op jit(solution)/shard_map/ppermute | solution.py:180
  81.4 0.0 collective-permute-done.1.refs_2_
  81.4 0.0 collective-permute-done.2.refs_3_
  81.4 0.1 collective-permute-start.8
  81.5 1.6 %collective-permute-start = (bf16[1024,512]{1,0:T(8,128)(2,1)}, bf16[1024,512]{1,0:T(8,128)(2,1)}, u32[]{:S(2)}, u32[]{:S(2)}) collective-permute-start(bf16[1024,512]{1,0:T(8,128)(2,1)} %get-tuple-element.17.refs_1_), channel_id=1, source_target_pairs={{0,8},{4,12},{8,0},{12,4},{1,9},{5,13},{9,1},{13,5},{2,10},{6,14},... | collective-permute-start | bytes 3145736 | tf_op jit(solution)/shard_map/ppermute | solution.py:187
  83.0 1.8 %collective-permute-start.10 = (bf16[96,8192]{1,0:T(8,128)(2,1)}, bf16[96,8192]{1,0:T(8,128)(2,1)}, u32[]{:S(2)}, u32[]{:S(2)}) collective-permute-start(bf16[96,8192]{1,0:T(8,128)(2,1)} %collective-permute-done.5.refs_2_), channel_id=1, source_target_pairs={{2,3},{6,7},{10,11},{14,15},{18,19},{22,23},{26,27},{30,31}} | collective-permute-start | bytes 4718600 | tf_op jit(solution)/shard_map/ppermute | solution.py:177
  84.8 1.3 collective-permute-start.11
  86.1 0.6 dynamic_slice.6
  88.7 0.6 select_reduce_fusion.block_ref
  89.4 0.0 collective-permute-done.8.refs_5_
  89.4 11.5 %shard_map.65.refs_2_ = bf16[8192,512]{1,0:T(8,128)(2,1)} custom-call(s32[128]{0:T(128)} %select_reduce_fusion.block_ref, bf16[8192,512]{1,0:T(8,128)(2,1)} %base_ref.3, bf16[3072,512]{1,0:T(8,128)(2,1)} %get-tuple-element.18.refs_0_, bf16[1024,512]{1,0:T(8,128)(2,1)} %get-tuple-element.17.refs_1_, bf16[3072,512]{1,0:T(8,128)(2,1)} %collective-permute-done.1.refs_2_, ...), custom_call_target="tpu_custom_call" | custom-call | flops 1 | bytes 1 | tf_op jit(solution)/shard_map/pallas_call | solution.py:237
  100.8 6.5 %collective-permute-done.refs_0_ = bf16[1024,512]{1,0:T(8,128)(2,1)} collective-permute-done((bf16[1024,512]{1,0:T(8,128)(2,1)}, bf16[1024,512]{1,0:T(8,128)(2,1)}, u32[]{:S(2)}, u32[]{:S(2)}) %collective-permute-start) | collective-permute-done | bytes 1048608 | tf_op jit(solution)/shard_map/ppermute | solution.py:187
  107.4 0.0 collective-permute-start.9
  107.4 2.9 %collective-permute-done.9.refs_1_ = bf16[1024,512]{1,0:T(8,128)(2,1)S(1)} collective-permute-done((bf16[1024,512]{1,0:T(8,128)(2,1)}, bf16[1024,512]{1,0:T(8,128)(2,1)S(1)}, u32[]{:S(2)}, u32[]{:S(2)}) %collective-permute-start.9) | collective-permute-done | bytes 1048608 | tf_op jit(solution)/shard_map/ppermute | solution.py:190
  110.2 1.0 copy-done.3
  111.2 4.5 %shard_map.66.weight_ref = bf16[8192,512]{1,0:T(8,128)(2,1)} custom-call(s32[128]{0:T(128)} %select_reduce_fusion.block_ref, bf16[8192,512]{1,0:T(8,128)(2,1)} %base_ref.3, bf16[1024,512]{1,0:T(8,128)(2,1)} %collective-permute-done.refs_0_, bf16[1024,512]{1,0:T(8,128)(2,1)} %copy-done.3, ...), custom_call_target="tpu_custom_call", output_to_operand_aliasing={{}: (4, {})} | custom-call | flops 1 | bytes 1 | tf_op jit(solution)/shard_map/pallas_call | solution.py:237
  115.7 6.4 %shard_map.67.refs_7_ = bf16[384,512]{1,0:T(8,128)(2,1)} custom-call(bf16[8192,512]{1,0:T(8,128)(2,1)} %shard_map.66.weight_ref, bf16[96,8192]{1,0:T(8,128)(2,1)} %refs_0_.3, bf16[96,8192]{1,0:T(8,128)(2,1)} %copy-done, bf16[96,8192]{1,0:T(8,128)(2,1)} %collective-permute-done.5.refs_2_, bf16[96,8192]{1,0:T(8,128)(2,1)} %copy-done.1, ...), custom_call_target="tpu_custom_call" | custom-call | flops 1 | bytes 1 | tf_op jit(solution)/shard_map/pallas_call | solution.py:272
  122.2 0.0 collective-permute-done.10.refs_3_
  122.2 1.3 %collective-permute-done.11.refs_6_ = bf16[96,8192]{1,0:T(8,128)(2,1)} collective-permute-done((bf16[96,8192]{1,0:T(8,128)(2,1)}, bf16[96,8192]{1,0:T(8,128)(2,1)}, u32[]{:S(2)}, u32[]{:S(2)}) %collective-permute-start.11) | collective-permute-done | bytes 1572896 | tf_op jit(solution)/shard_map/ppermute | solution.py:180
  123.5 5.1 %shard_map.68 = bf16[384,512]{1,0:T(8,128)(2,1)} custom-call(bf16[8192,512]{1,0:T(8,128)(2,1)} %shard_map.66.weight_ref, bf16[96,8192]{1,0:T(8,128)(2,1)} %refs_0_.3, bf16[96,8192]{1,0:T(8,128)(2,1)} %copy-done, bf16[96,8192]{1,0:T(8,128)(2,1)} %collective-permute-done.5.refs_2_, ...), custom_call_target="tpu_custom_call", output_to_operand_aliasing={{}: (8, {})} | custom-call | flops 1 | bytes 1 | tf_op jit(solution)/shard_map/pallas_call | solution.py:272
  (12 shorter events, 0.1 us)
Async XLA Ops:
  0.0 86.1 %copy-start.5 = (s32[4]{0:T(128)S(1)}, s32[4]{0:T(128)}, u32[]{:S(2)}) copy-start(s32[4]{0:T(128)} %param.10) | copy-start | bytes 52
  0.0 88.7 %copy-start.4 = (s32[2,64]{1,0:T(2,128)S(1)}, s32[2,64]{1,0:T(2,128)}, u32[]{:S(2)}) copy-start(s32[2,64]{1,0:T(2,128)} %param.11) | copy-start | bytes 1540
  0.0 39.0 %collective-permute-start.4 = (bf16[96,8192]{1,0:T(8,128)(2,1)}, bf16[96,8192]{1,0:T(8,128)(2,1)S(1)}, u32[]{:S(2)}, u32[]{:S(2)}) collective-permute-start(bf16[96,8192]{1,0:T(8,128)(2,1)} %refs_0_.3), channel_id=1, source_target_pairs={{0,1},{1,2},{2,3},{4,5},{5,6},{6,7},{8,9},{9,10},{10,11},{12,13},{... | collective-permute-start | bytes 4718600 | tf_op jit(solution)/shard_map/ppermute | solution.py:177
  5.2 38.0 %collective-permute-start.6 = (bf16[96,8192]{1,0:T(8,128)(2,1)}, bf16[96,8192]{1,0:T(8,128)(2,1)S(1)}, u32[]{:S(2)}, u32[]{:S(2)}) collective-permute-start(bf16[96,8192]{1,0:T(8,128)(2,1)} %refs_0_.3), channel_id=1, source_target_pairs={{1,0},{2,1},{3,2},{5,4},{6,5},{7,6},{9,8},{10,9},{11,10},{13,12},{... | collective-permute-start | bytes 4718600 | tf_op jit(solution)/shard_map/ppermute | solution.py:180
  11.4 70.0 %collective-permute-start.1 = (bf16[3072,512]{1,0:T(8,128)(2,1)}, bf16[3072,512]{1,0:T(8,128)(2,1)}, u32[]{:S(2)}, u32[]{:S(2)}) collective-permute-start(bf16[3072,512]{1,0:T(8,128)(2,1)} %get-tuple-element.18.refs_0_), channel_id=1, source_target_pairs={{0,8},{4,12},{8,0},{12,4},{1,9},{5,13},{9,1},{13,5},{2,10},{6,14},... | collective-permute-start | bytes 9437192 | tf_op jit(solution)/shard_map/ppermute | solution.py:187
  12.9 68.5 %collective-permute-start.2 = (bf16[3072,512]{1,0:T(8,128)(2,1)}, bf16[3072,512]{1,0:T(8,128)(2,1)}, u32[]{:S(2)}, u32[]{:S(2)}) collective-permute-start(bf16[3072,512]{1,0:T(8,128)(2,1)} %get-tuple-element.18.refs_0_), channel_id=1, source_target_pairs={{0,4},{4,0},{8,12},{12,8},{1,5},{5,1},{9,13},{13,9},{2,6},{6,2},{1... | collective-permute-start | bytes 9437192 | tf_op jit(solution)/shard_map/ppermute | solution.py:190
  39.0 61.8 %copy-start = (bf16[96,8192]{1,0:T(8,128)(2,1)}, bf16[96,8192]{1,0:T(8,128)(2,1)S(1)}, u32[]{:S(2)}) copy-start(bf16[96,8192]{1,0:T(8,128)(2,1)S(1)} %collective-permute-done.4.refs_1_) | copy-start | bytes 4718596
  39.0 8.3 %collective-permute-start.5 = (bf16[96,8192]{1,0:T(8,128)(2,1)S(1)}, bf16[96,8192]{1,0:T(8,128)(2,1)}, u32[]{:S(2)}, u32[]{:S(2)}) collective-permute-start(bf16[96,8192]{1,0:T(8,128)(2,1)S(1)} %collective-permute-done.4.refs_1_), channel_id=1, source_target_pairs={{1,2},{2,3},{5,6},{6,7},{9,10},{10,11},{13,14},{14,15},{17,18},{18... | collective-permute-start | bytes 4718600 | tf_op jit(solution)/shard_map/ppermute | solution.py:177
  43.1 57.7 %copy-start.1 = (bf16[96,8192]{1,0:T(8,128)(2,1)}, bf16[96,8192]{1,0:T(8,128)(2,1)S(1)}, u32[]{:S(2)}) copy-start(bf16[96,8192]{1,0:T(8,128)(2,1)S(1)} %collective-permute-done.6.refs_3_.refs_4_) | copy-start | bytes 4718596
  43.1 38.3 %collective-permute-start.7 = (bf16[96,8192]{1,0:T(8,128)(2,1)S(1)}, bf16[96,8192]{1,0:T(8,128)(2,1)}, u32[]{:S(2)}, u32[]{:S(2)}) collective-permute-start(bf16[96,8192]{1,0:T(8,128)(2,1)S(1)} %collective-permute-done.6.refs_3_.refs_4_), channel_id=1, source_target_pairs={{1,0},{2,1},{5,4},{6,5},{9,8},{10,9},{13,12},{14,13},{17,16},{18,1... | collective-permute-start | bytes 4718600 | tf_op jit(solution)/shard_map/ppermute | solution.py:180
  44.4 2.9 %collective-permute-start.3 = (bf16[1024,512]{1,0:T(8,128)(2,1)}, bf16[1024,512]{1,0:T(8,128)(2,1)S(1)}, u32[]{:S(2)}, u32[]{:S(2)}) collective-permute-start(bf16[1024,512]{1,0:T(8,128)(2,1)} %get-tuple-element.17.refs_1_), channel_id=1, source_target_pairs={{0,4},{4,0},{8,12},{12,8},{1,5},{5,1},{9,13},{13,9},{2,6},{6,2},{1... | collective-permute-start | bytes 3145736 | tf_op jit(solution)/shard_map/ppermute | solution.py:190
  47.4 34.0 %copy-start.2 = (bf16[1024,512]{1,0:T(8,128)(2,1)}, bf16[1024,512]{1,0:T(8,128)(2,1)S(1)}, u32[]{:S(2)}) copy-start(bf16[1024,512]{1,0:T(8,128)(2,1)S(1)} %collective-permute-done.3.refs_4_) | copy-start | bytes 3145732
  81.4 8.0 %collective-permute-start.8 = (bf16[3072,512]{1,0:T(8,128)(2,1)}, bf16[3072,512]{1,0:T(8,128)(2,1)}, u32[]{:S(2)}, u32[]{:S(2)}) collective-permute-start(bf16[3072,512]{1,0:T(8,128)(2,1)} %collective-permute-done.1.refs_2_), channel_id=1, source_target_pairs={{0,4},{4,0},{8,12},{12,8},{1,5},{5,1},{9,13},{13,9},{2,6},{6,2},{1... | collective-permute-start | bytes 9437192 | tf_op jit(solution)/shard_map/ppermute | solution.py:190
  81.5 25.9 %collective-permute-start = (bf16[1024,512]{1,0:T(8,128)(2,1)}, bf16[1024,512]{1,0:T(8,128)(2,1)}, u32[]{:S(2)}, u32[]{:S(2)}) collective-permute-start(bf16[1024,512]{1,0:T(8,128)(2,1)} %get-tuple-element.17.refs_1_), channel_id=1, source_target_pairs={{0,8},{4,12},{8,0},{12,4},{1,9},{5,13},{9,1},{13,5},{2,10},{6,14},... | collective-permute-start | bytes 3145736 | tf_op jit(solution)/shard_map/ppermute | solution.py:187
  83.0 39.1 %collective-permute-start.10 = (bf16[96,8192]{1,0:T(8,128)(2,1)}, bf16[96,8192]{1,0:T(8,128)(2,1)}, u32[]{:S(2)}, u32[]{:S(2)}) collective-permute-start(bf16[96,8192]{1,0:T(8,128)(2,1)} %collective-permute-done.5.refs_2_), channel_id=1, source_target_pairs={{2,3},{6,7},{10,11},{14,15},{18,19},{22,23},{26,27},{30,31}} | collective-permute-start | bytes 4718600 | tf_op jit(solution)/shard_map/ppermute | solution.py:177
  84.8 38.7 %collective-permute-start.11 = (bf16[96,8192]{1,0:T(8,128)(2,1)}, bf16[96,8192]{1,0:T(8,128)(2,1)}, u32[]{:S(2)}, u32[]{:S(2)}) collective-permute-start(bf16[96,8192]{1,0:T(8,128)(2,1)} %collective-permute-done.7.refs_4_.refs_5_), channel_id=1, source_target_pairs={{1,0},{5,4},{9,8},{13,12},{17,16},{21,20},{25,24},{29,28}} | collective-permute-start | bytes 4718600 | tf_op jit(solution)/shard_map/ppermute | solution.py:180
  107.4 2.9 %collective-permute-start.9 = (bf16[1024,512]{1,0:T(8,128)(2,1)}, bf16[1024,512]{1,0:T(8,128)(2,1)S(1)}, u32[]{:S(2)}, u32[]{:S(2)}) collective-permute-start(bf16[1024,512]{1,0:T(8,128)(2,1)} %collective-permute-done.refs_0_), channel_id=1, source_target_pairs={{0,4},{4,0},{8,12},{12,8},{1,5},{5,1},{9,13},{13,9},{2,6},{6,2},{1... | collective-permute-start | bytes 3145736 | tf_op jit(solution)/shard_map/ppermute | solution.py:190
  110.2 1.0 copy-start.3

commit v15 on v14

--- a/solution.py
+++ b/solution.py
@@ -89,7 +89,8 @@
     star = lax.rem(2 * rank + 1, ranks)
 
     def columns(chunk):
-        return pl.ds(pl.multiple_of(chunk * span, span), span)
+        start = chunk * span
+        return pl.ds(start if isinstance(start, int) else pl.multiple_of(start, span), span)
 
     def origin_rows(hop):
         return pl.ds(pl.multiple_of(lax.rem(rank - hop + ranks, ranks) * rows, rows), rows)
@@ -136,12 +137,17 @@
 
     total[...] = jnp.zeros_like(total)
 
-    @pl.loop(0, chunks)
-    def _(chunk):
+    def add(chunk):
         weight_copy(chunk).wait()
         each(lambda hop: token_copy(chunk, hop, own).wait())
         at = columns(chunk)
         total[...] += jnp.dot(token_buf[:, at], weight_buf[at, :], preferred_element_type=jnp.float32)
+
+    if last:
+        for chunk in range(chunks):
+            add(chunk)
+    else:
+        pl.loop(0, chunks)(add)
 
     if last:
         result = refs[-1]
@@ -257,20 +263,19 @@
     held[-1] = held[-1] + sent
     twins[-1] = twins[-1] + [turn(value) for value in sent]
     weight = merge(weight, [(chips - 1, piece) for piece in range(1, pieces)])
-    chunks = blocks // CHUNK_BLOCKS
-
     def product(arrays, prior):
         last = prior is not None
         count = 1 if last else ranks - 1
+        span = CHUNK_BLOCKS * block * (2 if last else 1)
         inputs = [weight] + arrays + ([prior] if last else [])
         scratch = [
             pltpu.VMEM((count * rows, depth), jnp.bfloat16),
             pltpu.VMEM((depth, width), jnp.bfloat16),
             pltpu.VMEM((count * rows, width), jnp.float32),
-            pltpu.SemaphoreType.DMA((chunks, ranks + 1)),
+            pltpu.SemaphoreType.DMA((depth // span, ranks + 1)),
         ]
         return pl.pallas_call(
-            functools.partial(product_kernel, (ranks, CHUNK_BLOCKS * block, last)),
+            functools.partial(product_kernel, (ranks, span, last)),
             out_shape=jax.ShapeDtypeStruct((ranks * rows, width), jnp.bfloat16),
             in_specs=[HBM] * len(inputs),
             out_specs=HBM if last else VMEM,

time: 129 us -> 129 us (level)
  no operation moved by 1% of the time
where the time goes in v15:
time: 129 us
  waiting for transfers between devices  76.1 us (59%)
  Pallas kernels  32.3 us (25%)
  starting transfers between devices  15.8 us (12%)
  between operations  2.1 us (2%)
  local copies, waits for them, and re-layouts  1.57 us (1%)
    ppermute x3, waiting for transfers between devices, left(): lax.ppermute(value, 'tp', [(i, i - 1) for i in range(1, ranks - hop + 1)])  37.5 us
    ppermute x3, waiting for transfers between devices, right(): lax.ppermute(value, 'tp', [(i, i + 1) for i in range(hop - 1, ranks - 1)])  26.1 us
    pallas_call x2, Pallas kernels, merge(): pl.pallas_call(functools.partial(merge_kernel, block, tuple(parts)), out_...  15.9 us
    pallas_call x2, Pallas kernels, product(): pl.pallas_call(functools.partial(product_kernel, (ranks, span, last)), ou...  11.5 us
    ppermute x3, starting transfers between devices, right(): lax.ppermute(value, 'tp', [(i, i + 1) for i in range(hop - 1, ranks - 1)])  8.78 us
    ppermute x2, waiting for transfers between devices, across(): return lax.ppermute(store, 'rep', ring)  6.77 us
    ppermute x4, waiting for transfers between devices, turn(): return lax.ppermute(store, 'rep', swap)  5.73 us
    pallas_call x1, Pallas kernels, local(): pl.pallas_call(functools.partial(scale_kernel, block), out_shape=[jax.Sha...  4.92 us
  transfers between devices with their start and end apart: 12, of which 7 were waited for; matrix products, arithmetic and copies ran while one was open for 1% of the time, Pallas kernels for 21%

profile of v15, /device:TPU:0, one launch (start us, length us, event | category | flops | bytes accessed | tf_op | source)
XLA Modules:
  0.0 128.6 jit_solution(3063218506271346460)
XLA Ops:
  0.0 5.1 %collective-permute-start.4 = (bf16[96,8192]{1,0:T(8,128)(2,1)}, bf16[96,8192]{1,0:T(8,128)(2,1)S(1)}, u32[]{:S(2)}, u32[]{:S(2)}) collective-permute-start(bf16[96,8192]{1,0:T(8,128)(2,1)} %refs_0_.3), channel_id=1, source_target_pairs={{0,1},{1,2},{2,3},{4,5},{5,6},{6,7},{8,9},{9,10},{10,11},{12,13},{... | collective-permute-start | bytes 4718600 | tf_op jit(solution)/shard_map/ppermute | solution.py:183
  5.2 1.3 %collective-permute-start.6 = (bf16[96,8192]{1,0:T(8,128)(2,1)}, bf16[96,8192]{1,0:T(8,128)(2,1)S(1)}, u32[]{:S(2)}, u32[]{:S(2)}) collective-permute-start(bf16[96,8192]{1,0:T(8,128)(2,1)} %refs_0_.3), channel_id=1, source_target_pairs={{1,0},{2,1},{3,2},{5,4},{6,5},{7,6},{9,8},{10,9},{11,10},{13,12},{... | collective-permute-start | bytes 4718600 | tf_op jit(solution)/shard_map/ppermute | solution.py:186
  6.5 4.9 %shard_map.64 = (bf16[3072,512]{1,0:T(8,128)(2,1)}, bf16[1024,512]{1,0:T(8,128)(2,1)}) custom-call(bf16[4,32]{1,0:T(4,128)(2,1)} %bitcast.4, bf16[4096,512]{1,0:T(8,128)(2,1)} %codes_ref.1), custom_call_target="tpu_custom_call" | custom-call | flops 1 | bytes 1 | tf_op jit(solution)/shard_map/pallas_call | solution.py:206
  11.4 1.5 %collective-permute-start.1 = (bf16[3072,512]{1,0:T(8,128)(2,1)}, bf16[3072,512]{1,0:T(8,128)(2,1)}, u32[]{:S(2)}, u32[]{:S(2)}) collective-permute-start(bf16[3072,512]{1,0:T(8,128)(2,1)} %get-tuple-element.18.refs_0_), channel_id=1, source_target_pairs={{0,8},{4,12},{8,0},{12,4},{1,9},{5,13},{9,1},{13,5},{2,10},{6,14},... | collective-permute-start | bytes 9437192 | tf_op jit(solution)/shard_map/ppermute | solution.py:193
  12.9 0.0 collective-permute-start.2
  12.9 26.1 %collective-permute-done.4.refs_1_ = bf16[96,8192]{1,0:T(8,128)(2,1)S(1)} collective-permute-done((bf16[96,8192]{1,0:T(8,128)(2,1)}, bf16[96,8192]{1,0:T(8,128)(2,1)S(1)}, u32[]{:S(2)}, u32[]{:S(2)}) %collective-permute-start.4) | collective-permute-done | bytes 1572896 | tf_op jit(solution)/shard_map/ppermute | solution.py:183
  39.0 1.8 %collective-permute-start.5 = (bf16[96,8192]{1,0:T(8,128)(2,1)S(1)}, bf16[96,8192]{1,0:T(8,128)(2,1)}, u32[]{:S(2)}, u32[]{:S(2)}) collective-permute-start(bf16[96,8192]{1,0:T(8,128)(2,1)S(1)} %collective-permute-done.4.refs_1_), channel_id=1, source_target_pairs={{1,2},{2,3},{5,6},{6,7},{9,10},{10,11},{13,14},{14,15},{17,18},{18... | collective-permute-start | bytes 4718600 | tf_op jit(solution)/shard_map/ppermute | solution.py:183
  40.8 2.3 %collective-permute-done.6.refs_3_.refs_4_ = bf16[96,8192]{1,0:T(8,128)(2,1)S(1)} collective-permute-done((bf16[96,8192]{1,0:T(8,128)(2,1)}, bf16[96,8192]{1,0:T(8,128)(2,1)S(1)}, u32[]{:S(2)}, u32[]{:S(2)}) %collective-permute-start.6) | collective-permute-done | bytes 1572896 | tf_op jit(solution)/shard_map/ppermute | solution.py:186
  43.1 1.3 collective-permute-start.7
  44.4 0.1 collective-permute-start.3
  44.5 2.9 %collective-permute-done.3.refs_4_ = bf16[1024,512]{1,0:T(8,128)(2,1)S(1)} collective-permute-done((bf16[1024,512]{1,0:T(8,128)(2,1)}, bf16[1024,512]{1,0:T(8,128)(2,1)S(1)}, u32[]{:S(2)}, u32[]{:S(2)}) %collective-permute-start.3) | collective-permute-done | bytes 1048608 | tf_op jit(solution)/shard_map/ppermute | solution.py:196
  47.4 0.0 collective-permute-done.5.refs_2_
  47.4 34.0 %collective-permute-done.7.refs_4_.refs_5_ = bf16[96,8192]{1,0:T(8,128)(2,1)} collective-permute-done((bf16[96,8192]{1,0:T(8,128)(2,1)S(1)}, bf16[96,8192]{1,0:T(8,128)(2,1)}, u32[]{:S(2)}, u32[]{:S(2)}) %collective-permute-start.7) | collective-permute-done | bytes 1572896 | tf_op jit(solution)/shard_map/ppermute | solution.py:186
  81.4 0.0 collective-permute-done.1.refs_2_
  81.4 0.0 collective-permute-done.2.refs_3_
  81.4 0.1 collective-permute-start.8
  81.5 1.6 %collective-permute-start = (bf16[1024,512]{1,0:T(8,128)(2,1)}, bf16[1024,512]{1,0:T(8,128)(2,1)}, u32[]{:S(2)}, u32[]{:S(2)}) collective-permute-start(bf16[1024,512]{1,0:T(8,128)(2,1)} %get-tuple-element.17.refs_1_), channel_id=1, source_target_pairs={{0,8},{4,12},{8,0},{12,4},{1,9},{5,13},{9,1},{13,5},{2,10},{6,14},... | collective-permute-start | bytes 3145736 | tf_op jit(solution)/shard_map/ppermute | solution.py:193
  83.0 1.8 %collective-permute-start.10 = (bf16[96,8192]{1,0:T(8,128)(2,1)}, bf16[96,8192]{1,0:T(8,128)(2,1)}, u32[]{:S(2)}, u32[]{:S(2)}) collective-permute-start(bf16[96,8192]{1,0:T(8,128)(2,1)} %collective-permute-done.5.refs_2_), channel_id=1, source_target_pairs={{2,3},{6,7},{10,11},{14,15},{18,19},{22,23},{26,27},{30,31}} | collective-permute-start | bytes 4718600 | tf_op jit(solution)/shard_map/ppermute | solution.py:183
  84.8 1.3 collective-permute-start.11
  86.1 0.6 dynamic_slice.6
  88.7 0.6 select_reduce_fusion.block_ref
  89.4 0.0 collective-permute-done.8.refs_5_
  89.4 11.2 %shard_map.65.refs_2_ = bf16[8192,512]{1,0:T(8,128)(2,1)} custom-call(s32[128]{0:T(128)} %select_reduce_fusion.block_ref, bf16[8192,512]{1,0:T(8,128)(2,1)} %base_ref.3, bf16[3072,512]{1,0:T(8,128)(2,1)} %get-tuple-element.18.refs_0_, bf16[1024,512]{1,0:T(8,128)(2,1)} %get-tuple-element.17.refs_1_, bf16[3072,512]{1,0:T(8,128)(2,1)} %collective-permute-done.1.refs_2_, ...), custom_call_target="tpu_custom_call" | custom-call | flops 1 | bytes 1 | tf_op jit(solution)/shard_map/pallas_call | solution.py:243
  100.6 6.8 %collective-permute-done.refs_0_ = bf16[1024,512]{1,0:T(8,128)(2,1)} collective-permute-done((bf16[1024,512]{1,0:T(8,128)(2,1)}, bf16[1024,512]{1,0:T(8,128)(2,1)}, u32[]{:S(2)}, u32[]{:S(2)}) %collective-permute-start) | collective-permute-done | bytes 1048608 | tf_op jit(solution)/shard_map/ppermute | solution.py:193
  107.4 0.0 collective-permute-start.9
  107.4 2.9 %collective-permute-done.9.refs_1_ = bf16[1024,512]{1,0:T(8,128)(2,1)S(1)} collective-permute-done((bf16[1024,512]{1,0:T(8,128)(2,1)}, bf16[1024,512]{1,0:T(8,128)(2,1)S(1)}, u32[]{:S(2)}, u32[]{:S(2)}) %collective-permute-start.9) | collective-permute-done | bytes 1048608 | tf_op jit(solution)/shard_map/ppermute | solution.py:196
  110.2 1.0 copy-done.3
  111.2 4.7 %shard_map.66.weight_ref = bf16[8192,512]{1,0:T(8,128)(2,1)} custom-call(s32[128]{0:T(128)} %select_reduce_fusion.block_ref, bf16[8192,512]{1,0:T(8,128)(2,1)} %base_ref.3, bf16[1024,512]{1,0:T(8,128)(2,1)} %collective-permute-done.refs_0_, bf16[1024,512]{1,0:T(8,128)(2,1)} %copy-done.3, ...), custom_call_target="tpu_custom_call", output_to_operand_aliasing={{}: (4, {})} | custom-call | flops 1 | bytes 1 | tf_op jit(solution)/shard_map/pallas_call | solution.py:243
  115.9 6.4 %shard_map.67.refs_7_ = bf16[384,512]{1,0:T(8,128)(2,1)} custom-call(bf16[8192,512]{1,0:T(8,128)(2,1)} %shard_map.66.weight_ref, bf16[96,8192]{1,0:T(8,128)(2,1)} %refs_0_.3, bf16[96,8192]{1,0:T(8,128)(2,1)} %copy-done, bf16[96,8192]{1,0:T(8,128)(2,1)} %collective-permute-done.5.refs_2_, bf16[96,8192]{1,0:T(8,128)(2,1)} %copy-done.1, ...), custom_call_target="tpu_custom_call" | custom-call | flops 1 | bytes 1 | tf_op jit(solution)/shard_map/pallas_call | solution.py:277
  122.3 0.0 collective-permute-done.10.refs_3_
  122.3 1.2 collective-permute-done.11.refs_6_
  123.5 5.1 %shard_map.68 = bf16[384,512]{1,0:T(8,128)(2,1)} custom-call(bf16[8192,512]{1,0:T(8,128)(2,1)} %shard_map.66.weight_ref, bf16[96,8192]{1,0:T(8,128)(2,1)} %refs_0_.3, bf16[96,8192]{1,0:T(8,128)(2,1)} %copy-done, bf16[96,8192]{1,0:T(8,128)(2,1)} %collective-permute-done.5.refs_2_, ...), custom_call_target="tpu_custom_call", output_to_operand_aliasing={{}: (8, {})} | custom-call | flops 1 | bytes 1 | tf_op jit(solution)/shard_map/pallas_call | solution.py:277
  (12 shorter events, 0.1 us)
Async XLA Ops:
  0.0 86.1 %copy-start.5 = (s32[4]{0:T(128)S(1)}, s32[4]{0:T(128)}, u32[]{:S(2)}) copy-start(s32[4]{0:T(128)} %param.10) | copy-start | bytes 52
  0.0 88.7 %copy-start.4 = (s32[2,64]{1,0:T(2,128)S(1)}, s32[2,64]{1,0:T(2,128)}, u32[]{:S(2)}) copy-start(s32[2,64]{1,0:T(2,128)} %param.11) | copy-start | bytes 1540
  0.0 39.0 %collective-permute-start.4 = (bf16[96,8192]{1,0:T(8,128)(2,1)}, bf16[96,8192]{1,0:T(8,128)(2,1)S(1)}, u32[]{:S(2)}, u32[]{:S(2)}) collective-permute-start(bf16[96,8192]{1,0:T(8,128)(2,1)} %refs_0_.3), channel_id=1, source_target_pairs={{0,1},{1,2},{2,3},{4,5},{5,6},{6,7},{8,9},{9,10},{10,11},{12,13},{... | collective-permute-start | bytes 4718600 | tf_op jit(solution)/shard_map/ppermute | solution.py:183
  5.2 38.0 %collective-permute-start.6 = (bf16[96,8192]{1,0:T(8,128)(2,1)}, bf16[96,8192]{1,0:T(8,128)(2,1)S(1)}, u32[]{:S(2)}, u32[]{:S(2)}) collective-permute-start(bf16[96,8192]{1,0:T(8,128)(2,1)} %refs_0_.3), channel_id=1, source_target_pairs={{1,0},{2,1},{3,2},{5,4},{6,5},{7,6},{9,8},{10,9},{11,10},{13,12},{... | collective-permute-start | bytes 4718600 | tf_op jit(solution)/shard_map/ppermute | solution.py:186
  11.4 70.0 %collective-permute-start.1 = (bf16[3072,512]{1,0:T(8,128)(2,1)}, bf16[3072,512]{1,0:T(8,128)(2,1)}, u32[]{:S(2)}, u32[]{:S(2)}) collective-permute-start(bf16[3072,512]{1,0:T(8,128)(2,1)} %get-tuple-element.18.refs_0_), channel_id=1, source_target_pairs={{0,8},{4,12},{8,0},{12,4},{1,9},{5,13},{9,1},{13,5},{2,10},{6,14},... | collective-permute-start | bytes 9437192 | tf_op jit(solution)/shard_map/ppermute | solution.py:193
  12.9 68.5 %collective-permute-start.2 = (bf16[3072,512]{1,0:T(8,128)(2,1)}, bf16[3072,512]{1,0:T(8,128)(2,1)}, u32[]{:S(2)}, u32[]{:S(2)}) collective-permute-start(bf16[3072,512]{1,0:T(8,128)(2,1)} %get-tuple-element.18.refs_0_), channel_id=1, source_target_pairs={{0,4},{4,0},{8,12},{12,8},{1,5},{5,1},{9,13},{13,9},{2,6},{6,2},{1... | collective-permute-start | bytes 9437192 | tf_op jit(solution)/shard_map/ppermute | solution.py:196
  39.0 61.6 %copy-start = (bf16[96,8192]{1,0:T(8,128)(2,1)}, bf16[96,8192]{1,0:T(8,128)(2,1)S(1)}, u32[]{:S(2)}) copy-start(bf16[96,8192]{1,0:T(8,128)(2,1)S(1)} %collective-permute-done.4.refs_1_) | copy-start | bytes 4718596
  39.0 8.3 %collective-permute-start.5 = (bf16[96,8192]{1,0:T(8,128)(2,1)S(1)}, bf16[96,8192]{1,0:T(8,128)(2,1)}, u32[]{:S(2)}, u32[]{:S(2)}) collective-permute-start(bf16[96,8192]{1,0:T(8,128)(2,1)S(1)} %collective-permute-done.4.refs_1_), channel_id=1, source_target_pairs={{1,2},{2,3},{5,6},{6,7},{9,10},{10,11},{13,14},{14,15},{17,18},{18... | collective-permute-start | bytes 4718600 | tf_op jit(solution)/shard_map/ppermute | solution.py:183
  43.1 57.5 %copy-start.1 = (bf16[96,8192]{1,0:T(8,128)(2,1)}, bf16[96,8192]{1,0:T(8,128)(2,1)S(1)}, u32[]{:S(2)}) copy-start(bf16[96,8192]{1,0:T(8,128)(2,1)S(1)} %collective-permute-done.6.refs_3_.refs_4_) | copy-start | bytes 4718596
  43.1 38.3 %collective-permute-start.7 = (bf16[96,8192]{1,0:T(8,128)(2,1)S(1)}, bf16[96,8192]{1,0:T(8,128)(2,1)}, u32[]{:S(2)}, u32[]{:S(2)}) collective-permute-start(bf16[96,8192]{1,0:T(8,128)(2,1)S(1)} %collective-permute-done.6.refs_3_.refs_4_), channel_id=1, source_target_pairs={{1,0},{2,1},{5,4},{6,5},{9,8},{10,9},{13,12},{14,13},{17,16},{18,1... | collective-permute-start | bytes 4718600 | tf_op jit(solution)/shard_map/ppermute | solution.py:186
  44.4 2.9 %collective-permute-start.3 = (bf16[1024,512]{1,0:T(8,128)(2,1)}, bf16[1024,512]{1,0:T(8,128)(2,1)S(1)}, u32[]{:S(2)}, u32[]{:S(2)}) collective-permute-start(bf16[1024,512]{1,0:T(8,128)(2,1)} %get-tuple-element.17.refs_1_), channel_id=1, source_target_pairs={{0,4},{4,0},{8,12},{12,8},{1,5},{5,1},{9,13},{13,9},{2,6},{6,2},{1... | collective-permute-start | bytes 3145736 | tf_op jit(solution)/shard_map/ppermute | solution.py:196
  47.4 34.0 %copy-start.2 = (bf16[1024,512]{1,0:T(8,128)(2,1)}, bf16[1024,512]{1,0:T(8,128)(2,1)S(1)}, u32[]{:S(2)}) copy-start(bf16[1024,512]{1,0:T(8,128)(2,1)S(1)} %collective-permute-done.3.refs_4_) | copy-start | bytes 3145732
  81.4 8.0 %collective-permute-start.8 = (bf16[3072,512]{1,0:T(8,128)(2,1)}, bf16[3072,512]{1,0:T(8,128)(2,1)}, u32[]{:S(2)}, u32[]{:S(2)}) collective-permute-start(bf16[3072,512]{1,0:T(8,128)(2,1)} %collective-permute-done.1.refs_2_), channel_id=1, source_target_pairs={{0,4},{4,0},{8,12},{12,8},{1,5},{5,1},{9,13},{13,9},{2,6},{6,2},{1... | collective-permute-start | bytes 9437192 | tf_op jit(solution)/shard_map/ppermute | solution.py:196
  81.5 25.9 %collective-permute-start = (bf16[1024,512]{1,0:T(8,128)(2,1)}, bf16[1024,512]{1,0:T(8,128)(2,1)}, u32[]{:S(2)}, u32[]{:S(2)}) collective-permute-start(bf16[1024,512]{1,0:T(8,128)(2,1)} %get-tuple-element.17.refs_1_), channel_id=1, source_target_pairs={{0,8},{4,12},{8,0},{12,4},{1,9},{5,13},{9,1},{13,5},{2,10},{6,14},... | collective-permute-start | bytes 3145736 | tf_op jit(solution)/shard_map/ppermute | solution.py:193
  83.0 39.3 %collective-permute-start.10 = (bf16[96,8192]{1,0:T(8,128)(2,1)}, bf16[96,8192]{1,0:T(8,128)(2,1)}, u32[]{:S(2)}, u32[]{:S(2)}) collective-permute-start(bf16[96,8192]{1,0:T(8,128)(2,1)} %collective-permute-done.5.refs_2_), channel_id=1, source_target_pairs={{2,3},{6,7},{10,11},{14,15},{18,19},{22,23},{26,27},{30,31}} | collective-permute-start | bytes 4718600 | tf_op jit(solution)/shard_map/ppermute | solution.py:183
  84.8 38.7 %collective-permute-start.11 = (bf16[96,8192]{1,0:T(8,128)(2,1)}, bf16[96,8192]{1,0:T(8,128)(2,1)}, u32[]{:S(2)}, u32[]{:S(2)}) collective-permute-start(bf16[96,8192]{1,0:T(8,128)(2,1)} %collective-permute-done.7.refs_4_.refs_5_), channel_id=1, source_target_pairs={{1,0},{5,4},{9,8},{13,12},{17,16},{21,20},{25,24},{29,28}} | collective-permute-start | bytes 4718600 | tf_op jit(solution)/shard_map/ppermute | solution.py:186
  107.4 2.9 %collective-permute-start.9 = (bf16[1024,512]{1,0:T(8,128)(2,1)}, bf16[1024,512]{1,0:T(8,128)(2,1)S(1)}, u32[]{:S(2)}, u32[]{:S(2)}) collective-permute-start(bf16[1024,512]{1,0:T(8,128)(2,1)} %collective-permute-done.refs_0_), channel_id=1, source_target_pairs={{0,4},{4,0},{8,12},{12,8},{1,5},{5,1},{9,13},{13,9},{2,6},{6,2},{1... | collective-permute-start | bytes 3145736 | tf_op jit(solution)/shard_map/ppermute | solution.py:196
  110.2 1.0 copy-start.3
